TPU v7x, 32 devices: a whole 2x2x4 slice. The times are simulated.
32 devices in a mesh: dp: 8 (over y, x, core), mp: 4 (over z).
Axes of the slice: x: 2, y: 2, z: 4, core: 2. Of those that a mesh axis runs over, the one named last changes fastest.
Arguments:
- tokens: bfloat16 [4096, 768], P(('dp', 'mp')), may hold values from -6 to 6
- page_lengths: int32 [8, 8], P('dp'), may hold values from 1 to 256, 512 in all within a row
- norm_gains: float32 [2, 768], replicated, may hold values from 0.1 to 1.9
- norm_biases: float32 [2, 768], replicated, may hold values from -1.5 to 1.5
- layer_scales: float32 [2, 768], replicated, may hold values from 0.5 to 2
- w_qkv: bfloat16 [768, 3, 768], P(None, None, 'mp'), may hold values from -0.3125 to 0.3125
- rel_table: float32 [32, 12], replicated, may hold values from -4 to 4
- w_out: bfloat16 [768, 768], P('mp'), may hold values from -0.875 to 0.875
- w_up: bfloat16 [768, 3072], P(None, 'mp'), may hold values from -0.21875 to 0.21875
- w_down: bfloat16 [3072, 768], P('mp'), may hold values from -0.109375 to 0.109375
- cotangent: bfloat16 [4096, 768], P(('dp', 'mp')), may hold values from -6 to 6
Outputs:
- output: bfloat16 [4096, 768], P(('dp', 'mp'))
- grad_input: bfloat16 [4096, 768], P(('dp', 'mp'))
- grad_norm_gains: float32 [2, 768], replicated
- grad_norm_biases: float32 [2, 768], replicated
- grad_layer_scales: float32 [2, 768], replicated
- grad_w_qkv: float32 [768, 3, 768], P('dp', None, 'mp')
- grad_rel_table: float32 [32, 12], replicated
- grad_w_out: float32 [768, 768], P('mp', 'dp')
- grad_w_up: float32 [768, 3072], P('dp', 'mp')
- grad_w_down: float32 [3072, 768], P('mp', 'dp')
Inputs may be any that keep to these rules, and one draw needn't show every extreme that they name: Each row of page_lengths sums to 512, and its largest entry is exactly 256; the last page of each row is padding.
All inputs are finite; a program needn't handle non-finite values.
Results may differ from a plain program's by a relative error of at most 0.013.
The roundings to bfloat16 on the way count: a program that leaves them out, or rounds other values in their place, can miss the bound.
Values may be sent and summed in bfloat16 or wider, within the bound.
No kernel may reach another device: no remote copies, remote signals or barrier semaphores. Data moves between devices by JAX's collectives and lax.ppermute only.
A program may use at most 128 MiB of HBM per device.

v0:
```python
import jax
import jax.numpy as jnp
from jax import lax
from jax.sharding import PartitionSpec as P

HEAD_DIM = 64


norm_eps = 1e-06
masked_score = -1000000000.0


def layer_norm(values, norm_gain, norm_shift):
    row_mean = jnp.mean(values, axis=-1, keepdims=True)
    centred = values - row_mean
    spread = jnp.mean(centred * centred, axis=-1, keepdims=True)
    return centred * lax.rsqrt(spread + norm_eps) * norm_gain + norm_shift


def gelu_exact(values):
    return jax.nn.gelu(values, approximate=False)


def page_layout(page_lengths, group_rows):
    page_ends = jnp.cumsum(page_lengths, dtype=jnp.int32)
    positions = jnp.arange(group_rows, dtype=jnp.int32)
    segment = jnp.sum(
        (positions[:, None] >= page_ends[None, :]).astype(jnp.int32), axis=1, dtype=jnp.int32
    )
    live_rows = segment < page_lengths.shape[0] - 1
    return (positions, segment, live_rows)


def body(
    tokens,
    page_lengths,
    norm_gains,
    norm_biases,
    layer_scales,
    w_qkv,
    rel_table,
    w_out,
    w_up,
    w_down,
    cotangent,
):
    local_rows = tokens.shape[0]
    group_rows = local_rows * lax.axis_size("mp")
    channels = w_qkv.shape[2]
    head_count = channels // HEAD_DIM
    buckets = rel_table.shape[0]
    half_span = buckets // 2
    head_first = lax.axis_index("mp") * head_count
    table_here = lax.dynamic_slice_in_dim(rel_table, head_first, head_count, 1)
    table_heads = table_here.T
    positions, segment, live_rows = page_layout(page_lengths[0], group_rows)
    block_rows = min(512, group_rows)
    block_count = group_rows // block_rows
    starts = jnp.arange(block_count, dtype=jnp.int32) * block_rows
    score_scale = HEAD_DIM ** (-0.5)
    labels = jnp.arange(buckets, dtype=jnp.int32)
    x_rows = tokens.astype(jnp.float32)

    def first_input():
        normed = layer_norm(x_rows, norm_gains[0], norm_biases[0]).astype(jnp.bfloat16)
        return lax.all_gather(normed, "mp", axis=0, tiled=True)

    def second_input(middle):
        normed = layer_norm(middle, norm_gains[1], norm_biases[1]).astype(jnp.bfloat16)
        return lax.all_gather(normed, "mp", axis=0, tiled=True)

    def project(gathered):
        packed = jnp.einsum(
            "td,dce->tce", gathered, w_qkv, preferred_element_type=jnp.float32
        ).astype(jnp.bfloat16)
        packed = packed.reshape(group_rows, 3, head_count, HEAD_DIM)
        return (packed[:, 0], packed[:, 1], packed[:, 2])

    def masked_scores(query_block, key_rows, start_row):
        raw_scores = (
            jnp.einsum("qhe,khe->hqk", query_block, key_rows, preferred_element_type=jnp.float32)
            * score_scale
        )
        query_pos = start_row + jnp.arange(block_rows, dtype=jnp.int32)
        bucket_ids = (
            jnp.clip(query_pos[:, None] - positions[None, :], -half_span, half_span - 1) + half_span
        )
        hits = bucket_ids[None, :, :, None] == labels
        bias_terms = jnp.sum(jnp.where(hits, table_heads[:, None, None, :], 0.0), axis=-1)
        raw_scores = raw_scores + bias_terms
        allowed = (segment[:, None] == segment[None, :]) & live_rows[None, :]
        return (jnp.where(allowed[None], raw_scores, masked_score), allowed, bucket_ids)

    gathered_first = first_input()
    queries, key_rows, value_rows = project(gathered_first)

    def attend_block(start_row):
        scores, allowed, bucket_ids = masked_scores(queries, key_rows, start_row)
        row_top = jnp.max(scores, axis=-1, keepdims=True)
        raised = jnp.exp(scores - row_top)
        row_total = jnp.sum(raised, axis=-1, keepdims=True)
        weights = (raised / row_total).astype(jnp.bfloat16)
        mixed_rows = jnp.einsum(
            "hqk,khe->qhe", weights, value_rows, preferred_element_type=jnp.float32
        )
        mixed_rows = jnp.where(live_rows[:, None, None], mixed_rows, 0.0).astype(jnp.bfloat16)
        return (mixed_rows, (row_top + jnp.log(row_total))[:, :, 0])

    mixed_all, lse_all = lax.map(attend_block, starts)
    attended = mixed_all.reshape(group_rows, channels)
    row_piece = attended
    attn_rows = lax.psum_scatter(
        jnp.dot(row_piece, w_out, preferred_element_type=jnp.float32),
        "mp",
        scatter_dimension=0,
        tiled=True,
    )
    middle = x_rows + layer_scales[0] * attn_rows
    gathered_second = second_input(middle)
    up_rows = jnp.dot(gathered_second, w_up, preferred_element_type=jnp.float32)
    act_rows = gelu_exact(up_rows).astype(jnp.bfloat16)
    row_piece = act_rows
    mlp_rows = lax.psum_scatter(
        jnp.dot(row_piece, w_down, preferred_element_type=jnp.float32).astype(jnp.bfloat16),
        "mp",
        scatter_dimension=0,
        tiled=True,
    ).astype(jnp.float32)
    output = (middle + layer_scales[1] * mlp_rows).astype(jnp.bfloat16)
    upstream = cotangent.astype(jnp.float32)
    grad_scale_mlp = jnp.sum(upstream * mlp_rows, axis=0)
    mlp_grad_rows = lax.all_gather(
        (upstream * layer_scales[1]).astype(jnp.bfloat16), "mp", axis=0, tiled=True
    )
    again_second = second_input(middle)
    up_again = jnp.dot(again_second, w_up, preferred_element_type=jnp.float32)
    act_again, gelu_back = jax.vjp(gelu_exact, up_again)
    act_low = act_again.astype(jnp.bfloat16)
    grad_w_down = jnp.einsum(
        "tf,td->fd", act_low, mlp_grad_rows, preferred_element_type=jnp.float32
    )
    act_grad = jnp.einsum("td,fd->tf", mlp_grad_rows, w_down, preferred_element_type=jnp.float32)
    up_grad = gelu_back(act_grad)[0].astype(jnp.bfloat16)
    grad_w_up = jnp.einsum("td,tf->df", again_second, up_grad, preferred_element_type=jnp.float32)
    row_piece = up_grad
    second_grad = lax.psum_scatter(
        jnp.einsum("tf,df->td", row_piece, w_up, preferred_element_type=jnp.float32),
        "mp",
        scatter_dimension=0,
        tiled=True,
    )
    unused, second_back = jax.vjp(layer_norm, middle, norm_gains[1], norm_biases[1])
    middle_norm_grad, grad_gain_two, grad_bias_two = second_back(second_grad)
    middle_grad = upstream + middle_norm_grad
    grad_scale_attn = jnp.sum(middle_grad * attn_rows, axis=0)
    attn_grad_rows = lax.all_gather(
        (middle_grad * layer_scales[0]).astype(jnp.bfloat16), "mp", axis=0, tiled=True
    )
    grad_w_out = jnp.einsum(
        "tc,td->cd", attended, attn_grad_rows, preferred_element_type=jnp.float32
    )
    attended_grad = jnp.einsum(
        "td,cd->tc", attn_grad_rows, w_out, preferred_element_type=jnp.float32
    ).astype(jnp.bfloat16)
    attended_grad = attended_grad.reshape(block_count, block_rows, head_count, HEAD_DIM)
    again_first = first_input()
    queries_again, keys_again, values_again = project(again_first)

    def back_block(carried, inputs):
        key_grads, value_grads, table_grads = carried
        start_row, row_lse, block_grad = inputs
        scores, allowed, bucket_ids = masked_scores(queries_again, keys_again, start_row)
        probs = jnp.exp(scores - row_lse[:, :, None])
        mixed_grad = jnp.where(live_rows[:, None, None], block_grad, jnp.zeros_like(block_grad))
        value_grads = value_grads + jnp.einsum(
            "hqk,qhe->khe",
            probs.astype(jnp.bfloat16),
            mixed_grad,
            preferred_element_type=jnp.float32,
        )
        probs_grad = jnp.einsum(
            "qhe,khe->hqk", mixed_grad, values_again, preferred_element_type=jnp.float32
        )
        score_grad = probs * (probs_grad - jnp.sum(probs_grad * probs, axis=-1, keepdims=True))
        score_grad = jnp.where(allowed[None], score_grad, 0.0).astype(jnp.bfloat16)
        query_grad = (
            jnp.einsum("hqk,khe->qhe", score_grad, keys_again, preferred_element_type=jnp.float32)
            * score_scale
        )
        key_grads = (
            key_grads
            + jnp.einsum(
                "hqk,qhe->khe", score_grad, queries_again, preferred_element_type=jnp.float32
            )
            * score_scale
        )
        hits = bucket_ids[None, :, :, None] == labels
        table_grads = table_grads + jnp.sum(
            jnp.where(hits, score_grad.astype(jnp.float32)[..., None], 0.0), axis=(1, 2)
        )
        return ((key_grads, value_grads, table_grads), query_grad)

    zero_rows = jnp.zeros((group_rows, head_count, HEAD_DIM), jnp.float32)
    zero_table = jnp.zeros((head_count, buckets), jnp.float32)
    carried, query_grads = lax.scan(
        back_block, (zero_rows, zero_rows, zero_table), (starts, lse_all, attended_grad)
    )
    key_grads, value_grads, table_grads = carried
    query_grads = query_grads.reshape(group_rows, head_count, HEAD_DIM)
    packed_grad = (
        jnp.stack([query_grads, key_grads, value_grads], axis=1)
        .reshape(group_rows, 3, channels)
        .astype(jnp.bfloat16)
    )
    grad_w_qkv = jnp.einsum(
        "td,tce->dce", again_first, packed_grad, preferred_element_type=jnp.float32
    )
    row_piece = packed_grad
    first_grad = lax.psum_scatter(
        jnp.einsum("tce,dce->td", row_piece, w_qkv, preferred_element_type=jnp.float32),
        "mp",
        scatter_dimension=0,
        tiled=True,
    )
    unused, first_back = jax.vjp(layer_norm, x_rows, norm_gains[0], norm_biases[0])
    input_norm_grad, grad_gain_one, grad_bias_one = first_back(first_grad)
    grad_input = (middle_grad + input_norm_grad).astype(jnp.bfloat16)
    full_table = lax.dynamic_update_slice_in_dim(
        jnp.zeros((buckets, rel_table.shape[1]), jnp.float32), table_grads.T, head_first, 1
    )
    grad_gains, grad_biases, grad_scales, grad_table = lax.psum(
        (
            jnp.stack([grad_gain_one, grad_gain_two]),
            jnp.stack([grad_bias_one, grad_bias_two]),
            jnp.stack([grad_scale_attn, grad_scale_mlp]),
            full_table,
        ),
        ("dp", "mp"),
    )
    summed_qkv, summed_out, summed_up, summed_down = (
        lax.psum_scatter(grad_w_qkv, "dp", scatter_dimension=0, tiled=True),
        lax.psum_scatter(grad_w_out, "dp", scatter_dimension=1, tiled=True),
        lax.psum_scatter(grad_w_up, "dp", scatter_dimension=0, tiled=True),
        lax.psum_scatter(grad_w_down, "dp", scatter_dimension=1, tiled=True),
    )
    return (
        output,
        grad_input,
        grad_gains,
        grad_biases,
        grad_scales,
        summed_qkv,
        grad_table,
        summed_out,
        summed_up,
        summed_down,
    )


def solution(mesh):
    placed = (
        P(("dp", "mp"), None),
        P("dp", None),
        P(),
        P(),
        P(),
        P(None, None, "mp"),
        P(),
        P("mp", None),
        P(None, "mp"),
        P("mp", None),
        P(("dp", "mp"), None),
    )
    return jax.shard_map(
        body,
        mesh=mesh,
        in_specs=placed,
        out_specs=(
            P(("dp", "mp"), None),
            P(("dp", "mp"), None),
            P(),
            P(),
            P(),
            P("dp", None, "mp"),
            P(),
            P("mp", "dp"),
            P("dp", "mp"),
            P("mp", "dp"),
        ),
        check_vma=False,
    )
```

profile of v0, /device:TPU:0, one launch (start us, length us, event | category | flops | bytes accessed | tf_op | source)
XLA Modules:
  0.0 537.8 jit_solution(17039175371282938372)
XLA Ops:
  7.3 0.1 clamp_add_fusion
  7.4 0.9 reduce-window.8
  8.3 1.0 convert_reduce_fusion
  9.4 1.1 fusion.37
  10.5 0.6 copy-done.36
  11.2 0.2 compare_and_fusion
  11.5 0.2 fusion.33
  11.7 21.3 %all_gather.14 = bf16[512,768]{1,0:T(8,128)(2,1)S(1)} all-gather(bf16[128,768]{1,0:T(8,128)(2,1)S(1)} %fusion.33), channel_id=1, replica_groups=mesh['dp'=8,'mp'=4] {'mp'}, dimensions={0}, use_global_device_ids=true | all-gather | bytes 983040 | tf_op jit(solution)/shard_map/all_gather | solution.py:66
  33.0 2.1 fusion.64
  35.2 8.6 %iota_compare_fusion = pred[512,512,32]{1,2,0:T(8,128)(4,1)} fusion(s32[512,512]{1,0:T(8,128)S(1)} %clamp_add_fusion), kind=kLoop, calls=%fused_computation.3 | loop fusion | flops 8388608 | bytes 9437184 | tf_op jit(solution)/shard_map/while/body/eval_jaxpr/eq | solution.py:88
  43.8 0.7 dynamic-slice_bitcast_fusion
  44.5 109.9 %select_reduce_fusion.1 = f32[3,512,512]{2,1,0:T(8,128)} fusion(f32[3,32]{1,0:T(4,128)S(1)} %dynamic-slice_bitcast_fusion, pred[512,512,32]{1,2,0:T(8,128)(4,1)} %iota_compare_fusion), kind=kLoop, calls=%fused_computation.2 | loop fusion | flops 49545216 | bytes 11534720 | tf_op jit(solution)/shard_map/while/body/eval_jaxpr/reduce_sum | solution.py:89
  154.4 3.6 copy.33
  158.0 2.8 fusion.63
  160.8 0.4 fusion.2
  161.3 1.3 copy-done.1
  162.6 0.7 fusion.23
  163.2 0.7 copy-done.17
  163.9 1.6 fusion.65
  165.7 25.2 %all_gather.16 = bf16[512,768]{1,0:T(8,128)(2,1)} all-gather(bf16[128,768]{1,0:T(8,128)(2,1)S(1)} %fusion.39), channel_id=1, replica_groups=mesh['dp'=8,'mp'=4] {'mp'}, dimensions={0}, use_global_device_ids=true | all-gather | bytes 983040 | tf_op jit(solution)/shard_map/all_gather | solution.py:132
  190.9 16.9 %reduce-scatter.11.cloned.1.call-done = f32[128,768]{1,0:T(8,128)} async-done(((f32[512,768]{1,0:T(8,128)}), f32[128,768]{1,0:T(8,128)}) %reduce-scatter.11.cloned.1.call-update) | async-done | bytes 393232 | tf_op jit(solution)/shard_map/reduce_scatter | solution.py:112
  207.7 1.2 fusion.62
  209.0 0.2 multiply_reduce_fusion.4
  209.2 0.1 add_convert_fusion.2
  209.3 18.7 %all_gather.15 = bf16[512,768]{1,0:T(8,128)(2,1)S(1)} all-gather(bf16[128,768]{1,0:T(8,128)(2,1)S(1)} %add_convert_fusion.2), channel_id=1, replica_groups=mesh['dp'=8,'mp'=4] {'mp'}, dimensions={0}, use_global_device_ids=true | all-gather | bytes 983040 | tf_op jit(solution)/shard_map/all_gather | solution.py:70
  228.0 0.8 fusion.66
  228.8 0.1 copy-done.4
  228.9 0.5 copy-done.8
  229.4 5.1 add_convert_fusion
  234.6 0.9 copy-done.16
  235.5 2.0 fusion.67
  237.6 2.1 multiply_convert_fusion
  239.7 1.7 convolution_convert_fusion
  241.5 30.9 %reduce-scatter.15.cloned.1.call-done = f32[128,768]{1,0:T(8,128)} async-done(((f32[512,768]{1,0:T(8,128)}), f32[128,768]{1,0:T(8,128)}) %reduce-scatter.15.cloned.1.call-update) | async-done | bytes 393232 | tf_op jit(solution)/shard_map/reduce_scatter | solution.py:146
  272.4 1.8 multiply_reduce_fusion.2
  274.2 22.8 %reduce-scatter.13.cloned.1.call-done = bf16[128,768]{1,0:T(8,128)(2,1)} async-done(((bf16[512,768]{1,0:T(8,128)(2,1)}), bf16[128,768]{1,0:T(8,128)(2,1)}) %reduce-scatter.13.cloned.1.call-update) | async-done | bytes 196624 | tf_op jit(solution)/shard_map/reduce_scatter | solution.py:123
  297.0 1.9 fusion.60
  299.0 0.8 multiply_reduce_fusion.1
  299.7 18.0 %all_gather.17 = bf16[512,768]{1,0:T(8,128)(2,1)S(1)} all-gather(bf16[128,768]{1,0:T(8,128)(2,1)S(1)} %get-tuple-element.113), channel_id=1, replica_groups=mesh['dp'=8,'mp'=4] {'mp'}, dimensions={0}, use_global_device_ids=true | all-gather | bytes 983040 | tf_op jit(solution)/shard_map/all_gather | solution.py:156
  317.8 1.1 convolution_convert_fusion.1
  318.9 1.3 convolution_bitcast_fusion.1
  320.2 0.3 reduce-scatter.17.cloned.1.call-start
  320.5 4.9 select_convert_fusion
  325.4 1.7 fusion.18
  327.1 1.4 fusion.17
  328.5 0.6 fusion.19
  329.2 0.6 copy-done.22
  329.8 2.0 convolution_bitcast_fusion
  331.9 3.7 fusion.69
  335.7 3.6 fusion.68
  339.3 2.2 copy.39
  341.5 0.7 stack.36
  342.2 3.6 fusion.24
  345.9 19.6 %select_reduce_fusion = f32[3,32]{1,0:T(4,128)S(1)} fusion(f32[3,512,512]{2,1,0:T(8,128)} %copy.39, pred[512,512,32]{1,2,0:T(8,128)(4,1)} %iota_compare_fusion), kind=kLoop, calls=%fused_computation.1 | loop fusion | flops 50331552 | bytes 11534720 | tf_op jit(solution)/shard_map/while/body/eval_jaxpr/reduce_sum | solution.py:198
  365.4 0.1 dynamic_update_slice.12
  365.6 1.6 copy.47
  367.3 24.9 %reduce-scatter.17.cloned.1.call-done = f32[128,768]{1,0:T(8,128)} async-done(((f32[512,768]{1,0:T(8,128)}), f32[128,768]{1,0:T(8,128)}) %reduce-scatter.17.cloned.1.call-update) | async-done | bytes 393232 | tf_op jit(solution)/shard_map/reduce_scatter | solution.py:219
  392.2 1.2 fusion.59
  393.4 1.3 fusion.34
  394.7 40.1 %all-reduce = (f32[2,768]{1,0:T(2,128)}, f32[2,768]{1,0:T(2,128)}, f32[2,768]{1,0:T(2,128)}, f32[32,12]{0,1:T(8,128)}) all-reduce(f32[2,768]{1,0:T(2,128)S(1)} %pad_maximum_fusion.3, f32[2,768]{1,0:T(2,128)S(1)} %pad_maximum_fusion.4, f32[2,768]{1,0:T(2,128)S(1)} %pad_maximum_fusion.5, ...), channel_id=1, replica_groups=mesh['dp'=8,'mp'=4] {'dp','mp'}, use_global_device_ids=true, to_apply=%region_20.21 | all-reduce | flops 4992 | bytes 39936 | tf_op jit(solution)/shard_map/psum | solution.py:231
  434.8 1.9 add_convert_fusion.1
  436.7 0.9 reduce-scatter.23.cloned.1.call-done
  437.6 46.9 %reduce-scatter.21.cloned.1.call-done = f32[96,768]{1,0:T(8,128)} async-done(((f32[768,768]{1,0:T(8,128)}), f32[96,768]{1,0:T(8,128)}) %reduce-scatter.21.cloned.1.call-update) | async-done | bytes 294928 | tf_op jit(solution)/shard_map/reduce_scatter | solution.py:243
  484.5 46.4 %reduce-scatter.19.cloned.1.call-done = f32[96,3,192]{2,0,1:T(8,128)} async-done(((f32[768,3,192]{2,0,1:T(8,128)}), f32[96,3,192]{2,0,1:T(8,128)}) %reduce-scatter.19.cloned.1.call-update) | async-done | bytes 221200 | tf_op jit(solution)/shard_map/reduce_scatter | solution.py:241
  (111 shorter events, 1.0 us)
Async XLA Ops:
  7.2 221.7 %copy-start = (bf16[768,768]{1,0:T(8,128)(2,1)S(1)}, bf16[768,768]{1,0:T(8,128)(2,1)}, u32[]{:S(2)}) copy-start(bf16[768,768]{1,0:T(8,128)(2,1)} %param.20) | copy-start | bytes 3538948
  7.2 4.3 copy-start.3
  7.2 4.2 copy-start.27
  7.2 4.2 copy-start.28
  7.2 200.5 %reduce-scatter.11.cloned.1.call-start = ((), (), s32[]{:S(2)}) async-start(), calls=%async_computation.8 | async-start | bytes 1966080 | tf_op jit(solution)/shard_map/reduce_scatter | solution.py:112
  9.4 25.7 %copy-start.25 = (f32[128]{0:T(128)}, f32[128]{0:T(128)S(1)}, u32[]{:S(2)}) copy-start(f32[128]{0:T(128)S(1)} %broadcast_multiply_fusion.1) | copy-start | bytes 1540
  10.5 0.6 copy-start.36
  10.5 24.6 %copy-start.30 = (f32[128]{0:T(128)}, f32[128]{0:T(128)S(1)}, u32[]{:S(2)}) copy-start(f32[128]{0:T(128)S(1)} %fusion.49) | copy-start | bytes 1540
  11.2 150.1 %copy-start.32 = (pred[512]{0:T(512)(128)(4,1)}, pred[512]{0:T(512)(128)(4,1)S(1)}, u32[]{:S(2)}) copy-start(pred[512]{0:T(512)(128)(4,1)S(1)} %broadcast_compare_fusion) | copy-start | bytes 1540
  11.5 146.6 %copy-start.13 = (pred[512,512]{0,1:T(8,128)(4,1)}, pred[512,512]{0,1:T(8,128)(4,1)S(1)}, u32[]{:S(2)}) copy-start(pred[512,512]{0,1:T(8,128)(4,1)S(1)} %compare_and_fusion) | copy-start | bytes 786436
  33.0 2.1 copy-start.7
  35.2 126.1 %copy-start.6 = (bf16[512,3,192]{0,2,1:T(8,128)(2,1)}, bf16[512,3,192]{0,2,1:T(8,128)(2,1)S(1)}, u32[]{:S(2)}) copy-start(bf16[512,3,192]{0,2,1:T(8,128)(2,1)S(1)} %convert_element_type.76) | copy-start | bytes 1769476
  160.8 1.8 copy-start.1
  162.6 1.4 copy-start.12
  163.2 0.7 copy-start.17
  163.9 1.7 copy-start.29
  163.9 1.7 copy-start.9
  165.5 106.9 %reduce-scatter.15.cloned.1.call-start = ((), (), s32[]{:S(2)}) async-start(), calls=%async_computation.10 | async-start | bytes 1966080 | tf_op jit(solution)/shard_map/reduce_scatter | solution.py:146
  207.7 20.3 %copy-start.38 = (bf16[768,768]{1,0:T(8,128)(2,1)S(1)}, bf16[768,768]{1,0:T(8,128)(2,1)}, u32[]{:S(2)}) copy-start(bf16[768,768]{1,0:T(8,128)(2,1)} %param.19) | copy-start | bytes 3538948
  228.0 0.9 copy-start.4
  228.0 1.4 copy-start.8
  229.4 5.2 copy-start.11
  234.6 0.9 copy-start.16
  237.5 59.5 %reduce-scatter.13.cloned.1.call-start = ((), (), s32[]{:S(2)}) async-start(), calls=%async_computation.9 | async-start | bytes 983040 | tf_op jit(solution)/shard_map/reduce_scatter | solution.py:123
  239.7 1.7 copy-start.5
  241.4 57.5 %copy-start.10 = (f32[128,768]{1,0:T(8,128)S(1)}, f32[128,768]{1,0:T(8,128)}, u32[]{:S(2)}) copy-start(f32[128,768]{1,0:T(8,128)} %reduce-scatter.11.cloned.1.call-done) | copy-start | bytes 1179652
  241.4 124.2 %reduce-scatter.25.cloned.1.call-start = ((), (), s32[]{:S(2)}) async-start(), calls=%async_computation.15 | async-start | bytes 884736
  297.0 1.9 copy-start.15
  298.9 19.9 %copy-start.34 = (f32[128]{0:T(128)}, f32[128]{0:T(128)S(1)}, u32[]{:S(2)}) copy-start(f32[128]{0:T(128)S(1)} %negate_multiply_fusion.2) | copy-start | bytes 1540
  299.0 19.9 %copy-start.18 = (bf16[3,64,512]{2,1,0:T(8,128)(2,1)S(1)}, bf16[3,64,512]{2,1,0:T(8,128)(2,1)}, u32[]{:S(2)}) copy-start(bf16[3,64,512]{2,1,0:T(8,128)(2,1)} %copy-done.17) | copy-start | bytes 589828
  320.2 71.9 %reduce-scatter.17.cloned.1.call-start = ((), (), s32[]{:S(2)}) async-start(), calls=%async_computation.11 | async-start | bytes 1966080 | tf_op jit(solution)/shard_map/reduce_scatter | solution.py:219
  325.3 3.1 copy-start.2
  325.4 3.1 copy-start.19
  325.4 3.1 copy-start.33
  327.1 2.1 copy-start.20
  328.5 0.7 copy-start.21
  328.5 1.3 copy-start.14
  329.1 0.7 copy-start.22
  331.8 105.8 %reduce-scatter.23.cloned.1.call-start = ((), (), s32[]{:S(2)}) async-start(), calls=%async_computation.14 | async-start | bytes 2654208 | tf_op jit(solution)/shard_map/reduce_scatter | solution.py:244
  335.6 148.9 %reduce-scatter.21.cloned.1.call-start = ((), (), s32[]{:S(2)}) async-start(), calls=%async_computation.13 | async-start | bytes 2654208 | tf_op jit(solution)/shard_map/reduce_scatter | solution.py:243
  339.3 2.2 copy-start.23
  339.3 2.9 copy-start.24
  339.3 191.7 %reduce-scatter.19.cloned.1.call-start = ((), (), s32[]{:S(2)}) async-start(), calls=%async_computation.12 | async-start | bytes 2654208 | tf_op jit(solution)/shard_map/reduce_scatter | solution.py:241
  345.8 46.3 %copy-start.26 = (f32[128]{0:T(128)S(1)}, f32[128]{0:T(128)}, u32[]{:S(2)}) copy-start(f32[128]{0:T(128)} %copy-done.25) | copy-start | bytes 1540
  345.8 47.5 %copy-start.37 = (f32[128]{0:T(128)S(1)}, f32[128]{0:T(128)}, u32[]{:S(2)}) copy-start(f32[128]{0:T(128)} %copy-done.36) | copy-start | bytes 1540
  345.8 47.6 %copy-start.31 = (f32[128]{0:T(128)S(1)}, f32[128]{0:T(128)}, u32[]{:S(2)}) copy-start(f32[128]{0:T(128)} %copy-done.30) | copy-start | bytes 1540
  345.9 89.0 %copy-start.35 = (f32[128]{0:T(128)S(1)}, f32[128]{0:T(128)}, u32[]{:S(2)}) copy-start(f32[128]{0:T(128)} %copy-done.34) | copy-start | bytes 1540
Sparse Core Ops, SparseCore 0:
  165.7 42.0 reduce-scatter.10
  237.6 34.7 reduce-scatter.14
  274.7 22.2 reduce-scatter.12
  320.3 34.3 reduce-scatter.24
  356.8 35.2 reduce-scatter.16
  395.9 41.6 reduce-scatter.22
  441.9 42.5 reduce-scatter.20
  488.4 42.4 reduce-scatter.18
where the time goes:
time: 539 us; the launch traced here: 538 us
  waiting for transfers between devices  190 us (35%)
  other arithmetic  155 us (29%)
  blocking collectives  123 us (23%)
  matrix products  40.6 us (8%)
  between operations  14.7 us (3%)
  local copies, waits for them, and re-layouts  13.9 us (3%)
    reduce_sum x1, other arithmetic, masked_scores(): jnp.sum(jnp.where(hits, table_heads[:, None, None, :], 0.0), axis=-1)  110 us
    reduce_scatter x1, waiting for transfers between devices, body(): lax.psum_scatter(grad_w_up, 'dp', scatter_dimension=0, tiled=True)  46.9 us
    reduce_scatter x1, waiting for transfers between devices, body(): lax.psum_scatter(grad_w_qkv, 'dp', scatter_dimension=0, tiled=True)  46.4 us
    psum x1, blocking collectives, body(): lax.psum((jnp.stack([grad_gain_one, grad_gain_two]), jnp.stack([grad_bias...  40.1 us
    reduce_scatter x1, waiting for transfers between devices, body(): lax.psum_scatter(jnp.einsum('tf,df->td', row_piece, w_up, preferred_eleme...  30.9 us
    all_gather x1, blocking collectives, body(): lax.all_gather((upstream * layer_scales[1]).astype(jnp.bfloat16), 'mp', a...  25.2 us
    reduce_scatter x1, waiting for transfers between devices, body(): lax.psum_scatter(jnp.einsum('tce,dce->td', row_piece, w_qkv, preferred_el...  24.9 us
    reduce_scatter x1, waiting for transfers between devices, body(): lax.psum_scatter(jnp.dot(row_piece, w_down, preferred_element_type=jnp.fl...  22.8 us
  transfers between devices with their start and end apart: 8, of which 7 were waited for; matrix products, arithmetic and copies ran while one was open for 10% of the time, Pallas kernels for 0%

commit v1 on v0

v1 whole, which is shorter than its diff:
```python
import jax
import jax.numpy as jnp
from jax import lax
from jax.experimental import pallas as pl
from jax.experimental.pallas import tpu as pltpu
from jax.sharding import PartitionSpec as P

HEAD_DIM = 64
norm_eps = 1e-06
masked_score = -1000000000.0
F32 = jnp.float32
BF16 = jnp.bfloat16
SMEM = pl.BlockSpec(memory_space=pltpu.SMEM)
VMEM = pl.BlockSpec(memory_space=pltpu.VMEM)
CHUNK = 64
GAIN0, BIAS0, GAIN1, BIAS1, SCALE0, SCALE1 = range(6)


def call(kernel, outs, args, n_smem=0, scratch=(), flops=0, limit=40):
    moved = sum(a.size * a.dtype.itemsize for a in args) + sum(
        o.size * o.dtype.itemsize for o in outs
    )
    return pl.pallas_call(
        kernel,
        out_shape=tuple(outs),
        in_specs=[SMEM] * n_smem + [VMEM] * (len(args) - n_smem),
        out_specs=tuple([VMEM] * len(outs)),
        scratch_shapes=list(scratch),
        compiler_params=pltpu.CompilerParams(vmem_limit_bytes=limit << 20),
        cost_estimate=pl.CostEstimate(flops=flops, bytes_accessed=moved, transcendentals=0),
    )(*args)


def like(shape, dtype):
    return jax.ShapeDtypeStruct(shape, dtype)


def nn(a, b):
    return lax.dot_general(a, b, (((1,), (0,)), ((), ())), preferred_element_type=F32)


def nt(a, b):
    return lax.dot_general(a, b, (((1,), (1,)), ((), ())), preferred_element_type=F32)


def fold(v):
    return jnp.sum(v.reshape(v.shape[0] // 8, 8, v.shape[1]), axis=0)


def across(v):
    return jnp.sum(v, axis=0, keepdims=True)


def passes(rows, step, start):
    return lax.fori_loop(0, rows // CHUNK, step, start)


def chunk(i):
    return pl.ds(pl.multiple_of(i * CHUNK, CHUNK), CHUNK)


def page_ids(lengths, shape, axis, dead):
    at = lax.broadcasted_iota(jnp.int32, shape, axis)
    page = jnp.zeros(shape, jnp.int32)
    end = jnp.int32(0)
    pages = lengths.shape[1]
    for p in range(pages):
        end = end + lengths[0, p]
        page = page + (at >= end).astype(jnp.int32)
    return jnp.where(page < pages - 1, page, dead)


def turn_kernel(wq, wu, wd, wq_o, wu_o, wd_o):
    wq_o[...] = wq[...].T
    wu_o[...] = wu[...].T
    wd_o[...] = wd[...].T


def out_weight_kernel(place, *refs):
    pieces, (w_o, wt_o) = refs[:-2], refs[-2:]
    m, d = place[0], place[1]
    rows, cols = pieces[0].shape[-2:]
    shard = rows * 4
    n = 0
    for c in range(2):
        for b in range(4):
            s = d ^ (c + 2 * b)
            half = s & 1
            quarter = (s >> 1) & 3
            ref = pieces[n]
            n += 1
            for k in range(4):
                at = pl.multiple_of((m ^ k) * shard + quarter * rows, 16)
                w_o[pl.ds(at, rows), pl.ds(pl.multiple_of(half * cols, 128), cols)] = ref[k]
    wt_o[...] = w_o[...].T


def head_kernel(
    place, lengths, table, x0, x1, x2, x3, cols, wq,
    xt_o, h1_o, stat_o, qkv_o, pt_o, att_o,
    score, ids, pattern,
):
    m = place[0]
    rows = x0.shape[0]
    width, tokens = xt_o.shape
    channels = att_o.shape[0]
    heads = channels // HEAD_DIM
    buckets = table.shape[0]
    half = buckets // 2
    for k, ref in enumerate((x0, x1, x2, x3)):
        at = pl.multiple_of((m ^ k) * rows, rows)
        xt_o[:, pl.ds(at, rows)] = ref[...].T

    def add(i, acc):
        return acc + fold(xt_o[chunk(i), :].astype(F32))

    zero = jnp.zeros((8, tokens), F32)
    mean = across(passes(width, add, zero)) / width

    def spread(i, acc):
        v = xt_o[chunk(i), :].astype(F32) - mean
        return acc + fold(v * v)

    rstd = lax.rsqrt(across(passes(width, spread, zero)) / width + norm_eps)
    stat_o[0:1, :] = mean
    stat_o[1:2, :] = rstd

    def norm(i, carry):
        v = (xt_o[chunk(i), :].astype(F32) - mean) * rstd
        w = cols[chunk(i), :]
        h1_o[chunk(i), :] = (v * w[:, GAIN0 : GAIN0 + 1] + w[:, BIAS0 : BIAS0 + 1]).astype(BF16)
        return carry

    passes(width, norm, 0)
    qkv_o[...] = nn(wq[...], h1_o[...]).astype(BF16)
    qkv_o[0:channels, :] = qkv_o[0:channels, :] * BF16(HEAD_DIM**-0.5)

    ids[...] = page_ids(lengths, ids.shape, 0, -2)
    own_ids = page_ids(lengths, (1, tokens), 1, -1)
    live = (own_ids >= 0).astype(F32)
    blk = 128
    n_blk = tokens // blk
    off = lax.broadcasted_iota(jnp.int32, (blk, blk), 1) - lax.broadcasted_iota(
        jnp.int32, (blk, blk), 0
    )

    def one_head(h, carry):
        col = m * heads + h
        low, high = table[0, col], table[buckets - 1, col]
        near = jnp.where(off >= half - 1, high, low)
        for b in range(1, buckets - 1):
            near = jnp.where(off == b - half, table[b, col], near)
        pattern[1] = near
        before = jnp.full((blk, blk), low, F32)
        for b in range(1, half):
            before = jnp.where(off - blk == b - half, table[b, col], before)
        pattern[0] = before
        after = jnp.full((blk, blk), high, F32)
        for b in range(half + 1, buckets - 1):
            after = jnp.where(off + blk == b - half, table[b, col], after)
        pattern[2] = after

        def rows_of(which):
            return pl.ds(pl.multiple_of(which * channels + h * HEAD_DIM, HEAD_DIM), HEAD_DIM)

        q, k, v = qkv_o[rows_of(0), :], qkv_o[rows_of(1), :], qkv_o[rows_of(2), :]
        score[...] = nn(k.T, q)
        for i in range(n_blk):
            lanes = slice(i * blk, (i + 1) * blk)
            query_id = own_ids[:, lanes]
            top = jnp.full((8, blk), -3e38, F32)
            for j in range(n_blk):
                at = slice(j * blk, (j + 1) * blk)
                if abs(i - j) <= 1:
                    bias = pattern[i - j + 1]
                else:
                    bias = low if i < j else high
                s = jnp.where(ids[at, :] == query_id, score[at, lanes] + bias, masked_score)
                score[at, lanes] = s
                top = jnp.maximum(top, jnp.max(s.reshape(blk // 8, 8, blk), axis=0))
            top = jnp.max(top, axis=0, keepdims=True)
            total = jnp.zeros((8, blk), F32)
            for j in range(n_blk):
                at = slice(j * blk, (j + 1) * blk)
                e = jnp.exp(score[at, lanes] - top)
                score[at, lanes] = e
                total = total + fold(e)
            scale = 1.0 / across(total)
            for j in range(n_blk):
                at = slice(j * blk, (j + 1) * blk)
                pt_o[h, at, lanes] = (score[at, lanes] * scale).astype(BF16)
        mixed = nn(v, pt_o[h]) * live
        att_o[pl.ds(pl.multiple_of(h * HEAD_DIM, HEAD_DIM), HEAD_DIM), :] = mixed.astype(BF16)
        return carry

    lax.fori_loop(0, heads, one_head, 0)


def middle_kernel(
    place, a0, a1, a2, a3, c0, c1, c2, c3, xt, cols, w_out, w_out_t, w_up, w_up_t, w_down,
    d0, d1, d2, d3, nb_o, h2_o, act_o, dup_o, gm_o, ga_o, at_o, dy_o, mid_o, vec_o,
    attn, mid, wide, other, sums,
):
    m = place[0]
    rows = c0.shape[0]
    channels = a0.shape[0]
    width, tokens = xt.shape
    hidden = w_up.shape[1]
    for k, (a, c) in enumerate(zip((a0, a1, a2, a3), (c0, c1, c2, c3))):
        at_o[pl.ds(pl.multiple_of((m ^ k) * channels, channels), channels), :] = a[...]
        dy_o[:, pl.ds(pl.multiple_of((m ^ k) * rows, rows), rows)] = c[...].T
    attn[...] = nn(w_out_t[...], at_o[...])
    zero = jnp.zeros((8, tokens), F32)

    def residual(i, acc):
        w = cols[chunk(i), :]
        v = xt[chunk(i), :].astype(F32) + w[:, SCALE0 : SCALE0 + 1] * attn[chunk(i), :]
        mid[chunk(i), :] = v
        gm_o[chunk(i), :] = (
            dy_o[chunk(i), :].astype(F32) * w[:, SCALE1 : SCALE1 + 1]
        ).astype(BF16)
        return acc + fold(v)

    mean = across(passes(width, residual, zero)) / width
    mid_o[...] = mid[:, pl.ds(pl.multiple_of(m * rows, rows), rows)]

    def spread(i, acc):
        v = mid[chunk(i), :] - mean
        return acc + fold(v * v)

    rstd = lax.rsqrt(across(passes(width, spread, zero)) / width + norm_eps)

    def norm(i, carry):
        w = cols[chunk(i), :]
        v = (mid[chunk(i), :] - mean) * rstd
        mid[chunk(i), :] = v
        h2_o[chunk(i), :] = (v * w[:, GAIN1 : GAIN1 + 1] + w[:, BIAS1 : BIAS1 + 1]).astype(BF16)
        return carry

    passes(width, norm, 0)
    wide[...] = nn(w_up_t[...], h2_o[...])
    other[...] = nn(w_down[...], gm_o[...])

    def gelu(i, carry):
        u = wide[chunk(i), :]
        cdf = 0.5 + 0.5 * lax.erf(u * (0.5**0.5))
        act_o[chunk(i), :] = (u * cdf).astype(BF16)
        slope = cdf + u * (jnp.exp(-0.5 * u * u) * 0.3989422804014327)
        dup_o[chunk(i), :] = (slope * other[chunk(i), :]).astype(BF16)
        return carry

    passes(hidden, gelu, 0)
    wide[...] = nn(w_up[...], dup_o[...])

    def gather(i, acc):
        d = wide[chunk(i), :]
        hat = mid[chunk(i), :]
        u = d * cols[chunk(i), :][:, GAIN1 : GAIN1 + 1]
        sums[chunk(i), 0:1] = jnp.sum(d * hat, axis=1, keepdims=True)
        sums[chunk(i), 1:2] = jnp.sum(d, axis=1, keepdims=True)
        return acc[0] + fold(u), acc[1] + fold(u * hat)

    first, second = passes(width, gather, (zero, zero))
    first, second = across(first) / width, across(second) / width
    lane = lax.broadcasted_iota(jnp.int32, (1, tokens), 1)
    mine = ((lane >= m * rows) & (lane < (m + 1) * rows)).astype(F32)

    def back(i, carry):
        w = cols[chunk(i), :]
        u = wide[chunk(i), :] * w[:, GAIN1 : GAIN1 + 1]
        v = rstd * (u - first - mid[chunk(i), :] * second)
        nb_o[chunk(i), :] = v
        v = v + mine * dy_o[chunk(i), :].astype(F32)
        sums[chunk(i), 2:3] = jnp.sum(v * attn[chunk(i), :], axis=1, keepdims=True)
        ga_o[chunk(i), :] = (v * w[:, SCALE0 : SCALE0 + 1]).astype(BF16)
        return carry

    passes(width, back, 0)
    other[...] = nn(w_out[...], ga_o[...])
    for k, ref in enumerate((d0, d1, d2, d3)):
        ref[...] = other[
            pl.ds(pl.multiple_of((m ^ k) * channels, channels), channels), :
        ].astype(BF16)
    turned = sums[...].T
    vec_o[...] = jnp.zeros(vec_o.shape, F32)
    vec_o[1:2, :] = turned[0:1, :]
    vec_o[3:4, :] = turned[1:2, :]
    vec_o[4:5, :] = turned[2:3, :]


def mlp_kernel(
    place, vec, act, dup, gm, ga, att, h2, dy, w_down_t,
    m0, m1, m2, m3, g_o, vec_o,
    mlp, sums,
):
    m = place[0]
    rows = m0.shape[1]
    width, tokens = dy.shape
    mlp[...] = nn(w_down_t[...], act[...])
    for k, ref in enumerate((m0, m1, m2, m3)):
        ref[...] = mlp[:, pl.ds(pl.multiple_of((m ^ k) * rows, rows), rows)].astype(BF16)

    def scale(i, carry):
        v = dy[chunk(i), :].astype(F32) * mlp[chunk(i), :]
        sums[chunk(i), 0:1] = jnp.sum(v, axis=1, keepdims=True)
        return carry

    passes(width, scale, 0)
    vec_o[...] = vec[...]
    vec_o[5:6, :] = sums[...].T[0:1, :]
    hidden = act.shape[0]
    g_o[:, 0:hidden] = nt(h2[...], dup[...]).astype(BF16)
    g_o[:, hidden : 2 * hidden] = nt(gm[...], act[...]).astype(BF16)
    g_o[:, 2 * hidden : 2 * hidden + width] = nt(ga[...], att[...]).astype(BF16)


def back_kernel(
    place, lengths, d0, d1, d2, d3, qkv, pt, xt, stat, nb, cols, wq_t, vec,
    p0, p1, p2, p3, dqkv_o, vec_o,
    score, ds, acc, buckets_of, wide, sums,
):
    m = place[0]
    channels, tokens = d0.shape
    heads = channels // HEAD_DIM
    width = xt.shape[0]
    rows = p0.shape[1]
    blk = 128
    n_blk = tokens // blk
    n_rows = buckets_of.shape[0]
    buckets = n_rows // heads
    half = buckets // 2
    live = (page_ids(lengths, (1, tokens), 1, -1) >= 0).astype(F32)
    off = lax.broadcasted_iota(jnp.int32, (blk, blk), 1) - lax.broadcasted_iota(
        jnp.int32, (blk, blk), 0
    )

    def one_head(h, carry):
        def rows_of(which):
            return pl.ds(pl.multiple_of(which * channels + h * HEAD_DIM, HEAD_DIM), HEAD_DIM)

        q, k, v = qkv[rows_of(0), :], qkv[rows_of(1), :], qkv[rows_of(2), :]
        mine = rows_of(0)
        d_att = (
            d0[mine, :].astype(F32) + d1[mine, :].astype(F32)
            + d2[mine, :].astype(F32) + d3[mine, :].astype(F32)
        )
        d_att = (d_att.astype(BF16).astype(F32) * live).astype(BF16)
        dqkv_o[rows_of(2), :] = nt(d_att, pt[h]).astype(BF16)
        score[...] = nn(v.T, d_att)
        acc[...] = jnp.zeros(acc.shape, F32)
        for i in range(n_blk):
            lanes = slice(i * blk, (i + 1) * blk)
            total = jnp.zeros((8, blk), F32)
            for j in range(n_blk):
                at = slice(j * blk, (j + 1) * blk)
                prod = score[at, lanes] * pt[h, at, lanes].astype(F32)
                score[at, lanes] = prod
                total = total + fold(prod)
            total = across(total)
            for j in range(n_blk):
                at = slice(j * blk, (j + 1) * blk)
                g = score[at, lanes] - pt[h, at, lanes].astype(F32) * total
                g = g.astype(BF16)
                ds[at, lanes] = g
                slot = max(min(i - j, 2), -2) + 2
                acc[slot] = acc[slot] + g.astype(F32)
        dqkv_o[rows_of(0), :] = (nn(k, ds[...]) * HEAD_DIM**-0.5).astype(BF16)
        dqkv_o[rows_of(1), :] = nt(q, ds[...]).astype(BF16)
        near, before, after = acc[2], acc[1], acc[3]
        corner_b, off_b = before[0:16, :], off[0:16, :] - blk
        corner_a, off_a = after[blk - 16 : blk, :], off[blk - 16 : blk, :] + blk
        first = h * buckets
        for b in range(buckets):
            if b == 0:
                v = fold(acc[0]) + fold(jnp.where(off - blk <= -half, before, 0.0))
                v = v + fold(jnp.where(off <= -half, near, 0.0))
            elif b == buckets - 1:
                v = fold(acc[4]) + fold(jnp.where(off + blk >= half - 1, after, 0.0))
                v = v + fold(jnp.where(off >= half - 1, near, 0.0))
            else:
                v = fold(jnp.where(off == b - half, near, 0.0))
                if b < half:
                    v = v + fold(jnp.where(off_b == b - half, corner_b, 0.0))
                elif b > half:
                    v = v + fold(jnp.where(off_a == b - half, corner_a, 0.0))
            buckets_of[pl.ds(first + b, 1), :] = across(v)
        return carry

    lax.fori_loop(0, heads, one_head, 0)
    wide[...] = nn(wq_t[...], dqkv_o[...])
    mean, rstd = stat[0:1, :], stat[1:2, :]
    zero = jnp.zeros((8, tokens), F32)

    def gather(i, part):
        d = wide[chunk(i), :]
        hat = (xt[chunk(i), :].astype(F32) - mean) * rstd
        u = d * cols[chunk(i), :][:, GAIN0 : GAIN0 + 1]
        sums[chunk(i), 0:1] = jnp.sum(d * hat, axis=1, keepdims=True)
        sums[chunk(i), 1:2] = jnp.sum(d, axis=1, keepdims=True)
        return part[0] + fold(u), part[1] + fold(u * hat)

    first, second = passes(width, gather, (zero, zero))
    first, second = across(first) / width, across(second) / width

    def back(i, carry):
        hat = (xt[chunk(i), :].astype(F32) - mean) * rstd
        u = wide[chunk(i), :] * cols[chunk(i), :][:, GAIN0 : GAIN0 + 1]
        wide[chunk(i), :] = nb[chunk(i), :] + rstd * (u - first - hat * second)
        return carry

    passes(width, back, 0)
    for k, ref in enumerate((p0, p1, p2, p3)):
        ref[...] = wide[:, pl.ds(pl.multiple_of((m ^ k) * rows, rows), rows)].astype(ref.dtype)
    turned = sums[...].T
    vec_o[...] = vec[...]
    vec_o[0:1, :] = turned[0:1, :]
    vec_o[2:3, :] = turned[1:2, :]
    each = jnp.sum(buckets_of[...], axis=1, keepdims=True)
    shape = (n_rows, width)
    lane = lax.broadcasted_iota(jnp.int32, shape, 1)
    row = lax.broadcasted_iota(jnp.int32, shape, 0)
    vec_o[6:7, :] = across(jnp.where(lane == row + m * n_rows, each, 0.0))


def qkv_grad_kernel(h1, dqkv, g_o):
    g_o[...] = nt(h1[...], dqkv[...]).astype(BF16)


def input_kernel(p0, p1, p2, p3, dy, out):
    total = p0[...] + p1[...].astype(F32) + p2[...].astype(F32) + p3[...].astype(F32)
    out[...] = (dy[...].astype(F32) + total.T).astype(BF16)


def output_kernel(m0, m1, m2, m3, mid, cols, out):
    total = m0[...].astype(F32) + m1[...].astype(F32) + m2[...].astype(F32) + m3[...].astype(F32)
    out[...] = (mid[...] + cols[:, SCALE1 : SCALE1 + 1] * total).T.astype(BF16)


def body(
    tokens,
    page_lengths,
    norm_gains,
    norm_biases,
    layer_scales,
    w_qkv,
    rel_table,
    w_out,
    w_up,
    w_down,
    cotangent,
):
    mp, dp = lax.axis_size("mp"), lax.axis_size("dp")
    rows, width = tokens.shape
    group = rows * mp
    channels = w_qkv.shape[2]
    hidden = w_up.shape[1]
    heads = channels // HEAD_DIM
    buckets = rel_table.shape[0]
    m, d = lax.axis_index("mp"), lax.axis_index("dp")
    place = jnp.stack([m, d]).astype(jnp.int32)

    def swap(v, k, axis="mp"):
        n = mp if axis == "mp" else dp
        return lax.ppermute(v, axis, [(i, i ^ k) for i in range(n)])

    def gathered(v):
        return [v] + [swap(v, k) for k in range(1, mp)]

    cols = jnp.concatenate(
        [norm_gains[0:1], norm_biases[0:1], norm_gains[1:2], norm_biases[1:2], layer_scales]
    ).T
    wq = jnp.transpose(w_qkv, (1, 2, 0)).reshape(3 * channels, width)

    x = gathered(tokens)

    piece_rows, piece_cols = channels // 4, width // 2
    piece = lax.dynamic_slice(
        w_out, (((d >> 1) & 3) * piece_rows, (d & 1) * piece_cols), (piece_rows, piece_cols)
    )
    part = jnp.stack(gathered(piece))
    one = swap(part, 4, "dp")
    two = swap(jnp.stack([part, one]), 2, "dp")
    mine4 = jnp.stack([part, two[0], one, two[1]])
    three = swap(mine4, 1, "dp")
    pieces = [mine4[i] for i in range(4)] + [three[i] for i in range(4)]
    w_out_full, w_out_t = call(
        out_weight_kernel,
        [like((width, width), BF16)] * 2,
        [place] + pieces,
        n_smem=1,
    )
    wq_t, w_up_t, w_down_t = call(
        turn_kernel,
        [like((width, 3 * channels), BF16), like((hidden, width), BF16), like((width, hidden), BF16)],
        [wq, w_up, w_down],
    )

    cot_after, x3 = lax.optimization_barrier((cotangent, x[3]))
    x[3] = x3
    dy = gathered(cot_after)
    xt, h1, stat, qkv, pt, att = call(
        head_kernel,
        [
            like((width, group), BF16),
            like((width, group), BF16),
            like((8, group), F32),
            like((3 * channels, group), BF16),
            like((heads, group, group), BF16),
            like((channels, group), BF16),
        ],
        [place, page_lengths, rel_table] + x + [cols, wq],
        n_smem=3,
        scratch=[
            pltpu.VMEM((group, group), F32),
            pltpu.VMEM((group, 128), jnp.int32),
            pltpu.VMEM((3, 128, 128), F32),
        ],
        flops=2 * group * width * 3 * channels + 4 * heads * group * group * HEAD_DIM,
    )
    atts = gathered(att)
    act_like = like((width, group), BF16)
    hid_like = like((hidden, group), BF16)
    d0, d1, d2, d3, nb, h2, act, dup, gm, ga, att_all, dy_t, mid, vec = call(
        middle_kernel,
        [like((channels, group), BF16)] * 4
        + [like((width, group), F32), act_like, hid_like, hid_like, act_like, act_like]
        + [act_like, act_like, like((width, rows), F32), like((8, width), F32)],
        [place] + atts + dy + [xt, cols, w_out_full, w_out_t, w_up, w_up_t, w_down],
        n_smem=1,
        scratch=[
            pltpu.VMEM((width, group), F32),
            pltpu.VMEM((width, group), F32),
            pltpu.VMEM((hidden, group), F32),
            pltpu.VMEM((hidden, group), F32),
            pltpu.VMEM((width, 128), F32),
        ],
        flops=10 * width * width * group,
    )
    d_att = [d0] + [swap(v, k) for k, v in ((1, d1), (2, d2), (3, d3))]
    m0, m1, m2, m3, grads, vec = call(
        mlp_kernel,
        [like((width, rows), BF16)] * 4
        + [like((width, 2 * hidden + width), BF16), like((8, width), F32)],
        [place, vec, act, dup, gm, ga, att_all, h2, dy_t, w_down_t],
        n_smem=1,
        scratch=[pltpu.VMEM((width, group), F32), pltpu.VMEM((width, 128), F32)],
        flops=8 * width * width * group,
    )
    mlp = [m0] + [swap(v, k) for k, v in ((1, m1), (2, m2), (3, m3))]

    p0, p1, p2, p3, dqkv, vec = call(
        back_kernel,
        [like((width, rows), F32)]
        + [like((width, rows), BF16)] * 3
        + [like((3 * channels, group), BF16), like((8, width), F32)],
        [place, page_lengths] + d_att + [qkv, pt, xt, stat, nb, cols, wq_t, vec],
        n_smem=2,
        scratch=[
            pltpu.VMEM((group, group), F32),
            pltpu.VMEM((group, group), BF16),
            pltpu.VMEM((5, 128, 128), F32),
            pltpu.VMEM((heads * buckets, 128), F32),
            pltpu.VMEM((width, group), F32),
            pltpu.VMEM((width, 128), F32),
        ],
        flops=2 * group * width * 3 * channels + 8 * heads * group * group * HEAD_DIM,
    )
    back = [p0] + [swap(v, k) for k, v in ((1, p1), (2, p2), (3, p3))]
    (qkv_grads,) = call(
        qkv_grad_kernel,
        [like((width, 3 * channels), BF16)],
        [h1, dqkv],
        flops=2 * group * width * 3 * channels,
    )

    def reduced(g):
        g = g.reshape(dp, width // dp, g.shape[1])
        bit = 1
        while bit < dp:
            g = g.reshape(g.shape[0] // 2, 2, width // dp, g.shape[-1])
            here = (d & bit) // bit
            sent = lax.dynamic_index_in_dim(g, 1 - here, 1, keepdims=False)
            kept = lax.dynamic_index_in_dim(g, here, 1, keepdims=False)
            g = kept.astype(F32) + swap(sent, bit, "dp").astype(F32)
            bit *= 2
            if bit < dp:
                g = g.astype(BF16)
        return g[0]

    grads = reduced(grads)
    qkv_grads = reduced(qkv_grads)
    out_grad = grads[:, 2 * hidden :]

    def out_part(k):
        return lax.dynamic_slice_in_dim(out_grad, (m ^ k) * channels, channels, 1)

    out_sum = out_part(0)
    for k in range(1, mp):
        out_sum = out_sum + swap(out_part(k).astype(BF16), k).astype(F32)

    bit = 1
    while bit < dp:
        vec = vec + swap(vec, bit, "dp")
        bit *= 2
    for k in (1, 2):
        vec = vec + swap(vec, k)

    (output,) = call(output_kernel, [like((rows, width), BF16)], mlp + [mid, cols])
    (grad_input,) = call(input_kernel, [like((rows, width), BF16)], back + [cotangent])
    grad_table = vec[6, : heads * mp * buckets].reshape(heads * mp, buckets).T
    return (
        output,
        grad_input,
        vec[0:2],
        vec[2:4],
        vec[4:6],
        qkv_grads.reshape(width // dp, 3, channels),
        grad_table,
        out_sum.T,
        grads[:, :hidden],
        grads[:, hidden : 2 * hidden].T,
    )


def solution(mesh):
    placed = (
        P(("dp", "mp"), None),
        P("dp", None),
        P(),
        P(),
        P(),
        P(None, None, "mp"),
        P(),
        P("mp", None),
        P(None, "mp"),
        P("mp", None),
        P(("dp", "mp"), None),
    )
    return jax.shard_map(
        body,
        mesh=mesh,
        in_specs=placed,
        out_specs=(
            P(("dp", "mp"), None),
            P(("dp", "mp"), None),
            P(),
            P(),
            P(),
            P("dp", None, "mp"),
            P(),
            P("mp", "dp"),
            P("dp", "mp"),
            P("mp", "dp"),
        ),
        check_vma=False,
    )
```

time: 539 us -> 217 us (0.40)
  other arithmetic: 155 us -> 9.61 us
  blocking collectives: 123 us -> 0 us
  waiting for transfers between devices: 190 us -> 74.2 us
  starting transfers between devices: 0.55 us -> 57.4 us
  matrix products: 40.6 us -> 0 us
  Pallas kernels: 0 us -> 38 us
  local copies, waits for them, and re-layouts: 13.9 us -> 36 us
  between operations: 14.7 us -> 1.1 us
    reduce_scatter x7 -> x0, waiting for transfers between devices: 190 us -> none  [the longest x1 46.9 us: body(): lax.psum_scatter(grad_w_up, 'dp', scatter_dimension=0, tiled=True)]
    reduce_sum x13 -> x0, other arithmetic: 141 us -> none  [the longest x1 110 us: masked_scores(): jnp.sum(jnp.where(hits, table_heads[:, None, None, :], 0.0), axis=-1)]
    all_gather x4 -> x0, blocking collectives: 83.2 us -> none  [the longest x1 25.2 us: body(): lax.all_gather((upstream * layer_scales[1]).astype(jnp.bfloat16), 'mp', a...]
    ppermute x0 -> x38, waiting for transfers between devices: none -> 74.2 us  [swap(): return lax.ppermute(v, axis, [(i, i ^ k) for i in range(n)])]
    ppermute x0 -> x38, starting transfers between devices: none -> 57.4 us  [swap(): return lax.ppermute(v, axis, [(i, i ^ k) for i in range(n)])]
    psum x1 -> x0, blocking collectives: 40.1 us -> none  [body(): lax.psum((jnp.stack([grad_gain_one, grad_gain_two]), jnp.stack([grad_bias...]
    pallas_call x0 -> x9, Pallas kernels: none -> 38 us  [call(): pl.pallas_call(kernel, out_shape=tuple(outs), in_specs=[SMEM] * n_smem +...]
    dot_general x15 -> x0, matrix products: 32.3 us -> none  [the longest x1 5.15 us: body(): jnp.einsum('td,fd->tf', mlp_grad_rows, w_down, preferred_element_type=jnp...]
  transfers between devices with their start and end apart: 8 -> 38, of which waited for: 7 -> 16; matrix products, arithmetic and copies ran while one was open for 10% -> 9% of each run, Pallas kernels for 0% -> 9%
where the time goes in v1:
time: 217 us; the launch traced here: 216 us
  waiting for transfers between devices  74.2 us (34%)
  starting transfers between devices  57.4 us (26%)
  Pallas kernels  38 us (18%)
  local copies, waits for them, and re-layouts  36 us (17%)
  other arithmetic  9.61 us (4%)
    ppermute x38, waiting for transfers between devices, swap(): return lax.ppermute(v, axis, [(i, i ^ k) for i in range(n)])  74.2 us
    ppermute x38, starting transfers between devices, swap(): return lax.ppermute(v, axis, [(i, i ^ k) for i in range(n)])  57.4 us
    pallas_call x9, Pallas kernels, call(): pl.pallas_call(kernel, out_shape=tuple(outs), in_specs=[SMEM] * n_smem +...  38 us
    unnamed x111, local copies, waits for them, and re-layouts  25.7 us
    convert_element_type x4, other arithmetic, reduced(): g = g.astype(BF16)  5.94 us
  transfers between devices with their start and end apart: 38, of which 16 were waited for; matrix products, arithmetic and copies ran while one was open for 9% of the time, Pallas kernels for 9%

profile of v1, /device:TPU:0, one launch (start us, length us, event | category | flops | bytes accessed | tf_op | source)
XLA Modules:
  0.0 216.2 jit_solution(3750570983873943432)
XLA Ops:
  1.5 3.0 %collective-permute-start.9 = (bf16[48,384]{1,0:T(8,128)(2,1)S(1)}, bf16[48,384]{1,0:T(8,128)(2,1)S(1)}, u32[]{:S(2)}, u32[]{:S(2)}) collective-permute-start(bf16[48,384]{1,0:T(8,128)(2,1)S(1)} %dynamic_slice.49), channel_id=1, source_target_pairs={{0,1},{1,0},{2,3},{3,2},{4,5},{5,4},{6,7},{7,6},{8,9},{9,8},{10,11... | collective-permute-start | bytes 110600 | tf_op jit(solution)/shard_map/ppermute | solution.py:464
  4.5 2.6 %collective-permute-start.10 = (bf16[48,384]{1,0:T(8,128)(2,1)S(1)}, bf16[48,384]{1,0:T(8,128)(2,1)S(1)}, u32[]{:S(2)}, u32[]{:S(2)}) collective-permute-start(bf16[48,384]{1,0:T(8,128)(2,1)S(1)} %dynamic_slice.49), channel_id=1, source_target_pairs={{0,2},{1,3},{2,0},{3,1},{4,6},{5,7},{6,4},{7,5},{8,10},{9,11},{10,... | collective-permute-start | bytes 110600 | tf_op jit(solution)/shard_map/ppermute | solution.py:464
  7.9 2.2 collective-permute-done.10
  10.0 2.8 %collective-permute-done.11 = bf16[48,384]{1,0:T(8,128)(2,1)S(1)} collective-permute-done((bf16[48,384]{1,0:T(8,128)(2,1)S(1)}, bf16[48,384]{1,0:T(8,128)(2,1)S(1)}, u32[]{:S(2)}, u32[]{:S(2)}) %collective-permute-start.11) | collective-permute-done | bytes 36896 | tf_op jit(solution)/shard_map/ppermute | solution.py:464
  12.9 1.6 collective-permute-start.12
  14.5 3.6 %collective-permute-done.12.refs_2_ = bf16[4,48,384]{2,1,0:T(8,128)(2,1)S(1)} collective-permute-done((bf16[4,48,384]{2,1,0:T(8,128)(2,1)S(1)}, bf16[4,48,384]{2,1,0:T(8,128)(2,1)S(1)}, u32[]{:S(2)}, u32[]{:S(2)}) %collective-permute-start.12) | collective-permute-done | bytes 147488 | tf_op jit(solution)/shard_map/ppermute | solution.py:464
  18.1 1.6 collective-permute-start.13
  20.2 3.9 %collective-permute-start.1 = (bf16[128,768]{1,0:T(8,128)(2,1)}, bf16[128,768]{1,0:T(8,128)(2,1)S(1)}, u32[]{:S(2)}, u32[]{:S(2)}) collective-permute-start(bf16[128,768]{1,0:T(8,128)(2,1)} %x0.1), channel_id=1, source_target_pairs={{0,2},{1,3},{2,0},{3,1},{4,6},{5,7},{6,4},{7,5},{8,10},{9,11},{10,... | collective-permute-start | bytes 589832 | tf_op jit(solution)/shard_map/ppermute | solution.py:464
  25.7 0.9 pad_maximum_fusion
  27.0 2.6 %collective-permute-done.2.x3 = bf16[128,768]{1,0:T(8,128)(2,1)S(1)} collective-permute-done((bf16[128,768]{1,0:T(8,128)(2,1)}, bf16[128,768]{1,0:T(8,128)(2,1)S(1)}, u32[]{:S(2)}, u32[]{:S(2)}) %collective-permute-start.2) | collective-permute-done | bytes 196640 | tf_op jit(solution)/shard_map/ppermute | solution.py:464
  31.0 4.9 %collective-permute-done.1.x2 = bf16[128,768]{1,0:T(8,128)(2,1)S(1)} collective-permute-done((bf16[128,768]{1,0:T(8,128)(2,1)}, bf16[128,768]{1,0:T(8,128)(2,1)S(1)}, u32[]{:S(2)}, u32[]{:S(2)}) %collective-permute-start.1) | collective-permute-done | bytes 196640 | tf_op jit(solution)/shard_map/ppermute | solution.py:464
  36.6 1.2 copy-done.6
  37.7 0.9 copy-done.30
  38.6 0.9 copy-done.43
  39.6 0.9 copy-done.45
  40.5 0.9 copy-done.47
  41.4 6.9 %shard_map.186 = (bf16[768,512]{1,0:T(8,128)(2,1)S(1)}, bf16[768,512]{1,0:T(8,128)(2,1)S(1)}, f32[8,512]{1,0:T(8,128)S(1)}, bf16[576,512]{1,0:T(8,128)(2,1)S(1)}...) custom-call(s32[2]{0:T(128)S(1)} %pad_add_fusion.place, s32[1,8]{1,0:T(1,128)S(1)} %copy-done.24, ...), custom_call_target="tpu_custom_call" | custom-call | flops 654311424 | bytes 5639720 | tf_op jit(solution)/shard_map/pallas_call | solution.py:23
  51.0 1.3 copy-done.3
  52.2 1.2 copy-done.7
  54.3 0.9 copy-done.4
  55.3 1.0 copy-done.26
  56.3 1.0 copy-done.28
  57.3 1.1 collective-permute-start.4
  58.4 3.3 %collective-permute-start.5 = (bf16[192,512]{1,0:T(8,128)(2,1)}, bf16[192,512]{1,0:T(8,128)(2,1)S(1)}, u32[]{:S(2)}, u32[]{:S(2)}) collective-permute-start(bf16[192,512]{1,0:T(8,128)(2,1)} %get-tuple-element.50.a0), channel_id=1, source_target_pairs={{0,3},{1,2},{2,1},{3,0},{4,7},{5,6},{6,5},{7,4},{8,11},{9,10},{10,... | collective-permute-start | bytes 589832 | tf_op jit(solution)/shard_map/ppermute | solution.py:464
  61.7 1.1 collective-permute-start.7
  62.8 3.3 %collective-permute-start.8 = (bf16[128,768]{1,0:T(8,128)(2,1)}, bf16[128,768]{1,0:T(8,128)(2,1)S(1)}, u32[]{:S(2)}, u32[]{:S(2)}) collective-permute-start(bf16[128,768]{1,0:T(8,128)(2,1)} %dy.1), channel_id=1, source_target_pairs={{0,3},{1,2},{2,1},{3,0},{4,7},{5,6},{6,5},{7,4},{8,11},{9,10},{10,... | collective-permute-start | bytes 589832 | tf_op jit(solution)/shard_map/ppermute | solution.py:464
  66.1 1.2 slice_bitcast_fusion.1
  69.1 1.0 shard_map.187
  70.1 4.7 %collective-permute-done.4.a2 = bf16[192,512]{1,0:T(8,128)(2,1)S(1)} collective-permute-done((bf16[192,512]{1,0:T(8,128)(2,1)}, bf16[192,512]{1,0:T(8,128)(2,1)S(1)}, u32[]{:S(2)}, u32[]{:S(2)}) %collective-permute-start.4) | collective-permute-done | bytes 196640 | tf_op jit(solution)/shard_map/ppermute | solution.py:464
  74.8 12.6 %collective-permute-done.7.c2 = bf16[128,768]{1,0:T(8,128)(2,1)S(1)} collective-permute-done((bf16[128,768]{1,0:T(8,128)(2,1)}, bf16[128,768]{1,0:T(8,128)(2,1)S(1)}, u32[]{:S(2)}, u32[]{:S(2)}) %collective-permute-start.7) | collective-permute-done | bytes 196640 | tf_op jit(solution)/shard_map/ppermute | solution.py:464
  87.5 1.3 copy-done.29
  88.7 12.9 %shard_map.189 = (bf16[192,512]{1,0:T(8,128)(2,1)S(1)}, bf16[192,512]{1,0:T(8,128)(2,1)S(1)}, bf16[192,512]{1,0:T(8,128)(2,1)S(1)}, bf16[192,512]{1,0:T(8,128)(2...) custom-call(s32[2]{0:T(128)S(1)} %pad_add_fusion.place, ...), custom_call_target="tpu_custom_call" | custom-call | flops 3019898880 | bytes 16558088 | tf_op jit(solution)/shard_map/pallas_call | solution.py:23
  102.4 5.0 %shard_map.190 = (bf16[768,128]{1,0:T(8,128)(2,1)S(1)}, bf16[768,128]{1,0:T(8,128)(2,1)S(1)}, bf16[768,128]{1,0:T(8,128)(2,1)S(1)}, bf16[768,128]{1,0:T(8,128)(2...) custom-call(s32[2]{0:T(128)S(1)} %pad_add_fusion.place, f32[8,768]{1,0:T(8,128)S(1)} %get-tuple-element.56.vec, ...), custom_call_target="tpu_custom_call" | custom-call | flops 2415919104 | bytes 11059208 | tf_op jit(solution)/shard_map/pallas_call | solution.py:23
  109.5 1.4 dynamic-slice_bitcast_fusion
  111.2 3.5 %collective-permute-start.18 = (bf16[192,512]{1,0:T(8,128)(2,1)S(1)}, bf16[192,512]{1,0:T(8,128)(2,1)S(1)}, u32[]{:S(2)}, u32[]{:S(2)}) collective-permute-start(bf16[192,512]{1,0:T(8,128)(2,1)S(1)} %get-tuple-element.71), channel_id=1, source_target_pairs={{0,1},{1,0},{2,3},{3,2},{4,5},{5,4},{6,7},{7,6},{8,9},{9,8},{10,11... | collective-permute-start | bytes 589832 | tf_op jit(solution)/shard_map/ppermute | solution.py:464
  114.7 2.4 %collective-permute-start.20 = (bf16[192,512]{1,0:T(8,128)(2,1)S(1)}, bf16[192,512]{1,0:T(8,128)(2,1)S(1)}, u32[]{:S(2)}, u32[]{:S(2)}) collective-permute-start(bf16[192,512]{1,0:T(8,128)(2,1)S(1)} %get-tuple-element.73), channel_id=1, source_target_pairs={{0,3},{1,2},{2,1},{3,0},{4,7},{5,6},{6,5},{7,4},{8,11},{9,10},{10,... | collective-permute-start | bytes 589832 | tf_op jit(solution)/shard_map/ppermute | solution.py:464
  117.1 6.2 %collective-permute-done.18.d1 = bf16[192,512]{1,0:T(8,128)(2,1)S(1)} collective-permute-done((bf16[192,512]{1,0:T(8,128)(2,1)S(1)}, bf16[192,512]{1,0:T(8,128)(2,1)S(1)}, u32[]{:S(2)}, u32[]{:S(2)}) %collective-permute-start.18) | collective-permute-done | bytes 196640 | tf_op jit(solution)/shard_map/ppermute | solution.py:464
  123.3 8.5 %collective-permute-done.19.d2 = bf16[192,512]{1,0:T(8,128)(2,1)S(1)} collective-permute-done((bf16[192,512]{1,0:T(8,128)(2,1)S(1)}, bf16[192,512]{1,0:T(8,128)(2,1)S(1)}, u32[]{:S(2)}, u32[]{:S(2)}) %collective-permute-start.19) | collective-permute-done | bytes 196640 | tf_op jit(solution)/shard_map/ppermute | solution.py:464
  131.9 8.6 %shard_map.192 = (f32[768,128]{1,0:T(8,128)S(1)}, bf16[768,128]{1,0:T(8,128)(2,1)S(1)}, bf16[768,128]{1,0:T(8,128)(2,1)S(1)}, bf16[768,128]{1,0:T(8,128)(2,1)S(1...) custom-call(s32[2]{0:T(128)S(1)} %copy-done.23, s32[1,8]{1,0:T(1,128)S(1)} %copy-done.25, ...), custom_call_target="tpu_custom_call" | custom-call | flops 855638016 | bytes 7850024 | tf_op jit(solution)/shard_map/pallas_call | solution.py:23
  143.3 1.2 collective-permute-done.24
  145.0 4.1 %collective-permute-start.15 = (bf16[768,128]{1,0:T(8,128)(2,1)}, bf16[768,128]{1,0:T(8,128)(2,1)S(1)}, u32[]{:S(2)}, u32[]{:S(2)}) collective-permute-start(bf16[768,128]{1,0:T(8,128)(2,1)} %copy-done.41), channel_id=1, source_target_pairs={{0,1},{1,0},{2,3},{3,2},{4,5},{5,4},{6,7},{7,6},{8,9},{9,8},{10,11... | collective-permute-start | bytes 589832 | tf_op jit(solution)/shard_map/ppermute | solution.py:464
  149.1 1.6 collective-permute-start.26
  151.5 1.5 collective-permute-done.26
  153.0 3.2 %collective-permute-start.27 = (f32[8,768]{1,0:T(8,128)S(1)}, f32[8,768]{1,0:T(8,128)S(1)}, u32[]{:S(2)}, u32[]{:S(2)}) collective-permute-start(f32[8,768]{1,0:T(8,128)S(1)} %add.100), channel_id=1, source_target_pairs={{0,1},{1,0},{2,3},{3,2},{4,5},{5,4},{6,7},{7,6},{8,9},{9,8},{10,11... | collective-permute-start | bytes 73736 | tf_op jit(solution)/shard_map/ppermute | solution.py:464
  156.2 2.4 %fusion = bf16[4,96,2304]{2,1,0:T(8,128)(2,1)S(1)} fusion(bf16[4,96,2304]{2,1,0:T(8,128)(2,1)} %collective-permute-done.32, bf16[4,2,96,2304]{3,2,1,0:T(8,128)(2,1)} %bitcast.69, s32[]{:T(128)S(6)} %select_n.62), kind=kLoop, calls=%fused_computation.1 | loop fusion | flops 3538944 | bytes 5308420 | tf_op jit(solution)/shard_map/convert_element_type | solution.py:587
  158.7 1.0 dynamic-slice_bitcast_fusion.1
  161.1 2.4 %collective-permute-start.17 = (bf16[768,128]{1,0:T(8,128)(2,1)S(1)}, bf16[768,128]{1,0:T(8,128)(2,1)S(1)}, u32[]{:S(2)}, u32[]{:S(2)}) collective-permute-start(bf16[768,128]{1,0:T(8,128)(2,1)S(1)} %copy-done.38), channel_id=1, source_target_pairs={{0,3},{1,2},{2,1},{3,0},{4,7},{5,6},{6,5},{7,4},{8,11},{9,10},{10,... | collective-permute-start | bytes 589832 | tf_op jit(solution)/shard_map/ppermute | solution.py:464
  164.1 1.1 collective-permute-start.28
  165.1 12.6 %collective-permute-done.16.m2 = bf16[768,128]{1,0:T(8,128)(2,1)S(1)} collective-permute-done((bf16[768,128]{1,0:T(8,128)(2,1)S(1)}, bf16[768,128]{1,0:T(8,128)(2,1)S(1)}, u32[]{:S(2)}, u32[]{:S(2)}) %collective-permute-start.16) | collective-permute-done | bytes 196640 | tf_op jit(solution)/shard_map/ppermute | solution.py:464
  177.7 5.0 %collective-permute-start.22 = (bf16[768,128]{1,0:T(8,128)(2,1)S(1)}, bf16[768,128]{1,0:T(8,128)(2,1)S(1)}, u32[]{:S(2)}, u32[]{:S(2)}) collective-permute-start(bf16[768,128]{1,0:T(8,128)(2,1)S(1)} %copy-done.34), channel_id=1, source_target_pairs={{0,2},{1,3},{2,0},{3,1},{4,6},{5,7},{6,4},{7,5},{8,10},{9,11},{10,... | collective-permute-start | bytes 589832 | tf_op jit(solution)/shard_map/ppermute | solution.py:464
  182.8 0.9 shard_map.191
  183.7 2.1 collective-permute-start.23
  187.2 1.1 fusion.2
  188.4 1.6 collective-permute-start.30
  190.0 1.4 fusion.1
  192.1 1.5 collective-permute-start.34
  194.4 2.6 %collective-permute-done.22.p2 = bf16[768,128]{1,0:T(8,128)(2,1)S(1)} collective-permute-done((bf16[768,128]{1,0:T(8,128)(2,1)S(1)}, bf16[768,128]{1,0:T(8,128)(2,1)S(1)}, u32[]{:S(2)}, u32[]{:S(2)}) %collective-permute-start.22) | collective-permute-done | bytes 196640 | tf_op jit(solution)/shard_map/ppermute | solution.py:464
  197.8 1.0 fusion.3
  198.8 1.6 collective-permute-start.31
  200.4 4.6 %collective-permute-done.34 = bf16[1,96,2304]{2,1,0:T(8,128)(2,1)} collective-permute-done((bf16[1,96,2304]{2,1,0:T(8,128)(2,1)}, bf16[1,96,2304]{2,1,0:T(8,128)(2,1)}, u32[]{:S(2)}, u32[]{:S(2)}) %collective-permute-start.34) | collective-permute-done | bytes 442400 | tf_op jit(solution)/shard_map/ppermute | solution.py:464
  205.0 1.1 add_bitcast_fusion
  207.2 2.3 %collective-permute-start.36 = (bf16[96,192]{1,0:T(8,128)(2,1)S(1)}, bf16[96,192]{1,0:T(8,128)(2,1)S(1)}, u32[]{:S(2)}, u32[]{:S(2)}) collective-permute-start(bf16[96,192]{1,0:T(8,128)(2,1)S(1)} %get-tuple-element.137), channel_id=1, source_target_pairs={{0,2},{1,3},{2,0},{3,1},{4,6},{5,7},{6,4},{7,5},{8,10},{9,11},{10,... | collective-permute-start | bytes 110600 | tf_op jit(solution)/shard_map/ppermute | solution.py:464
  209.5 2.1 collective-permute-start.37
  212.7 2.7 %collective-permute-done.37 = bf16[96,192]{1,0:T(8,128)(2,1)S(1)} collective-permute-done((bf16[96,192]{1,0:T(8,128)(2,1)S(1)}, bf16[96,192]{1,0:T(8,128)(2,1)S(1)}, u32[]{:S(2)}, u32[]{:S(2)}) %collective-permute-start.37) | collective-permute-done | bytes 36896 | tf_op jit(solution)/shard_map/ppermute | solution.py:464
  (167 shorter events, 27.7 us)
Async XLA Ops:
  0.6 26.0 %copy-start.52 = (f32[2,768]{1,0:T(2,128)S(1)}, f32[2,768]{1,0:T(2,128)}, u32[]{:S(2)}) copy-start(f32[2,768]{1,0:T(2,128)} %param.13) | copy-start | bytes 18436
  0.7 25.9 %copy-start.51 = (f32[2,768]{1,0:T(2,128)S(1)}, f32[2,768]{1,0:T(2,128)}, u32[]{:S(2)}) copy-start(f32[2,768]{1,0:T(2,128)} %param.14) | copy-start | bytes 18436
  0.7 26.0 %copy-start.53 = (f32[2,768]{1,0:T(2,128)S(1)}, f32[2,768]{1,0:T(2,128)}, u32[]{:S(2)}) copy-start(f32[2,768]{1,0:T(2,128)} %param.15) | copy-start | bytes 18436
  1.5 6.4 %collective-permute-start.9 = (bf16[48,384]{1,0:T(8,128)(2,1)S(1)}, bf16[48,384]{1,0:T(8,128)(2,1)S(1)}, u32[]{:S(2)}, u32[]{:S(2)}) collective-permute-start(bf16[48,384]{1,0:T(8,128)(2,1)S(1)} %dynamic_slice.49), channel_id=1, source_target_pairs={{0,1},{1,0},{2,3},{3,2},{4,5},{5,4},{6,7},{7,6},{8,9},{9,8},{10,11... | collective-permute-start | bytes 110600 | tf_op jit(solution)/shard_map/ppermute | solution.py:464
  4.5 5.5 %collective-permute-start.10 = (bf16[48,384]{1,0:T(8,128)(2,1)S(1)}, bf16[48,384]{1,0:T(8,128)(2,1)S(1)}, u32[]{:S(2)}, u32[]{:S(2)}) collective-permute-start(bf16[48,384]{1,0:T(8,128)(2,1)S(1)} %dynamic_slice.49), channel_id=1, source_target_pairs={{0,2},{1,3},{2,0},{3,1},{4,6},{5,7},{6,4},{7,5},{8,10},{9,11},{10,... | collective-permute-start | bytes 110600 | tf_op jit(solution)/shard_map/ppermute | solution.py:464
  7.1 5.8 %collective-permute-start.11 = (bf16[48,384]{1,0:T(8,128)(2,1)S(1)}, bf16[48,384]{1,0:T(8,128)(2,1)S(1)}, u32[]{:S(2)}, u32[]{:S(2)}) collective-permute-start(bf16[48,384]{1,0:T(8,128)(2,1)S(1)} %dynamic_slice.49), channel_id=1, source_target_pairs={{0,3},{1,2},{2,1},{3,0},{4,7},{5,6},{6,5},{7,4},{8,11},{9,10},{10,... | collective-permute-start | bytes 110600 | tf_op jit(solution)/shard_map/ppermute | solution.py:464
  12.8 14.0 %copy-start.50 = (f32[32,12]{0,1:T(8,128)S(1)}, f32[32,12]{0,1:T(8,128)}, u32[]{:S(2)}) copy-start(f32[32,12]{0,1:T(8,128)} %param.17) | copy-start | bytes 4612
  12.8 23.7 %copy-start.24 = (s32[1,8]{1,0:T(1,128)S(1)}, s32[1,8]{1,0:T(1,128)}, u32[]{:S(2)}) copy-start(s32[1,8]{1,0:T(1,128)} %lengths.3) | copy-start | bytes 100
  12.9 5.2 %collective-permute-start.12 = (bf16[4,48,384]{2,1,0:T(8,128)(2,1)S(1)}, bf16[4,48,384]{2,1,0:T(8,128)(2,1)S(1)}, u32[]{:S(2)}, u32[]{:S(2)}) collective-permute-start(bf16[4,48,384]{2,1,0:T(8,128)(2,1)S(1)} %get-tuple-element.143.refs_0_), channel_id=1, source_target_pairs={{0,16},{4,20},{8,24},{12,28},{16,0},{20,4},{24,8},{28,12},{1,17},{... | collective-permute-start | bytes 442376 | tf_op jit(solution)/shard_map/ppermute | solution.py:464
  18.1 6.8 %collective-permute-start.13 = (bf16[2,4,48,384]{3,2,1,0:T(8,128)(2,1)S(1)}, bf16[2,4,48,384]{3,2,1,0:T(8,128)(2,1)S(1)}, u32[]{:S(2)}, u32[]{:S(2)}) collective-permute-start(bf16[2,4,48,384]{3,2,1,0:T(8,128)(2,1)S(1)} %pad_maximum_fusion.1), channel_id=1, source_target_pairs={{0,8},{4,12},{8,0},{12,4},{16,24},{20,28},{24,16},{28,20},{1,9},{5... | collective-permute-start | bytes 884744 | tf_op jit(solution)/shard_map/ppermute | solution.py:464
  19.7 9.9 %collective-permute-start.2 = (bf16[128,768]{1,0:T(8,128)(2,1)}, bf16[128,768]{1,0:T(8,128)(2,1)S(1)}, u32[]{:S(2)}, u32[]{:S(2)}) collective-permute-start(bf16[128,768]{1,0:T(8,128)(2,1)} %x0.1), channel_id=1, source_target_pairs={{0,3},{1,2},{2,1},{3,0},{4,7},{5,6},{6,5},{7,4},{8,11},{9,10},{10,... | collective-permute-start | bytes 589832 | tf_op jit(solution)/shard_map/ppermute | solution.py:464
  20.2 10.1 %collective-permute-start = (bf16[128,768]{1,0:T(8,128)(2,1)}, bf16[128,768]{1,0:T(8,128)(2,1)S(1)}, u32[]{:S(2)}, u32[]{:S(2)}) collective-permute-start(bf16[128,768]{1,0:T(8,128)(2,1)} %x0.1), channel_id=1, source_target_pairs={{0,1},{1,0},{2,3},{3,2},{4,5},{5,4},{6,7},{7,6},{8,9},{9,8},{10,11... | collective-permute-start | bytes 589832 | tf_op jit(solution)/shard_map/ppermute | solution.py:464
  20.2 15.7 %collective-permute-start.1 = (bf16[128,768]{1,0:T(8,128)(2,1)}, bf16[128,768]{1,0:T(8,128)(2,1)S(1)}, u32[]{:S(2)}, u32[]{:S(2)}) collective-permute-start(bf16[128,768]{1,0:T(8,128)(2,1)} %x0.1), channel_id=1, source_target_pairs={{0,2},{1,3},{2,0},{3,1},{4,6},{5,7},{6,4},{7,5},{8,10},{9,11},{10,... | collective-permute-start | bytes 589832 | tf_op jit(solution)/shard_map/ppermute | solution.py:464
  26.6 24.4 %copy-start.2 = (bf16[768,768]{1,0:T(8,128)(2,1)S(1)}, bf16[768,768]{1,0:T(8,128)(2,1)}, u32[]{:S(2)}) copy-start(bf16[768,768]{1,0:T(8,128)(2,1)} %w_up.1) | copy-start | bytes 3538948
  26.6 36.2 %collective-permute-start.14 = (bf16[4,4,48,384]{3,2,1,0:T(8,128)(2,1)}, bf16[4,4,48,384]{3,2,1,0:T(8,128)(2,1)}, u32[]{:S(2)}, u32[]{:S(2)}) collective-permute-start(bf16[4,4,48,384]{3,2,1,0:T(8,128)(2,1)} %pad_maximum_fusion), channel_id=1, source_target_pairs={{0,4},{4,0},{8,12},{12,8},{16,20},{20,16},{24,28},{28,24},{1,5},{5... | collective-permute-start | bytes 1769480 | tf_op jit(solution)/shard_map/ppermute | solution.py:464
  27.0 75.4 %copy-start.22 = (s32[2]{0:T(128)}, s32[2]{0:T(128)S(1)}, u32[]{:S(2)}) copy-start(s32[2]{0:T(128)S(1)} %pad_add_fusion.place) | copy-start | bytes 28
  51.0 10.7 %collective-permute-start.3 = (bf16[192,512]{1,0:T(8,128)(2,1)}, bf16[192,512]{1,0:T(8,128)(2,1)}, u32[]{:S(2)}, u32[]{:S(2)}) collective-permute-start(bf16[192,512]{1,0:T(8,128)(2,1)} %get-tuple-element.50.a0), channel_id=1, source_target_pairs={{0,1},{1,0},{2,3},{3,2},{4,5},{5,4},{6,7},{7,6},{8,9},{9,8},{10,11... | collective-permute-start | bytes 589832 | tf_op jit(solution)/shard_map/ppermute | solution.py:464
  57.3 30.1 %copy-start.11 = (bf16[768,512]{1,0:T(8,128)(2,1)S(1)}, bf16[768,512]{1,0:T(8,128)(2,1)}, u32[]{:S(2)}) copy-start(bf16[768,512]{1,0:T(8,128)(2,1)} %copy-done.10) | copy-start | bytes 2359300
  57.3 30.1 %copy-start.20 = (bf16[128,768]{1,0:T(8,128)(2,1)S(1)}, bf16[128,768]{1,0:T(8,128)(2,1)}, u32[]{:S(2)}) copy-start(bf16[128,768]{1,0:T(8,128)(2,1)} %dy.1) | copy-start | bytes 589828
  57.3 17.5 %collective-permute-start.4 = (bf16[192,512]{1,0:T(8,128)(2,1)}, bf16[192,512]{1,0:T(8,128)(2,1)S(1)}, u32[]{:S(2)}, u32[]{:S(2)}) collective-permute-start(bf16[192,512]{1,0:T(8,128)(2,1)} %get-tuple-element.50.a0), channel_id=1, source_target_pairs={{0,2},{1,3},{2,0},{3,1},{4,6},{5,7},{6,4},{7,5},{8,10},{9,11},{10,... | collective-permute-start | bytes 589832 | tf_op jit(solution)/shard_map/ppermute | solution.py:464
  58.4 16.4 %collective-permute-start.5 = (bf16[192,512]{1,0:T(8,128)(2,1)}, bf16[192,512]{1,0:T(8,128)(2,1)S(1)}, u32[]{:S(2)}, u32[]{:S(2)}) collective-permute-start(bf16[192,512]{1,0:T(8,128)(2,1)} %get-tuple-element.50.a0), channel_id=1, source_target_pairs={{0,3},{1,2},{2,1},{3,0},{4,7},{5,6},{6,5},{7,4},{8,11},{9,10},{10,... | collective-permute-start | bytes 589832 | tf_op jit(solution)/shard_map/ppermute | solution.py:464
  61.7 13.1 %collective-permute-start.6 = (bf16[128,768]{1,0:T(8,128)(2,1)}, bf16[128,768]{1,0:T(8,128)(2,1)S(1)}, u32[]{:S(2)}, u32[]{:S(2)}) collective-permute-start(bf16[128,768]{1,0:T(8,128)(2,1)} %dy.1), channel_id=1, source_target_pairs={{0,1},{1,0},{2,3},{3,2},{4,5},{5,4},{6,7},{7,6},{8,9},{9,8},{10,11... | collective-permute-start | bytes 589832 | tf_op jit(solution)/shard_map/ppermute | solution.py:464
  61.7 25.7 %collective-permute-start.7 = (bf16[128,768]{1,0:T(8,128)(2,1)}, bf16[128,768]{1,0:T(8,128)(2,1)S(1)}, u32[]{:S(2)}, u32[]{:S(2)}) collective-permute-start(bf16[128,768]{1,0:T(8,128)(2,1)} %dy.1), channel_id=1, source_target_pairs={{0,2},{1,3},{2,0},{3,1},{4,6},{5,7},{6,4},{7,5},{8,10},{9,11},{10,... | collective-permute-start | bytes 589832 | tf_op jit(solution)/shard_map/ppermute | solution.py:464
  62.8 24.6 %collective-permute-start.8 = (bf16[128,768]{1,0:T(8,128)(2,1)}, bf16[128,768]{1,0:T(8,128)(2,1)S(1)}, u32[]{:S(2)}, u32[]{:S(2)}) collective-permute-start(bf16[128,768]{1,0:T(8,128)(2,1)} %dy.1), channel_id=1, source_target_pairs={{0,3},{1,2},{2,1},{3,0},{4,7},{5,6},{6,5},{7,4},{8,11},{9,10},{10,... | collective-permute-start | bytes 589832 | tf_op jit(solution)/shard_map/ppermute | solution.py:464
  88.7 13.7 %copy-start.27 = (bf16[768,768]{1,0:T(8,128)(2,1)S(1)}, bf16[768,768]{1,0:T(8,128)(2,1)}, u32[]{:S(2)}) copy-start(bf16[768,768]{1,0:T(8,128)(2,1)} %copy-done.26) | copy-start | bytes 3538948
  108.8 2.5 %copy-start = (bf16[768,2304]{1,0:T(8,128)(2,1)}, bf16[768,2304]{1,0:T(8,128)(2,1)S(1)}, u32[]{:S(2)}) copy-start(bf16[768,2304]{1,0:T(8,128)(2,1)S(1)} %get-tuple-element.87) | copy-start | bytes 10616836
  109.4 22.4 %copy-start.1 = (f32[768,512]{1,0:T(8,128)S(1)}, f32[768,512]{1,0:T(8,128)}, u32[]{:S(2)}) copy-start(f32[768,512]{1,0:T(8,128)} %get-tuple-element.77.nb) | copy-start | bytes 4718596
  109.4 22.4 %copy-start.5 = (bf16[768,576]{1,0:T(8,128)(2,1)S(1)}, bf16[768,576]{1,0:T(8,128)(2,1)}, u32[]{:S(2)}) copy-start(bf16[768,576]{1,0:T(8,128)(2,1)} %copy-done.4) | copy-start | bytes 2654212
  109.4 22.4 %copy-start.15 = (bf16[576,512]{1,0:T(8,128)(2,1)S(1)}, bf16[576,512]{1,0:T(8,128)(2,1)}, u32[]{:S(2)}) copy-start(bf16[576,512]{1,0:T(8,128)(2,1)} %copy-done.14) | copy-start | bytes 1769476
  109.4 22.4 %copy-start.23 = (s32[2]{0:T(128)S(1)}, s32[2]{0:T(128)}, u32[]{:S(2)}) copy-start(s32[2]{0:T(128)} %copy-done.22) | copy-start | bytes 28
  109.4 22.4 %copy-start.25 = (s32[1,8]{1,0:T(1,128)S(1)}, s32[1,8]{1,0:T(1,128)}, u32[]{:S(2)}) copy-start(s32[1,8]{1,0:T(1,128)} %lengths.3) | copy-start | bytes 100
  111.2 45.0 %collective-permute-start.32 = (bf16[4,96,2304]{2,1,0:T(8,128)(2,1)}, bf16[4,96,2304]{2,1,0:T(8,128)(2,1)}, u32[]{:S(2)}, u32[]{:S(2)}) collective-permute-start(bf16[4,96,2304]{2,1,0:T(8,128)(2,1)} %dynamic-slice_bitcast_fusion), channel_id=1, source_target_pairs={{0,4},{4,0},{8,12},{12,8},{16,20},{20,16},{24,28},{28,24},{1,5},{5... | collective-permute-start | bytes 5308424 | tf_op jit(solution)/shard_map/ppermute | solution.py:464
  111.2 12.1 %collective-permute-start.18 = (bf16[192,512]{1,0:T(8,128)(2,1)S(1)}, bf16[192,512]{1,0:T(8,128)(2,1)S(1)}, u32[]{:S(2)}, u32[]{:S(2)}) collective-permute-start(bf16[192,512]{1,0:T(8,128)(2,1)S(1)} %get-tuple-element.71), channel_id=1, source_target_pairs={{0,1},{1,0},{2,3},{3,2},{4,5},{5,4},{6,7},{7,6},{8,9},{9,8},{10,11... | collective-permute-start | bytes 589832 | tf_op jit(solution)/shard_map/ppermute | solution.py:464
  114.7 17.1 %collective-permute-start.19 = (bf16[192,512]{1,0:T(8,128)(2,1)S(1)}, bf16[192,512]{1,0:T(8,128)(2,1)S(1)}, u32[]{:S(2)}, u32[]{:S(2)}) collective-permute-start(bf16[192,512]{1,0:T(8,128)(2,1)S(1)} %get-tuple-element.72), channel_id=1, source_target_pairs={{0,2},{1,3},{2,0},{3,1},{4,6},{5,7},{6,4},{7,5},{8,10},{9,11},{10,... | collective-permute-start | bytes 589832 | tf_op jit(solution)/shard_map/ppermute | solution.py:464
  114.7 17.1 %collective-permute-start.20 = (bf16[192,512]{1,0:T(8,128)(2,1)S(1)}, bf16[192,512]{1,0:T(8,128)(2,1)S(1)}, u32[]{:S(2)}, u32[]{:S(2)}) collective-permute-start(bf16[192,512]{1,0:T(8,128)(2,1)S(1)} %get-tuple-element.73), channel_id=1, source_target_pairs={{0,3},{1,2},{2,1},{3,0},{4,7},{5,6},{6,5},{7,4},{8,11},{9,10},{10,... | collective-permute-start | bytes 589832 | tf_op jit(solution)/shard_map/ppermute | solution.py:464
  131.8 18.8 %copy-start.9 = (bf16[768,512]{1,0:T(8,128)(2,1)S(1)}, bf16[768,512]{1,0:T(8,128)(2,1)}, u32[]{:S(2)}) copy-start(bf16[768,512]{1,0:T(8,128)(2,1)} %copy-done.8) | copy-start | bytes 2359300
  143.3 1.2 collective-permute-start.24
  144.5 4.6 %collective-permute-start.25 = (f32[8,768]{1,0:T(8,128)S(1)}, f32[8,768]{1,0:T(8,128)S(1)}, u32[]{:S(2)}, u32[]{:S(2)}) collective-permute-start(f32[8,768]{1,0:T(8,128)S(1)} %add.98), channel_id=1, source_target_pairs={{0,8},{4,12},{8,0},{12,4},{16,24},{20,28},{24,16},{28,20},{1,9},{5... | collective-permute-start | bytes 73736 | tf_op jit(solution)/shard_map/ppermute | solution.py:464
  145.0 19.1 %collective-permute-start.15 = (bf16[768,128]{1,0:T(8,128)(2,1)}, bf16[768,128]{1,0:T(8,128)(2,1)S(1)}, u32[]{:S(2)}, u32[]{:S(2)}) collective-permute-start(bf16[768,128]{1,0:T(8,128)(2,1)} %copy-done.41), channel_id=1, source_target_pairs={{0,1},{1,0},{2,3},{3,2},{4,5},{5,4},{6,7},{7,6},{8,9},{9,8},{10,11... | collective-permute-start | bytes 589832 | tf_op jit(solution)/shard_map/ppermute | solution.py:464
  149.1 3.9 %collective-permute-start.26 = (f32[8,768]{1,0:T(8,128)S(1)}, f32[8,768]{1,0:T(8,128)S(1)}, u32[]{:S(2)}, u32[]{:S(2)}) collective-permute-start(f32[8,768]{1,0:T(8,128)S(1)} %add.99), channel_id=1, source_target_pairs={{0,16},{4,20},{8,24},{12,28},{16,0},{20,4},{24,8},{28,12},{1,17},{... | collective-permute-start | bytes 73736 | tf_op jit(solution)/shard_map/ppermute | solution.py:464
  153.0 8.1 %collective-permute-start.27 = (f32[8,768]{1,0:T(8,128)S(1)}, f32[8,768]{1,0:T(8,128)S(1)}, u32[]{:S(2)}, u32[]{:S(2)}) collective-permute-start(f32[8,768]{1,0:T(8,128)S(1)} %add.100), channel_id=1, source_target_pairs={{0,1},{1,0},{2,3},{3,2},{4,5},{5,4},{6,7},{7,6},{8,9},{9,8},{10,11... | collective-permute-start | bytes 73736 | tf_op jit(solution)/shard_map/ppermute | solution.py:464
  158.6 5.4 %copy-start.48 = (bf16[4,96,2304]{2,1,0:T(8,128)(2,1)}, bf16[4,96,2304]{2,1,0:T(8,128)(2,1)S(1)}, u32[]{:S(2)}) copy-start(bf16[4,96,2304]{2,1,0:T(8,128)(2,1)S(1)} %fusion) | copy-start | bytes 5308420
  158.6 2.4 %copy-start.38 = (bf16[768,128]{1,0:T(8,128)(2,1)S(1)}, bf16[768,128]{1,0:T(8,128)(2,1)}, u32[]{:S(2)}) copy-start(bf16[768,128]{1,0:T(8,128)(2,1)} %copy-done.37) | copy-start | bytes 589828
  158.7 19.1 %copy-start.36 = (bf16[768,128]{1,0:T(8,128)(2,1)S(1)}, bf16[768,128]{1,0:T(8,128)(2,1)}, u32[]{:S(2)}) copy-start(bf16[768,128]{1,0:T(8,128)(2,1)} %copy-done.35) | copy-start | bytes 589828
  158.7 19.1 %copy-start.34 = (bf16[768,128]{1,0:T(8,128)(2,1)S(1)}, bf16[768,128]{1,0:T(8,128)(2,1)}, u32[]{:S(2)}) copy-start(bf16[768,128]{1,0:T(8,128)(2,1)} %copy-done.33) | copy-start | bytes 589828
  158.7 24.1 %copy-start.17 = (f32[768,128]{1,0:T(8,128)S(1)}, f32[768,128]{1,0:T(8,128)}, u32[]{:S(2)}) copy-start(f32[768,128]{1,0:T(8,128)} %copy-done.16) | copy-start | bytes 1179652
  159.7 24.0 %copy-start.32 = (bf16[768,128]{1,0:T(8,128)(2,1)S(1)}, bf16[768,128]{1,0:T(8,128)(2,1)}, u32[]{:S(2)}) copy-start(bf16[768,128]{1,0:T(8,128)(2,1)} %copy-done.31) | copy-start | bytes 589828
  159.7 30.3 %collective-permute-start.33 = (bf16[2,96,2304]{2,1,0:T(8,128)(2,1)}, bf16[2,96,2304]{2,1,0:T(8,128)(2,1)}, u32[]{:S(2)}, u32[]{:S(2)}) collective-permute-start(bf16[2,96,2304]{2,1,0:T(8,128)(2,1)} %dynamic-slice_bitcast_fusion.1), channel_id=1, source_target_pairs={{0,8},{4,12},{8,0},{12,4},{16,24},{20,28},{24,16},{28,20},{1,9},{5... | collective-permute-start | bytes 2654216 | tf_op jit(solution)/shard_map/ppermute | solution.py:464
  161.0 26.1 %collective-permute-start.29 = (bf16[4,96,576]{2,1,0:T(8,128)(2,1)}, bf16[4,96,576]{2,1,0:T(8,128)(2,1)}, u32[]{:S(2)}, u32[]{:S(2)}) collective-permute-start(bf16[4,96,576]{2,1,0:T(8,128)(2,1)} %dynamic-slice_bitcast_fusion.2), channel_id=1, source_target_pairs={{0,4},{4,0},{8,12},{12,8},{16,20},{20,16},{24,28},{28,24},{1,5},{5... | collective-permute-start | bytes 1327112 | tf_op jit(solution)/shard_map/ppermute | solution.py:464
  161.0 16.7 %collective-permute-start.16 = (bf16[768,128]{1,0:T(8,128)(2,1)S(1)}, bf16[768,128]{1,0:T(8,128)(2,1)S(1)}, u32[]{:S(2)}, u32[]{:S(2)}) collective-permute-start(bf16[768,128]{1,0:T(8,128)(2,1)S(1)} %copy-done.40), channel_id=1, source_target_pairs={{0,2},{1,3},{2,0},{3,1},{4,6},{5,7},{6,4},{7,5},{8,10},{9,11},{10,... | collective-permute-start | bytes 589832 | tf_op jit(solution)/shard_map/ppermute | solution.py:464
  161.1 16.6 %collective-permute-start.17 = (bf16[768,128]{1,0:T(8,128)(2,1)S(1)}, bf16[768,128]{1,0:T(8,128)(2,1)S(1)}, u32[]{:S(2)}, u32[]{:S(2)}) collective-permute-start(bf16[768,128]{1,0:T(8,128)(2,1)S(1)} %copy-done.38), channel_id=1, source_target_pairs={{0,3},{1,2},{2,1},{3,0},{4,7},{5,6},{6,5},{7,4},{8,11},{9,10},{10,... | collective-permute-start | bytes 589832 | tf_op jit(solution)/shard_map/ppermute | solution.py:464
  164.1 19.6 %collective-permute-start.28 = (f32[8,768]{1,0:T(8,128)}, f32[8,768]{1,0:T(8,128)}, u32[]{:S(2)}, u32[]{:S(2)}) collective-permute-start(f32[8,768]{1,0:T(8,128)} %add.101), channel_id=1, source_target_pairs={{0,2},{1,3},{2,0},{3,1},{4,6},{5,7},{6,4},{7,5},{8,10},{9,11},{10,... | collective-permute-start | bytes 73736 | tf_op jit(solution)/shard_map/ppermute | solution.py:464
  177.7 16.7 %collective-permute-start.21 = (bf16[768,128]{1,0:T(8,128)(2,1)S(1)}, bf16[768,128]{1,0:T(8,128)(2,1)S(1)}, u32[]{:S(2)}, u32[]{:S(2)}) collective-permute-start(bf16[768,128]{1,0:T(8,128)(2,1)S(1)} %copy-done.36), channel_id=1, source_target_pairs={{0,1},{1,0},{2,3},{3,2},{4,5},{5,4},{6,7},{7,6},{8,9},{9,8},{10,11... | collective-permute-start | bytes 589832 | tf_op jit(solution)/shard_map/ppermute | solution.py:464
  177.7 19.2 %collective-permute-start.22 = (bf16[768,128]{1,0:T(8,128)(2,1)S(1)}, bf16[768,128]{1,0:T(8,128)(2,1)S(1)}, u32[]{:S(2)}, u32[]{:S(2)}) collective-permute-start(bf16[768,128]{1,0:T(8,128)(2,1)S(1)} %copy-done.34), channel_id=1, source_target_pairs={{0,2},{1,3},{2,0},{3,1},{4,6},{5,7},{6,4},{7,5},{8,10},{9,11},{10,... | collective-permute-start | bytes 589832 | tf_op jit(solution)/shard_map/ppermute | solution.py:464
  182.8 7.2 %copy-start.49 = (bf16[4,96,2304]{2,1,0:T(8,128)(2,1)S(1)}, bf16[4,96,2304]{2,1,0:T(8,128)(2,1)}, u32[]{:S(2)}) copy-start(bf16[4,96,2304]{2,1,0:T(8,128)(2,1)} %copy-done.48) | copy-start | bytes 5308420
  183.7 13.2 %collective-permute-start.23 = (bf16[768,128]{1,0:T(8,128)(2,1)S(1)}, bf16[768,128]{1,0:T(8,128)(2,1)S(1)}, u32[]{:S(2)}, u32[]{:S(2)}) collective-permute-start(bf16[768,128]{1,0:T(8,128)(2,1)S(1)} %copy-done.32), channel_id=1, source_target_pairs={{0,3},{1,2},{2,1},{3,0},{4,7},{5,6},{6,5},{7,4},{8,11},{9,10},{10,... | collective-permute-start | bytes 589832 | tf_op jit(solution)/shard_map/ppermute | solution.py:464
  188.4 8.6 %copy-start.19 = (f32[768,128]{1,0:T(8,128)S(1)}, f32[768,128]{1,0:T(8,128)}, u32[]{:S(2)}) copy-start(f32[768,128]{1,0:T(8,128)} %copy-done.18) | copy-start | bytes 1179652
  188.4 8.6 %copy-start.21 = (bf16[128,768]{1,0:T(8,128)(2,1)S(1)}, bf16[128,768]{1,0:T(8,128)(2,1)}, u32[]{:S(2)}) copy-start(bf16[128,768]{1,0:T(8,128)(2,1)} %dy.1) | copy-start | bytes 589828
  188.4 9.4 %collective-permute-start.30 = (bf16[2,96,576]{2,1,0:T(8,128)(2,1)S(1)}, bf16[2,96,576]{2,1,0:T(8,128)(2,1)}, u32[]{:S(2)}, u32[]{:S(2)}) collective-permute-start(bf16[2,96,576]{2,1,0:T(8,128)(2,1)S(1)} %dynamic-slice_bitcast_fusion.3), channel_id=1, source_target_pairs={{0,8},{4,12},{8,0},{12,4},{16,24},{20,28},{24,16},{28,20},{1,9},{5... | collective-permute-start | bytes 663560 | tf_op jit(solution)/shard_map/ppermute | solution.py:464
  192.1 12.9 %collective-permute-start.34 = (bf16[1,96,2304]{2,1,0:T(8,128)(2,1)}, bf16[1,96,2304]{2,1,0:T(8,128)(2,1)}, u32[]{:S(2)}, u32[]{:S(2)}) collective-permute-start(bf16[1,96,2304]{2,1,0:T(8,128)(2,1)} %constant_dynamic-slice_fusion), channel_id=1, source_target_pairs={{0,16},{4,20},{8,24},{12,28},{16,0},{20,4},{24,8},{28,12},{1,17},{... | collective-permute-start | bytes 1327112 | tf_op jit(solution)/shard_map/ppermute | solution.py:464
  198.8 12.8 %collective-permute-start.31 = (bf16[1,96,576]{2,1,0:T(8,128)(2,1)S(1)}, bf16[1,96,576]{2,1,0:T(8,128)(2,1)S(1)}, u32[]{:S(2)}, u32[]{:S(2)}) collective-permute-start(bf16[1,96,576]{2,1,0:T(8,128)(2,1)S(1)} %constant_dynamic-slice_fusion.1), channel_id=1, source_target_pairs={{0,16},{4,20},{8,24},{12,28},{16,0},{20,4},{24,8},{28,12},{1,17},{... | collective-permute-start | bytes 331784 | tf_op jit(solution)/shard_map/ppermute | solution.py:464
  207.2 5.5 %collective-permute-start.35 = (bf16[96,192]{1,0:T(8,128)(2,1)S(1)}, bf16[96,192]{1,0:T(8,128)(2,1)S(1)}, u32[]{:S(2)}, u32[]{:S(2)}) collective-permute-start(bf16[96,192]{1,0:T(8,128)(2,1)S(1)} %get-tuple-element.135), channel_id=1, source_target_pairs={{0,1},{1,0},{2,3},{3,2},{4,5},{5,4},{6,7},{7,6},{8,9},{9,8},{10,11... | collective-permute-start | bytes 110600 | tf_op jit(solution)/shard_map/ppermute | solution.py:464
  207.2 5.4 %collective-permute-start.36 = (bf16[96,192]{1,0:T(8,128)(2,1)S(1)}, bf16[96,192]{1,0:T(8,128)(2,1)S(1)}, u32[]{:S(2)}, u32[]{:S(2)}) collective-permute-start(bf16[96,192]{1,0:T(8,128)(2,1)S(1)} %get-tuple-element.137), channel_id=1, source_target_pairs={{0,2},{1,3},{2,0},{3,1},{4,6},{5,7},{6,4},{7,5},{8,10},{9,11},{10,... | collective-permute-start | bytes 110600 | tf_op jit(solution)/shard_map/ppermute | solution.py:464
  209.5 5.9 %collective-permute-start.37 = (bf16[96,192]{1,0:T(8,128)(2,1)S(1)}, bf16[96,192]{1,0:T(8,128)(2,1)S(1)}, u32[]{:S(2)}, u32[]{:S(2)}) collective-permute-start(bf16[96,192]{1,0:T(8,128)(2,1)S(1)} %get-tuple-element.136), channel_id=1, source_target_pairs={{0,3},{1,2},{2,1},{3,0},{4,7},{5,6},{6,5},{7,4},{8,11},{9,10},{10,... | collective-permute-start | bytes 110600 | tf_op jit(solution)/shard_map/ppermute | solution.py:464
  (28 other events, 26.0 us)

commit v2 on v1

--- a/solution.py
+++ b/solution.py
@@ -6,6 +6,7 @@
 from jax.sharding import PartitionSpec as P
 
 HEAD_DIM = 64
+SPEED = 1.15e9
 norm_eps = 1e-06
 masked_score = -1000000000.0
 F32 = jnp.float32
@@ -16,10 +17,7 @@
 GAIN0, BIAS0, GAIN1, BIAS1, SCALE0, SCALE1 = range(6)
 
 
-def call(kernel, outs, args, n_smem=0, scratch=(), flops=0, limit=40):
-    moved = sum(a.size * a.dtype.itemsize for a in args) + sum(
-        o.size * o.dtype.itemsize for o in outs
-    )
+def call(kernel, outs, args, n_smem=0, scratch=(), us=0.01, limit=16):
     return pl.pallas_call(
         kernel,
         out_shape=tuple(outs),
@@ -27,7 +25,8 @@
         out_specs=tuple([VMEM] * len(outs)),
         scratch_shapes=list(scratch),
         compiler_params=pltpu.CompilerParams(vmem_limit_bytes=limit << 20),
-        cost_estimate=pl.CostEstimate(flops=flops, bytes_accessed=moved, transcendentals=0),
+        name=kernel.__name__,
+        cost_estimate=pl.CostEstimate(flops=int(us * SPEED), bytes_accessed=8, transcendentals=0),
     )(*args)
 
 
@@ -76,22 +75,30 @@
     wd_o[...] = wd[...].T
 
 
-def out_weight_kernel(place, *refs):
-    pieces, (w_o, wt_o) = refs[:-2], refs[-2:]
+def message_kernel(place, tokens, w_out, out):
+    d = place[1]
+    rows, half = tokens.shape[0], tokens.shape[1] // 2
+    n = w_out.shape[0] // 2
+    out[0:rows, :] = tokens[:, :half]
+    out[rows : 2 * rows, :] = tokens[:, half:]
+    piece = w_out[pl.ds(pl.multiple_of(((d >> 1) & 1) * n, n), n), :]
+    out[2 * rows :, :] = jnp.where((d & 1) == 0, piece[:, :half], piece[:, half:])
+
+
+def pieces_kernel(x0, x1, x2, x3, out):
+    n = out.shape[1]
+    for k, ref in enumerate((x0, x1, x2, x3)):
+        out[k] = ref[ref.shape[0] - n :, :]
+
+
+def out_weight_kernel(place, p00, p01, p10, p11, w_o, wt_o):
     m, d = place[0], place[1]
-    rows, cols = pieces[0].shape[-2:]
-    shard = rows * 4
-    n = 0
-    for c in range(2):
-        for b in range(4):
-            s = d ^ (c + 2 * b)
-            half = s & 1
-            quarter = (s >> 1) & 3
-            ref = pieces[n]
-            n += 1
-            for k in range(4):
-                at = pl.multiple_of((m ^ k) * shard + quarter * rows, 16)
-                w_o[pl.ds(at, rows), pl.ds(pl.multiple_of(half * cols, 128), cols)] = ref[k]
+    _, rows, cols = p00.shape
+    for c, b, ref in ((0, 0, p00), (0, 1, p01), (1, 0, p10), (1, 1, p11)):
+        half, part = (d & 1) ^ c, ((d >> 1) & 1) ^ b
+        for k in range(4):
+            at = pl.multiple_of((m ^ k) * 2 * rows + part * rows, rows)
+            w_o[pl.ds(at, rows), pl.ds(pl.multiple_of(half * cols, cols), cols)] = ref[k]
     wt_o[...] = w_o[...].T
 
 
@@ -101,15 +108,16 @@
     score, ids, pattern,
 ):
     m = place[0]
-    rows = x0.shape[0]
     width, tokens = xt_o.shape
+    rows = tokens // 4
     channels = att_o.shape[0]
     heads = channels // HEAD_DIM
     buckets = table.shape[0]
     half = buckets // 2
     for k, ref in enumerate((x0, x1, x2, x3)):
         at = pl.multiple_of((m ^ k) * rows, rows)
-        xt_o[:, pl.ds(at, rows)] = ref[...].T
+        xt_o[: width // 2, pl.ds(at, rows)] = ref[0:rows, :].T
+        xt_o[width // 2 :, pl.ds(at, rows)] = ref[rows : 2 * rows, :].T
 
     def add(i, acc):
         return acc + fold(xt_o[chunk(i), :].astype(F32))
@@ -290,10 +298,10 @@
 
 def mlp_kernel(
     place, vec, act, dup, gm, ga, att, h2, dy, w_down_t,
-    m0, m1, m2, m3, g_o, vec_o,
-    mlp, sums,
+    m0, m1, m2, m3, vec_o, *rest,
 ):
-    m = place[0]
+    grads, (mlp, sums) = rest[:-2], rest[-2:]
+    m, d = place[0], place[1]
     rows = m0.shape[1]
     width, tokens = dy.shape
     mlp[...] = nn(w_down_t[...], act[...])
@@ -308,10 +316,28 @@
     passes(width, scale, 0)
     vec_o[...] = vec[...]
     vec_o[5:6, :] = sums[...].T[0:1, :]
-    hidden = act.shape[0]
-    g_o[:, 0:hidden] = nt(h2[...], dup[...]).astype(BF16)
-    g_o[:, hidden : 2 * hidden] = nt(gm[...], act[...]).astype(BF16)
-    g_o[:, 2 * hidden : 2 * hidden + width] = nt(ga[...], att[...]).astype(BF16)
+    pairs = ((h2, dup), (gm, act), (ga, att))
+    put_blocks([nt(a[...], b[...]).astype(BF16) for a, b in pairs], d & 1, grads)
+
+
+def put_blocks(parts, here, grads):
+    at = 0
+    for p in parts:
+        cols = slice(at, at + p.shape[1])
+        at += p.shape[1]
+        if len(grads) == 1:
+            grads[0][:, cols] = p
+            continue
+        sent, kept = grads
+        n = sent.shape[0] // 4
+        for b in range(4):
+            even, odd = p[2 * b * n : (2 * b + 1) * n], p[(2 * b + 1) * n : (2 * b + 2) * n]
+            sent[b * n : (b + 1) * n, cols] = pick(here, odd, even)
+            kept[b * n : (b + 1) * n, cols] = pick(here, even, odd)
+
+
+def pick(bit, a, b):
+    return jnp.where(bit == 0, a, b)
 
 
 def back_kernel(
@@ -422,8 +448,48 @@
     vec_o[6:7, :] = across(jnp.where(lane == row + m * n_rows, each, 0.0))
 
 
-def qkv_grad_kernel(h1, dqkv, g_o):
-    g_o[...] = nt(h1[...], dqkv[...]).astype(BF16)
+def qkv_grad_kernel(place, h1, dqkv, *grads):
+    put_blocks([nt(h1[...], dqkv[...]).astype(BF16)], place[1] & 1, grads)
+
+
+def plane_kernel(place, keep, recv, b0, b1, b2, b3):
+    at = (place[1] >> 1) & 3
+    n = b0.shape[0]
+    for k, ref in enumerate((b0, b1, b2, b3)):
+        rows = pl.ds(pl.multiple_of((at ^ k) * n, n), n)
+        total = keep[rows, :].astype(F32) + recv[rows, :].astype(F32)
+        ref[...] = total.astype(ref.dtype)
+
+
+def four(refs):
+    total = refs[0][...].astype(F32)
+    for r in refs[1:]:
+        total = total + r[...].astype(F32)
+    return total
+
+
+def grads_last_kernel(place, b0, b1, b2, b3, up_o, down_o, o0, o1, o2, o3, turned):
+    m = place[0]
+    hidden = up_o.shape[1]
+    channels = o0.shape[0]
+    g = four((b0, b1, b2, b3))
+    up_o[...] = g[:, :hidden]
+    down_o[...] = g[:, hidden : 2 * hidden]
+    turned[...] = g[:, 2 * hidden :].T
+    for k, ref in enumerate((o0, o1, o2, o3)):
+        v = turned[pl.ds(pl.multiple_of((m ^ k) * channels, channels), channels), :]
+        ref[...] = v.astype(ref.dtype)
+
+
+def out_sum_kernel(o0, o1, o2, o3, out):
+    out[...] = four((o0, o1, o2, o3))
+
+
+def qkv_last_kernel(b0, b1, b2, b3, out):
+    total = four((b0, b1, b2, b3))
+    channels = out.shape[2]
+    for i in range(3):
+        out[i] = total[:, i * channels : (i + 1) * channels]
 
 
 def input_kernel(p0, p1, p2, p3, dy, out):
@@ -459,45 +525,36 @@
     m, d = lax.axis_index("mp"), lax.axis_index("dp")
     place = jnp.stack([m, d]).astype(jnp.int32)
 
-    def swap(v, k, axis="mp"):
+    def swap(v, k, axis="mp", name="rows"):
         n = mp if axis == "mp" else dp
-        return lax.ppermute(v, axis, [(i, i ^ k) for i in range(n)])
-
-    def gathered(v):
-        return [v] + [swap(v, k) for k in range(1, mp)]
+        with jax.named_scope(name):
+            return lax.ppermute(v, axis, [(i, i ^ k) for i in range(n)])
+
+    def after(v, *seen):
+        return lax.optimization_barrier((v,) + seen)[0]
+
+    fast = dp == 8 and (width // dp) % 16 == 0 and hidden == width
 
     cols = jnp.concatenate(
         [norm_gains[0:1], norm_biases[0:1], norm_gains[1:2], norm_biases[1:2], layer_scales]
     ).T
     wq = jnp.transpose(w_qkv, (1, 2, 0)).reshape(3 * channels, width)
 
-    x = gathered(tokens)
-
-    piece_rows, piece_cols = channels // 4, width // 2
-    piece = lax.dynamic_slice(
-        w_out, (((d >> 1) & 3) * piece_rows, (d & 1) * piece_cols), (piece_rows, piece_cols)
-    )
-    part = jnp.stack(gathered(piece))
-    one = swap(part, 4, "dp")
-    two = swap(jnp.stack([part, one]), 2, "dp")
-    mine4 = jnp.stack([part, two[0], one, two[1]])
-    three = swap(mine4, 1, "dp")
-    pieces = [mine4[i] for i in range(4)] + [three[i] for i in range(4)]
-    w_out_full, w_out_t = call(
-        out_weight_kernel,
-        [like((width, width), BF16)] * 2,
-        [place] + pieces,
-        n_smem=1,
-    )
+    piece = (channels // 2, width // 2)
+    (sent,) = call(
+        message_kernel, [like((2 * rows + piece[0], piece[1]), BF16)], [place, tokens, w_out], n_smem=1
+    )
+    x = [sent] + [swap(sent, k, name="x") for k in (1, 2, 3)]
+    dy1 = swap(cotangent, 1, name="dy")
     wq_t, w_up_t, w_down_t = call(
         turn_kernel,
         [like((width, 3 * channels), BF16), like((hidden, width), BF16), like((width, hidden), BF16)],
         [wq, w_up, w_down],
     )
-
-    cot_after, x3 = lax.optimization_barrier((cotangent, x[3]))
-    x[3] = x3
-    dy = gathered(cot_after)
+    (part,) = call(pieces_kernel, [like((4,) + piece, BF16)], x)
+    part_x = swap(part, 2, "dp", name="w")
+    dy2 = swap(after(cotangent, x[3]), 2, name="dy")
+    wq_now = after(wq, wq_t, w_up_t, w_down_t)
     xt, h1, stat, qkv, pt, att = call(
         head_kernel,
         [
@@ -508,16 +565,21 @@
             like((heads, group, group), BF16),
             like((channels, group), BF16),
         ],
-        [place, page_lengths, rel_table] + x + [cols, wq],
+        [place, page_lengths, rel_table] + x + [cols, wq_now],
         n_smem=3,
         scratch=[
             pltpu.VMEM((group, group), F32),
             pltpu.VMEM((group, 128), jnp.int32),
             pltpu.VMEM((3, 128, 128), F32),
         ],
-        flops=2 * group * width * 3 * channels + 4 * heads * group * group * HEAD_DIM,
-    )
-    atts = gathered(att)
+        us=7,
+    )
+    atts = [att] + [swap(att, k, name="att") for k in (1, 2, 3)]
+    dy = [cotangent, dy1, dy2, swap(after(dy2, atts[1]), 1, name="dy")]
+    w_pieces = [part, part_x, swap(part, 1, "dp", name="w"), swap(part_x, 1, "dp", name="w")]
+    w_out_full, w_out_t = call(
+        out_weight_kernel, [like((width, width), BF16)] * 2, [place] + w_pieces, n_smem=1
+    )
     act_like = like((width, group), BF16)
     hid_like = like((hidden, group), BF16)
     d0, d1, d2, d3, nb, h2, act, dup, gm, ga, att_all, dy_t, mid, vec = call(
@@ -534,19 +596,34 @@
             pltpu.VMEM((hidden, group), F32),
             pltpu.VMEM((width, 128), F32),
         ],
-        flops=10 * width * width * group,
-    )
-    d_att = [d0] + [swap(v, k) for k, v in ((1, d1), (2, d2), (3, d3))]
-    m0, m1, m2, m3, grads, vec = call(
+        us=12,
+    )
+    d_att = [d0] + [swap(v, k, name="d_att") for k, v in ((1, d1), (2, d2), (3, d3))]
+    grad_cols = 2 * hidden + width
+    share = width // dp
+    grad_like = [like((width // 2, grad_cols), BF16)] * 2 if fast else [like((width, grad_cols), BF16)]
+    m0, m1, m2, m3, vec, *grads = call(
         mlp_kernel,
-        [like((width, rows), BF16)] * 4
-        + [like((width, 2 * hidden + width), BF16), like((8, width), F32)],
+        [like((width, rows), BF16)] * 4 + [like((8, width), F32)] + grad_like,
         [place, vec, act, dup, gm, ga, att_all, h2, dy_t, w_down_t],
         n_smem=1,
         scratch=[pltpu.VMEM((width, group), F32), pltpu.VMEM((width, 128), F32)],
-        flops=8 * width * width * group,
-    )
-    mlp = [m0] + [swap(v, k) for k, v in ((1, m1), (2, m2), (3, m3))]
+    )
+    mlp = [m0] + [swap(v, k, name="mlp") for k, v in ((1, m1), (2, m2), (3, m3))]
+
+    def planes(grads, n, name):
+        kept = grads[1]
+        recv = swap(grads[0], 1, "dp", name=name + "_core")
+        b = call(
+            plane_kernel,
+            [like((share, n), F32)] + [like((share, n), BF16)] * 3,
+            [place, kept, recv],
+            n_smem=1,
+        )
+        return [b[0]] + [swap(b[k], 2 * k, "dp", name=name + "_plane") for k in (1, 2, 3)]
+
+    if fast:
+        blocks = planes(grads, grad_cols, "grads")
 
     p0, p1, p2, p3, dqkv, vec = call(
         back_kernel,
@@ -563,15 +640,14 @@
             pltpu.VMEM((width, group), F32),
             pltpu.VMEM((width, 128), F32),
         ],
-        flops=2 * group * width * 3 * channels + 8 * heads * group * group * HEAD_DIM,
-    )
-    back = [p0] + [swap(v, k) for k, v in ((1, p1), (2, p2), (3, p3))]
-    (qkv_grads,) = call(
-        qkv_grad_kernel,
-        [like((width, 3 * channels), BF16)],
-        [h1, dqkv],
-        flops=2 * group * width * 3 * channels,
-    )
+        us=9,
+    )
+    (output,) = call(output_kernel, [like((rows, width), BF16)], mlp + [mid, cols])
+    p1, p2, p3, output = lax.optimization_barrier((p1, p2, p3, output))
+    back = [p0] + [swap(v, k, name="back") for k, v in ((1, p1), (2, p2), (3, p3))]
+    n = 3 * channels
+    grad_like = [like((width // 2, n), BF16)] * 2 if fast else [like((width, n), BF16)]
+    qkv_grads = call(qkv_grad_kernel, grad_like, [place, h1, dqkv], n_smem=1)
 
     def reduced(g):
         g = g.reshape(dp, width // dp, g.shape[1])
@@ -587,23 +663,40 @@
                 g = g.astype(BF16)
         return g[0]
 
-    grads = reduced(grads)
-    qkv_grads = reduced(qkv_grads)
-    out_grad = grads[:, 2 * hidden :]
-
-    def out_part(k):
-        return lax.dynamic_slice_in_dim(out_grad, (m ^ k) * channels, channels, 1)
-
-    out_sum = out_part(0)
-    for k in range(1, mp):
-        out_sum = out_sum + swap(out_part(k).astype(BF16), k).astype(F32)
+    if fast:
+        qkv_blocks = planes(qkv_grads, n, "qkv")
+        grad_up, grad_down, o0, o1, o2, o3 = call(
+            grads_last_kernel,
+            [like((share, hidden), F32)] * 2
+            + [like((channels, share), F32)]
+            + [like((channels, share), BF16)] * 3,
+            [place] + blocks,
+            n_smem=1,
+            scratch=[pltpu.VMEM((width, share), F32)],
+        )
+        o1, o2, o3 = (swap(v, k, name="out") for k, v in ((1, o1), (2, o2), (3, o3)))
+        (grad_out,) = call(out_sum_kernel, [like((channels, share), F32)], [o0, o1, o2, o3])
+        (grad_qkv,) = call(qkv_last_kernel, [like((3, share, channels), F32)], qkv_blocks)
+        grad_qkv = jnp.transpose(grad_qkv, (1, 0, 2))
+    else:
+        summed = reduced(grads[0])
+        grad_qkv = reduced(qkv_grads[0]).reshape(share, 3, channels)
+        grad_up, grad_down = summed[:, :hidden], summed[:, hidden : 2 * hidden]
+        turned = summed[:, 2 * hidden :].T
+
+        def out_part(k):
+            return lax.dynamic_slice_in_dim(turned, (m ^ k) * channels, channels, 0)
+
+        grad_out = out_part(0)
+        for k in range(1, mp):
+            grad_out = grad_out + swap(out_part(k).astype(BF16), k).astype(F32)
 
     bit = 1
     while bit < dp:
-        vec = vec + swap(vec, bit, "dp")
+        vec = vec + swap(vec, bit, "dp", name="vec")
         bit *= 2
     for k in (1, 2):
-        vec = vec + swap(vec, k)
+        vec = vec + swap(vec, k, name="vec")
 
     (output,) = call(output_kernel, [like((rows, width), BF16)], mlp + [mid, cols])
     (grad_input,) = call(input_kernel, [like((rows, width), BF16)], back + [cotangent])
@@ -614,11 +707,11 @@
         vec[0:2],
         vec[2:4],
         vec[4:6],
-        qkv_grads.reshape(width // dp, 3, channels),
+        grad_qkv,
         grad_table,
-        out_sum.T,
-        grads[:, :hidden],
-        grads[:, hidden : 2 * hidden].T,
+        grad_out,
+        grad_up,
+        grad_down.T,
     )
 
 

time: 217 us -> 176 us (0.81)
  local copies, waits for them, and re-layouts: 36 us -> 8.2 us
  starting transfers between devices: 57.4 us -> 45.8 us
  other arithmetic: 9.61 us -> 0.1 us
  waiting for transfers between devices: 74.2 us -> 78.4 us
  Pallas kernels: 38 us -> 42 us
    unnamed x111 -> x19, local copies, waits for them, and re-layouts: 25.7 us -> 5.2 us
    ppermute x38 -> x37, starting transfers between devices: 57.4 us -> 45.8 us  [swap(): return lax.ppermute(v, axis, [(i, i ^ k) for i in range(n)])]
    convert_element_type x4 -> x0, other arithmetic: 5.94 us -> none  [reduced(): g = g.astype(BF16)]
    squeeze x7 -> x0, local copies, waits for them, and re-layouts: 5.26 us -> none  [the longest x6 4.07 us: reduced(): sent = lax.dynamic_index_in_dim(g, 1 - here, 1, keepdims=False)]
    ppermute x38 -> x37, waiting for transfers between devices: 74.2 us -> 78.4 us  [swap(): return lax.ppermute(v, axis, [(i, i ^ k) for i in range(n)])]
    pallas_call x9 -> x16, Pallas kernels: 38 us -> 42 us  [call(): pl.pallas_call(kernel, out_shape=tuple(outs), in_specs=[SMEM] * n_smem +...]
  transfers between devices with their start and end apart: 38 -> 37, of which waited for: 16 -> 17; matrix products, arithmetic and copies ran while one was open for 9% -> 2% of each run, Pallas kernels for 9% -> 14%
where the time goes in v2:
time: 176 us; the launch traced here: 175 us
  waiting for transfers between devices  78.4 us (45%)
  starting transfers between devices  45.8 us (26%)
  Pallas kernels  42 us (24%)
  local copies, waits for them, and re-layouts  8.2 us (5%)
    ppermute x37, waiting for transfers between devices, swap(): return lax.ppermute(v, axis, [(i, i ^ k) for i in range(n)])  78.4 us
    ppermute x37, starting transfers between devices, swap(): return lax.ppermute(v, axis, [(i, i ^ k) for i in range(n)])  45.8 us
    pallas_call x16, Pallas kernels, call(): pl.pallas_call(kernel, out_shape=tuple(outs), in_specs=[SMEM] * n_smem +...  42 us
    unnamed x19, local copies, waits for them, and re-layouts  5.2 us
  transfers between devices with their start and end apart: 37, of which 17 were waited for; matrix products, arithmetic and copies ran while one was open for 2% of the time, Pallas kernels for 14%

profile of v2, /device:TPU:0, one launch (start us, length us, event | category | flops | bytes accessed | tf_op | source)
XLA Modules:
  0.0 175.4 jit_solution(12524077510061325918)
XLA Ops:
  0.7 1.0 copy-done.5
  1.8 0.9 copy-done.6
  2.7 0.6 message_kernel.1.x0
  3.3 5.1 %collective-permute-start.2 = (bf16[352,384]{1,0:T(8,128)(2,1)S(1)}, bf16[352,384]{1,0:T(8,128)(2,1)S(1)}, u32[]{:S(2)}, u32[]{:S(2)}) collective-permute-start(bf16[352,384]{1,0:T(8,128)(2,1)S(1)} %message_kernel.1.x0), channel_id=1, source_target_pairs={{0,3},{1,2},{2,1},{3,0},{4,7},{5,6},{6,5},{7,4},{8,11},{9,10},{10,... | collective-permute-start | bytes 811016 | tf_op jit(solution)/shard_map/x/ppermute | solution.py:531
  8.4 0.6 collective-permute-start
  9.0 0.8 copy.28.table
  9.8 0.8 fusion.1
  10.6 0.7 concatenate.3
  11.5 1.3 copy-done.1
  12.8 1.2 copy-done.3
  14.0 0.9 turn_kernel.1
  14.9 0.9 collective-permute-done.2.x3
  15.8 15.6 %collective-permute-done.1.x2 = bf16[352,384]{1,0:T(8,128)(2,1)S(1)} collective-permute-done((bf16[352,384]{1,0:T(8,128)(2,1)S(1)}, bf16[352,384]{1,0:T(8,128)(2,1)S(1)}, u32[]{:S(2)}, u32[]{:S(2)}) %collective-permute-start.1) | collective-permute-done | bytes 270368 | tf_op jit(solution)/shard_map/x/ppermute | solution.py:531
  31.5 1.6 collective-permute-start.9
  33.1 6.3 %head_kernel.1 = (bf16[768,512]{1,0:T(8,128)(2,1)S(1)}, bf16[768,512]{1,0:T(8,128)(2,1)S(1)}, f32[8,512]{1,0:T(8,128)S(1)}, bf16[576,512]{1,0:T(8,128)(2,1)S(1)}...) custom-call(s32[2]{0:T(128)S(1)} %pad_add_fusion.place, s32[1,8]{1,0:T(1,128)S(1)} %copy-done.8, ...), custom_call_target="tpu_custom_call" | custom-call | flops 8049999872 | bytes 8 | tf_op jit(solution)/shard_map/head_kernel/pallas_call | solution.py:21
  39.4 3.1 %collective-permute-start.3 = (bf16[192,512]{1,0:T(8,128)(2,1)S(1)}, bf16[192,512]{1,0:T(8,128)(2,1)S(1)}, u32[]{:S(2)}, u32[]{:S(2)}) collective-permute-start(bf16[192,512]{1,0:T(8,128)(2,1)S(1)} %get-tuple-element.74.a0), channel_id=1, source_target_pairs={{0,1},{1,0},{2,3},{3,2},{4,5},{5,4},{6,7},{7,6},{8,9},{9,8},{10,11... | collective-permute-start | bytes 589832 | tf_op jit(solution)/shard_map/att/ppermute | solution.py:531
  42.6 2.5 %collective-permute-done.7.c2 = bf16[128,768]{1,0:T(8,128)(2,1)S(1)} collective-permute-done((bf16[128,768]{1,0:T(8,128)(2,1)S(1)}, bf16[128,768]{1,0:T(8,128)(2,1)S(1)}, u32[]{:S(2)}, u32[]{:S(2)}) %collective-permute-start.7) | collective-permute-done | bytes 196640 | tf_op jit(solution)/shard_map/dy/ppermute | solution.py:531
  45.1 1.3 collective-permute-start.5
  46.4 2.8 %collective-permute-done.3.a1 = bf16[192,512]{1,0:T(8,128)(2,1)S(1)} collective-permute-done((bf16[192,512]{1,0:T(8,128)(2,1)S(1)}, bf16[192,512]{1,0:T(8,128)(2,1)S(1)}, u32[]{:S(2)}, u32[]{:S(2)}) %collective-permute-start.3) | collective-permute-done | bytes 196640 | tf_op jit(solution)/shard_map/att/ppermute | solution.py:531
  49.3 0.9 collective-permute-start.4
  50.1 1.1 collective-permute-start.8
  51.2 1.0 out_weight_kernel.1
  52.2 6.1 %collective-permute-done.6.c1 = bf16[128,768]{1,0:T(8,128)(2,1)S(1)} collective-permute-done((bf16[128,768]{1,0:T(8,128)(2,1)S(1)}, bf16[128,768]{1,0:T(8,128)(2,1)S(1)}, u32[]{:S(2)}, u32[]{:S(2)}) %collective-permute-start.6) | collective-permute-done | bytes 196640 | tf_op jit(solution)/shard_map/dy/ppermute | solution.py:531
  58.3 6.7 %collective-permute-done.4.a2 = bf16[192,512]{1,0:T(8,128)(2,1)S(1)} collective-permute-done((bf16[192,512]{1,0:T(8,128)(2,1)S(1)}, bf16[192,512]{1,0:T(8,128)(2,1)S(1)}, u32[]{:S(2)}, u32[]{:S(2)}) %collective-permute-start.4) | collective-permute-done | bytes 196640 | tf_op jit(solution)/shard_map/att/ppermute | solution.py:531
  65.0 1.1 collective-permute-done.8.c3
  66.1 11.7 %middle_kernel.1 = (bf16[192,512]{1,0:T(8,128)(2,1)S(1)}, bf16[192,512]{1,0:T(8,128)(2,1)S(1)}, bf16[192,512]{1,0:T(8,128)(2,1)S(1)}, bf16[192,512]{1,0:T(8,128)...) custom-call(s32[2]{0:T(128)S(1)} %pad_add_fusion.place, ...), custom_call_target="tpu_custom_call" | custom-call | flops 13799999488 | bytes 8 | tf_op jit(solution)/shard_map/middle_kernel/pallas_call | solution.py:21
  77.7 5.0 %mlp_kernel.1 = (bf16[768,128]{1,0:T(8,128)(2,1)S(1)}, bf16[768,128]{1,0:T(8,128)(2,1)S(1)}, bf16[768,128]{1,0:T(8,128)(2,1)S(1)}, bf16[768,128]{1,0:T(8,128)(2,...) custom-call(s32[2]{0:T(128)S(1)} %pad_add_fusion.place, ...), custom_call_target="tpu_custom_call" | custom-call | flops 11500000 | bytes 8 | tf_op jit(solution)/shard_map/mlp_kernel/pallas_call | solution.py:21
  82.9 1.9 %collective-permute-start.16 = (bf16[192,512]{1,0:T(8,128)(2,1)S(1)}, bf16[192,512]{1,0:T(8,128)(2,1)S(1)}, u32[]{:S(2)}, u32[]{:S(2)}) collective-permute-start(bf16[192,512]{1,0:T(8,128)(2,1)S(1)} %get-tuple-element.95), channel_id=1, source_target_pairs={{0,2},{1,3},{2,0},{3,1},{4,6},{5,7},{6,4},{7,5},{8,10},{9,11},{10,... | collective-permute-start | bytes 589832 | tf_op jit(solution)/shard_map/d_att/ppermute | solution.py:531
  84.8 2.5 %collective-permute-start.17 = (bf16[192,512]{1,0:T(8,128)(2,1)S(1)}, bf16[192,512]{1,0:T(8,128)(2,1)S(1)}, u32[]{:S(2)}, u32[]{:S(2)}) collective-permute-start(bf16[192,512]{1,0:T(8,128)(2,1)S(1)} %get-tuple-element.96), channel_id=1, source_target_pairs={{0,3},{1,2},{2,1},{3,0},{4,7},{5,6},{6,5},{7,4},{8,11},{9,10},{10,... | collective-permute-start | bytes 589832 | tf_op jit(solution)/shard_map/d_att/ppermute | solution.py:531
  87.3 5.8 %collective-permute-done.15.d1 = bf16[192,512]{1,0:T(8,128)(2,1)S(1)} collective-permute-done((bf16[192,512]{1,0:T(8,128)(2,1)S(1)}, bf16[192,512]{1,0:T(8,128)(2,1)S(1)}, u32[]{:S(2)}, u32[]{:S(2)}) %collective-permute-start.15) | collective-permute-done | bytes 196640 | tf_op jit(solution)/shard_map/d_att/ppermute | solution.py:531
  93.1 6.9 %collective-permute-done.16.d2 = bf16[192,512]{1,0:T(8,128)(2,1)S(1)} collective-permute-done((bf16[192,512]{1,0:T(8,128)(2,1)S(1)}, bf16[192,512]{1,0:T(8,128)(2,1)S(1)}, u32[]{:S(2)}, u32[]{:S(2)}) %collective-permute-start.16) | collective-permute-done | bytes 196640 | tf_op jit(solution)/shard_map/d_att/ppermute | solution.py:531
  100.1 8.6 %back_kernel.1 = (f32[768,128]{1,0:T(8,128)S(1)}, bf16[768,128]{1,0:T(8,128)(2,1)S(1)}, bf16[768,128]{1,0:T(8,128)(2,1)S(1)}, bf16[768,128]{1,0:T(8,128)(2,1)S(1...) custom-call(s32[2]{0:T(128)S(1)} %pad_add_fusion.place, s32[1,8]{1,0:T(1,128)S(1)} %copy-done.8, ...), custom_call_target="tpu_custom_call" | custom-call | flops 10350000128 | bytes 8 | tf_op jit(solution)/shard_map/back_kernel/pallas_call | solution.py:21
  108.8 1.2 collective-permute-done.21
  110.0 0.5 collective-permute-start.22
  110.5 3.3 %collective-permute-done.22 = f32[8,768]{1,0:T(8,128)S(1)} collective-permute-done((f32[8,768]{1,0:T(8,128)S(1)}, f32[8,768]{1,0:T(8,128)S(1)}, u32[]{:S(2)}, u32[]{:S(2)}) %collective-permute-start.22) | collective-permute-done | bytes 24608 | tf_op jit(solution)/shard_map/vec/ppermute | solution.py:531
  113.8 1.5 collective-permute-start.23
  115.3 1.3 qkv_grad_kernel.1
  116.8 0.9 plane_kernel.3
  117.7 0.6 collective-permute-start.31
  118.9 4.2 %collective-permute-start.12 = (bf16[768,128]{1,0:T(8,128)(2,1)S(1)}, bf16[768,128]{1,0:T(8,128)(2,1)S(1)}, u32[]{:S(2)}, u32[]{:S(2)}) collective-permute-start(bf16[768,128]{1,0:T(8,128)(2,1)S(1)} %get-tuple-element.89), channel_id=1, source_target_pairs={{0,1},{1,0},{2,3},{3,2},{4,5},{5,4},{6,7},{7,6},{8,9},{9,8},{10,11... | collective-permute-start | bytes 589832 | tf_op jit(solution)/shard_map/mlp/ppermute | solution.py:531
  123.1 8.1 %collective-permute-done.12.m1 = bf16[768,128]{1,0:T(8,128)(2,1)S(1)} collective-permute-done((bf16[768,128]{1,0:T(8,128)(2,1)S(1)}, bf16[768,128]{1,0:T(8,128)(2,1)S(1)}, u32[]{:S(2)}, u32[]{:S(2)}) %collective-permute-start.12) | collective-permute-done | bytes 196640 | tf_op jit(solution)/shard_map/mlp/ppermute | solution.py:531
  131.2 3.5 %collective-permute-done.13.m2 = bf16[768,128]{1,0:T(8,128)(2,1)S(1)} collective-permute-done((bf16[768,128]{1,0:T(8,128)(2,1)S(1)}, bf16[768,128]{1,0:T(8,128)(2,1)S(1)}, u32[]{:S(2)}, u32[]{:S(2)}) %collective-permute-start.13) | collective-permute-done | bytes 196640 | tf_op jit(solution)/shard_map/mlp/ppermute | solution.py:531
  134.7 1.5 collective-permute-start.14
  136.2 2.4 %collective-permute-start.33 = (bf16[96,2304]{1,0:T(8,128)(2,1)S(1)}, bf16[96,2304]{1,0:T(8,128)(2,1)S(1)}, u32[]{:S(2)}, u32[]{:S(2)}) collective-permute-start(bf16[96,2304]{1,0:T(8,128)(2,1)S(1)} %get-tuple-element.123), channel_id=1, source_target_pairs={{0,24},{4,28},{8,16},{12,20},{16,8},{20,12},{24,0},{28,4},{1,25},{... | collective-permute-start | bytes 1327112 | tf_op jit(solution)/shard_map/grads_plane/ppermute | solution.py:531
  138.6 3.6 %collective-permute-done.14.m3 = bf16[768,128]{1,0:T(8,128)(2,1)S(1)} collective-permute-done((bf16[768,128]{1,0:T(8,128)(2,1)S(1)}, bf16[768,128]{1,0:T(8,128)(2,1)S(1)}, u32[]{:S(2)}, u32[]{:S(2)}) %collective-permute-start.14) | collective-permute-done | bytes 196640 | tf_op jit(solution)/shard_map/mlp/ppermute | solution.py:531
  142.3 2.5 %collective-permute-start.25 = (f32[8,768]{1,0:T(8,128)S(1)}, f32[8,768]{1,0:T(8,128)S(1)}, u32[]{:S(2)}, u32[]{:S(2)}) collective-permute-start(f32[8,768]{1,0:T(8,128)S(1)} %add.18), channel_id=1, source_target_pairs={{0,2},{1,3},{2,0},{3,1},{4,6},{5,7},{6,4},{7,5},{8,10},{9,11},{10,... | collective-permute-start | bytes 73736 | tf_op jit(solution)/shard_map/vec/ppermute | solution.py:531
  144.8 1.0 output_kernel.1
  145.7 1.5 collective-permute-done.25
  147.3 1.6 collective-permute-start.18
  148.8 0.7 collective-permute-start.19
  149.6 0.7 plane_kernel.2
  150.3 2.2 %collective-permute-start.20 = (bf16[768,128]{1,0:T(8,128)(2,1)S(1)}, bf16[768,128]{1,0:T(8,128)(2,1)S(1)}, u32[]{:S(2)}, u32[]{:S(2)}) collective-permute-start(bf16[768,128]{1,0:T(8,128)(2,1)S(1)} %get-tuple-element.108), channel_id=1, source_target_pairs={{0,3},{1,2},{2,1},{3,0},{4,7},{5,6},{6,5},{7,4},{8,11},{9,10},{10,... | collective-permute-start | bytes 589832 | tf_op jit(solution)/shard_map/back/ppermute | solution.py:531
  152.5 1.5 collective-permute-start.27
  154.0 0.6 fusion
  154.6 1.5 collective-permute-start.28
  156.1 1.6 grads_last_kernel.1
  158.2 7.1 %collective-permute-done.19.p2 = bf16[768,128]{1,0:T(8,128)(2,1)S(1)} collective-permute-done((bf16[768,128]{1,0:T(8,128)(2,1)S(1)}, bf16[768,128]{1,0:T(8,128)(2,1)S(1)}, u32[]{:S(2)}, u32[]{:S(2)}) %collective-permute-start.19) | collective-permute-done | bytes 196640 | tf_op jit(solution)/shard_map/back/ppermute | solution.py:531
  165.3 3.5 %collective-permute-start.35 = (bf16[192,96]{1,0:T(8,128)(2,1)S(1)}, bf16[192,96]{1,0:T(8,128)(2,1)S(1)}, u32[]{:S(2)}, u32[]{:S(2)}) collective-permute-start(bf16[192,96]{1,0:T(8,128)(2,1)S(1)} %get-tuple-element.126), channel_id=1, source_target_pairs={{0,2},{1,3},{2,0},{3,1},{4,6},{5,7},{6,4},{7,5},{8,10},{9,11},{10,... | collective-permute-start | bytes 110600 | tf_op jit(solution)/shard_map/out/ppermute | solution.py:531
  168.8 1.9 %collective-permute-start.36 = (bf16[192,96]{1,0:T(8,128)(2,1)S(1)}, bf16[192,96]{1,0:T(8,128)(2,1)S(1)}, u32[]{:S(2)}, u32[]{:S(2)}) collective-permute-start(bf16[192,96]{1,0:T(8,128)(2,1)S(1)} %get-tuple-element.127), channel_id=1, source_target_pairs={{0,3},{1,2},{2,1},{3,0},{4,7},{5,6},{6,5},{7,4},{8,11},{9,10},{10,... | collective-permute-start | bytes 110600 | tf_op jit(solution)/shard_map/out/ppermute | solution.py:531
  170.7 0.7 reshape_squeeze.3
  171.4 0.9 input_kernel.1
  172.3 0.8 qkv_last_kernel.1
  173.1 1.6 collective-permute-done.36.o3
  174.7 0.7 out_sum_kernel.1
  (57 shorter events, 2.0 us)
Async XLA Ops:
  0.6 10.9 %copy-start = (bf16[768,768]{1,0:T(8,128)(2,1)S(1)}, bf16[768,768]{1,0:T(8,128)(2,1)}, u32[]{:S(2)}) copy-start(bf16[768,768]{1,0:T(8,128)(2,1)} %w_up.1) | copy-start | bytes 3538948
  0.7 1.0 copy-start.5
  1.8 0.9 copy-start.6
  3.3 12.6 %collective-permute-start.2 = (bf16[352,384]{1,0:T(8,128)(2,1)S(1)}, bf16[352,384]{1,0:T(8,128)(2,1)S(1)}, u32[]{:S(2)}, u32[]{:S(2)}) collective-permute-start(bf16[352,384]{1,0:T(8,128)(2,1)S(1)} %message_kernel.1.x0), channel_id=1, source_target_pairs={{0,3},{1,2},{2,1},{3,0},{4,7},{5,6},{6,5},{7,4},{8,11},{9,10},{10,... | collective-permute-start | bytes 811016 | tf_op jit(solution)/shard_map/x/ppermute | solution.py:531
  8.4 23.0 %collective-permute-start.1 = (bf16[352,384]{1,0:T(8,128)(2,1)S(1)}, bf16[352,384]{1,0:T(8,128)(2,1)S(1)}, u32[]{:S(2)}, u32[]{:S(2)}) collective-permute-start(bf16[352,384]{1,0:T(8,128)(2,1)S(1)} %message_kernel.1.x0), channel_id=1, source_target_pairs={{0,2},{1,3},{2,0},{3,1},{4,6},{5,7},{6,4},{7,5},{8,10},{9,11},{10,... | collective-permute-start | bytes 811016 | tf_op jit(solution)/shard_map/x/ppermute | solution.py:531
  8.4 23.0 %collective-permute-start = (bf16[352,384]{1,0:T(8,128)(2,1)S(1)}, bf16[352,384]{1,0:T(8,128)(2,1)S(1)}, u32[]{:S(2)}, u32[]{:S(2)}) collective-permute-start(bf16[352,384]{1,0:T(8,128)(2,1)S(1)} %message_kernel.1.x0), channel_id=1, source_target_pairs={{0,1},{1,0},{2,3},{3,2},{4,5},{5,4},{6,7},{7,6},{8,9},{9,8},{10,11... | collective-permute-start | bytes 811016 | tf_op jit(solution)/shard_map/x/ppermute | solution.py:531
  11.5 1.3 copy-start.1
  12.8 1.2 copy-start.3
  14.9 18.2 %copy-start.7 = (bf16[128,768]{1,0:T(8,128)(2,1)S(1)}, bf16[128,768]{1,0:T(8,128)(2,1)}, u32[]{:S(2)}) copy-start(bf16[128,768]{1,0:T(8,128)(2,1)} %dy.1) | copy-start | bytes 589828
  14.9 18.2 %copy-start.4 = (bf16[768,3,192]{0,2,1:T(8,128)(2,1)S(1)}, bf16[768,3,192]{0,2,1:T(8,128)(2,1)}, u32[]{:S(2)}) copy-start(bf16[768,3,192]{0,2,1:T(8,128)(2,1)} %param.16) | copy-start | bytes 2654212
  14.9 18.2 %copy-start.8 = (s32[1,8]{1,0:T(1,128)S(1)}, s32[1,8]{1,0:T(1,128)}, u32[]{:S(2)}) copy-start(s32[1,8]{1,0:T(1,128)} %lengths.3) | copy-start | bytes 100
  31.4 18.7 %collective-permute-start.10 = (bf16[4,96,384]{2,1,0:T(8,128)(2,1)S(1)}, bf16[4,96,384]{2,1,0:T(8,128)(2,1)S(1)}, u32[]{:S(2)}, u32[]{:S(2)}) collective-permute-start(bf16[4,96,384]{2,1,0:T(8,128)(2,1)S(1)} %pieces_kernel.1.p00), channel_id=1, source_target_pairs={{0,4},{4,0},{8,12},{12,8},{16,20},{20,16},{24,28},{28,24},{1,5},{5... | collective-permute-start | bytes 884744 | tf_op jit(solution)/shard_map/w/ppermute | solution.py:531
  31.5 10.9 %collective-permute-start.9 = (bf16[4,96,384]{2,1,0:T(8,128)(2,1)S(1)}, bf16[4,96,384]{2,1,0:T(8,128)(2,1)S(1)}, u32[]{:S(2)}, u32[]{:S(2)}) collective-permute-start(bf16[4,96,384]{2,1,0:T(8,128)(2,1)S(1)} %pieces_kernel.1.p00), channel_id=1, source_target_pairs={{0,8},{4,12},{8,0},{12,4},{16,24},{20,28},{24,16},{28,20},{1,9},{5... | collective-permute-start | bytes 884744 | tf_op jit(solution)/shard_map/w/ppermute | solution.py:531
  33.1 12.0 %collective-permute-start.7 = (bf16[128,768]{1,0:T(8,128)(2,1)S(1)}, bf16[128,768]{1,0:T(8,128)(2,1)S(1)}, u32[]{:S(2)}, u32[]{:S(2)}) collective-permute-start(bf16[128,768]{1,0:T(8,128)(2,1)S(1)} %copy-done.7), channel_id=1, source_target_pairs={{0,2},{1,3},{2,0},{3,1},{4,6},{5,7},{6,4},{7,5},{8,10},{9,11},{10,... | collective-permute-start | bytes 589832 | tf_op jit(solution)/shard_map/dy/ppermute | solution.py:531
  39.4 26.7 %copy-start.2 = (bf16[768,768]{1,0:T(8,128)(2,1)S(1)}, bf16[768,768]{1,0:T(8,128)(2,1)}, u32[]{:S(2)}) copy-start(bf16[768,768]{1,0:T(8,128)(2,1)} %w_down.1) | copy-start | bytes 3538948
  39.4 9.9 %collective-permute-start.3 = (bf16[192,512]{1,0:T(8,128)(2,1)S(1)}, bf16[192,512]{1,0:T(8,128)(2,1)S(1)}, u32[]{:S(2)}, u32[]{:S(2)}) collective-permute-start(bf16[192,512]{1,0:T(8,128)(2,1)S(1)} %get-tuple-element.74.a0), channel_id=1, source_target_pairs={{0,1},{1,0},{2,3},{3,2},{4,5},{5,4},{6,7},{7,6},{8,9},{9,8},{10,11... | collective-permute-start | bytes 589832 | tf_op jit(solution)/shard_map/att/ppermute | solution.py:531
  42.5 8.7 %collective-permute-start.11 = (bf16[4,96,384]{2,1,0:T(8,128)(2,1)S(1)}, bf16[4,96,384]{2,1,0:T(8,128)(2,1)S(1)}, u32[]{:S(2)}, u32[]{:S(2)}) collective-permute-start(bf16[4,96,384]{2,1,0:T(8,128)(2,1)S(1)} %collective-permute-done.9.p01), channel_id=1, source_target_pairs={{0,4},{4,0},{8,12},{12,8},{16,20},{20,16},{24,28},{28,24},{1,5},{5... | collective-permute-start | bytes 884744 | tf_op jit(solution)/shard_map/w/ppermute | solution.py:531
  42.5 15.8 %collective-permute-start.6 = (bf16[128,768]{1,0:T(8,128)(2,1)S(1)}, bf16[128,768]{1,0:T(8,128)(2,1)S(1)}, u32[]{:S(2)}, u32[]{:S(2)}) collective-permute-start(bf16[128,768]{1,0:T(8,128)(2,1)S(1)} %copy-done.7), channel_id=1, source_target_pairs={{0,1},{1,0},{2,3},{3,2},{4,5},{5,4},{6,7},{7,6},{8,9},{9,8},{10,11... | collective-permute-start | bytes 589832 | tf_op jit(solution)/shard_map/dy/ppermute | solution.py:531
  45.1 13.2 %collective-permute-start.5 = (bf16[192,512]{1,0:T(8,128)(2,1)S(1)}, bf16[192,512]{1,0:T(8,128)(2,1)S(1)}, u32[]{:S(2)}, u32[]{:S(2)}) collective-permute-start(bf16[192,512]{1,0:T(8,128)(2,1)S(1)} %get-tuple-element.74.a0), channel_id=1, source_target_pairs={{0,3},{1,2},{2,1},{3,0},{4,7},{5,6},{6,5},{7,4},{8,11},{9,10},{10,... | collective-permute-start | bytes 589832 | tf_op jit(solution)/shard_map/att/ppermute | solution.py:531
  49.3 15.7 %collective-permute-start.4 = (bf16[192,512]{1,0:T(8,128)(2,1)S(1)}, bf16[192,512]{1,0:T(8,128)(2,1)S(1)}, u32[]{:S(2)}, u32[]{:S(2)}) collective-permute-start(bf16[192,512]{1,0:T(8,128)(2,1)S(1)} %get-tuple-element.74.a0), channel_id=1, source_target_pairs={{0,2},{1,3},{2,0},{3,1},{4,6},{5,7},{6,4},{7,5},{8,10},{9,11},{10,... | collective-permute-start | bytes 589832 | tf_op jit(solution)/shard_map/att/ppermute | solution.py:531
  50.1 15.9 %collective-permute-start.8 = (bf16[128,768]{1,0:T(8,128)(2,1)S(1)}, bf16[128,768]{1,0:T(8,128)(2,1)S(1)}, u32[]{:S(2)}, u32[]{:S(2)}) collective-permute-start(bf16[128,768]{1,0:T(8,128)(2,1)S(1)} %collective-permute-done.7.c2), channel_id=1, source_target_pairs={{0,1},{1,0},{2,3},{3,2},{4,5},{5,4},{6,7},{7,6},{8,9},{9,8},{10,11... | collective-permute-start | bytes 589832 | tf_op jit(solution)/shard_map/dy/ppermute | solution.py:531
  82.8 34.0 %collective-permute-start.30 = (bf16[384,2304]{1,0:T(8,128)(2,1)S(1)}, bf16[384,2304]{1,0:T(8,128)(2,1)S(1)}, u32[]{:S(2)}, u32[]{:S(2)}) collective-permute-start(bf16[384,2304]{1,0:T(8,128)(2,1)S(1)} %get-tuple-element.119), channel_id=1, source_target_pairs={{0,4},{4,0},{8,12},{12,8},{16,20},{20,16},{24,28},{28,24},{1,5},{5... | collective-permute-start | bytes 5308424 | tf_op jit(solution)/shard_map/grads_core/ppermute | solution.py:531
  82.9 10.3 %collective-permute-start.15 = (bf16[192,512]{1,0:T(8,128)(2,1)S(1)}, bf16[192,512]{1,0:T(8,128)(2,1)S(1)}, u32[]{:S(2)}, u32[]{:S(2)}) collective-permute-start(bf16[192,512]{1,0:T(8,128)(2,1)S(1)} %get-tuple-element.94), channel_id=1, source_target_pairs={{0,1},{1,0},{2,3},{3,2},{4,5},{5,4},{6,7},{7,6},{8,9},{9,8},{10,11... | collective-permute-start | bytes 589832 | tf_op jit(solution)/shard_map/d_att/ppermute | solution.py:531
  82.9 17.2 %collective-permute-start.16 = (bf16[192,512]{1,0:T(8,128)(2,1)S(1)}, bf16[192,512]{1,0:T(8,128)(2,1)S(1)}, u32[]{:S(2)}, u32[]{:S(2)}) collective-permute-start(bf16[192,512]{1,0:T(8,128)(2,1)S(1)} %get-tuple-element.95), channel_id=1, source_target_pairs={{0,2},{1,3},{2,0},{3,1},{4,6},{5,7},{6,4},{7,5},{8,10},{9,11},{10,... | collective-permute-start | bytes 589832 | tf_op jit(solution)/shard_map/d_att/ppermute | solution.py:531
  84.8 15.3 %collective-permute-start.17 = (bf16[192,512]{1,0:T(8,128)(2,1)S(1)}, bf16[192,512]{1,0:T(8,128)(2,1)S(1)}, u32[]{:S(2)}, u32[]{:S(2)}) collective-permute-start(bf16[192,512]{1,0:T(8,128)(2,1)S(1)} %get-tuple-element.96), channel_id=1, source_target_pairs={{0,3},{1,2},{2,1},{3,0},{4,7},{5,6},{6,5},{7,4},{8,11},{9,10},{10,... | collective-permute-start | bytes 589832 | tf_op jit(solution)/shard_map/d_att/ppermute | solution.py:531
  108.7 1.3 collective-permute-start.21
  110.0 3.8 %collective-permute-start.22 = (f32[8,768]{1,0:T(8,128)S(1)}, f32[8,768]{1,0:T(8,128)S(1)}, u32[]{:S(2)}, u32[]{:S(2)}) collective-permute-start(f32[8,768]{1,0:T(8,128)S(1)} %add.15), channel_id=1, source_target_pairs={{0,8},{4,12},{8,0},{12,4},{16,24},{20,28},{24,16},{28,20},{1,9},{5... | collective-permute-start | bytes 73736 | tf_op jit(solution)/shard_map/vec/ppermute | solution.py:531
  113.8 9.2 %collective-permute-start.23 = (f32[8,768]{1,0:T(8,128)S(1)}, f32[8,768]{1,0:T(8,128)S(1)}, u32[]{:S(2)}, u32[]{:S(2)}) collective-permute-start(f32[8,768]{1,0:T(8,128)S(1)} %add.16), channel_id=1, source_target_pairs={{0,16},{4,20},{8,24},{12,28},{16,0},{20,4},{24,8},{28,12},{1,17},{... | collective-permute-start | bytes 73736 | tf_op jit(solution)/shard_map/vec/ppermute | solution.py:531
  116.7 32.1 %collective-permute-start.26 = (bf16[384,576]{1,0:T(8,128)(2,1)S(1)}, bf16[384,576]{1,0:T(8,128)(2,1)S(1)}, u32[]{:S(2)}, u32[]{:S(2)}) collective-permute-start(bf16[384,576]{1,0:T(8,128)(2,1)S(1)} %get-tuple-element.113), channel_id=1, source_target_pairs={{0,4},{4,0},{8,12},{12,8},{16,20},{20,16},{24,28},{28,24},{1,5},{5... | collective-permute-start | bytes 1327112 | tf_op jit(solution)/shard_map/qkv_core/ppermute | solution.py:531
  117.7 32.5 %collective-permute-start.31 = (bf16[96,2304]{1,0:T(8,128)(2,1)S(1)}, bf16[96,2304]{1,0:T(8,128)(2,1)S(1)}, u32[]{:S(2)}, u32[]{:S(2)}) collective-permute-start(bf16[96,2304]{1,0:T(8,128)(2,1)S(1)} %get-tuple-element.121), channel_id=1, source_target_pairs={{0,8},{4,12},{8,0},{12,4},{16,24},{20,28},{24,16},{28,20},{1,9},{5... | collective-permute-start | bytes 1327112 | tf_op jit(solution)/shard_map/grads_plane/ppermute | solution.py:531
  118.3 34.1 %collective-permute-start.32 = (bf16[96,2304]{1,0:T(8,128)(2,1)S(1)}, bf16[96,2304]{1,0:T(8,128)(2,1)S(1)}, u32[]{:S(2)}, u32[]{:S(2)}) collective-permute-start(bf16[96,2304]{1,0:T(8,128)(2,1)S(1)} %get-tuple-element.122), channel_id=1, source_target_pairs={{0,16},{4,20},{8,24},{12,28},{16,0},{20,4},{24,8},{28,12},{1,17},{... | collective-permute-start | bytes 1327112 | tf_op jit(solution)/shard_map/grads_plane/ppermute | solution.py:531
  118.9 12.3 %collective-permute-start.12 = (bf16[768,128]{1,0:T(8,128)(2,1)S(1)}, bf16[768,128]{1,0:T(8,128)(2,1)S(1)}, u32[]{:S(2)}, u32[]{:S(2)}) collective-permute-start(bf16[768,128]{1,0:T(8,128)(2,1)S(1)} %get-tuple-element.89), channel_id=1, source_target_pairs={{0,1},{1,0},{2,3},{3,2},{4,5},{5,4},{6,7},{7,6},{8,9},{9,8},{10,11... | collective-permute-start | bytes 589832 | tf_op jit(solution)/shard_map/mlp/ppermute | solution.py:531
  123.1 11.6 %collective-permute-start.13 = (bf16[768,128]{1,0:T(8,128)(2,1)S(1)}, bf16[768,128]{1,0:T(8,128)(2,1)S(1)}, u32[]{:S(2)}, u32[]{:S(2)}) collective-permute-start(bf16[768,128]{1,0:T(8,128)(2,1)S(1)} %get-tuple-element.90), channel_id=1, source_target_pairs={{0,2},{1,3},{2,0},{3,1},{4,6},{5,7},{6,4},{7,5},{8,10},{9,11},{10,... | collective-permute-start | bytes 589832 | tf_op jit(solution)/shard_map/mlp/ppermute | solution.py:531
  131.2 5.0 %collective-permute-start.24 = (f32[8,768]{1,0:T(8,128)S(1)}, f32[8,768]{1,0:T(8,128)S(1)}, u32[]{:S(2)}, u32[]{:S(2)}) collective-permute-start(f32[8,768]{1,0:T(8,128)S(1)} %add.17), channel_id=1, source_target_pairs={{0,1},{1,0},{2,3},{3,2},{4,5},{5,4},{6,7},{7,6},{8,9},{9,8},{10,11... | collective-permute-start | bytes 73736 | tf_op jit(solution)/shard_map/vec/ppermute | solution.py:531
  134.7 7.6 %collective-permute-start.14 = (bf16[768,128]{1,0:T(8,128)(2,1)S(1)}, bf16[768,128]{1,0:T(8,128)(2,1)S(1)}, u32[]{:S(2)}, u32[]{:S(2)}) collective-permute-start(bf16[768,128]{1,0:T(8,128)(2,1)S(1)} %get-tuple-element.91), channel_id=1, source_target_pairs={{0,3},{1,2},{2,1},{3,0},{4,7},{5,6},{6,5},{7,4},{8,11},{9,10},{10,... | collective-permute-start | bytes 589832 | tf_op jit(solution)/shard_map/mlp/ppermute | solution.py:531
  136.2 18.4 %collective-permute-start.33 = (bf16[96,2304]{1,0:T(8,128)(2,1)S(1)}, bf16[96,2304]{1,0:T(8,128)(2,1)S(1)}, u32[]{:S(2)}, u32[]{:S(2)}) collective-permute-start(bf16[96,2304]{1,0:T(8,128)(2,1)S(1)} %get-tuple-element.123), channel_id=1, source_target_pairs={{0,24},{4,28},{8,16},{12,20},{16,8},{20,12},{24,0},{28,4},{1,25},{... | collective-permute-start | bytes 1327112 | tf_op jit(solution)/shard_map/grads_plane/ppermute | solution.py:531
  142.3 5.0 %collective-permute-start.25 = (f32[8,768]{1,0:T(8,128)S(1)}, f32[8,768]{1,0:T(8,128)S(1)}, u32[]{:S(2)}, u32[]{:S(2)}) collective-permute-start(f32[8,768]{1,0:T(8,128)S(1)} %add.18), channel_id=1, source_target_pairs={{0,2},{1,3},{2,0},{3,1},{4,6},{5,7},{6,4},{7,5},{8,10},{9,11},{10,... | collective-permute-start | bytes 73736 | tf_op jit(solution)/shard_map/vec/ppermute | solution.py:531
  147.3 10.4 %collective-permute-start.18 = (bf16[768,128]{1,0:T(8,128)(2,1)S(1)}, bf16[768,128]{1,0:T(8,128)(2,1)S(1)}, u32[]{:S(2)}, u32[]{:S(2)}) collective-permute-start(bf16[768,128]{1,0:T(8,128)(2,1)S(1)} %get-tuple-element.106), channel_id=1, source_target_pairs={{0,1},{1,0},{2,3},{3,2},{4,5},{5,4},{6,7},{7,6},{8,9},{9,8},{10,11... | collective-permute-start | bytes 589832 | tf_op jit(solution)/shard_map/back/ppermute | solution.py:531
  148.8 16.4 %collective-permute-start.19 = (bf16[768,128]{1,0:T(8,128)(2,1)S(1)}, bf16[768,128]{1,0:T(8,128)(2,1)S(1)}, u32[]{:S(2)}, u32[]{:S(2)}) collective-permute-start(bf16[768,128]{1,0:T(8,128)(2,1)S(1)} %get-tuple-element.107), channel_id=1, source_target_pairs={{0,2},{1,3},{2,0},{3,1},{4,6},{5,7},{6,4},{7,5},{8,10},{9,11},{10,... | collective-permute-start | bytes 589832 | tf_op jit(solution)/shard_map/back/ppermute | solution.py:531
  150.3 15.0 %collective-permute-start.20 = (bf16[768,128]{1,0:T(8,128)(2,1)S(1)}, bf16[768,128]{1,0:T(8,128)(2,1)S(1)}, u32[]{:S(2)}, u32[]{:S(2)}) collective-permute-start(bf16[768,128]{1,0:T(8,128)(2,1)S(1)} %get-tuple-element.108), channel_id=1, source_target_pairs={{0,3},{1,2},{2,1},{3,0},{4,7},{5,6},{6,5},{7,4},{8,11},{9,10},{10,... | collective-permute-start | bytes 589832 | tf_op jit(solution)/shard_map/back/ppermute | solution.py:531
  152.5 16.3 %collective-permute-start.27 = (bf16[96,576]{1,0:T(8,128)(2,1)S(1)}, bf16[96,576]{1,0:T(8,128)(2,1)S(1)}, u32[]{:S(2)}, u32[]{:S(2)}) collective-permute-start(bf16[96,576]{1,0:T(8,128)(2,1)S(1)} %get-tuple-element.115), channel_id=1, source_target_pairs={{0,8},{4,12},{8,0},{12,4},{16,24},{20,28},{24,16},{28,20},{1,9},{5... | collective-permute-start | bytes 331784 | tf_op jit(solution)/shard_map/qkv_plane/ppermute | solution.py:531
  154.6 17.7 %collective-permute-start.28 = (bf16[96,576]{1,0:T(8,128)(2,1)S(1)}, bf16[96,576]{1,0:T(8,128)(2,1)S(1)}, u32[]{:S(2)}, u32[]{:S(2)}) collective-permute-start(bf16[96,576]{1,0:T(8,128)(2,1)S(1)} %get-tuple-element.116), channel_id=1, source_target_pairs={{0,16},{4,20},{8,24},{12,28},{16,0},{20,4},{24,8},{28,12},{1,17},{... | collective-permute-start | bytes 331784 | tf_op jit(solution)/shard_map/qkv_plane/ppermute | solution.py:531
  157.7 14.6 %collective-permute-start.29 = (bf16[96,576]{1,0:T(8,128)(2,1)S(1)}, bf16[96,576]{1,0:T(8,128)(2,1)S(1)}, u32[]{:S(2)}, u32[]{:S(2)}) collective-permute-start(bf16[96,576]{1,0:T(8,128)(2,1)S(1)} %get-tuple-element.117), channel_id=1, source_target_pairs={{0,24},{4,28},{8,16},{12,20},{16,8},{20,12},{24,0},{28,4},{1,25},{... | collective-permute-start | bytes 331784 | tf_op jit(solution)/shard_map/qkv_plane/ppermute | solution.py:531
  165.3 7.8 %collective-permute-start.34 = (bf16[192,96]{1,0:T(8,128)(2,1)S(1)}, bf16[192,96]{1,0:T(8,128)(2,1)S(1)}, u32[]{:S(2)}, u32[]{:S(2)}) collective-permute-start(bf16[192,96]{1,0:T(8,128)(2,1)S(1)} %get-tuple-element.125), channel_id=1, source_target_pairs={{0,1},{1,0},{2,3},{3,2},{4,5},{5,4},{6,7},{7,6},{8,9},{9,8},{10,11... | collective-permute-start | bytes 110600 | tf_op jit(solution)/shard_map/out/ppermute | solution.py:531
  165.3 7.8 %collective-permute-start.35 = (bf16[192,96]{1,0:T(8,128)(2,1)S(1)}, bf16[192,96]{1,0:T(8,128)(2,1)S(1)}, u32[]{:S(2)}, u32[]{:S(2)}) collective-permute-start(bf16[192,96]{1,0:T(8,128)(2,1)S(1)} %get-tuple-element.126), channel_id=1, source_target_pairs={{0,2},{1,3},{2,0},{3,1},{4,6},{5,7},{6,4},{7,5},{8,10},{9,11},{10,... | collective-permute-start | bytes 110600 | tf_op jit(solution)/shard_map/out/ppermute | solution.py:531
  168.8 5.9 %collective-permute-start.36 = (bf16[192,96]{1,0:T(8,128)(2,1)S(1)}, bf16[192,96]{1,0:T(8,128)(2,1)S(1)}, u32[]{:S(2)}, u32[]{:S(2)}) collective-permute-start(bf16[192,96]{1,0:T(8,128)(2,1)S(1)} %get-tuple-element.127), channel_id=1, source_target_pairs={{0,3},{1,2},{2,1},{3,0},{4,7},{5,6},{6,5},{7,4},{8,11},{9,10},{10,... | collective-permute-start | bytes 110600 | tf_op jit(solution)/shard_map/out/ppermute | solution.py:531

commit v3 on v2

--- a/solution.py
+++ b/solution.py
@@ -75,30 +75,26 @@
     wd_o[...] = wd[...].T
 
 
-def message_kernel(place, tokens, w_out, out):
-    d = place[1]
-    rows, half = tokens.shape[0], tokens.shape[1] // 2
-    n = w_out.shape[0] // 2
-    out[0:rows, :] = tokens[:, :half]
-    out[rows : 2 * rows, :] = tokens[:, half:]
-    piece = w_out[pl.ds(pl.multiple_of(((d >> 1) & 1) * n, n), n), :]
-    out[2 * rows :, :] = jnp.where((d & 1) == 0, piece[:, :half], piece[:, half:])
-
-
 def pieces_kernel(x0, x1, x2, x3, out):
     n = out.shape[1]
     for k, ref in enumerate((x0, x1, x2, x3)):
         out[k] = ref[ref.shape[0] - n :, :]
 
 
-def out_weight_kernel(place, p00, p01, p10, p11, w_o, wt_o):
+def pair_kernel(a, b, out):
+    out[0:4] = a[...]
+    out[4:8] = b[...]
+
+
+def out_weight_kernel(place, here, there, w_o, wt_o):
     m, d = place[0], place[1]
-    _, rows, cols = p00.shape
-    for c, b, ref in ((0, 0, p00), (0, 1, p01), (1, 0, p10), (1, 1, p11)):
-        half, part = (d & 1) ^ c, ((d >> 1) & 1) ^ b
-        for k in range(4):
-            at = pl.multiple_of((m ^ k) * 2 * rows + part * rows, rows)
-            w_o[pl.ds(at, rows), pl.ds(pl.multiple_of(half * cols, cols), cols)] = ref[k]
+    rows = here.shape[1]
+    for c, ref in enumerate((here, there)):
+        for b in range(2):
+            part = (d & 3) ^ (c + 2 * b)
+            for k in range(4):
+                at = pl.multiple_of((m ^ k) * 4 * rows + part * rows, rows)
+                w_o[pl.ds(at, rows), :] = ref[4 * b + k]
     wt_o[...] = w_o[...].T
 
 
@@ -116,8 +112,7 @@
     half = buckets // 2
     for k, ref in enumerate((x0, x1, x2, x3)):
         at = pl.multiple_of((m ^ k) * rows, rows)
-        xt_o[: width // 2, pl.ds(at, rows)] = ref[0:rows, :].T
-        xt_o[width // 2 :, pl.ds(at, rows)] = ref[rows : 2 * rows, :].T
+        xt_o[:, pl.ds(at, rows)] = ref[0:rows, :].T
 
     def add(i, acc):
         return acc + fold(xt_o[chunk(i), :].astype(F32))
@@ -298,15 +293,14 @@
 
 def mlp_kernel(
     place, vec, act, dup, gm, ga, att, h2, dy, w_down_t,
-    m0, m1, m2, m3, vec_o, *rest,
+    m0, m2, m13, vec_o, *rest,
 ):
     grads, (mlp, sums) = rest[:-2], rest[-2:]
     m, d = place[0], place[1]
     rows = m0.shape[1]
     width, tokens = dy.shape
     mlp[...] = nn(w_down_t[...], act[...])
-    for k, ref in enumerate((m0, m1, m2, m3)):
-        ref[...] = mlp[:, pl.ds(pl.multiple_of((m ^ k) * rows, rows), rows)].astype(BF16)
+    put_halves(m, mlp, m0, m2, m13)
 
     def scale(i, carry):
         v = dy[chunk(i), :].astype(F32) * mlp[chunk(i), :]
@@ -318,6 +312,23 @@
     vec_o[5:6, :] = sums[...].T[0:1, :]
     pairs = ((h2, dup), (gm, act), (ga, att))
     put_blocks([nt(a[...], b[...]).astype(BF16) for a, b in pairs], d & 1, grads)
+
+
+def put_halves(m, ref, own, next_to, sent):
+    rows, width = own.shape[1], own.shape[0]
+
+    def of(k):
+        return ref[:, pl.ds(pl.multiple_of((m ^ k) * rows, rows), rows)]
+
+    own[...], next_to[...] = of(0), of(2)
+    sent[0:width, :] = of(1).astype(BF16)
+    sent[width:, :] = of(3).astype(BF16)
+
+
+def halve_kernel(own, next_to, recv, own_o, sent):
+    width = own.shape[0]
+    own_o[...] = own[...] + recv[0:width, :].astype(F32)
+    sent[...] = (next_to[...] + recv[width:, :].astype(F32)).astype(BF16)
 
 
 def put_blocks(parts, here, grads):
@@ -329,7 +340,7 @@
             grads[0][:, cols] = p
             continue
         sent, kept = grads
-        n = sent.shape[0] // 4
+        n = kept.shape[0] // 4
         for b in range(4):
             even, odd = p[2 * b * n : (2 * b + 1) * n], p[(2 * b + 1) * n : (2 * b + 2) * n]
             sent[b * n : (b + 1) * n, cols] = pick(here, odd, even)
@@ -342,7 +353,7 @@
 
 def back_kernel(
     place, lengths, d0, d1, d2, d3, qkv, pt, xt, stat, nb, cols, wq_t, vec,
-    p0, p1, p2, p3, dqkv_o, vec_o,
+    p0, p2, p13, dqkv_o, vec_o,
     score, ds, acc, buckets_of, wide, sums,
 ):
     m = place[0]
@@ -435,8 +446,7 @@
         return carry
 
     passes(width, back, 0)
-    for k, ref in enumerate((p0, p1, p2, p3)):
-        ref[...] = wide[:, pl.ds(pl.multiple_of((m ^ k) * rows, rows), rows)].astype(ref.dtype)
+    put_halves(m, wide, p0, p2, p13)
     turned = sums[...].T
     vec_o[...] = vec[...]
     vec_o[0:1, :] = turned[0:1, :]
@@ -448,57 +458,137 @@
     vec_o[6:7, :] = across(jnp.where(lane == row + m * n_rows, each, 0.0))
 
 
-def qkv_grad_kernel(place, h1, dqkv, *grads):
+def qkv_grad_kernel(place, h1, dqkv, vec, *grads):
     put_blocks([nt(h1[...], dqkv[...]).astype(BF16)], place[1] & 1, grads)
-
-
-def plane_kernel(place, keep, recv, b0, b1, b2, b3):
-    at = (place[1] >> 1) & 3
-    n = b0.shape[0]
-    for k, ref in enumerate((b0, b1, b2, b3)):
-        rows = pl.ds(pl.multiple_of((at ^ k) * n, n), n)
-        total = keep[rows, :].astype(F32) + recv[rows, :].astype(F32)
-        ref[...] = total.astype(ref.dtype)
-
-
-def four(refs):
-    total = refs[0][...].astype(F32)
-    for r in refs[1:]:
-        total = total + r[...].astype(F32)
-    return total
-
-
-def grads_last_kernel(place, b0, b1, b2, b3, up_o, down_o, o0, o1, o2, o3, turned):
+    if len(grads) > 1:
+        put_vec(vec[...], grads[0])
+
+
+def put_vec(vec, ref):
+    half = vec.shape[1] // 2
+    v = jnp.concatenate([vec[:, :half], vec[:, half:]])
+    high = v.astype(BF16)
+    n, rows = ref.shape[0], v.shape[0]
+    ref[n - 2 * rows : n - rows, :half] = high
+    ref[n - rows :, :half] = (v - high.astype(F32)).astype(BF16)
+
+
+def get_vec(ref, width):
+    n, rows, half = ref.shape[0], 16, width // 2
+    v = ref[n - 2 * rows : n - rows, :half].astype(F32) + ref[n - rows :, :half].astype(F32)
+    return jnp.concatenate([v[:8], v[8:]], axis=1)
+
+
+def grads_second_kernel(place, keep, recv, a_sent, a_kept, b_sent, b_kept):
+    x, y = (place[1] >> 1) & 1, (place[1] >> 2) & 1
+    n = keep.shape[0] // 4
+    half = a_sent.shape[1]
+
+    def block(i, cols):
+        rows = pl.ds(pl.multiple_of(i * n, n), n)
+        return keep[rows, cols].astype(F32) + recv[rows, cols].astype(F32)
+
+    left, right = slice(0, half), slice(half, 2 * half)
+    for i in range(2):
+        at = slice(i * n, (i + 1) * n)
+        a_sent[at, :] = block(2 * i + 1 - x, left).astype(BF16)
+        a_kept[at, :] = block(2 * i + x, left)
+        b_sent[at, :] = block(2 * (1 - y) + i, right).astype(BF16)
+        b_kept[at, :] = block(2 * y + i, right)
+
+
+def grads_third_kernel(place, a_keep, a_recv, b_keep, b_recv, a_sent, a_kept, b_sent, b_kept):
+    x, y = (place[1] >> 1) & 1, (place[1] >> 2) & 1
+    halve_rows(y, a_keep, a_recv, a_sent, a_kept)
+    halve_rows(x, b_keep, b_recv, b_sent, b_kept)
+
+
+def halve_rows(bit, keep, recv, sent, kept):
+    n = kept.shape[0]
+    for ref, b in ((sent, 1 - bit), (kept, bit)):
+        rows = pl.ds(pl.multiple_of(b * n, n), n)
+        ref[0:n, :] = (keep[rows, :] + recv[rows, :].astype(F32)).astype(ref.dtype)
+
+
+def qkv_second_kernel(place, vec, keep, recv, sent, kept, vec_o):
+    x = (place[1] >> 1) & 1
+    n = kept.shape[0] // 2
+    for i in range(2):
+        for ref, b in ((sent, 1 - x), (kept, x)):
+            rows = pl.ds(pl.multiple_of((2 * i + b) * n, n), n)
+            total = keep[rows, :].astype(F32) + recv[rows, :].astype(F32)
+            ref[i * n : (i + 1) * n, :] = total.astype(ref.dtype)
+    vec_o[...] = vec[...] + get_vec(recv, vec.shape[1])
+    put_vec(vec_o[...], sent)
+
+
+def qkv_third_kernel(place, vec, keep, recv, sent, kept, vec_o):
+    halve_rows((place[1] >> 2) & 1, keep, recv, sent, kept)
+    vec_o[...] = vec[...] + get_vec(recv, vec.shape[1])
+    put_vec(vec_o[...], sent)
+
+
+def last_kernel(
+    place, vec, a_keep, a_recv, b_keep, b_recv, q_keep, q_recv,
+    up_o, down_o, qkv_o, vec_o, o0, o1, o2, o3, turned,
+):
     m = place[0]
     hidden = up_o.shape[1]
     channels = o0.shape[0]
-    g = four((b0, b1, b2, b3))
-    up_o[...] = g[:, :hidden]
-    down_o[...] = g[:, hidden : 2 * hidden]
-    turned[...] = g[:, 2 * hidden :].T
+    a = a_keep[...] + a_recv[...].astype(F32)
+    b = b_keep[...] + b_recv[...].astype(F32)
+    share, half = a.shape
+    up_o[...] = a[:, :hidden]
+    down_o[:, : half - hidden] = a[:, hidden:]
+    down_o[:, half - hidden :] = b[:, : 2 * hidden - half]
+    turned[...] = b[:, 2 * hidden - half :].T
+    v = vec[...] + get_vec(q_recv, vec.shape[1])
+    vec_o[...] = v
+    tiles = v.shape[1] // 128
+    high = v.astype(BF16)
+    low = (v - high.astype(F32)).astype(BF16)
+    both = jnp.concatenate([high.astype(F32), low.astype(F32)]).astype(BF16)
     for k, ref in enumerate((o0, o1, o2, o3)):
-        v = turned[pl.ds(pl.multiple_of((m ^ k) * channels, channels), channels), :]
-        ref[...] = v.astype(ref.dtype)
-
-
-def out_sum_kernel(o0, o1, o2, o3, out):
-    out[...] = four((o0, o1, o2, o3))
-
-
-def qkv_last_kernel(b0, b1, b2, b3, out):
-    total = four((b0, b1, b2, b3))
-    channels = out.shape[2]
+        t = turned[pl.ds(pl.multiple_of((m ^ k) * channels, channels), channels), :]
+        ref[0:channels, 0:share] = t.astype(ref.dtype)
+        if k:
+            for i in range(tiles):
+                at = channels + 16 * i
+                ref[at : at + 16, :] = both[:, 128 * i : 128 * (i + 1)]
+    q = q_keep[...] + q_recv[0:share, :].astype(F32)
     for i in range(3):
-        out[i] = total[:, i * channels : (i + 1) * channels]
-
-
-def input_kernel(p0, p1, p2, p3, dy, out):
-    total = p0[...] + p1[...].astype(F32) + p2[...].astype(F32) + p3[...].astype(F32)
+        qkv_o[i] = q[:, i * channels : (i + 1) * channels]
+
+
+def small_kernel(vec, o0, o1, o2, o3, out, gains, biases, scales, table):
+    channels, share = out.shape
+    others = (o1, o2, o3)
+    total = o0[...]
+    v = vec[...]
+    for ref in others:
+        total = total + ref[0:channels, 0:share].astype(F32)
+        parts = []
+        for i in range(v.shape[1] // 128):
+            at = channels + 16 * i
+            both = ref[at : at + 16, :].astype(F32)
+            parts.append(both[:8] + both[8:])
+        v = v + jnp.concatenate(parts, axis=1)
+    out[...] = total
+    gains[...] = v[0:2]
+    biases[...] = v[2:4]
+    scales[...] = v[4:6]
+    n = table.shape[1]
+    for h in range(table.shape[0]):
+        table[h : h + 1, :] = v[6:7, h * n : (h + 1) * n]
+
+
+def input_kernel(own, recv, dy, out):
+    total = own[...] + recv[...].astype(F32)
     out[...] = (dy[...].astype(F32) + total.T).astype(BF16)
 
 
-def output_kernel(m0, m1, m2, m3, mid, cols, out):
-    total = m0[...].astype(F32) + m1[...].astype(F32) + m2[...].astype(F32) + m3[...].astype(F32)
+def output_kernel(own, recv, mid, cols, out):
+    total = own[...] + recv[...].astype(F32)
     out[...] = (mid[...] + cols[:, SCALE1 : SCALE1 + 1] * total).T.astype(BF16)
 
 
@@ -540,10 +630,8 @@
     ).T
     wq = jnp.transpose(w_qkv, (1, 2, 0)).reshape(3 * channels, width)
 
-    piece = (channels // 2, width // 2)
-    (sent,) = call(
-        message_kernel, [like((2 * rows + piece[0], piece[1]), BF16)], [place, tokens, w_out], n_smem=1
-    )
+    piece = channels // 4
+    sent = jnp.concatenate([tokens, lax.dynamic_slice_in_dim(w_out, (d & 3) * piece, piece, 0)])
     x = [sent] + [swap(sent, k, name="x") for k in (1, 2, 3)]
     dy1 = swap(cotangent, 1, name="dy")
     wq_t, w_up_t, w_down_t = call(
@@ -551,10 +639,11 @@
         [like((width, 3 * channels), BF16), like((hidden, width), BF16), like((width, hidden), BF16)],
         [wq, w_up, w_down],
     )
-    (part,) = call(pieces_kernel, [like((4,) + piece, BF16)], x)
+    x[1:] = lax.optimization_barrier((x[1:], wq_t))[0]
+    (part,) = call(pieces_kernel, [like((4, piece, width), BF16)], x)
     part_x = swap(part, 2, "dp", name="w")
-    dy2 = swap(after(cotangent, x[3]), 2, name="dy")
-    wq_now = after(wq, wq_t, w_up_t, w_down_t)
+    dy2 = swap(after(cotangent, *x[1:]), 2, name="dy")
+    wq_now = after(wq, wq_t, w_up_t, w_down_t, dy1)
     xt, h1, stat, qkv, pt, att = call(
         head_kernel,
         [
@@ -572,11 +661,13 @@
             pltpu.VMEM((group, 128), jnp.int32),
             pltpu.VMEM((3, 128, 128), F32),
         ],
-        us=7,
-    )
-    atts = [att] + [swap(att, k, name="att") for k in (1, 2, 3)]
-    dy = [cotangent, dy1, dy2, swap(after(dy2, atts[1]), 1, name="dy")]
-    w_pieces = [part, part_x, swap(part, 1, "dp", name="w"), swap(part_x, 1, "dp", name="w")]
+        us=200,
+    )
+    (parts,) = call(pair_kernel, [like((8, piece, width), BF16)], [part, after(part_x, att, dy2)])
+    att_sent = after(att, parts)
+    atts = [att] + [swap(att_sent, k, name="att") for k in (1, 2, 3)]
+    dy = [cotangent, dy1, dy2, swap(after(dy2, parts), 1, name="dy")]
+    w_pieces = [parts, swap(parts, 1, "dp", name="w")]
     w_out_full, w_out_t = call(
         out_weight_kernel, [like((width, width), BF16)] * 2, [place] + w_pieces, n_smem=1
     )
@@ -596,40 +687,35 @@
             pltpu.VMEM((hidden, group), F32),
             pltpu.VMEM((width, 128), F32),
         ],
-        us=12,
+        us=200,
     )
     d_att = [d0] + [swap(v, k, name="d_att") for k, v in ((1, d1), (2, d2), (3, d3))]
     grad_cols = 2 * hidden + width
     share = width // dp
     grad_like = [like((width // 2, grad_cols), BF16)] * 2 if fast else [like((width, grad_cols), BF16)]
-    m0, m1, m2, m3, vec, *grads = call(
+    block = like((width, rows), F32)
+    blocks = [block, block, like((2 * width, rows), BF16)]
+    m0, m2, m13, vec, *grads = call(
         mlp_kernel,
-        [like((width, rows), BF16)] * 4 + [like((8, width), F32)] + grad_like,
+        blocks + [like((8, width), F32)] + grad_like,
         [place, vec, act, dup, gm, ga, att_all, h2, dy_t, w_down_t],
         n_smem=1,
         scratch=[pltpu.VMEM((width, group), F32), pltpu.VMEM((width, 128), F32)],
     )
-    mlp = [m0] + [swap(v, k, name="mlp") for k, v in ((1, m1), (2, m2), (3, m3))]
-
-    def planes(grads, n, name):
-        kept = grads[1]
-        recv = swap(grads[0], 1, "dp", name=name + "_core")
-        b = call(
-            plane_kernel,
-            [like((share, n), F32)] + [like((share, n), BF16)] * 3,
-            [place, kept, recv],
-            n_smem=1,
-        )
-        return [b[0]] + [swap(b[k], 2 * k, "dp", name=name + "_plane") for k in (1, 2, 3)]
-
+
+    def halved(own, next_to, recv, name):
+        half_like = [block, like((width, rows), BF16)]
+        own, sent = call(halve_kernel, half_like, [own, next_to, recv])
+        return [own, swap(sent, 2, name=name)]
+
+    m_recv = swap(after(m13, *d_att[1:]), 1, name="mlp")
+    half = grad_cols // 2
     if fast:
-        blocks = planes(grads, grad_cols, "grads")
-
-    p0, p1, p2, p3, dqkv, vec = call(
+        g_recv = swap(grads[0], 1, "dp", name="grads_core")
+
+    p0, p2, p13, dqkv, vec = call(
         back_kernel,
-        [like((width, rows), F32)]
-        + [like((width, rows), BF16)] * 3
-        + [like((3 * channels, group), BF16), like((8, width), F32)],
+        blocks + [like((3 * channels, group), BF16), like((8, width), F32)],
         [place, page_lengths] + d_att + [qkv, pt, xt, stat, nb, cols, wq_t, vec],
         n_smem=2,
         scratch=[
@@ -640,14 +726,18 @@
             pltpu.VMEM((width, group), F32),
             pltpu.VMEM((width, 128), F32),
         ],
-        us=9,
-    )
-    (output,) = call(output_kernel, [like((rows, width), BF16)], mlp + [mid, cols])
-    p1, p2, p3, output = lax.optimization_barrier((p1, p2, p3, output))
-    back = [p0] + [swap(v, k, name="back") for k, v in ((1, p1), (2, p2), (3, p3))]
+        us=200,
+    )
+    mlp = halved(m0, m2, m_recv, "mlp")
+    p_recv = swap(after(p13, m_recv), 1, name="back")
+    back = halved(after(p0, mlp[1]), p2, p_recv, "back")
     n = 3 * channels
-    grad_like = [like((width // 2, n), BF16)] * 2 if fast else [like((width, n), BF16)]
-    qkv_grads = call(qkv_grad_kernel, grad_like, [place, h1, dqkv], n_smem=1)
+    extra = 4 * vec.shape[0]
+    if fast:
+        grad_like = [like((width // 2 + extra, n), BF16), like((width // 2, n), BF16)]
+    else:
+        grad_like = [like((width, n), BF16)]
+    qkv_grads = call(qkv_grad_kernel, grad_like, [place, h1, dqkv, vec], n_smem=1)
 
     def reduced(g):
         g = g.reshape(dp, width // dp, g.shape[1])
@@ -664,19 +754,57 @@
         return g[0]
 
     if fast:
-        qkv_blocks = planes(qkv_grads, n, "qkv")
-        grad_up, grad_down, o0, o1, o2, o3 = call(
-            grads_last_kernel,
+        q_recv = swap(after(qkv_grads[0], m_recv), 1, "dp", name="qkv_core")
+        a_sent, a_kept, b_sent, b_kept = call(
+            grads_second_kernel,
+            [like((2 * share, half), BF16), like((2 * share, half), F32)] * 2,
+            [place, after(grads[1], q_recv), g_recv],
+            n_smem=1,
+        )
+        a_recv = swap(a_sent, 2, "dp", name="grads_a")
+        b_recv = swap(b_sent, 4, "dp", name="grads_b")
+        vec_like = [like(vec.shape, F32)]
+        sent, kept, vec = call(
+            qkv_second_kernel,
+            [like((2 * share + extra, n), BF16), like((2 * share, n), F32)] + vec_like,
+            [place, vec, qkv_grads[1], q_recv],
+            n_smem=1,
+        )
+        recv = swap(sent, 2, "dp", name="qkv_x")
+        sent, kept, vec = call(
+            qkv_third_kernel,
+            [like((share + extra, n), BF16), like((share, n), F32)] + vec_like,
+            [place, vec, kept, recv],
+            n_smem=1,
+        )
+        recv = swap(sent, 4, "dp", name="qkv_y")
+        a_sent, a_kept, b_sent, b_kept = call(
+            grads_third_kernel,
+            [like((share, half), BF16), like((share, half), F32)] * 2,
+            [place, after(a_kept, kept, back[0]), a_recv, b_kept, b_recv],
+            n_smem=1,
+        )
+        a_recv = swap(a_sent, 4, "dp", name="grads_a")
+        b_recv = swap(b_sent, 2, "dp", name="grads_b")
+        message = like((channels + 2 * vec.size // 128, 128), BF16)
+        grad_up, grad_down, grad_qkv, vec, o0, o1, o2, o3 = call(
+            last_kernel,
             [like((share, hidden), F32)] * 2
+            + [like((3, share, channels), F32), like(vec.shape, F32)]
             + [like((channels, share), F32)]
-            + [like((channels, share), BF16)] * 3,
-            [place] + blocks,
+            + [message] * 3,
+            [place, vec, a_kept, a_recv, b_kept, b_recv, kept, recv],
             n_smem=1,
             scratch=[pltpu.VMEM((width, share), F32)],
         )
         o1, o2, o3 = (swap(v, k, name="out") for k, v in ((1, o1), (2, o2), (3, o3)))
-        (grad_out,) = call(out_sum_kernel, [like((channels, share), F32)], [o0, o1, o2, o3])
-        (grad_qkv,) = call(qkv_last_kernel, [like((3, share, channels), F32)], qkv_blocks)
+        grad_out, gains, biases, scales, grad_table = call(
+            small_kernel,
+            [like((channels, share), F32)]
+            + [like((2, width), F32)] * 3
+            + [like((heads * mp, buckets), F32)],
+            [vec, o0, o1, o2, o3],
+        )
         grad_qkv = jnp.transpose(grad_qkv, (1, 0, 2))
     else:
         summed = reduced(grads[0])
@@ -690,25 +818,25 @@
         grad_out = out_part(0)
         for k in range(1, mp):
             grad_out = grad_out + swap(out_part(k).astype(BF16), k).astype(F32)
-
-    bit = 1
-    while bit < dp:
-        vec = vec + swap(vec, bit, "dp", name="vec")
-        bit *= 2
-    for k in (1, 2):
-        vec = vec + swap(vec, k, name="vec")
+        bit = 1
+        while bit < dp:
+            vec = vec + swap(vec, bit, "dp", name="vec")
+            bit *= 2
+        for k in (1, 2):
+            vec = vec + swap(vec, k, name="vec")
+        gains, biases, scales = vec[0:2], vec[2:4], vec[4:6]
+        grad_table = vec[6, : heads * mp * buckets].reshape(heads * mp, buckets)
 
     (output,) = call(output_kernel, [like((rows, width), BF16)], mlp + [mid, cols])
     (grad_input,) = call(input_kernel, [like((rows, width), BF16)], back + [cotangent])
-    grad_table = vec[6, : heads * mp * buckets].reshape(heads * mp, buckets).T
     return (
         output,
         grad_input,
-        vec[0:2],
-        vec[2:4],
-        vec[4:6],
+        gains,
+        biases,
+        scales,
         grad_qkv,
-        grad_table,
+        grad_table.T,
         grad_out,
         grad_up,
         grad_down.T,

time: 176 us -> 154 us (0.88)
  waiting for transfers between devices: 78.4 us -> 60.3 us
  starting transfers between devices: 45.8 us -> 37.2 us
  Pallas kernels: 42 us -> 48.7 us
  local copies, waits for them, and re-layouts: 8.2 us -> 5.87 us
    ppermute x37 -> x29, waiting for transfers between devices: 78.4 us -> 60.3 us  [swap(): return lax.ppermute(v, axis, [(i, i ^ k) for i in range(n)])]
    ppermute x37 -> x29, starting transfers between devices: 45.8 us -> 37.2 us  [swap(): return lax.ppermute(v, axis, [(i, i ^ k) for i in range(n)])]
    pallas_call x16 -> x19, Pallas kernels: 42 us -> 48.7 us  [call(): pl.pallas_call(kernel, out_shape=tuple(outs), in_specs=[SMEM] * n_smem +...]
    unnamed x19 -> x17, local copies, waits for them, and re-layouts: 5.2 us -> 4.18 us
  transfers between devices with their start and end apart: 37 -> 29, of which waited for: 17 -> 13; matrix products, arithmetic and copies ran while one was open for 2% -> 2% of each run, Pallas kernels for 14% -> 20%
where the time goes in v3:
time: 154 us
  waiting for transfers between devices  60.3 us (39%)
  Pallas kernels  48.7 us (32%)
  starting transfers between devices  37.2 us (24%)
  local copies, waits for them, and re-layouts  5.87 us (4%)
    ppermute x29, waiting for transfers between devices, swap(): return lax.ppermute(v, axis, [(i, i ^ k) for i in range(n)])  60.3 us
    pallas_call x19, Pallas kernels, call(): pl.pallas_call(kernel, out_shape=tuple(outs), in_specs=[SMEM] * n_smem +...  48.7 us
    ppermute x29, starting transfers between devices, swap(): return lax.ppermute(v, axis, [(i, i ^ k) for i in range(n)])  37.2 us
    unnamed x17, local copies, waits for them, and re-layouts  4.18 us
  transfers between devices with their start and end apart: 29, of which 13 were waited for; matrix products, arithmetic and copies ran while one was open for 2% of the time, Pallas kernels for 20%

profile of v3, /device:TPU:0, one launch (start us, length us, event | category | flops | bytes accessed | tf_op | source)
XLA Modules:
  0.0 154.0 jit_solution(9480606067350747652)
XLA Ops:
  0.7 0.9 copy-done
  1.6 0.9 pad_maximum_fusion.x0
  2.6 5.1 %collective-permute-start.2 = (bf16[176,768]{1,0:T(8,128)(2,1)S(1)}, bf16[176,768]{1,0:T(8,128)(2,1)S(1)}, u32[]{:S(2)}, u32[]{:S(2)}) collective-permute-start(bf16[176,768]{1,0:T(8,128)(2,1)S(1)} %pad_maximum_fusion.x0), channel_id=1, source_target_pairs={{0,3},{1,2},{2,1},{3,0},{4,7},{5,6},{6,5},{7,4},{8,11},{9,10},{10,... | collective-permute-start | bytes 811016 | tf_op jit(solution)/shard_map/x/ppermute | solution.py:621
  7.7 0.6 collective-permute-start
  8.3 1.4 collective-permute-start.3
  9.7 0.8 fusion
  10.5 0.8 copy.28.table
  11.3 0.7 concatenate.7
  12.0 0.2 copy.27
  12.2 1.3 copy-done.2
  13.5 1.2 copy-done.4
  14.6 0.9 turn_kernel.1
  15.7 13.8 %collective-permute-done.3.c1 = bf16[128,768]{1,0:T(8,128)(2,1)S(1)} collective-permute-done((bf16[128,768]{1,0:T(8,128)(2,1)}, bf16[128,768]{1,0:T(8,128)(2,1)S(1)}, u32[]{:S(2)}, u32[]{:S(2)}) %collective-permute-start.3) | collective-permute-done | bytes 196640 | tf_op jit(solution)/shard_map/dy/ppermute | solution.py:621
  29.4 1.3 collective-permute-done.1.x2
  30.7 0.7 pieces_kernel.1.a
  31.4 1.1 collective-permute-start.5
  32.6 1.5 collective-permute-start.4
  34.1 6.3 %head_kernel.1 = (bf16[768,512]{1,0:T(8,128)(2,1)S(1)}, bf16[768,512]{1,0:T(8,128)(2,1)S(1)}, f32[8,512]{1,0:T(8,128)S(1)}, bf16[576,512]{1,0:T(8,128)(2,1)S(1)}...) custom-call(s32[2]{0:T(128)S(1)} %pad_add_fusion.place, s32[1,8]{1,0:T(1,128)S(1)} %copy-done.6, ...), custom_call_target="tpu_custom_call" | custom-call | flops 230000001024 | bytes 8 | tf_op jit(solution)/shard_map/head_kernel/pallas_call | solution.py:21
  40.3 2.5 %collective-permute-done.5.c2 = bf16[128,768]{1,0:T(8,128)(2,1)} collective-permute-done((bf16[128,768]{1,0:T(8,128)(2,1)}, bf16[128,768]{1,0:T(8,128)(2,1)}, u32[]{:S(2)}, u32[]{:S(2)}) %collective-permute-start.5) | collective-permute-done | bytes 196640 | tf_op jit(solution)/shard_map/dy/ppermute | solution.py:621
  42.8 1.2 pair_kernel.1.here
  44.1 1.7 %collective-permute-start.8 = (bf16[192,512]{1,0:T(8,128)(2,1)S(1)}, bf16[192,512]{1,0:T(8,128)(2,1)S(1)}, u32[]{:S(2)}, u32[]{:S(2)}) collective-permute-start(bf16[192,512]{1,0:T(8,128)(2,1)S(1)} %get-tuple-element.103.a0), channel_id=1, source_target_pairs={{0,3},{1,2},{2,1},{3,0},{4,7},{5,6},{6,5},{7,4},{8,11},{9,10},{10,... | collective-permute-start | bytes 589832 | tf_op jit(solution)/shard_map/att/ppermute | solution.py:621
  45.8 0.8 collective-permute-start.7
  46.7 1.9 %collective-permute-start.6 = (bf16[192,512]{1,0:T(8,128)(2,1)S(1)}, bf16[192,512]{1,0:T(8,128)(2,1)S(1)}, u32[]{:S(2)}, u32[]{:S(2)}) collective-permute-start(bf16[192,512]{1,0:T(8,128)(2,1)S(1)} %get-tuple-element.103.a0), channel_id=1, source_target_pairs={{0,1},{1,0},{2,3},{3,2},{4,5},{5,4},{6,7},{7,6},{8,9},{9,8},{10,11... | collective-permute-start | bytes 589832 | tf_op jit(solution)/shard_map/att/ppermute | solution.py:621
  48.5 0.2 collective-permute-start.9
  48.7 1.0 out_weight_kernel.1
  49.7 4.1 %collective-permute-done.8.a3 = bf16[192,512]{1,0:T(8,128)(2,1)S(1)} collective-permute-done((bf16[192,512]{1,0:T(8,128)(2,1)S(1)}, bf16[192,512]{1,0:T(8,128)(2,1)S(1)}, u32[]{:S(2)}, u32[]{:S(2)}) %collective-permute-start.8) | collective-permute-done | bytes 196640 | tf_op jit(solution)/shard_map/att/ppermute | solution.py:621
  53.8 10.8 %collective-permute-done.7.a2 = bf16[192,512]{1,0:T(8,128)(2,1)S(1)} collective-permute-done((bf16[192,512]{1,0:T(8,128)(2,1)S(1)}, bf16[192,512]{1,0:T(8,128)(2,1)S(1)}, u32[]{:S(2)}, u32[]{:S(2)}) %collective-permute-start.7) | collective-permute-done | bytes 196640 | tf_op jit(solution)/shard_map/att/ppermute | solution.py:621
  64.7 1.3 collective-permute-done.9.c3
  66.0 12.2 %middle_kernel.1 = (bf16[192,512]{1,0:T(8,128)(2,1)S(1)}, bf16[192,512]{1,0:T(8,128)(2,1)S(1)}, bf16[192,512]{1,0:T(8,128)(2,1)S(1)}, bf16[192,512]{1,0:T(8,128)...) custom-call(s32[2]{0:T(128)S(1)} %pad_add_fusion.place, ...), custom_call_target="tpu_custom_call" | custom-call | flops 230000001024 | bytes 8 | tf_op jit(solution)/shard_map/middle_kernel/pallas_call | solution.py:21
  78.2 2.2 %collective-permute-start.12 = (bf16[192,512]{1,0:T(8,128)(2,1)S(1)}, bf16[192,512]{1,0:T(8,128)(2,1)S(1)}, u32[]{:S(2)}, u32[]{:S(2)}) collective-permute-start(bf16[192,512]{1,0:T(8,128)(2,1)S(1)} %get-tuple-element.120), channel_id=1, source_target_pairs={{0,2},{1,3},{2,0},{3,1},{4,6},{5,7},{6,4},{7,5},{8,10},{9,11},{10,... | collective-permute-start | bytes 589832 | tf_op jit(solution)/shard_map/d_att/ppermute | solution.py:621
  80.4 2.1 %collective-permute-start.13 = (bf16[192,512]{1,0:T(8,128)(2,1)S(1)}, bf16[192,512]{1,0:T(8,128)(2,1)S(1)}, u32[]{:S(2)}, u32[]{:S(2)}) collective-permute-start(bf16[192,512]{1,0:T(8,128)(2,1)S(1)} %get-tuple-element.121), channel_id=1, source_target_pairs={{0,3},{1,2},{2,1},{3,0},{4,7},{5,6},{6,5},{7,4},{8,11},{9,10},{10,... | collective-permute-start | bytes 589832 | tf_op jit(solution)/shard_map/d_att/ppermute | solution.py:621
  82.6 6.4 %mlp_kernel.1 = (f32[768,128]{1,0:T(8,128)S(1)}, f32[768,128]{1,0:T(8,128)S(1)}, bf16[1536,128]{1,0:T(8,128)(2,1)}, f32[8,768]{1,0:T(8,128)S(1)}, bf16[384,2304]...) custom-call(s32[2]{0:T(128)S(1)} %pad_add_fusion.place, f32[8,768]{1,0:T(8,128)S(1)} %get-tuple-element.108.vec, ...), custom_call_target="tpu_custom_call" | custom-call | flops 11500000 | bytes 8 | tf_op jit(solution)/shard_map/mlp_kernel/pallas_call | solution.py:21
  88.9 6.5 %collective-permute-done.12.d2 = bf16[192,512]{1,0:T(8,128)(2,1)S(1)} collective-permute-done((bf16[192,512]{1,0:T(8,128)(2,1)S(1)}, bf16[192,512]{1,0:T(8,128)(2,1)S(1)}, u32[]{:S(2)}, u32[]{:S(2)}) %collective-permute-start.12) | collective-permute-done | bytes 196640 | tf_op jit(solution)/shard_map/d_att/ppermute | solution.py:621
  95.4 3.8 %collective-permute-start.14 = (bf16[1536,128]{1,0:T(8,128)(2,1)}, bf16[1536,128]{1,0:T(8,128)(2,1)}, u32[]{:S(2)}, u32[]{:S(2)}) collective-permute-start(bf16[1536,128]{1,0:T(8,128)(2,1)} %get-tuple-element.122), channel_id=1, source_target_pairs={{0,1},{1,0},{2,3},{3,2},{4,5},{5,4},{6,7},{7,6},{8,9},{9,8},{10,11... | collective-permute-start | bytes 1179656 | tf_op jit(solution)/shard_map/mlp/ppermute | solution.py:621
  99.2 8.6 %back_kernel.1 = (f32[768,128]{1,0:T(8,128)S(1)}, f32[768,128]{1,0:T(8,128)S(1)}, bf16[1536,128]{1,0:T(8,128)(2,1)S(1)}, bf16[576,512]{1,0:T(8,128)(2,1)S(1)}, f32[8,768]{1,0:T(8,128)S(1)}) custom-call(s32[2]{0:T(128)S(1)} %pad_add_fusion.place, s32[1,8]{1,0:T(1,128)S(1)} %copy-done.7, bf16[192,512]{1,0:T(8,128)(2,1)S(1)} %get-tuple-element.126.d0, ...), custom_call_target="tpu_custom_call" | custom-call | flops 230000001024 | bytes 8 | tf_op jit(solution)/shard_map/back_kernel/pallas_call | solution.py:21
  107.9 1.4 qkv_grad_kernel.1
  109.3 1.9 %collective-permute-done.18.recv = bf16[416,576]{1,0:T(8,128)(2,1)S(1)} collective-permute-done((bf16[416,576]{1,0:T(8,128)(2,1)S(1)}, bf16[416,576]{1,0:T(8,128)(2,1)S(1)}, u32[]{:S(2)}, u32[]{:S(2)}) %collective-permute-start.18) | collective-permute-done | bytes 479264 | tf_op jit(solution)/shard_map/qkv_core/ppermute | solution.py:621
  111.2 1.9 %grads_second_kernel.1 = (bf16[192,1152]{1,0:T(8,128)(2,1)S(1)}, f32[192,1152]{1,0:T(8,128)S(1)}, bf16[192,1152]{1,0:T(8,128)(2,1)S(1)}, f32[192,1152]{1,0:T(8,128)S(1)}) custom-call(s32[2]{0:T(128)S(1)} %pad_add_fusion.place, bf16[384,2304]{1,0:T(8,128)(2,1)S(1)} %get-tuple-element.150.keep, bf16[384,2304]{1,0:T(8,128)(2,1)} %collective-permute-done.20.recv), custom_call_target="tpu_custom_call" | custom-call | flops 11500000 | bytes 8 | tf_op jit(solution)/shard_map/grads_second_kernel/pallas_call | solution.py:21
  113.1 1.6 %collective-permute-start.21 = (bf16[192,1152]{1,0:T(8,128)(2,1)S(1)}, bf16[192,1152]{1,0:T(8,128)(2,1)S(1)}, u32[]{:S(2)}, u32[]{:S(2)}) collective-permute-start(bf16[192,1152]{1,0:T(8,128)(2,1)S(1)} %get-tuple-element.155), channel_id=1, source_target_pairs={{0,8},{4,12},{8,0},{12,4},{16,24},{20,28},{24,16},{28,20},{1,9},{5... | collective-permute-start | bytes 1327112 | tf_op jit(solution)/shard_map/grads_a/ppermute | solution.py:621
  114.7 1.5 collective-permute-start.22
  116.2 0.4 collective-permute-start.16
  116.6 0.7 qkv_second_kernel.1
  117.3 0.6 collective-permute-start.19
  117.9 1.1 halve_kernel.2
  119.0 1.9 %collective-permute-start.15 = (bf16[768,128]{1,0:T(8,128)(2,1)S(1)}, bf16[768,128]{1,0:T(8,128)(2,1)S(1)}, u32[]{:S(2)}, u32[]{:S(2)}) collective-permute-start(bf16[768,128]{1,0:T(8,128)(2,1)S(1)} %get-tuple-element.124), channel_id=1, source_target_pairs={{0,2},{1,3},{2,0},{3,1},{4,6},{5,7},{6,4},{7,5},{8,10},{9,11},{10,... | collective-permute-start | bytes 589832 | tf_op jit(solution)/shard_map/mlp/ppermute | solution.py:621
  120.9 8.0 %collective-permute-done.15.recv = bf16[768,128]{1,0:T(8,128)(2,1)S(1)} collective-permute-done((bf16[768,128]{1,0:T(8,128)(2,1)S(1)}, bf16[768,128]{1,0:T(8,128)(2,1)S(1)}, u32[]{:S(2)}, u32[]{:S(2)}) %collective-permute-start.15) | collective-permute-done | bytes 196640 | tf_op jit(solution)/shard_map/mlp/ppermute | solution.py:621
  129.0 2.0 %collective-permute-done.16.recv = bf16[1536,128]{1,0:T(8,128)(2,1)S(1)} collective-permute-done((bf16[1536,128]{1,0:T(8,128)(2,1)S(1)}, bf16[1536,128]{1,0:T(8,128)(2,1)S(1)}, u32[]{:S(2)}, u32[]{:S(2)}) %collective-permute-start.16) | collective-permute-done | bytes 393248 | tf_op jit(solution)/shard_map/back/ppermute | solution.py:621
  131.0 0.1 halve_kernel.3
  131.1 0.5 collective-permute-done.19.recv
  131.5 0.6 qkv_third_kernel.1
  132.2 0.7 grads_third_kernel.1
  132.9 1.6 %collective-permute-start.23 = (bf16[96,1152]{1,0:T(8,128)(2,1)S(1)}, bf16[96,1152]{1,0:T(8,128)(2,1)S(1)}, u32[]{:S(2)}, u32[]{:S(2)}) collective-permute-start(bf16[96,1152]{1,0:T(8,128)(2,1)S(1)} %get-tuple-element.159), channel_id=1, source_target_pairs={{0,16},{4,20},{8,24},{12,28},{16,0},{20,4},{24,8},{28,12},{1,17},{... | collective-permute-start | bytes 663560 | tf_op jit(solution)/shard_map/grads_a/ppermute | solution.py:621
  134.5 1.5 collective-permute-start.24
  136.0 0.5 collective-permute-start.25
  136.5 0.4 collective-permute-start.17
  136.9 6.2 %collective-permute-done.25.q_recv = bf16[128,576]{1,0:T(8,128)(2,1)S(1)} collective-permute-done((bf16[128,576]{1,0:T(8,128)(2,1)S(1)}, bf16[128,576]{1,0:T(8,128)(2,1)S(1)}, u32[]{:S(2)}, u32[]{:S(2)}) %collective-permute-start.25) | collective-permute-done | bytes 147488 | tf_op jit(solution)/shard_map/qkv_y/ppermute | solution.py:621
  143.1 1.6 %last_kernel.1 = (f32[96,768]{1,0:T(8,128)}, f32[96,768]{1,0:T(8,128)}, f32[3,96,192]{2,1,0:T(8,128)}, f32[8,768]{1,0:T(8,128)S(1)}, f32[192,96]{1,0:T(8,128)S(1...) custom-call(s32[2]{0:T(128)S(1)} %pad_add_fusion.place, ...), custom_call_target="tpu_custom_call" | custom-call | flops 11500000 | bytes 8 | tf_op jit(solution)/shard_map/last_kernel/pallas_call | solution.py:21
  144.8 0.4 collective-permute-start.26
  145.2 1.8 %collective-permute-start.27 = (bf16[288,128]{1,0:T(8,128)(2,1)S(1)}, bf16[288,128]{1,0:T(8,128)(2,1)S(1)}, u32[]{:S(2)}, u32[]{:S(2)}) collective-permute-start(bf16[288,128]{1,0:T(8,128)(2,1)S(1)} %get-tuple-element.166), channel_id=1, source_target_pairs={{0,2},{1,3},{2,0},{3,1},{4,6},{5,7},{6,4},{7,5},{8,10},{9,11},{10,... | collective-permute-start | bytes 221192 | tf_op jit(solution)/shard_map/out/ppermute | solution.py:621
  147.0 2.1 %collective-permute-start.28 = (bf16[288,128]{1,0:T(8,128)(2,1)S(1)}, bf16[288,128]{1,0:T(8,128)(2,1)S(1)}, u32[]{:S(2)}, u32[]{:S(2)}) collective-permute-start(bf16[288,128]{1,0:T(8,128)(2,1)S(1)} %get-tuple-element.167), channel_id=1, source_target_pairs={{0,3},{1,2},{2,1},{3,0},{4,7},{5,6},{6,5},{7,4},{8,11},{9,10},{10,... | collective-permute-start | bytes 221192 | tf_op jit(solution)/shard_map/out/ppermute | solution.py:621
  149.1 0.9 output_kernel.1
  150.1 1.8 %input_kernel.1 = bf16[128,768]{1,0:T(8,128)(2,1)} custom-call(f32[768,128]{1,0:T(8,128)S(1)} %get-tuple-element.137.own, bf16[768,128]{1,0:T(8,128)(2,1)S(1)} %collective-permute-done.17.recv, bf16[128,768]{1,0:T(8,128)(2,1)} %dy.1), custom_call_target="tpu_custom_call" | custom-call | flops 11500000 | bytes 8 | tf_op jit(solution)/shard_map/input_kernel/pallas_call | solution.py:21
  151.9 1.4 collective-permute-done.28.o3
  153.3 0.7 small_kernel.1
  (36 shorter events, 0.4 us)
Async XLA Ops:
  0.6 1.0 copy-start
  0.7 11.5 %copy-start.1 = (bf16[768,768]{1,0:T(8,128)(2,1)S(1)}, bf16[768,768]{1,0:T(8,128)(2,1)}, u32[]{:S(2)}) copy-start(bf16[768,768]{1,0:T(8,128)(2,1)} %w_up.1) | copy-start | bytes 3538948
  2.6 26.9 %collective-permute-start.2 = (bf16[176,768]{1,0:T(8,128)(2,1)S(1)}, bf16[176,768]{1,0:T(8,128)(2,1)S(1)}, u32[]{:S(2)}, u32[]{:S(2)}) collective-permute-start(bf16[176,768]{1,0:T(8,128)(2,1)S(1)} %pad_maximum_fusion.x0), channel_id=1, source_target_pairs={{0,3},{1,2},{2,1},{3,0},{4,7},{5,6},{6,5},{7,4},{8,11},{9,10},{10,... | collective-permute-start | bytes 811016 | tf_op jit(solution)/shard_map/x/ppermute | solution.py:621
  7.7 23.0 %collective-permute-start.1 = (bf16[176,768]{1,0:T(8,128)(2,1)S(1)}, bf16[176,768]{1,0:T(8,128)(2,1)S(1)}, u32[]{:S(2)}, u32[]{:S(2)}) collective-permute-start(bf16[176,768]{1,0:T(8,128)(2,1)S(1)} %pad_maximum_fusion.x0), channel_id=1, source_target_pairs={{0,2},{1,3},{2,0},{3,1},{4,6},{5,7},{6,4},{7,5},{8,10},{9,11},{10,... | collective-permute-start | bytes 811016 | tf_op jit(solution)/shard_map/x/ppermute | solution.py:621
  7.7 23.0 %collective-permute-start = (bf16[176,768]{1,0:T(8,128)(2,1)S(1)}, bf16[176,768]{1,0:T(8,128)(2,1)S(1)}, u32[]{:S(2)}, u32[]{:S(2)}) collective-permute-start(bf16[176,768]{1,0:T(8,128)(2,1)S(1)} %pad_maximum_fusion.x0), channel_id=1, source_target_pairs={{0,1},{1,0},{2,3},{3,2},{4,5},{5,4},{6,7},{7,6},{8,9},{9,8},{10,11... | collective-permute-start | bytes 811016 | tf_op jit(solution)/shard_map/x/ppermute | solution.py:621
  8.3 21.1 %collective-permute-start.3 = (bf16[128,768]{1,0:T(8,128)(2,1)}, bf16[128,768]{1,0:T(8,128)(2,1)S(1)}, u32[]{:S(2)}, u32[]{:S(2)}) collective-permute-start(bf16[128,768]{1,0:T(8,128)(2,1)} %dy.1), channel_id=1, source_target_pairs={{0,1},{1,0},{2,3},{3,2},{4,5},{5,4},{6,7},{7,6},{8,9},{9,8},{10,11... | collective-permute-start | bytes 589832 | tf_op jit(solution)/shard_map/dy/ppermute | solution.py:621
  12.2 1.3 copy-start.2
  13.5 1.2 copy-start.4
  15.6 18.5 %copy-start.5 = (bf16[768,3,192]{0,2,1:T(8,128)(2,1)S(1)}, bf16[768,3,192]{0,2,1:T(8,128)(2,1)}, u32[]{:S(2)}) copy-start(bf16[768,3,192]{0,2,1:T(8,128)(2,1)} %param.16) | copy-start | bytes 2654212
  15.6 18.5 %copy-start.6 = (s32[1,8]{1,0:T(1,128)S(1)}, s32[1,8]{1,0:T(1,128)}, u32[]{:S(2)}) copy-start(s32[1,8]{1,0:T(1,128)} %lengths.3) | copy-start | bytes 100
  31.4 11.4 %collective-permute-start.5 = (bf16[128,768]{1,0:T(8,128)(2,1)}, bf16[128,768]{1,0:T(8,128)(2,1)}, u32[]{:S(2)}, u32[]{:S(2)}) collective-permute-start(bf16[128,768]{1,0:T(8,128)(2,1)} %dy.1), channel_id=1, source_target_pairs={{0,2},{1,3},{2,0},{3,1},{4,6},{5,7},{6,4},{7,5},{8,10},{9,11},{10,... | collective-permute-start | bytes 589832 | tf_op jit(solution)/shard_map/dy/ppermute | solution.py:621
  32.6 10.2 %collective-permute-start.4 = (bf16[4,48,768]{2,1,0:T(8,128)(2,1)}, bf16[4,48,768]{2,1,0:T(8,128)(2,1)}, u32[]{:S(2)}, u32[]{:S(2)}) collective-permute-start(bf16[4,48,768]{2,1,0:T(8,128)(2,1)} %pieces_kernel.1.a), channel_id=1, source_target_pairs={{0,8},{4,12},{8,0},{12,4},{16,24},{20,28},{24,16},{28,20},{1,9},{5... | collective-permute-start | bytes 884744 | tf_op jit(solution)/shard_map/w/ppermute | solution.py:621
  42.8 23.1 %copy-start.3 = (bf16[768,768]{1,0:T(8,128)(2,1)S(1)}, bf16[768,768]{1,0:T(8,128)(2,1)}, u32[]{:S(2)}) copy-start(bf16[768,768]{1,0:T(8,128)(2,1)} %w_down.1) | copy-start | bytes 3538948
  44.0 4.7 %collective-permute-start.10 = (bf16[8,48,768]{2,1,0:T(8,128)(2,1)S(1)}, bf16[8,48,768]{2,1,0:T(8,128)(2,1)S(1)}, u32[]{:S(2)}, u32[]{:S(2)}) collective-permute-start(bf16[8,48,768]{2,1,0:T(8,128)(2,1)S(1)} %pair_kernel.1.here), channel_id=1, source_target_pairs={{0,4},{4,0},{8,12},{12,8},{16,20},{20,16},{24,28},{28,24},{1,5},{5... | collective-permute-start | bytes 1769480 | tf_op jit(solution)/shard_map/w/ppermute | solution.py:621
  44.1 9.7 %collective-permute-start.8 = (bf16[192,512]{1,0:T(8,128)(2,1)S(1)}, bf16[192,512]{1,0:T(8,128)(2,1)S(1)}, u32[]{:S(2)}, u32[]{:S(2)}) collective-permute-start(bf16[192,512]{1,0:T(8,128)(2,1)S(1)} %get-tuple-element.103.a0), channel_id=1, source_target_pairs={{0,3},{1,2},{2,1},{3,0},{4,7},{5,6},{6,5},{7,4},{8,11},{9,10},{10,... | collective-permute-start | bytes 589832 | tf_op jit(solution)/shard_map/att/ppermute | solution.py:621
  45.8 18.8 %collective-permute-start.7 = (bf16[192,512]{1,0:T(8,128)(2,1)S(1)}, bf16[192,512]{1,0:T(8,128)(2,1)S(1)}, u32[]{:S(2)}, u32[]{:S(2)}) collective-permute-start(bf16[192,512]{1,0:T(8,128)(2,1)S(1)} %get-tuple-element.103.a0), channel_id=1, source_target_pairs={{0,2},{1,3},{2,0},{3,1},{4,6},{5,7},{6,4},{7,5},{8,10},{9,11},{10,... | collective-permute-start | bytes 589832 | tf_op jit(solution)/shard_map/att/ppermute | solution.py:621
  46.7 18.0 %collective-permute-start.6 = (bf16[192,512]{1,0:T(8,128)(2,1)S(1)}, bf16[192,512]{1,0:T(8,128)(2,1)S(1)}, u32[]{:S(2)}, u32[]{:S(2)}) collective-permute-start(bf16[192,512]{1,0:T(8,128)(2,1)S(1)} %get-tuple-element.103.a0), channel_id=1, source_target_pairs={{0,1},{1,0},{2,3},{3,2},{4,5},{5,4},{6,7},{7,6},{8,9},{9,8},{10,11... | collective-permute-start | bytes 589832 | tf_op jit(solution)/shard_map/att/ppermute | solution.py:621
  48.5 17.4 %collective-permute-start.9 = (bf16[128,768]{1,0:T(8,128)(2,1)}, bf16[128,768]{1,0:T(8,128)(2,1)S(1)}, u32[]{:S(2)}, u32[]{:S(2)}) collective-permute-start(bf16[128,768]{1,0:T(8,128)(2,1)} %collective-permute-done.5.c2), channel_id=1, source_target_pairs={{0,1},{1,0},{2,3},{3,2},{4,5},{5,4},{6,7},{7,6},{8,9},{9,8},{10,11... | collective-permute-start | bytes 589832 | tf_op jit(solution)/shard_map/dy/ppermute | solution.py:621
  78.1 10.8 %collective-permute-start.11 = (bf16[192,512]{1,0:T(8,128)(2,1)S(1)}, bf16[192,512]{1,0:T(8,128)(2,1)S(1)}, u32[]{:S(2)}, u32[]{:S(2)}) collective-permute-start(bf16[192,512]{1,0:T(8,128)(2,1)S(1)} %get-tuple-element.119), channel_id=1, source_target_pairs={{0,1},{1,0},{2,3},{3,2},{4,5},{5,4},{6,7},{7,6},{8,9},{9,8},{10,11... | collective-permute-start | bytes 589832 | tf_op jit(solution)/shard_map/d_att/ppermute | solution.py:621
  78.2 17.2 %collective-permute-start.12 = (bf16[192,512]{1,0:T(8,128)(2,1)S(1)}, bf16[192,512]{1,0:T(8,128)(2,1)S(1)}, u32[]{:S(2)}, u32[]{:S(2)}) collective-permute-start(bf16[192,512]{1,0:T(8,128)(2,1)S(1)} %get-tuple-element.120), channel_id=1, source_target_pairs={{0,2},{1,3},{2,0},{3,1},{4,6},{5,7},{6,4},{7,5},{8,10},{9,11},{10,... | collective-permute-start | bytes 589832 | tf_op jit(solution)/shard_map/d_att/ppermute | solution.py:621
  80.4 15.0 %collective-permute-start.13 = (bf16[192,512]{1,0:T(8,128)(2,1)S(1)}, bf16[192,512]{1,0:T(8,128)(2,1)S(1)}, u32[]{:S(2)}, u32[]{:S(2)}) collective-permute-start(bf16[192,512]{1,0:T(8,128)(2,1)S(1)} %get-tuple-element.121), channel_id=1, source_target_pairs={{0,3},{1,2},{2,1},{3,0},{4,7},{5,6},{6,5},{7,4},{8,11},{9,10},{10,... | collective-permute-start | bytes 589832 | tf_op jit(solution)/shard_map/d_att/ppermute | solution.py:621
  82.6 16.7 %copy-start.7 = (s32[1,8]{1,0:T(1,128)S(1)}, s32[1,8]{1,0:T(1,128)}, u32[]{:S(2)}) copy-start(s32[1,8]{1,0:T(1,128)} %lengths.3) | copy-start | bytes 100
  88.9 22.3 %collective-permute-start.20 = (bf16[384,2304]{1,0:T(8,128)(2,1)}, bf16[384,2304]{1,0:T(8,128)(2,1)}, u32[]{:S(2)}, u32[]{:S(2)}) collective-permute-start(bf16[384,2304]{1,0:T(8,128)(2,1)} %get-tuple-element.151), channel_id=1, source_target_pairs={{0,4},{4,0},{8,12},{12,8},{16,20},{20,16},{24,28},{28,24},{1,5},{5... | collective-permute-start | bytes 5308424 | tf_op jit(solution)/shard_map/grads_core/ppermute | solution.py:621
  95.4 13.8 %collective-permute-start.14 = (bf16[1536,128]{1,0:T(8,128)(2,1)}, bf16[1536,128]{1,0:T(8,128)(2,1)}, u32[]{:S(2)}, u32[]{:S(2)}) collective-permute-start(bf16[1536,128]{1,0:T(8,128)(2,1)} %get-tuple-element.122), channel_id=1, source_target_pairs={{0,1},{1,0},{2,3},{3,2},{4,5},{5,4},{6,7},{7,6},{8,9},{9,8},{10,11... | collective-permute-start | bytes 1179656 | tf_op jit(solution)/shard_map/mlp/ppermute | solution.py:621
  109.3 2.0 %collective-permute-start.18 = (bf16[416,576]{1,0:T(8,128)(2,1)S(1)}, bf16[416,576]{1,0:T(8,128)(2,1)S(1)}, u32[]{:S(2)}, u32[]{:S(2)}) collective-permute-start(bf16[416,576]{1,0:T(8,128)(2,1)S(1)} %get-tuple-element.144), channel_id=1, source_target_pairs={{0,4},{4,0},{8,12},{12,8},{16,20},{20,16},{24,28},{28,24},{1,5},{5... | collective-permute-start | bytes 1437704 | tf_op jit(solution)/shard_map/qkv_core/ppermute | solution.py:621
  113.1 19.0 %collective-permute-start.21 = (bf16[192,1152]{1,0:T(8,128)(2,1)S(1)}, bf16[192,1152]{1,0:T(8,128)(2,1)S(1)}, u32[]{:S(2)}, u32[]{:S(2)}) collective-permute-start(bf16[192,1152]{1,0:T(8,128)(2,1)S(1)} %get-tuple-element.155), channel_id=1, source_target_pairs={{0,8},{4,12},{8,0},{12,4},{16,24},{20,28},{24,16},{28,20},{1,9},{5... | collective-permute-start | bytes 1327112 | tf_op jit(solution)/shard_map/grads_a/ppermute | solution.py:621
  114.7 17.5 %collective-permute-start.22 = (bf16[192,1152]{1,0:T(8,128)(2,1)S(1)}, bf16[192,1152]{1,0:T(8,128)(2,1)S(1)}, u32[]{:S(2)}, u32[]{:S(2)}) collective-permute-start(bf16[192,1152]{1,0:T(8,128)(2,1)S(1)} %get-tuple-element.157), channel_id=1, source_target_pairs={{0,16},{4,20},{8,24},{12,28},{16,0},{20,4},{24,8},{28,12},{1,17},{... | collective-permute-start | bytes 1327112 | tf_op jit(solution)/shard_map/grads_b/ppermute | solution.py:621
  116.2 14.8 %collective-permute-start.16 = (bf16[1536,128]{1,0:T(8,128)(2,1)S(1)}, bf16[1536,128]{1,0:T(8,128)(2,1)S(1)}, u32[]{:S(2)}, u32[]{:S(2)}) collective-permute-start(bf16[1536,128]{1,0:T(8,128)(2,1)S(1)} %get-tuple-element.136), channel_id=1, source_target_pairs={{0,1},{1,0},{2,3},{3,2},{4,5},{5,4},{6,7},{7,6},{8,9},{9,8},{10,11... | collective-permute-start | bytes 1179656 | tf_op jit(solution)/shard_map/back/ppermute | solution.py:621
  117.3 14.2 %collective-permute-start.19 = (bf16[224,576]{1,0:T(8,128)(2,1)S(1)}, bf16[224,576]{1,0:T(8,128)(2,1)S(1)}, u32[]{:S(2)}, u32[]{:S(2)}) collective-permute-start(bf16[224,576]{1,0:T(8,128)(2,1)S(1)} %get-tuple-element.147), channel_id=1, source_target_pairs={{0,8},{4,12},{8,0},{12,4},{16,24},{20,28},{24,16},{28,20},{1,9},{5... | collective-permute-start | bytes 774152 | tf_op jit(solution)/shard_map/qkv_x/ppermute | solution.py:621
  119.0 9.9 %collective-permute-start.15 = (bf16[768,128]{1,0:T(8,128)(2,1)S(1)}, bf16[768,128]{1,0:T(8,128)(2,1)S(1)}, u32[]{:S(2)}, u32[]{:S(2)}) collective-permute-start(bf16[768,128]{1,0:T(8,128)(2,1)S(1)} %get-tuple-element.124), channel_id=1, source_target_pairs={{0,2},{1,3},{2,0},{3,1},{4,6},{5,7},{6,4},{7,5},{8,10},{9,11},{10,... | collective-permute-start | bytes 589832 | tf_op jit(solution)/shard_map/mlp/ppermute | solution.py:621
  132.9 10.2 %collective-permute-start.23 = (bf16[96,1152]{1,0:T(8,128)(2,1)S(1)}, bf16[96,1152]{1,0:T(8,128)(2,1)S(1)}, u32[]{:S(2)}, u32[]{:S(2)}) collective-permute-start(bf16[96,1152]{1,0:T(8,128)(2,1)S(1)} %get-tuple-element.159), channel_id=1, source_target_pairs={{0,16},{4,20},{8,24},{12,28},{16,0},{20,4},{24,8},{28,12},{1,17},{... | collective-permute-start | bytes 663560 | tf_op jit(solution)/shard_map/grads_a/ppermute | solution.py:621
  134.5 8.6 %collective-permute-start.24 = (bf16[96,1152]{1,0:T(8,128)(2,1)S(1)}, bf16[96,1152]{1,0:T(8,128)(2,1)S(1)}, u32[]{:S(2)}, u32[]{:S(2)}) collective-permute-start(bf16[96,1152]{1,0:T(8,128)(2,1)S(1)} %get-tuple-element.161), channel_id=1, source_target_pairs={{0,8},{4,12},{8,0},{12,4},{16,24},{20,28},{24,16},{28,20},{1,9},{5... | collective-permute-start | bytes 663560 | tf_op jit(solution)/shard_map/grads_b/ppermute | solution.py:621
  136.0 7.1 %collective-permute-start.25 = (bf16[128,576]{1,0:T(8,128)(2,1)S(1)}, bf16[128,576]{1,0:T(8,128)(2,1)S(1)}, u32[]{:S(2)}, u32[]{:S(2)}) collective-permute-start(bf16[128,576]{1,0:T(8,128)(2,1)S(1)} %get-tuple-element.162), channel_id=1, source_target_pairs={{0,16},{4,20},{8,24},{12,28},{16,0},{20,4},{24,8},{28,12},{1,17},{... | collective-permute-start | bytes 442376 | tf_op jit(solution)/shard_map/qkv_y/ppermute | solution.py:621
  136.5 13.6 %collective-permute-start.17 = (bf16[768,128]{1,0:T(8,128)(2,1)S(1)}, bf16[768,128]{1,0:T(8,128)(2,1)S(1)}, u32[]{:S(2)}, u32[]{:S(2)}) collective-permute-start(bf16[768,128]{1,0:T(8,128)(2,1)S(1)} %get-tuple-element.138), channel_id=1, source_target_pairs={{0,2},{1,3},{2,0},{3,1},{4,6},{5,7},{6,4},{7,5},{8,10},{9,11},{10,... | collective-permute-start | bytes 589832 | tf_op jit(solution)/shard_map/back/ppermute | solution.py:621
  144.8 7.1 %collective-permute-start.26 = (bf16[288,128]{1,0:T(8,128)(2,1)S(1)}, bf16[288,128]{1,0:T(8,128)(2,1)S(1)}, u32[]{:S(2)}, u32[]{:S(2)}) collective-permute-start(bf16[288,128]{1,0:T(8,128)(2,1)S(1)} %get-tuple-element.165), channel_id=1, source_target_pairs={{0,1},{1,0},{2,3},{3,2},{4,5},{5,4},{6,7},{7,6},{8,9},{9,8},{10,11... | collective-permute-start | bytes 221192 | tf_op jit(solution)/shard_map/out/ppermute | solution.py:621
  145.2 6.7 %collective-permute-start.27 = (bf16[288,128]{1,0:T(8,128)(2,1)S(1)}, bf16[288,128]{1,0:T(8,128)(2,1)S(1)}, u32[]{:S(2)}, u32[]{:S(2)}) collective-permute-start(bf16[288,128]{1,0:T(8,128)(2,1)S(1)} %get-tuple-element.166), channel_id=1, source_target_pairs={{0,2},{1,3},{2,0},{3,1},{4,6},{5,7},{6,4},{7,5},{8,10},{9,11},{10,... | collective-permute-start | bytes 221192 | tf_op jit(solution)/shard_map/out/ppermute | solution.py:621
  147.0 6.3 %collective-permute-start.28 = (bf16[288,128]{1,0:T(8,128)(2,1)S(1)}, bf16[288,128]{1,0:T(8,128)(2,1)S(1)}, u32[]{:S(2)}, u32[]{:S(2)}) collective-permute-start(bf16[288,128]{1,0:T(8,128)(2,1)S(1)} %get-tuple-element.167), channel_id=1, source_target_pairs={{0,3},{1,2},{2,1},{3,0},{4,7},{5,6},{6,5},{7,4},{8,11},{9,10},{10,... | collective-permute-start | bytes 221192 | tf_op jit(solution)/shard_map/out/ppermute | solution.py:621

commit v4 on v3

--- a/solution.py
+++ b/solution.py
@@ -17,7 +17,7 @@
 GAIN0, BIAS0, GAIN1, BIAS1, SCALE0, SCALE1 = range(6)
 
 
-def call(kernel, outs, args, n_smem=0, scratch=(), us=0.01, limit=16):
+def call(kernel, outs, args, n_smem=0, scratch=(), us=0.01, limit=8):
     return pl.pallas_call(
         kernel,
         out_shape=tuple(outs),
@@ -51,7 +51,7 @@
 
 
 def passes(rows, step, start):
-    return lax.fori_loop(0, rows // CHUNK, step, start)
+    return lax.fori_loop(0, rows // CHUNK, step, start, unroll=True)
 
 
 def chunk(i):
@@ -196,94 +196,117 @@
         att_o[pl.ds(pl.multiple_of(h * HEAD_DIM, HEAD_DIM), HEAD_DIM), :] = mixed.astype(BF16)
         return carry
 
-    lax.fori_loop(0, heads, one_head, 0)
-
-
-def middle_kernel(
-    place, a0, a1, a2, a3, c0, c1, c2, c3, xt, cols, w_out, w_out_t, w_up, w_up_t, w_down,
-    d0, d1, d2, d3, nb_o, h2_o, act_o, dup_o, gm_o, ga_o, at_o, dy_o, mid_o, vec_o,
-    attn, mid, wide, other, sums,
+    lax.fori_loop(0, heads, one_head, 0, unroll=True)
+
+
+def up_kernel(
+    place, a0, a1, a2, a3, xt, cols, w_out_t, w_up_t, w_down_t,
+    at_o, attn_o, hat_o, rstd_o, h2_o, act_o, slope_o, mid_o, mlp_o, m0, m2, m13,
+    wide,
 ):
     m = place[0]
-    rows = c0.shape[0]
+    rows = mid_o.shape[1]
     channels = a0.shape[0]
     width, tokens = xt.shape
-    hidden = w_up.shape[1]
-    for k, (a, c) in enumerate(zip((a0, a1, a2, a3), (c0, c1, c2, c3))):
+    hidden = act_o.shape[0]
+    for k, a in enumerate((a0, a1, a2, a3)):
         at_o[pl.ds(pl.multiple_of((m ^ k) * channels, channels), channels), :] = a[...]
-        dy_o[:, pl.ds(pl.multiple_of((m ^ k) * rows, rows), rows)] = c[...].T
-    attn[...] = nn(w_out_t[...], at_o[...])
+    attn_o[...] = nn(w_out_t[...], at_o[...])
     zero = jnp.zeros((8, tokens), F32)
 
     def residual(i, acc):
-        w = cols[chunk(i), :]
-        v = xt[chunk(i), :].astype(F32) + w[:, SCALE0 : SCALE0 + 1] * attn[chunk(i), :]
-        mid[chunk(i), :] = v
-        gm_o[chunk(i), :] = (
-            dy_o[chunk(i), :].astype(F32) * w[:, SCALE1 : SCALE1 + 1]
-        ).astype(BF16)
+        scale = cols[chunk(i), :][:, SCALE0 : SCALE0 + 1]
+        v = xt[chunk(i), :].astype(F32) + scale * attn_o[chunk(i), :]
+        hat_o[chunk(i), :] = v
         return acc + fold(v)
 
     mean = across(passes(width, residual, zero)) / width
-    mid_o[...] = mid[:, pl.ds(pl.multiple_of(m * rows, rows), rows)]
+    mid_o[...] = hat_o[:, pl.ds(pl.multiple_of(m * rows, rows), rows)]
 
     def spread(i, acc):
-        v = mid[chunk(i), :] - mean
+        v = hat_o[chunk(i), :] - mean
         return acc + fold(v * v)
 
     rstd = lax.rsqrt(across(passes(width, spread, zero)) / width + norm_eps)
+    rstd_o[0:1, :] = rstd
 
     def norm(i, carry):
         w = cols[chunk(i), :]
-        v = (mid[chunk(i), :] - mean) * rstd
-        mid[chunk(i), :] = v
+        v = (hat_o[chunk(i), :] - mean) * rstd
+        hat_o[chunk(i), :] = v
         h2_o[chunk(i), :] = (v * w[:, GAIN1 : GAIN1 + 1] + w[:, BIAS1 : BIAS1 + 1]).astype(BF16)
         return carry
 
     passes(width, norm, 0)
     wide[...] = nn(w_up_t[...], h2_o[...])
-    other[...] = nn(w_down[...], gm_o[...])
 
     def gelu(i, carry):
         u = wide[chunk(i), :]
         cdf = 0.5 + 0.5 * lax.erf(u * (0.5**0.5))
         act_o[chunk(i), :] = (u * cdf).astype(BF16)
-        slope = cdf + u * (jnp.exp(-0.5 * u * u) * 0.3989422804014327)
-        dup_o[chunk(i), :] = (slope * other[chunk(i), :]).astype(BF16)
+        slope_o[chunk(i), :] = cdf + u * (jnp.exp(-0.5 * u * u) * 0.3989422804014327)
         return carry
 
     passes(hidden, gelu, 0)
+    mlp_o[...] = nn(w_down_t[...], act_o[...])
+    put_halves(m, mlp_o, m0, m2, m13)
+
+
+def down_kernel(
+    place, c0, c1, c2, c3, cols, attn, hat, rstd, slope, w_out, w_up, w_down,
+    d0, d1, d2, d3, nb_o, dup_o, gm_o, ga_o, dy_o, vec_o,
+    wide, sums,
+):
+    m = place[0]
+    rows = c0.shape[0]
+    channels = d0.shape[0]
+    width, tokens = hat.shape
+    hidden = slope.shape[0]
+    for k, c in enumerate((c0, c1, c2, c3)):
+        at = pl.ds(pl.multiple_of((m ^ k) * rows, rows), rows)
+        turned = c[...].T
+        dy_o[:, at] = turned
+        scale = cols[:, SCALE1 : SCALE1 + 1]
+        gm_o[:, at] = (turned.astype(F32) * scale).astype(BF16)
+    wide[...] = nn(w_down[...], gm_o[...])
+
+    def d_up(i, carry):
+        dup_o[chunk(i), :] = (slope[chunk(i), :] * wide[chunk(i), :]).astype(BF16)
+        return carry
+
+    passes(hidden, d_up, 0)
     wide[...] = nn(w_up[...], dup_o[...])
+    zero = jnp.zeros((8, tokens), F32)
 
     def gather(i, acc):
         d = wide[chunk(i), :]
-        hat = mid[chunk(i), :]
         u = d * cols[chunk(i), :][:, GAIN1 : GAIN1 + 1]
-        sums[chunk(i), 0:1] = jnp.sum(d * hat, axis=1, keepdims=True)
-        sums[chunk(i), 1:2] = jnp.sum(d, axis=1, keepdims=True)
-        return acc[0] + fold(u), acc[1] + fold(u * hat)
+        return acc[0] + fold(u), acc[1] + fold(u * hat[chunk(i), :])
 
     first, second = passes(width, gather, (zero, zero))
     first, second = across(first) / width, across(second) / width
     lane = lax.broadcasted_iota(jnp.int32, (1, tokens), 1)
     mine = ((lane >= m * rows) & (lane < (m + 1) * rows)).astype(F32)
+    rstd = rstd[0:1, :]
 
     def back(i, carry):
         w = cols[chunk(i), :]
-        u = wide[chunk(i), :] * w[:, GAIN1 : GAIN1 + 1]
-        v = rstd * (u - first - mid[chunk(i), :] * second)
+        d = wide[chunk(i), :]
+        h = hat[chunk(i), :]
+        v = rstd * (d * w[:, GAIN1 : GAIN1 + 1] - first - h * second)
         nb_o[chunk(i), :] = v
         v = v + mine * dy_o[chunk(i), :].astype(F32)
+        ga_o[chunk(i), :] = (v * w[:, SCALE0 : SCALE0 + 1]).astype(BF16)
+        sums[chunk(i), 0:1] = jnp.sum(d * h, axis=1, keepdims=True)
+        sums[chunk(i), 1:2] = jnp.sum(d, axis=1, keepdims=True)
         sums[chunk(i), 2:3] = jnp.sum(v * attn[chunk(i), :], axis=1, keepdims=True)
-        ga_o[chunk(i), :] = (v * w[:, SCALE0 : SCALE0 + 1]).astype(BF16)
         return carry
 
     passes(width, back, 0)
-    other[...] = nn(w_out[...], ga_o[...])
+    wide[...] = nn(w_out[...], ga_o[...])
     for k, ref in enumerate((d0, d1, d2, d3)):
-        ref[...] = other[
-            pl.ds(pl.multiple_of((m ^ k) * channels, channels), channels), :
-        ].astype(BF16)
+        at = pl.ds(pl.multiple_of((m ^ k) * channels, channels), channels)
+        ref[...] = wide[at, :].astype(BF16)
     turned = sums[...].T
     vec_o[...] = jnp.zeros(vec_o.shape, F32)
     vec_o[1:2, :] = turned[0:1, :]
@@ -291,27 +314,52 @@
     vec_o[4:5, :] = turned[2:3, :]
 
 
-def mlp_kernel(
-    place, vec, act, dup, gm, ga, att, h2, dy, w_down_t,
-    m0, m2, m13, vec_o, *rest,
-):
-    grads, (mlp, sums) = rest[:-2], rest[-2:]
-    m, d = place[0], place[1]
-    rows = m0.shape[1]
-    width, tokens = dy.shape
-    mlp[...] = nn(w_down_t[...], act[...])
-    put_halves(m, mlp, m0, m2, m13)
+def mlp_grad_kernel(place, vec, mlp, act, dup, gm, ga, att, h2, dy, vec_o, *rest):
+    grads, sums = rest[:-1], rest[-1]
 
     def scale(i, carry):
         v = dy[chunk(i), :].astype(F32) * mlp[chunk(i), :]
         sums[chunk(i), 0:1] = jnp.sum(v, axis=1, keepdims=True)
         return carry
 
-    passes(width, scale, 0)
+    passes(dy.shape[0], scale, 0)
     vec_o[...] = vec[...]
     vec_o[5:6, :] = sums[...].T[0:1, :]
-    pairs = ((h2, dup), (gm, act), (ga, att))
-    put_blocks([nt(a[...], b[...]).astype(BF16) for a, b in pairs], d & 1, grads)
+    if len(grads) == 1:
+        at = 0
+        for a, b in ((h2, dup), (gm, act), (ga, att)):
+            grads[0][:, at : at + b.shape[0]] = nt(a[...], b[...]).astype(BF16)
+            at += b.shape[0]
+        return
+    x, y = (place[1] >> 1) & 1, (place[1] >> 2) & 1
+    a_sent, a_kept, b_sent, b_kept = grads
+    n, half = a_sent.shape[0] // 4, a_sent.shape[1]
+
+    def put(p, left, low, high):
+        block = [p[i * n : (i + 1) * n, low:high] for i in range(8)]
+        first = left + low < half
+        at = left + low - (0 if first else half)
+        cols = slice(at, at + high - low)
+        for i in range(4):
+            out = slice(i * n, (i + 1) * n)
+            if first:
+                zero, one = 4 * (i // 2) + i % 2, 4 * (i // 2) + 2 + i % 2
+                a_sent[out, cols] = pick(x, block[one], block[zero])
+                a_kept[out, cols] = pick(x, block[zero], block[one])
+            else:
+                b_sent[out, cols] = pick(y, block[4 + i], block[i])
+                b_kept[out, cols] = pick(y, block[i], block[4 + i])
+
+    left = 0
+    for a, b in ((h2, dup), (gm, act), (ga, att)):
+        p = nt(a[...], b[...]).astype(BF16)
+        n_cols = p.shape[1]
+        cut = min(max(half - left, 0), n_cols)
+        if cut > 0:
+            put(p, left, 0, cut)
+        if cut < n_cols:
+            put(p, left, cut, n_cols)
+        left += n_cols
 
 
 def put_halves(m, ref, own, next_to, sent):
@@ -423,7 +471,7 @@
             buckets_of[pl.ds(first + b, 1), :] = across(v)
         return carry
 
-    lax.fori_loop(0, heads, one_head, 0)
+    lax.fori_loop(0, heads, one_head, 0, unroll=True)
     wide[...] = nn(wq_t[...], dqkv_o[...])
     mean, rstd = stat[0:1, :], stat[1:2, :]
     zero = jnp.zeros((8, tokens), F32)
@@ -479,35 +527,30 @@
     return jnp.concatenate([v[:8], v[8:]], axis=1)
 
 
-def grads_second_kernel(place, keep, recv, a_sent, a_kept, b_sent, b_kept):
+def grads_second_kernel(place, a_keep, a_recv, b_keep, b_recv, sent, kept):
+    core = place[1] & 1
+    half, n = a_keep.shape[1], kept.shape[0] // 2
+    for at, keep, recv in ((0, a_keep, a_recv), (half, b_keep, b_recv)):
+        cols = slice(at, at + half)
+        for i in range(2):
+            rows = pl.ds(pl.multiple_of(2 * i * n, 2 * n), 2 * n)
+            out = slice(i * n, (i + 1) * n)
+            halve_rows(core, keep.at[rows], recv.at[rows], sent.at[out, cols], kept.at[out, cols])
+
+
+def grads_third_kernel(place, keep, recv, a_sent, a_kept, b_sent, b_kept):
     x, y = (place[1] >> 1) & 1, (place[1] >> 2) & 1
-    n = keep.shape[0] // 4
-    half = a_sent.shape[1]
-
-    def block(i, cols):
-        rows = pl.ds(pl.multiple_of(i * n, n), n)
-        return keep[rows, cols].astype(F32) + recv[rows, cols].astype(F32)
-
-    left, right = slice(0, half), slice(half, 2 * half)
-    for i in range(2):
-        at = slice(i * n, (i + 1) * n)
-        a_sent[at, :] = block(2 * i + 1 - x, left).astype(BF16)
-        a_kept[at, :] = block(2 * i + x, left)
-        b_sent[at, :] = block(2 * (1 - y) + i, right).astype(BF16)
-        b_kept[at, :] = block(2 * y + i, right)
-
-
-def grads_third_kernel(place, a_keep, a_recv, b_keep, b_recv, a_sent, a_kept, b_sent, b_kept):
-    x, y = (place[1] >> 1) & 1, (place[1] >> 2) & 1
-    halve_rows(y, a_keep, a_recv, a_sent, a_kept)
-    halve_rows(x, b_keep, b_recv, b_sent, b_kept)
+    half = a_kept.shape[1]
+    halve_rows(y, keep.at[:, :half], recv.at[:, :half], a_sent, a_kept)
+    halve_rows(x, keep.at[:, half:], recv.at[:, half:], b_sent, b_kept)
 
 
 def halve_rows(bit, keep, recv, sent, kept):
     n = kept.shape[0]
     for ref, b in ((sent, 1 - bit), (kept, bit)):
         rows = pl.ds(pl.multiple_of(b * n, n), n)
-        ref[0:n, :] = (keep[rows, :] + recv[rows, :].astype(F32)).astype(ref.dtype)
+        total = keep[rows, :].astype(F32) + recv[rows, :].astype(F32)
+        ref[0:n, :] = total.astype(ref.dtype)
 
 
 def qkv_second_kernel(place, vec, keep, recv, sent, kept, vec_o):
@@ -661,57 +704,67 @@
             pltpu.VMEM((group, 128), jnp.int32),
             pltpu.VMEM((3, 128, 128), F32),
         ],
-        us=200,
+        us=10,
     )
     (parts,) = call(pair_kernel, [like((8, piece, width), BF16)], [part, after(part_x, att, dy2)])
     att_sent = after(att, parts)
     atts = [att] + [swap(att_sent, k, name="att") for k in (1, 2, 3)]
-    dy = [cotangent, dy1, dy2, swap(after(dy2, parts), 1, name="dy")]
+    dy = [cotangent, dy1, dy2, swap(after(dy2, *atts[1:]), 1, name="dy")]
     w_pieces = [parts, swap(parts, 1, "dp", name="w")]
     w_out_full, w_out_t = call(
         out_weight_kernel, [like((width, width), BF16)] * 2, [place] + w_pieces, n_smem=1
     )
     act_like = like((width, group), BF16)
     hid_like = like((hidden, group), BF16)
-    d0, d1, d2, d3, nb, h2, act, dup, gm, ga, att_all, dy_t, mid, vec = call(
-        middle_kernel,
+    wide_like = like((width, group), F32)
+    block = like((width, rows), F32)
+    blocks = [block, block, like((2 * width, rows), BF16)]
+    att_all, attn, hat, rstd, h2, act, slope, mid, mlp_part, m0, m2, m13 = call(
+        up_kernel,
+        [act_like, wide_like, wide_like, like((8, group), F32), act_like, hid_like]
+        + [like((hidden, group), F32), block, wide_like]
+        + blocks,
+        [place] + atts + [xt, cols, w_out_t, w_up_t, w_down_t],
+        n_smem=1,
+        scratch=[pltpu.VMEM((hidden, group), F32)],
+        us=10,
+    )
+    m_recv = swap(m13, 1, name="mlp")
+    d0, d1, d2, d3, nb, dup, gm, ga, dy_t, vec = call(
+        down_kernel,
         [like((channels, group), BF16)] * 4
-        + [like((width, group), F32), act_like, hid_like, hid_like, act_like, act_like]
-        + [act_like, act_like, like((width, rows), F32), like((8, width), F32)],
-        [place] + atts + dy + [xt, cols, w_out_full, w_out_t, w_up, w_up_t, w_down],
+        + [wide_like, hid_like, act_like, act_like, act_like, like((8, width), F32)],
+        [place] + dy + [cols, attn, hat, rstd, slope, w_out_full, w_up, w_down],
         n_smem=1,
-        scratch=[
-            pltpu.VMEM((width, group), F32),
-            pltpu.VMEM((width, group), F32),
-            pltpu.VMEM((hidden, group), F32),
-            pltpu.VMEM((hidden, group), F32),
-            pltpu.VMEM((width, 128), F32),
-        ],
-        us=200,
+        scratch=[pltpu.VMEM((max(width, hidden), group), F32), pltpu.VMEM((width, 128), F32)],
+        us=10,
     )
     d_att = [d0] + [swap(v, k, name="d_att") for k, v in ((1, d1), (2, d2), (3, d3))]
     grad_cols = 2 * hidden + width
     share = width // dp
-    grad_like = [like((width // 2, grad_cols), BF16)] * 2 if fast else [like((width, grad_cols), BF16)]
-    block = like((width, rows), F32)
-    blocks = [block, block, like((2 * width, rows), BF16)]
-    m0, m2, m13, vec, *grads = call(
-        mlp_kernel,
-        blocks + [like((8, width), F32)] + grad_like,
-        [place, vec, act, dup, gm, ga, att_all, h2, dy_t, w_down_t],
-        n_smem=1,
-        scratch=[pltpu.VMEM((width, group), F32), pltpu.VMEM((width, 128), F32)],
-    )
-
-    def halved(own, next_to, recv, name):
-        half_like = [block, like((width, rows), BF16)]
-        own, sent = call(halve_kernel, half_like, [own, next_to, recv])
-        return [own, swap(sent, 2, name=name)]
-
-    m_recv = swap(after(m13, *d_att[1:]), 1, name="mlp")
     half = grad_cols // 2
     if fast:
-        g_recv = swap(grads[0], 1, "dp", name="grads_core")
+        grad_like = [like((width // 2, half), BF16)] * 4
+    else:
+        grad_like = [like((width, grad_cols), BF16)]
+    vec, *grads = call(
+        mlp_grad_kernel,
+        [like((8, width), F32)] + grad_like,
+        [place, vec, mlp_part, act, dup, gm, ga, att_all, h2, dy_t],
+        n_smem=1,
+        scratch=[pltpu.VMEM((width, 128), F32)],
+    )
+    if fast:
+        a_sent, a_kept, b_sent, b_kept = grads
+        a_recv = swap(a_sent, 2, "dp", name="grads_a")
+        b_recv = swap(b_sent, 4, "dp", name="grads_b")
+
+    def halved(own, next_to, recv, name, us=0.01, seen=()):
+        half_like = [block, like((width, rows), BF16)]
+        own, sent = call(halve_kernel, half_like, [own, next_to, recv], us=us)
+        return [own, swap(after(sent, *seen), 2, name=name)]
+
+    mlp = halved(m0, m2, m_recv, "mlp", seen=d_att[1:])
 
     p0, p2, p13, dqkv, vec = call(
         back_kernel,
@@ -726,11 +779,10 @@
             pltpu.VMEM((width, group), F32),
             pltpu.VMEM((width, 128), F32),
         ],
-        us=200,
-    )
-    mlp = halved(m0, m2, m_recv, "mlp")
-    p_recv = swap(after(p13, m_recv), 1, name="back")
-    back = halved(after(p0, mlp[1]), p2, p_recv, "back")
+        us=10,
+    )
+    p_recv = swap(after(p13, mlp[1]), 1, name="back")
+    back = halved(p0, p2, p_recv, "back", us=10)
     n = 3 * channels
     extra = 4 * vec.shape[0]
     if fast:
@@ -754,15 +806,14 @@
         return g[0]
 
     if fast:
-        q_recv = swap(after(qkv_grads[0], m_recv), 1, "dp", name="qkv_core")
-        a_sent, a_kept, b_sent, b_kept = call(
+        q_recv = swap(after(qkv_grads[0], mlp[1]), 1, "dp", name="qkv_core")
+        g_sent, g_kept = call(
             grads_second_kernel,
-            [like((2 * share, half), BF16), like((2 * share, half), F32)] * 2,
-            [place, after(grads[1], q_recv), g_recv],
+            [like((2 * share, grad_cols), BF16)] * 2,
+            [place, after(a_kept, q_recv), a_recv, b_kept, b_recv],
             n_smem=1,
         )
-        a_recv = swap(a_sent, 2, "dp", name="grads_a")
-        b_recv = swap(b_sent, 4, "dp", name="grads_b")
+        g_recv = swap(g_sent, 1, "dp", name="grads_core")
         vec_like = [like(vec.shape, F32)]
         sent, kept, vec = call(
             qkv_second_kernel,
@@ -771,21 +822,21 @@
             n_smem=1,
         )
         recv = swap(sent, 2, "dp", name="qkv_x")
-        sent, kept, vec = call(
-            qkv_third_kernel,
-            [like((share + extra, n), BF16), like((share, n), F32)] + vec_like,
-            [place, vec, kept, recv],
-            n_smem=1,
-        )
-        recv = swap(sent, 4, "dp", name="qkv_y")
         a_sent, a_kept, b_sent, b_kept = call(
             grads_third_kernel,
             [like((share, half), BF16), like((share, half), F32)] * 2,
-            [place, after(a_kept, kept, back[0]), a_recv, b_kept, b_recv],
+            [place, g_kept, g_recv],
             n_smem=1,
         )
         a_recv = swap(a_sent, 4, "dp", name="grads_a")
         b_recv = swap(b_sent, 2, "dp", name="grads_b")
+        sent, kept, vec = call(
+            qkv_third_kernel,
+            [like((share + extra, n), BF16), like((share, n), F32)] + vec_like,
+            [place, after(vec, a_kept, back[0]), kept, recv],
+            n_smem=1,
+        )
+        recv = swap(sent, 4, "dp", name="qkv_y")
         message = like((channels + 2 * vec.size // 128, 128), BF16)
         grad_up, grad_down, grad_qkv, vec, o0, o1, o2, o3 = call(
             last_kernel,

time: 154 us -> 136 us (0.88)
  Pallas kernels: 48.7 us -> 32.8 us
  waiting for transfers between devices: 60.3 us -> 56.5 us
  starting transfers between devices: 37.2 us -> 38.9 us
    pallas_call x19 -> x20, Pallas kernels: 48.7 us -> 32.8 us  [call(): pl.pallas_call(kernel, out_shape=tuple(outs), in_specs=[SMEM] * n_smem +...]
    ppermute x29, waiting for transfers between devices: 60.3 us -> 56.5 us  [swap(): return lax.ppermute(v, axis, [(i, i ^ k) for i in range(n)])]
    ppermute x29, starting transfers between devices: 37.2 us -> 38.9 us  [swap(): return lax.ppermute(v, axis, [(i, i ^ k) for i in range(n)])]
  transfers between devices with their start and end apart: 29 -> 29, of which waited for: 13 -> 15; matrix products, arithmetic and copies ran while one was open for 2% -> 2% of each run, Pallas kernels for 20% -> 23%
where the time goes in v4:
time: 136 us
  waiting for transfers between devices  56.5 us (42%)
  starting transfers between devices  38.9 us (29%)
  Pallas kernels  32.8 us (24%)
  local copies, waits for them, and re-layouts  5.87 us (4%)
    ppermute x29, waiting for transfers between devices, swap(): return lax.ppermute(v, axis, [(i, i ^ k) for i in range(n)])  56.5 us
    ppermute x29, starting transfers between devices, swap(): return lax.ppermute(v, axis, [(i, i ^ k) for i in range(n)])  38.9 us
    pallas_call x20, Pallas kernels, call(): pl.pallas_call(kernel, out_shape=tuple(outs), in_specs=[SMEM] * n_smem +...  32.8 us
    unnamed x17, local copies, waits for them, and re-layouts  4.18 us
  transfers between devices with their start and end apart: 29, of which 15 were waited for; matrix products, arithmetic and copies ran while one was open for 2% of the time, Pallas kernels for 23%

profile of v4, /device:TPU:0, one launch (start us, length us, event | category | flops | bytes accessed | tf_op | source)
XLA Modules:
  0.0 136.0 jit_solution(17012578128490997144)
XLA Ops:
  0.7 0.9 copy-done
  1.6 0.9 pad_maximum_fusion.x0
  2.6 5.1 %collective-permute-start.2 = (bf16[176,768]{1,0:T(8,128)(2,1)S(1)}, bf16[176,768]{1,0:T(8,128)(2,1)S(1)}, u32[]{:S(2)}, u32[]{:S(2)}) collective-permute-start(bf16[176,768]{1,0:T(8,128)(2,1)S(1)} %pad_maximum_fusion.x0), channel_id=1, source_target_pairs={{0,3},{1,2},{2,1},{3,0},{4,7},{5,6},{6,5},{7,4},{8,11},{9,10},{10,... | collective-permute-start | bytes 811016 | tf_op jit(solution)/shard_map/x/ppermute | solution.py:664
  7.7 0.6 collective-permute-start
  8.3 1.4 %collective-permute-start.3 = (bf16[128,768]{1,0:T(8,128)(2,1)}, bf16[128,768]{1,0:T(8,128)(2,1)S(1)}, u32[]{:S(2)}, u32[]{:S(2)}) collective-permute-start(bf16[128,768]{1,0:T(8,128)(2,1)} %dy.1), channel_id=1, source_target_pairs={{0,1},{1,0},{2,3},{3,2},{4,5},{5,4},{6,7},{7,6},{8,9},{9,8},{10,11... | collective-permute-start | bytes 589832 | tf_op jit(solution)/shard_map/dy/ppermute | solution.py:664
  9.7 0.8 fusion
  10.5 0.8 copy.28.table
  11.3 0.7 concatenate.7
  12.0 0.2 copy.27
  12.2 1.3 copy-done.2
  13.5 1.2 copy-done.4
  14.6 0.9 turn_kernel.1
  15.6 13.8 %collective-permute-done.3.c1 = bf16[128,768]{1,0:T(8,128)(2,1)S(1)} collective-permute-done((bf16[128,768]{1,0:T(8,128)(2,1)}, bf16[128,768]{1,0:T(8,128)(2,1)S(1)}, u32[]{:S(2)}, u32[]{:S(2)}) %collective-permute-start.3) | collective-permute-done | bytes 196640 | tf_op jit(solution)/shard_map/dy/ppermute | solution.py:664
  29.4 1.3 collective-permute-done.1.x2
  30.7 1.2 collective-permute-start.5
  31.9 1.5 %collective-permute-start.4 = (bf16[4,48,768]{2,1,0:T(8,128)(2,1)S(1)}, bf16[4,48,768]{2,1,0:T(8,128)(2,1)S(1)}, u32[]{:S(2)}, u32[]{:S(2)}) collective-permute-start(bf16[4,48,768]{2,1,0:T(8,128)(2,1)S(1)} %pieces_kernel.1.a), channel_id=1, source_target_pairs={{0,8},{4,12},{8,0},{12,4},{16,24},{20,28},{24,16},{28,20},{1,9},{5... | collective-permute-start | bytes 884744 | tf_op jit(solution)/shard_map/w/ppermute | solution.py:664
  33.4 4.7 %head_kernel.1 = (bf16[768,512]{1,0:T(8,128)(2,1)S(1)}, bf16[768,512]{1,0:T(8,128)(2,1)S(1)}, f32[8,512]{1,0:T(8,128)S(1)}, bf16[576,512]{1,0:T(8,128)(2,1)S(1)}...) custom-call(s32[2]{0:T(128)S(1)} %pad_add_fusion.place, s32[1,8]{1,0:T(1,128)S(1)} %copy-done.7, ...), custom_call_target="tpu_custom_call" | custom-call | flops 11500000256 | bytes 8 | tf_op jit(solution)/shard_map/head_kernel/pallas_call | solution.py:21
  38.2 3.7 %collective-permute-done.5.c2 = bf16[128,768]{1,0:T(8,128)(2,1)S(1)} collective-permute-done((bf16[128,768]{1,0:T(8,128)(2,1)S(1)}, bf16[128,768]{1,0:T(8,128)(2,1)S(1)}, u32[]{:S(2)}, u32[]{:S(2)}) %collective-permute-start.5) | collective-permute-done | bytes 196640 | tf_op jit(solution)/shard_map/dy/ppermute | solution.py:664
  42.0 1.7 %collective-permute-start.8 = (bf16[192,512]{1,0:T(8,128)(2,1)S(1)}, bf16[192,512]{1,0:T(8,128)(2,1)S(1)}, u32[]{:S(2)}, u32[]{:S(2)}) collective-permute-start(bf16[192,512]{1,0:T(8,128)(2,1)S(1)} %get-tuple-element.107.a0), channel_id=1, source_target_pairs={{0,3},{1,2},{2,1},{3,0},{4,7},{5,6},{6,5},{7,4},{8,11},{9,10},{10,... | collective-permute-start | bytes 589832 | tf_op jit(solution)/shard_map/att/ppermute | solution.py:664
  43.7 0.8 collective-permute-start.7
  44.6 1.9 %collective-permute-start.6 = (bf16[192,512]{1,0:T(8,128)(2,1)S(1)}, bf16[192,512]{1,0:T(8,128)(2,1)S(1)}, u32[]{:S(2)}, u32[]{:S(2)}) collective-permute-start(bf16[192,512]{1,0:T(8,128)(2,1)S(1)} %get-tuple-element.107.a0), channel_id=1, source_target_pairs={{0,1},{1,0},{2,3},{3,2},{4,5},{5,4},{6,7},{7,6},{8,9},{9,8},{10,11... | collective-permute-start | bytes 589832 | tf_op jit(solution)/shard_map/att/ppermute | solution.py:664
  46.4 5.3 %collective-permute-done.8.a3 = bf16[192,512]{1,0:T(8,128)(2,1)S(1)} collective-permute-done((bf16[192,512]{1,0:T(8,128)(2,1)S(1)}, bf16[192,512]{1,0:T(8,128)(2,1)S(1)}, u32[]{:S(2)}, u32[]{:S(2)}) %collective-permute-start.8) | collective-permute-done | bytes 196640 | tf_op jit(solution)/shard_map/att/ppermute | solution.py:664
  51.7 10.7 %collective-permute-done.7.a2 = bf16[192,512]{1,0:T(8,128)(2,1)S(1)} collective-permute-done((bf16[192,512]{1,0:T(8,128)(2,1)S(1)}, bf16[192,512]{1,0:T(8,128)(2,1)S(1)}, u32[]{:S(2)}, u32[]{:S(2)}) %collective-permute-start.7) | collective-permute-done | bytes 196640 | tf_op jit(solution)/shard_map/att/ppermute | solution.py:664
  62.5 1.0 out_weight_kernel.1
  63.5 4.1 %up_kernel.1 = (bf16[768,512]{1,0:T(8,128)(2,1)S(1)}, f32[768,512]{1,0:T(8,128)S(1)}, f32[768,512]{1,0:T(8,128)S(1)}, f32[8,512]{1,0:T(8,128)S(1)}, bf16[768,512...) custom-call(s32[2]{0:T(128)S(1)} %pad_add_fusion.place, ...), custom_call_target="tpu_custom_call" | custom-call | flops 11500000256 | bytes 8 | tf_op jit(solution)/shard_map/up_kernel/pallas_call | solution.py:21
  67.6 2.1 %collective-permute-start.10 = (bf16[1536,128]{1,0:T(8,128)(2,1)S(1)}, bf16[1536,128]{1,0:T(8,128)(2,1)S(1)}, u32[]{:S(2)}, u32[]{:S(2)}) collective-permute-start(bf16[1536,128]{1,0:T(8,128)(2,1)S(1)} %get-tuple-element.112), channel_id=1, source_target_pairs={{0,1},{1,0},{2,3},{3,2},{4,5},{5,4},{6,7},{7,6},{8,9},{9,8},{10,11... | collective-permute-start | bytes 1179656 | tf_op jit(solution)/shard_map/mlp/ppermute | solution.py:664
  69.7 4.5 %down_kernel.1 = (bf16[192,512]{1,0:T(8,128)(2,1)S(1)}, bf16[192,512]{1,0:T(8,128)(2,1)S(1)}, bf16[192,512]{1,0:T(8,128)(2,1)S(1)}, bf16[192,512]{1,0:T(8,128)(2...) custom-call(s32[2]{0:T(128)S(1)} %pad_add_fusion.place, ...), custom_call_target="tpu_custom_call" | custom-call | flops 11500000256 | bytes 8 | tf_op jit(solution)/shard_map/down_kernel/pallas_call | solution.py:21
  74.2 0.1 collective-permute-start.12
  74.3 1.7 %collective-permute-start.13 = (bf16[192,512]{1,0:T(8,128)(2,1)S(1)}, bf16[192,512]{1,0:T(8,128)(2,1)S(1)}, u32[]{:S(2)}, u32[]{:S(2)}) collective-permute-start(bf16[192,512]{1,0:T(8,128)(2,1)S(1)} %get-tuple-element.122), channel_id=1, source_target_pairs={{0,2},{1,3},{2,0},{3,1},{4,6},{5,7},{6,4},{7,5},{8,10},{9,11},{10,... | collective-permute-start | bytes 589832 | tf_op jit(solution)/shard_map/d_att/ppermute | solution.py:664
  76.0 2.7 %collective-permute-start.14 = (bf16[192,512]{1,0:T(8,128)(2,1)S(1)}, bf16[192,512]{1,0:T(8,128)(2,1)S(1)}, u32[]{:S(2)}, u32[]{:S(2)}) collective-permute-start(bf16[192,512]{1,0:T(8,128)(2,1)S(1)} %get-tuple-element.123), channel_id=1, source_target_pairs={{0,3},{1,2},{2,1},{3,0},{4,7},{5,6},{6,5},{7,4},{8,11},{9,10},{10,... | collective-permute-start | bytes 589832 | tf_op jit(solution)/shard_map/d_att/ppermute | solution.py:664
  78.6 2.6 %mlp_grad_kernel.1 = (f32[8,768]{1,0:T(8,128)S(1)}, bf16[384,1152]{1,0:T(8,128)(2,1)S(1)}, bf16[384,1152]{1,0:T(8,128)(2,1)S(1)}, bf16[384,1152]{1,0:T(8,128)(2,1)S(1)}, bf16[384,1152]{1,0:T(8,128)(2,1)S(1)}) custom-call(s32[2]{0:T(128)S(1)} %pad_add_fusion.place, f32[8,768]{1,0:T(8,128)S(1)} %get-tuple-element.131.vec, ...), custom_call_target="tpu_custom_call" | custom-call | flops 11500000 | bytes 8 | tf_op jit(solution)/shard_map/mlp_grad_kernel/pallas_call | solution.py:21
  81.2 1.6 %collective-permute-start.19 = (bf16[384,1152]{1,0:T(8,128)(2,1)S(1)}, bf16[384,1152]{1,0:T(8,128)(2,1)S(1)}, u32[]{:S(2)}, u32[]{:S(2)}) collective-permute-start(bf16[384,1152]{1,0:T(8,128)(2,1)S(1)} %get-tuple-element.156), channel_id=1, source_target_pairs={{0,8},{4,12},{8,0},{12,4},{16,24},{20,28},{24,16},{28,20},{1,9},{5... | collective-permute-start | bytes 2654216 | tf_op jit(solution)/shard_map/grads_a/ppermute | solution.py:664
  82.8 1.0 collective-permute-done.10.recv
  83.8 1.5 %collective-permute-start.20 = (bf16[384,1152]{1,0:T(8,128)(2,1)S(1)}, bf16[384,1152]{1,0:T(8,128)(2,1)S(1)}, u32[]{:S(2)}, u32[]{:S(2)}) collective-permute-start(bf16[384,1152]{1,0:T(8,128)(2,1)S(1)} %get-tuple-element.158), channel_id=1, source_target_pairs={{0,16},{4,20},{8,24},{12,28},{16,0},{20,4},{24,8},{28,12},{1,17},{... | collective-permute-start | bytes 2654216 | tf_op jit(solution)/shard_map/grads_b/ppermute | solution.py:664
  85.4 1.7 %collective-permute-done.12.d1 = bf16[192,512]{1,0:T(8,128)(2,1)S(1)} collective-permute-done((bf16[192,512]{1,0:T(8,128)(2,1)S(1)}, bf16[192,512]{1,0:T(8,128)(2,1)S(1)}, u32[]{:S(2)}, u32[]{:S(2)}) %collective-permute-start.12) | collective-permute-done | bytes 196640 | tf_op jit(solution)/shard_map/d_att/ppermute | solution.py:664
  87.1 0.6 collective-permute-done.13.d2
  87.8 4.4 %collective-permute-done.14.d3 = bf16[192,512]{1,0:T(8,128)(2,1)S(1)} collective-permute-done((bf16[192,512]{1,0:T(8,128)(2,1)S(1)}, bf16[192,512]{1,0:T(8,128)(2,1)S(1)}, u32[]{:S(2)}, u32[]{:S(2)}) %collective-permute-start.14) | collective-permute-done | bytes 196640 | tf_op jit(solution)/shard_map/d_att/ppermute | solution.py:664
  92.2 2.3 %collective-permute-start.15 = (bf16[768,128]{1,0:T(8,128)(2,1)S(1)}, bf16[768,128]{1,0:T(8,128)(2,1)S(1)}, u32[]{:S(2)}, u32[]{:S(2)}) collective-permute-start(bf16[768,128]{1,0:T(8,128)(2,1)S(1)} %get-tuple-element.124), channel_id=1, source_target_pairs={{0,2},{1,3},{2,0},{3,1},{4,6},{5,7},{6,4},{7,5},{8,10},{9,11},{10,... | collective-permute-start | bytes 589832 | tf_op jit(solution)/shard_map/mlp/ppermute | solution.py:664
  94.4 6.3 %back_kernel.1 = (f32[768,128]{1,0:T(8,128)S(1)}, f32[768,128]{1,0:T(8,128)S(1)}, bf16[1536,128]{1,0:T(8,128)(2,1)S(1)}, bf16[576,512]{1,0:T(8,128)(2,1)S(1)}, f32[8,768]{1,0:T(8,128)S(1)}) custom-call(s32[2]{0:T(128)S(1)} %pad_add_fusion.place, s32[1,8]{1,0:T(1,128)S(1)} %copy-done.7, bf16[192,512]{1,0:T(8,128)(2,1)S(1)} %get-tuple-element.126.d0, ...), custom_call_target="tpu_custom_call" | custom-call | flops 11500000256 | bytes 8 | tf_op jit(solution)/shard_map/back_kernel/pallas_call | solution.py:21
  100.7 1.4 %qkv_grad_kernel.1 = (bf16[416,576]{1,0:T(8,128)(2,1)S(1)}, bf16[384,576]{1,0:T(8,128)(2,1)S(1)}) custom-call(s32[2]{0:T(128)S(1)} %pad_add_fusion.place, bf16[768,512]{1,0:T(8,128)(2,1)S(1)} %get-tuple-element.148.h1, bf16[576,512]{1,0:T(8,128)(2,1)S(1)} %get-tuple-element.149.dqkv, f32[8,768]{1,0:T(8,128)S(1)} %get-tuple-element.147.vec), custom_call_target="tpu_custom_call" | custom-call | flops 11500000 | bytes 8 | tf_op jit(solution)/shard_map/qkv_grad_kernel/pallas_call | solution.py:21
  102.1 0.4 collective-permute-done.15.recv
  102.4 1.9 %collective-permute-done.18.recv = bf16[416,576]{1,0:T(8,128)(2,1)S(1)} collective-permute-done((bf16[416,576]{1,0:T(8,128)(2,1)S(1)}, bf16[416,576]{1,0:T(8,128)(2,1)S(1)}, u32[]{:S(2)}, u32[]{:S(2)}) %collective-permute-start.18) | collective-permute-done | bytes 479264 | tf_op jit(solution)/shard_map/qkv_core/ppermute | solution.py:664
  104.4 1.0 grads_second_kernel.1
  105.3 0.2 collective-permute-start.21
  105.5 0.6 collective-permute-start.16
  106.1 0.7 qkv_second_kernel.1
  106.8 1.6 %collective-permute-start.22 = (bf16[224,576]{1,0:T(8,128)(2,1)S(1)}, bf16[224,576]{1,0:T(8,128)(2,1)S(1)}, u32[]{:S(2)}, u32[]{:S(2)}) collective-permute-start(bf16[224,576]{1,0:T(8,128)(2,1)S(1)} %get-tuple-element.164), channel_id=1, source_target_pairs={{0,8},{4,12},{8,0},{12,4},{16,24},{20,28},{24,16},{28,20},{1,9},{5... | collective-permute-start | bytes 774152 | tf_op jit(solution)/shard_map/qkv_x/ppermute | solution.py:664
  108.4 0.7 grads_third_kernel.1
  109.1 1.6 %collective-permute-start.23 = (bf16[96,1152]{1,0:T(8,128)(2,1)S(1)}, bf16[96,1152]{1,0:T(8,128)(2,1)S(1)}, u32[]{:S(2)}, u32[]{:S(2)}) collective-permute-start(bf16[96,1152]{1,0:T(8,128)(2,1)S(1)} %get-tuple-element.166), channel_id=1, source_target_pairs={{0,16},{4,20},{8,24},{12,28},{16,0},{20,4},{24,8},{28,12},{1,17},{... | collective-permute-start | bytes 663560 | tf_op jit(solution)/shard_map/grads_a/ppermute | solution.py:664
  110.7 1.0 collective-permute-start.24
  111.7 5.3 %collective-permute-done.16.recv = bf16[1536,128]{1,0:T(8,128)(2,1)S(1)} collective-permute-done((bf16[1536,128]{1,0:T(8,128)(2,1)S(1)}, bf16[1536,128]{1,0:T(8,128)(2,1)S(1)}, u32[]{:S(2)}, u32[]{:S(2)}) %collective-permute-start.16) | collective-permute-done | bytes 393248 | tf_op jit(solution)/shard_map/back/ppermute | solution.py:664
  117.0 0.6 qkv_third_kernel.1
  117.6 1.6 %collective-permute-start.25 = (bf16[128,576]{1,0:T(8,128)(2,1)S(1)}, bf16[128,576]{1,0:T(8,128)(2,1)S(1)}, u32[]{:S(2)}, u32[]{:S(2)}) collective-permute-start(bf16[128,576]{1,0:T(8,128)(2,1)S(1)} %get-tuple-element.170), channel_id=1, source_target_pairs={{0,16},{4,20},{8,24},{12,28},{16,0},{20,4},{24,8},{28,12},{1,17},{... | collective-permute-start | bytes 442376 | tf_op jit(solution)/shard_map/qkv_y/ppermute | solution.py:664
  119.2 1.8 %collective-permute-start.17 = (bf16[768,128]{1,0:T(8,128)(2,1)S(1)}, bf16[768,128]{1,0:T(8,128)(2,1)S(1)}, u32[]{:S(2)}, u32[]{:S(2)}) collective-permute-start(bf16[768,128]{1,0:T(8,128)(2,1)S(1)} %get-tuple-element.146), channel_id=1, source_target_pairs={{0,2},{1,3},{2,0},{3,1},{4,6},{5,7},{6,4},{7,5},{8,10},{9,11},{10,... | collective-permute-start | bytes 589832 | tf_op jit(solution)/shard_map/back/ppermute | solution.py:664
  121.0 2.3 %collective-permute-done.25.q_recv = bf16[128,576]{1,0:T(8,128)(2,1)S(1)} collective-permute-done((bf16[128,576]{1,0:T(8,128)(2,1)S(1)}, bf16[128,576]{1,0:T(8,128)(2,1)S(1)}, u32[]{:S(2)}, u32[]{:S(2)}) %collective-permute-start.25) | collective-permute-done | bytes 147488 | tf_op jit(solution)/shard_map/qkv_y/ppermute | solution.py:664
  123.4 1.6 %last_kernel.1 = (f32[96,768]{1,0:T(8,128)}, f32[96,768]{1,0:T(8,128)}, f32[3,96,192]{2,1,0:T(8,128)}, f32[8,768]{1,0:T(8,128)S(1)}, f32[192,96]{1,0:T(8,128)S(1...) custom-call(s32[2]{0:T(128)S(1)} %pad_add_fusion.place, ...), custom_call_target="tpu_custom_call" | custom-call | flops 11500000 | bytes 8 | tf_op jit(solution)/shard_map/last_kernel/pallas_call | solution.py:21
  125.0 0.7 collective-permute-start.26
  125.7 2.1 %collective-permute-start.27 = (bf16[288,128]{1,0:T(8,128)(2,1)S(1)}, bf16[288,128]{1,0:T(8,128)(2,1)S(1)}, u32[]{:S(2)}, u32[]{:S(2)}) collective-permute-start(bf16[288,128]{1,0:T(8,128)(2,1)S(1)} %get-tuple-element.174), channel_id=1, source_target_pairs={{0,2},{1,3},{2,0},{3,1},{4,6},{5,7},{6,4},{7,5},{8,10},{9,11},{10,... | collective-permute-start | bytes 221192 | tf_op jit(solution)/shard_map/out/ppermute | solution.py:664
  127.8 1.6 %collective-permute-start.28 = (bf16[288,128]{1,0:T(8,128)(2,1)S(1)}, bf16[288,128]{1,0:T(8,128)(2,1)S(1)}, u32[]{:S(2)}, u32[]{:S(2)}) collective-permute-start(bf16[288,128]{1,0:T(8,128)(2,1)S(1)} %get-tuple-element.175), channel_id=1, source_target_pairs={{0,3},{1,2},{2,1},{3,0},{4,7},{5,6},{6,5},{7,4},{8,11},{9,10},{10,... | collective-permute-start | bytes 221192 | tf_op jit(solution)/shard_map/out/ppermute | solution.py:664
  129.4 0.9 output_kernel.1
  130.4 2.6 %collective-permute-done.17.recv = bf16[768,128]{1,0:T(8,128)(2,1)S(1)} collective-permute-done((bf16[768,128]{1,0:T(8,128)(2,1)S(1)}, bf16[768,128]{1,0:T(8,128)(2,1)S(1)}, u32[]{:S(2)}, u32[]{:S(2)}) %collective-permute-start.17) | collective-permute-done | bytes 196640 | tf_op jit(solution)/shard_map/back/ppermute | solution.py:664
  133.0 0.9 input_kernel.1
  133.8 1.5 %collective-permute-done.27.o2 = bf16[288,128]{1,0:T(8,128)(2,1)S(1)} collective-permute-done((bf16[288,128]{1,0:T(8,128)(2,1)S(1)}, bf16[288,128]{1,0:T(8,128)(2,1)S(1)}, u32[]{:S(2)}, u32[]{:S(2)}) %collective-permute-start.27) | collective-permute-done | bytes 73760 | tf_op jit(solution)/shard_map/out/ppermute | solution.py:664
  135.3 0.7 small_kernel.1
  (37 shorter events, 0.5 us)
Async XLA Ops:
  0.6 1.0 copy-start
  0.7 11.5 %copy-start.1 = (bf16[768,768]{1,0:T(8,128)(2,1)S(1)}, bf16[768,768]{1,0:T(8,128)(2,1)}, u32[]{:S(2)}) copy-start(bf16[768,768]{1,0:T(8,128)(2,1)} %w_up.1) | copy-start | bytes 3538948
  2.6 26.9 %collective-permute-start.2 = (bf16[176,768]{1,0:T(8,128)(2,1)S(1)}, bf16[176,768]{1,0:T(8,128)(2,1)S(1)}, u32[]{:S(2)}, u32[]{:S(2)}) collective-permute-start(bf16[176,768]{1,0:T(8,128)(2,1)S(1)} %pad_maximum_fusion.x0), channel_id=1, source_target_pairs={{0,3},{1,2},{2,1},{3,0},{4,7},{5,6},{6,5},{7,4},{8,11},{9,10},{10,... | collective-permute-start | bytes 811016 | tf_op jit(solution)/shard_map/x/ppermute | solution.py:664
  7.7 23.0 %collective-permute-start.1 = (bf16[176,768]{1,0:T(8,128)(2,1)S(1)}, bf16[176,768]{1,0:T(8,128)(2,1)S(1)}, u32[]{:S(2)}, u32[]{:S(2)}) collective-permute-start(bf16[176,768]{1,0:T(8,128)(2,1)S(1)} %pad_maximum_fusion.x0), channel_id=1, source_target_pairs={{0,2},{1,3},{2,0},{3,1},{4,6},{5,7},{6,4},{7,5},{8,10},{9,11},{10,... | collective-permute-start | bytes 811016 | tf_op jit(solution)/shard_map/x/ppermute | solution.py:664
  7.7 23.0 %collective-permute-start = (bf16[176,768]{1,0:T(8,128)(2,1)S(1)}, bf16[176,768]{1,0:T(8,128)(2,1)S(1)}, u32[]{:S(2)}, u32[]{:S(2)}) collective-permute-start(bf16[176,768]{1,0:T(8,128)(2,1)S(1)} %pad_maximum_fusion.x0), channel_id=1, source_target_pairs={{0,1},{1,0},{2,3},{3,2},{4,5},{5,4},{6,7},{7,6},{8,9},{9,8},{10,11... | collective-permute-start | bytes 811016 | tf_op jit(solution)/shard_map/x/ppermute | solution.py:664
  8.3 21.1 %collective-permute-start.3 = (bf16[128,768]{1,0:T(8,128)(2,1)}, bf16[128,768]{1,0:T(8,128)(2,1)S(1)}, u32[]{:S(2)}, u32[]{:S(2)}) collective-permute-start(bf16[128,768]{1,0:T(8,128)(2,1)} %dy.1), channel_id=1, source_target_pairs={{0,1},{1,0},{2,3},{3,2},{4,5},{5,4},{6,7},{7,6},{8,9},{9,8},{10,11... | collective-permute-start | bytes 589832 | tf_op jit(solution)/shard_map/dy/ppermute | solution.py:664
  12.2 1.3 copy-start.2
  13.5 1.2 copy-start.4
  14.6 16.1 %copy-start.6 = (bf16[128,768]{1,0:T(8,128)(2,1)S(1)}, bf16[128,768]{1,0:T(8,128)(2,1)}, u32[]{:S(2)}) copy-start(bf16[128,768]{1,0:T(8,128)(2,1)} %dy.1) | copy-start | bytes 589828
  14.6 18.8 %copy-start.5 = (bf16[768,3,192]{0,2,1:T(8,128)(2,1)S(1)}, bf16[768,3,192]{0,2,1:T(8,128)(2,1)}, u32[]{:S(2)}) copy-start(bf16[768,3,192]{0,2,1:T(8,128)(2,1)} %param.16) | copy-start | bytes 2654212
  14.6 18.8 %copy-start.7 = (s32[1,8]{1,0:T(1,128)S(1)}, s32[1,8]{1,0:T(1,128)}, u32[]{:S(2)}) copy-start(s32[1,8]{1,0:T(1,128)} %lengths.3) | copy-start | bytes 100
  30.7 11.1 %collective-permute-start.5 = (bf16[128,768]{1,0:T(8,128)(2,1)S(1)}, bf16[128,768]{1,0:T(8,128)(2,1)S(1)}, u32[]{:S(2)}, u32[]{:S(2)}) collective-permute-start(bf16[128,768]{1,0:T(8,128)(2,1)S(1)} %copy-done.6), channel_id=1, source_target_pairs={{0,2},{1,3},{2,0},{3,1},{4,6},{5,7},{6,4},{7,5},{8,10},{9,11},{10,... | collective-permute-start | bytes 589832 | tf_op jit(solution)/shard_map/dy/ppermute | solution.py:664
  31.9 9.9 %collective-permute-start.4 = (bf16[4,48,768]{2,1,0:T(8,128)(2,1)S(1)}, bf16[4,48,768]{2,1,0:T(8,128)(2,1)S(1)}, u32[]{:S(2)}, u32[]{:S(2)}) collective-permute-start(bf16[4,48,768]{2,1,0:T(8,128)(2,1)S(1)} %pieces_kernel.1.a), channel_id=1, source_target_pairs={{0,8},{4,12},{8,0},{12,4},{16,24},{20,28},{24,16},{28,20},{1,9},{5... | collective-permute-start | bytes 884744 | tf_op jit(solution)/shard_map/w/ppermute | solution.py:664
  41.9 20.5 %collective-permute-start.9 = (bf16[8,48,768]{2,1,0:T(8,128)(2,1)S(1)}, bf16[8,48,768]{2,1,0:T(8,128)(2,1)S(1)}, u32[]{:S(2)}, u32[]{:S(2)}) collective-permute-start(bf16[8,48,768]{2,1,0:T(8,128)(2,1)S(1)} %pair_kernel.1.here), channel_id=1, source_target_pairs={{0,4},{4,0},{8,12},{12,8},{16,20},{20,16},{24,28},{28,24},{1,5},{5... | collective-permute-start | bytes 1769480 | tf_op jit(solution)/shard_map/w/ppermute | solution.py:664
  42.0 9.7 %collective-permute-start.8 = (bf16[192,512]{1,0:T(8,128)(2,1)S(1)}, bf16[192,512]{1,0:T(8,128)(2,1)S(1)}, u32[]{:S(2)}, u32[]{:S(2)}) collective-permute-start(bf16[192,512]{1,0:T(8,128)(2,1)S(1)} %get-tuple-element.107.a0), channel_id=1, source_target_pairs={{0,3},{1,2},{2,1},{3,0},{4,7},{5,6},{6,5},{7,4},{8,11},{9,10},{10,... | collective-permute-start | bytes 589832 | tf_op jit(solution)/shard_map/att/ppermute | solution.py:664
  43.7 18.7 %collective-permute-start.7 = (bf16[192,512]{1,0:T(8,128)(2,1)S(1)}, bf16[192,512]{1,0:T(8,128)(2,1)S(1)}, u32[]{:S(2)}, u32[]{:S(2)}) collective-permute-start(bf16[192,512]{1,0:T(8,128)(2,1)S(1)} %get-tuple-element.107.a0), channel_id=1, source_target_pairs={{0,2},{1,3},{2,0},{3,1},{4,6},{5,7},{6,4},{7,5},{8,10},{9,11},{10,... | collective-permute-start | bytes 589832 | tf_op jit(solution)/shard_map/att/ppermute | solution.py:664
  44.6 17.9 %collective-permute-start.6 = (bf16[192,512]{1,0:T(8,128)(2,1)S(1)}, bf16[192,512]{1,0:T(8,128)(2,1)S(1)}, u32[]{:S(2)}, u32[]{:S(2)}) collective-permute-start(bf16[192,512]{1,0:T(8,128)(2,1)S(1)} %get-tuple-element.107.a0), channel_id=1, source_target_pairs={{0,1},{1,0},{2,3},{3,2},{4,5},{5,4},{6,7},{7,6},{8,9},{9,8},{10,11... | collective-permute-start | bytes 589832 | tf_op jit(solution)/shard_map/att/ppermute | solution.py:664
  62.5 7.3 %collective-permute-start.11 = (bf16[128,768]{1,0:T(8,128)(2,1)S(1)}, bf16[128,768]{1,0:T(8,128)(2,1)S(1)}, u32[]{:S(2)}, u32[]{:S(2)}) collective-permute-start(bf16[128,768]{1,0:T(8,128)(2,1)S(1)} %collective-permute-done.5.c2), channel_id=1, source_target_pairs={{0,1},{1,0},{2,3},{3,2},{4,5},{5,4},{6,7},{7,6},{8,9},{9,8},{10,11... | collective-permute-start | bytes 589832 | tf_op jit(solution)/shard_map/dy/ppermute | solution.py:664
  63.4 6.3 %copy-start.3 = (bf16[768,768]{1,0:T(8,128)(2,1)S(1)}, bf16[768,768]{1,0:T(8,128)(2,1)}, u32[]{:S(2)}) copy-start(bf16[768,768]{1,0:T(8,128)(2,1)} %w_down.1) | copy-start | bytes 3538948
  67.6 16.2 %collective-permute-start.10 = (bf16[1536,128]{1,0:T(8,128)(2,1)S(1)}, bf16[1536,128]{1,0:T(8,128)(2,1)S(1)}, u32[]{:S(2)}, u32[]{:S(2)}) collective-permute-start(bf16[1536,128]{1,0:T(8,128)(2,1)S(1)} %get-tuple-element.112), channel_id=1, source_target_pairs={{0,1},{1,0},{2,3},{3,2},{4,5},{5,4},{6,7},{7,6},{8,9},{9,8},{10,11... | collective-permute-start | bytes 1179656 | tf_op jit(solution)/shard_map/mlp/ppermute | solution.py:664
  74.2 12.9 %collective-permute-start.12 = (bf16[192,512]{1,0:T(8,128)(2,1)S(1)}, bf16[192,512]{1,0:T(8,128)(2,1)S(1)}, u32[]{:S(2)}, u32[]{:S(2)}) collective-permute-start(bf16[192,512]{1,0:T(8,128)(2,1)S(1)} %get-tuple-element.121), channel_id=1, source_target_pairs={{0,1},{1,0},{2,3},{3,2},{4,5},{5,4},{6,7},{7,6},{8,9},{9,8},{10,11... | collective-permute-start | bytes 589832 | tf_op jit(solution)/shard_map/d_att/ppermute | solution.py:664
  74.3 13.5 %collective-permute-start.13 = (bf16[192,512]{1,0:T(8,128)(2,1)S(1)}, bf16[192,512]{1,0:T(8,128)(2,1)S(1)}, u32[]{:S(2)}, u32[]{:S(2)}) collective-permute-start(bf16[192,512]{1,0:T(8,128)(2,1)S(1)} %get-tuple-element.122), channel_id=1, source_target_pairs={{0,2},{1,3},{2,0},{3,1},{4,6},{5,7},{6,4},{7,5},{8,10},{9,11},{10,... | collective-permute-start | bytes 589832 | tf_op jit(solution)/shard_map/d_att/ppermute | solution.py:664
  76.0 16.2 %collective-permute-start.14 = (bf16[192,512]{1,0:T(8,128)(2,1)S(1)}, bf16[192,512]{1,0:T(8,128)(2,1)S(1)}, u32[]{:S(2)}, u32[]{:S(2)}) collective-permute-start(bf16[192,512]{1,0:T(8,128)(2,1)S(1)} %get-tuple-element.123), channel_id=1, source_target_pairs={{0,3},{1,2},{2,1},{3,0},{4,7},{5,6},{6,5},{7,4},{8,11},{9,10},{10,... | collective-permute-start | bytes 589832 | tf_op jit(solution)/shard_map/d_att/ppermute | solution.py:664
  81.2 23.1 %collective-permute-start.19 = (bf16[384,1152]{1,0:T(8,128)(2,1)S(1)}, bf16[384,1152]{1,0:T(8,128)(2,1)S(1)}, u32[]{:S(2)}, u32[]{:S(2)}) collective-permute-start(bf16[384,1152]{1,0:T(8,128)(2,1)S(1)} %get-tuple-element.156), channel_id=1, source_target_pairs={{0,8},{4,12},{8,0},{12,4},{16,24},{20,28},{24,16},{28,20},{1,9},{5... | collective-permute-start | bytes 2654216 | tf_op jit(solution)/shard_map/grads_a/ppermute | solution.py:664
  83.8 20.6 %collective-permute-start.20 = (bf16[384,1152]{1,0:T(8,128)(2,1)S(1)}, bf16[384,1152]{1,0:T(8,128)(2,1)S(1)}, u32[]{:S(2)}, u32[]{:S(2)}) collective-permute-start(bf16[384,1152]{1,0:T(8,128)(2,1)S(1)} %get-tuple-element.158), channel_id=1, source_target_pairs={{0,16},{4,20},{8,24},{12,28},{16,0},{20,4},{24,8},{28,12},{1,17},{... | collective-permute-start | bytes 2654216 | tf_op jit(solution)/shard_map/grads_b/ppermute | solution.py:664
  92.2 10.3 %collective-permute-start.15 = (bf16[768,128]{1,0:T(8,128)(2,1)S(1)}, bf16[768,128]{1,0:T(8,128)(2,1)S(1)}, u32[]{:S(2)}, u32[]{:S(2)}) collective-permute-start(bf16[768,128]{1,0:T(8,128)(2,1)S(1)} %get-tuple-element.124), channel_id=1, source_target_pairs={{0,2},{1,3},{2,0},{3,1},{4,6},{5,7},{6,4},{7,5},{8,10},{9,11},{10,... | collective-permute-start | bytes 589832 | tf_op jit(solution)/shard_map/mlp/ppermute | solution.py:664
  102.4 1.9 %collective-permute-start.18 = (bf16[416,576]{1,0:T(8,128)(2,1)S(1)}, bf16[416,576]{1,0:T(8,128)(2,1)S(1)}, u32[]{:S(2)}, u32[]{:S(2)}) collective-permute-start(bf16[416,576]{1,0:T(8,128)(2,1)S(1)} %get-tuple-element.152), channel_id=1, source_target_pairs={{0,4},{4,0},{8,12},{12,8},{16,20},{20,16},{24,28},{28,24},{1,5},{5... | collective-permute-start | bytes 1437704 | tf_op jit(solution)/shard_map/qkv_core/ppermute | solution.py:664
  105.3 3.0 %collective-permute-start.21 = (bf16[192,2304]{1,0:T(8,128)(2,1)S(1)}, bf16[192,2304]{1,0:T(8,128)(2,1)S(1)}, u32[]{:S(2)}, u32[]{:S(2)}) collective-permute-start(bf16[192,2304]{1,0:T(8,128)(2,1)S(1)} %get-tuple-element.160), channel_id=1, source_target_pairs={{0,4},{4,0},{8,12},{12,8},{16,20},{20,16},{24,28},{28,24},{1,5},{5... | collective-permute-start | bytes 2654216 | tf_op jit(solution)/shard_map/grads_core/ppermute | solution.py:664
  105.5 11.4 %collective-permute-start.16 = (bf16[1536,128]{1,0:T(8,128)(2,1)S(1)}, bf16[1536,128]{1,0:T(8,128)(2,1)S(1)}, u32[]{:S(2)}, u32[]{:S(2)}) collective-permute-start(bf16[1536,128]{1,0:T(8,128)(2,1)S(1)} %get-tuple-element.144), channel_id=1, source_target_pairs={{0,1},{1,0},{2,3},{3,2},{4,5},{5,4},{6,7},{7,6},{8,9},{9,8},{10,11... | collective-permute-start | bytes 1179656 | tf_op jit(solution)/shard_map/back/ppermute | solution.py:664
  106.8 10.2 %collective-permute-start.22 = (bf16[224,576]{1,0:T(8,128)(2,1)S(1)}, bf16[224,576]{1,0:T(8,128)(2,1)S(1)}, u32[]{:S(2)}, u32[]{:S(2)}) collective-permute-start(bf16[224,576]{1,0:T(8,128)(2,1)S(1)} %get-tuple-element.164), channel_id=1, source_target_pairs={{0,8},{4,12},{8,0},{12,4},{16,24},{20,28},{24,16},{28,20},{1,9},{5... | collective-permute-start | bytes 774152 | tf_op jit(solution)/shard_map/qkv_x/ppermute | solution.py:664
  109.1 14.3 %collective-permute-start.23 = (bf16[96,1152]{1,0:T(8,128)(2,1)S(1)}, bf16[96,1152]{1,0:T(8,128)(2,1)S(1)}, u32[]{:S(2)}, u32[]{:S(2)}) collective-permute-start(bf16[96,1152]{1,0:T(8,128)(2,1)S(1)} %get-tuple-element.166), channel_id=1, source_target_pairs={{0,16},{4,20},{8,24},{12,28},{16,0},{20,4},{24,8},{28,12},{1,17},{... | collective-permute-start | bytes 663560 | tf_op jit(solution)/shard_map/grads_a/ppermute | solution.py:664
  110.7 12.7 %collective-permute-start.24 = (bf16[96,1152]{1,0:T(8,128)(2,1)S(1)}, bf16[96,1152]{1,0:T(8,128)(2,1)S(1)}, u32[]{:S(2)}, u32[]{:S(2)}) collective-permute-start(bf16[96,1152]{1,0:T(8,128)(2,1)S(1)} %get-tuple-element.168), channel_id=1, source_target_pairs={{0,8},{4,12},{8,0},{12,4},{16,24},{20,28},{24,16},{28,20},{1,9},{5... | collective-permute-start | bytes 663560 | tf_op jit(solution)/shard_map/grads_b/ppermute | solution.py:664
  117.6 5.7 %collective-permute-start.25 = (bf16[128,576]{1,0:T(8,128)(2,1)S(1)}, bf16[128,576]{1,0:T(8,128)(2,1)S(1)}, u32[]{:S(2)}, u32[]{:S(2)}) collective-permute-start(bf16[128,576]{1,0:T(8,128)(2,1)S(1)} %get-tuple-element.170), channel_id=1, source_target_pairs={{0,16},{4,20},{8,24},{12,28},{16,0},{20,4},{24,8},{28,12},{1,17},{... | collective-permute-start | bytes 442376 | tf_op jit(solution)/shard_map/qkv_y/ppermute | solution.py:664
  119.2 13.7 %collective-permute-start.17 = (bf16[768,128]{1,0:T(8,128)(2,1)S(1)}, bf16[768,128]{1,0:T(8,128)(2,1)S(1)}, u32[]{:S(2)}, u32[]{:S(2)}) collective-permute-start(bf16[768,128]{1,0:T(8,128)(2,1)S(1)} %get-tuple-element.146), channel_id=1, source_target_pairs={{0,2},{1,3},{2,0},{3,1},{4,6},{5,7},{6,4},{7,5},{8,10},{9,11},{10,... | collective-permute-start | bytes 589832 | tf_op jit(solution)/shard_map/back/ppermute | solution.py:664
  125.0 8.8 %collective-permute-start.26 = (bf16[288,128]{1,0:T(8,128)(2,1)S(1)}, bf16[288,128]{1,0:T(8,128)(2,1)S(1)}, u32[]{:S(2)}, u32[]{:S(2)}) collective-permute-start(bf16[288,128]{1,0:T(8,128)(2,1)S(1)} %get-tuple-element.173), channel_id=1, source_target_pairs={{0,1},{1,0},{2,3},{3,2},{4,5},{5,4},{6,7},{7,6},{8,9},{9,8},{10,11... | collective-permute-start | bytes 221192 | tf_op jit(solution)/shard_map/out/ppermute | solution.py:664
  125.7 9.6 %collective-permute-start.27 = (bf16[288,128]{1,0:T(8,128)(2,1)S(1)}, bf16[288,128]{1,0:T(8,128)(2,1)S(1)}, u32[]{:S(2)}, u32[]{:S(2)}) collective-permute-start(bf16[288,128]{1,0:T(8,128)(2,1)S(1)} %get-tuple-element.174), channel_id=1, source_target_pairs={{0,2},{1,3},{2,0},{3,1},{4,6},{5,7},{6,4},{7,5},{8,10},{9,11},{10,... | collective-permute-start | bytes 221192 | tf_op jit(solution)/shard_map/out/ppermute | solution.py:664
  127.8 7.5 %collective-permute-start.28 = (bf16[288,128]{1,0:T(8,128)(2,1)S(1)}, bf16[288,128]{1,0:T(8,128)(2,1)S(1)}, u32[]{:S(2)}, u32[]{:S(2)}) collective-permute-start(bf16[288,128]{1,0:T(8,128)(2,1)S(1)} %get-tuple-element.175), channel_id=1, source_target_pairs={{0,3},{1,2},{2,1},{3,0},{4,7},{5,6},{6,5},{7,4},{8,11},{9,10},{10,... | collective-permute-start | bytes 221192 | tf_op jit(solution)/shard_map/out/ppermute | solution.py:664

commit v5 on v4

--- a/solution.py
+++ b/solution.py
@@ -527,22 +527,43 @@
     return jnp.concatenate([v[:8], v[8:]], axis=1)
 
 
-def grads_second_kernel(place, a_keep, a_recv, b_keep, b_recv, sent, kept):
+def grads_second_kernel(place, a_keep, a_recv, b_keep, b_recv, s0, s1, s2, kept):
     core = place[1] & 1
-    half, n = a_keep.shape[1], kept.shape[0] // 2
-    for at, keep, recv in ((0, a_keep, a_recv), (half, b_keep, b_recv)):
-        cols = slice(at, at + half)
-        for i in range(2):
-            rows = pl.ds(pl.multiple_of(2 * i * n, 2 * n), 2 * n)
-            out = slice(i * n, (i + 1) * n)
-            halve_rows(core, keep.at[rows], recv.at[rows], sent.at[out, cols], kept.at[out, cols])
-
-
-def grads_third_kernel(place, keep, recv, a_sent, a_kept, b_sent, b_kept):
+    half, n, third = a_keep.shape[1], kept.shape[0] // 2, s0.shape[1]
+    for j, sent in enumerate((s0, s1, s2)):
+        for keep, recv, low, high in (
+            (a_keep, a_recv, j * third, min((j + 1) * third, half)),
+            (b_keep, b_recv, max(j * third, half) - half, (j + 1) * third - half),
+        ):
+            if low >= high:
+                continue
+            at = low + (half if keep is b_keep else 0)
+            from_, to = slice(low, high), slice(at - j * third, at - j * third + high - low)
+            for i in range(2):
+                rows = pl.ds(pl.multiple_of(2 * i * n, 2 * n), 2 * n)
+                out = slice(i * n, (i + 1) * n)
+                halve_rows(
+                    core, keep.at[rows, from_], recv.at[rows, from_],
+                    sent.at[out, to], kept.at[out, at : at + high - low],
+                )
+
+
+def grads_third_kernel(place, keep, r0, r1, r2, a_sent, a_kept, b_sent, b_kept):
     x, y = (place[1] >> 1) & 1, (place[1] >> 2) & 1
-    half = a_kept.shape[1]
-    halve_rows(y, keep.at[:, :half], recv.at[:, :half], a_sent, a_kept)
-    halve_rows(x, keep.at[:, half:], recv.at[:, half:], b_sent, b_kept)
+    half, third = a_kept.shape[1], r0.shape[1]
+    for j, recv in enumerate((r0, r1, r2)):
+        low, high = j * third, (j + 1) * third
+        for bit, sent, kept, first, start, stop in (
+            (y, a_sent, a_kept, 0, low, min(high, half)),
+            (x, b_sent, b_kept, half, max(low, half), high),
+        ):
+            if start >= stop:
+                continue
+            out = slice(start - first, stop - first)
+            halve_rows(
+                bit, keep.at[:, start:stop], recv.at[:, start - low : stop - low],
+                sent.at[:, out], kept.at[:, out],
+            )
 
 
 def halve_rows(bit, keep, recv, sent, kept):
@@ -571,20 +592,12 @@
     put_vec(vec_o[...], sent)
 
 
-def last_kernel(
-    place, vec, a_keep, a_recv, b_keep, b_recv, q_keep, q_recv,
-    up_o, down_o, qkv_o, vec_o, o0, o1, o2, o3, turned,
-):
+def message_kernel(place, vec, b_keep, b_recv, q_recv, vec_o, o0, o1, o2, o3, turned):
     m = place[0]
-    hidden = up_o.shape[1]
     channels = o0.shape[0]
-    a = a_keep[...] + a_recv[...].astype(F32)
-    b = b_keep[...] + b_recv[...].astype(F32)
-    share, half = a.shape
-    up_o[...] = a[:, :hidden]
-    down_o[:, : half - hidden] = a[:, hidden:]
-    down_o[:, half - hidden :] = b[:, : 2 * hidden - half]
-    turned[...] = b[:, 2 * hidden - half :].T
+    width, share = turned.shape
+    cols = slice(b_keep.shape[1] - width, b_keep.shape[1])
+    turned[...] = (b_keep[:, cols] + b_recv[:, cols].astype(F32)).T
     v = vec[...] + get_vec(q_recv, vec.shape[1])
     vec_o[...] = v
     tiles = v.shape[1] // 128
@@ -598,6 +611,17 @@
             for i in range(tiles):
                 at = channels + 16 * i
                 ref[at : at + 16, :] = both[:, 128 * i : 128 * (i + 1)]
+
+
+def last_kernel(a_keep, a_recv, b_keep, b_recv, q_keep, q_recv, up_o, down_o, qkv_o):
+    hidden = up_o.shape[1]
+    channels = qkv_o.shape[2]
+    a = a_keep[...] + a_recv[...].astype(F32)
+    share, half = a.shape
+    rest = slice(0, 2 * hidden - half)
+    up_o[...] = a[:, :hidden]
+    down_o[:, : half - hidden] = a[:, hidden:]
+    down_o[:, half - hidden :] = b_keep[:, rest] + b_recv[:, rest].astype(F32)
     q = q_keep[...] + q_recv[0:share, :].astype(F32)
     for i in range(3):
         qkv_o[i] = q[:, i * channels : (i + 1) * channels]
@@ -675,8 +699,9 @@
 
     piece = channels // 4
     sent = jnp.concatenate([tokens, lax.dynamic_slice_in_dim(w_out, (d & 3) * piece, piece, 0)])
-    x = [sent] + [swap(sent, k, name="x") for k in (1, 2, 3)]
-    dy1 = swap(cotangent, 1, name="dy")
+    x1, x2 = swap(sent, 1, name="x"), swap(sent, 2, name="x")
+    x = [sent, x1, x2, swap(after(x2, x1), 1, name="x")]
+    dy2 = swap(after(cotangent, x1, x2), 2, name="dy")
     wq_t, w_up_t, w_down_t = call(
         turn_kernel,
         [like((width, 3 * channels), BF16), like((hidden, width), BF16), like((width, hidden), BF16)],
@@ -685,8 +710,7 @@
     x[1:] = lax.optimization_barrier((x[1:], wq_t))[0]
     (part,) = call(pieces_kernel, [like((4, piece, width), BF16)], x)
     part_x = swap(part, 2, "dp", name="w")
-    dy2 = swap(after(cotangent, *x[1:]), 2, name="dy")
-    wq_now = after(wq, wq_t, w_up_t, w_down_t, dy1)
+    wq_now = after(wq, wq_t, w_up_t, w_down_t, dy2)
     xt, h1, stat, qkv, pt, att = call(
         head_kernel,
         [
@@ -706,10 +730,11 @@
         ],
         us=10,
     )
-    (parts,) = call(pair_kernel, [like((8, piece, width), BF16)], [part, after(part_x, att, dy2)])
+    (parts,) = call(pair_kernel, [like((8, piece, width), BF16)], [part, after(part_x, att)])
     att_sent = after(att, parts)
+    dy1 = swap(after(cotangent, parts), 1, name="dy")
     atts = [att] + [swap(att_sent, k, name="att") for k in (1, 2, 3)]
-    dy = [cotangent, dy1, dy2, swap(after(dy2, *atts[1:]), 1, name="dy")]
+    dy = [cotangent, dy1, dy2, swap(after(dy2, parts), 1, name="dy")]
     w_pieces = [parts, swap(parts, 1, "dp", name="w")]
     w_out_full, w_out_t = call(
         out_weight_kernel, [like((width, width), BF16)] * 2, [place] + w_pieces, n_smem=1
@@ -724,7 +749,7 @@
         [act_like, wide_like, wide_like, like((8, group), F32), act_like, hid_like]
         + [like((hidden, group), F32), block, wide_like]
         + blocks,
-        [place] + atts + [xt, cols, w_out_t, w_up_t, w_down_t],
+        [place] + atts + [after(xt, dy1), cols, w_out_t, w_up_t, w_down_t],
         n_smem=1,
         scratch=[pltpu.VMEM((hidden, group), F32)],
         us=10,
@@ -807,13 +832,6 @@
 
     if fast:
         q_recv = swap(after(qkv_grads[0], mlp[1]), 1, "dp", name="qkv_core")
-        g_sent, g_kept = call(
-            grads_second_kernel,
-            [like((2 * share, grad_cols), BF16)] * 2,
-            [place, after(a_kept, q_recv), a_recv, b_kept, b_recv],
-            n_smem=1,
-        )
-        g_recv = swap(g_sent, 1, "dp", name="grads_core")
         vec_like = [like(vec.shape, F32)]
         sent, kept, vec = call(
             qkv_second_kernel,
@@ -822,10 +840,17 @@
             n_smem=1,
         )
         recv = swap(sent, 2, "dp", name="qkv_x")
+        g0, g1, g2, g_kept = call(
+            grads_second_kernel,
+            [like((2 * share, grad_cols // 3), BF16)] * 3 + [like((2 * share, grad_cols), BF16)],
+            [place, after(a_kept, vec), a_recv, b_kept, b_recv],
+            n_smem=1,
+        )
+        g_recv = [swap(g, 1, "dp", name="grads_core") for g in (g0, g1, g2)]
         a_sent, a_kept, b_sent, b_kept = call(
             grads_third_kernel,
             [like((share, half), BF16), like((share, half), F32)] * 2,
-            [place, g_kept, g_recv],
+            [place, g_kept] + g_recv,
             n_smem=1,
         )
         a_recv = swap(a_sent, 4, "dp", name="grads_a")
@@ -838,15 +863,17 @@
         )
         recv = swap(sent, 4, "dp", name="qkv_y")
         message = like((channels + 2 * vec.size // 128, 128), BF16)
-        grad_up, grad_down, grad_qkv, vec, o0, o1, o2, o3 = call(
-            last_kernel,
-            [like((share, hidden), F32)] * 2
-            + [like((3, share, channels), F32), like(vec.shape, F32)]
-            + [like((channels, share), F32)]
-            + [message] * 3,
-            [place, vec, a_kept, a_recv, b_kept, b_recv, kept, recv],
+        vec, o0, o1, o2, o3 = call(
+            message_kernel,
+            vec_like + [like((channels, share), F32)] + [message] * 3,
+            [place, vec, b_kept, b_recv, recv],
             n_smem=1,
             scratch=[pltpu.VMEM((width, share), F32)],
+        )
+        grad_up, grad_down, grad_qkv = call(
+            last_kernel,
+            [like((share, hidden), F32)] * 2 + [like((3, share, channels), F32)],
+            [a_kept, a_recv, b_kept, b_recv, after(kept, o1), recv],
         )
         o1, o2, o3 = (swap(v, k, name="out") for k, v in ((1, o1), (2, o2), (3, o3)))
         grad_out, gains, biases, scales, grad_table = call(
@@ -879,7 +906,7 @@
         grad_table = vec[6, : heads * mp * buckets].reshape(heads * mp, buckets)
 
     (output,) = call(output_kernel, [like((rows, width), BF16)], mlp + [mid, cols])
-    (grad_input,) = call(input_kernel, [like((rows, width), BF16)], back + [cotangent])
+    (grad_input,) = call(input_kernel, [like((rows, width), BF16)], back + [cotangent], us=10)
     return (
         output,
         grad_input,

time: 136 us -> 133 us (0.978)
  waiting for transfers between devices: 56.5 us -> 54.4 us
  starting transfers between devices: 38.9 us -> 37.1 us
    ppermute x29 -> x31, waiting for transfers between devices: 56.5 us -> 54.4 us  [swap(): return lax.ppermute(v, axis, [(i, i ^ k) for i in range(n)])]
    ppermute x29 -> x31, starting transfers between devices: 38.9 us -> 37.1 us  [swap(): return lax.ppermute(v, axis, [(i, i ^ k) for i in range(n)])]
    pallas_call x20 -> x21, Pallas kernels: 32.8 us -> 32.9 us  [call(): pl.pallas_call(kernel, out_shape=tuple(outs), in_specs=[SMEM] * n_smem +...]
  transfers between devices with their start and end apart: 29 -> 31, of which waited for: 15 -> 19; matrix products, arithmetic and copies ran while one was open for 2% -> 2% of each run, Pallas kernels for 23% -> 24%
where the time goes in v5:
time: 133 us; the launch traced here: 132 us
  waiting for transfers between devices  54.4 us (41%)
  starting transfers between devices  37.1 us (28%)
  Pallas kernels  32.9 us (25%)
  local copies, waits for them, and re-layouts  5.87 us (4%)
    ppermute x31, waiting for transfers between devices, swap(): return lax.ppermute(v, axis, [(i, i ^ k) for i in range(n)])  54.4 us
    ppermute x31, starting transfers between devices, swap(): return lax.ppermute(v, axis, [(i, i ^ k) for i in range(n)])  37.1 us
    pallas_call x21, Pallas kernels, call(): pl.pallas_call(kernel, out_shape=tuple(outs), in_specs=[SMEM] * n_smem +...  32.9 us
    unnamed x17, local copies, waits for them, and re-layouts  4.17 us
  transfers between devices with their start and end apart: 31, of which 19 were waited for; matrix products, arithmetic and copies ran while one was open for 2% of the time, Pallas kernels for 24%

profile of v5, /device:TPU:0, one launch (start us, length us, event | category | flops | bytes accessed | tf_op | source)
XLA Modules:
  0.0 132.2 jit_solution(4970012636556145935)
XLA Ops:
  0.7 0.9 copy-done
  1.6 0.9 pad_maximum_fusion.x0
  2.6 4.1 %collective-permute-start.1 = (bf16[176,768]{1,0:T(8,128)(2,1)S(1)}, bf16[176,768]{1,0:T(8,128)(2,1)S(1)}, u32[]{:S(2)}, u32[]{:S(2)}) collective-permute-start(bf16[176,768]{1,0:T(8,128)(2,1)S(1)} %pad_maximum_fusion.x0), channel_id=1, source_target_pairs={{0,2},{1,3},{2,0},{3,1},{4,6},{5,7},{6,4},{7,5},{8,10},{9,11},{10,... | collective-permute-start | bytes 811016 | tf_op jit(solution)/shard_map/x/ppermute | solution.py:688
  6.7 1.6 %collective-permute-start = (bf16[176,768]{1,0:T(8,128)(2,1)S(1)}, bf16[176,768]{1,0:T(8,128)(2,1)S(1)}, u32[]{:S(2)}, u32[]{:S(2)}) collective-permute-start(bf16[176,768]{1,0:T(8,128)(2,1)S(1)} %pad_maximum_fusion.x0), channel_id=1, source_target_pairs={{0,1},{1,0},{2,3},{3,2},{4,5},{5,4},{6,7},{7,6},{8,9},{9,8},{10,11... | collective-permute-start | bytes 811016 | tf_op jit(solution)/shard_map/x/ppermute | solution.py:688
  8.2 10.8 %collective-permute-done.1.x2 = bf16[176,768]{1,0:T(8,128)(2,1)S(1)} collective-permute-done((bf16[176,768]{1,0:T(8,128)(2,1)S(1)}, bf16[176,768]{1,0:T(8,128)(2,1)S(1)}, u32[]{:S(2)}, u32[]{:S(2)}) %collective-permute-start.1) | collective-permute-done | bytes 270368 | tf_op jit(solution)/shard_map/x/ppermute | solution.py:688
  19.2 1.4 %collective-permute-start.3 = (bf16[128,768]{1,0:T(8,128)(2,1)}, bf16[128,768]{1,0:T(8,128)(2,1)S(1)}, u32[]{:S(2)}, u32[]{:S(2)}) collective-permute-start(bf16[128,768]{1,0:T(8,128)(2,1)} %dy.1), channel_id=1, source_target_pairs={{0,2},{1,3},{2,0},{3,1},{4,6},{5,7},{6,4},{7,5},{8,10},{9,11},{10,... | collective-permute-start | bytes 589832 | tf_op jit(solution)/shard_map/dy/ppermute | solution.py:688
  20.6 2.4 %collective-permute-start.2 = (bf16[176,768]{1,0:T(8,128)(2,1)S(1)}, bf16[176,768]{1,0:T(8,128)(2,1)S(1)}, u32[]{:S(2)}, u32[]{:S(2)}) collective-permute-start(bf16[176,768]{1,0:T(8,128)(2,1)S(1)} %collective-permute-done.1.x2), channel_id=1, source_target_pairs={{0,1},{1,0},{2,3},{3,2},{4,5},{5,4},{6,7},{7,6},{8,9},{9,8},{10,11... | collective-permute-start | bytes 811016 | tf_op jit(solution)/shard_map/x/ppermute | solution.py:688
  23.0 0.8 fusion
  23.8 0.8 copy.28.table
  24.6 0.7 concatenate.7
  25.5 1.3 copy-done.2
  26.8 1.2 copy-done.4
  28.0 0.9 turn_kernel.1
  29.0 1.5 %collective-permute-done.3.c2 = bf16[128,768]{1,0:T(8,128)(2,1)S(1)} collective-permute-done((bf16[128,768]{1,0:T(8,128)(2,1)}, bf16[128,768]{1,0:T(8,128)(2,1)S(1)}, u32[]{:S(2)}, u32[]{:S(2)}) %collective-permute-start.3) | collective-permute-done | bytes 196640 | tf_op jit(solution)/shard_map/dy/ppermute | solution.py:688
  30.5 1.5 %collective-permute-done.2.x3 = bf16[176,768]{1,0:T(8,128)(2,1)S(1)} collective-permute-done((bf16[176,768]{1,0:T(8,128)(2,1)S(1)}, bf16[176,768]{1,0:T(8,128)(2,1)S(1)}, u32[]{:S(2)}, u32[]{:S(2)}) %collective-permute-start.2) | collective-permute-done | bytes 270368 | tf_op jit(solution)/shard_map/x/ppermute | solution.py:688
  32.0 1.3 collective-permute-start.4
  33.3 4.7 %head_kernel.1 = (bf16[768,512]{1,0:T(8,128)(2,1)S(1)}, bf16[768,512]{1,0:T(8,128)(2,1)S(1)}, f32[8,512]{1,0:T(8,128)S(1)}, bf16[576,512]{1,0:T(8,128)(2,1)S(1)}...) custom-call(s32[2]{0:T(128)S(1)} %pad_add_fusion.place, s32[1,8]{1,0:T(1,128)S(1)} %copy-done.7, ...), custom_call_target="tpu_custom_call" | custom-call | flops 11500000256 | bytes 8 | tf_op jit(solution)/shard_map/head_kernel/pallas_call | solution.py:21
  38.1 2.1 %collective-permute-done.4.b = bf16[4,48,768]{2,1,0:T(8,128)(2,1)S(1)} collective-permute-done((bf16[4,48,768]{2,1,0:T(8,128)(2,1)S(1)}, bf16[4,48,768]{2,1,0:T(8,128)(2,1)S(1)}, u32[]{:S(2)}, u32[]{:S(2)}) %collective-permute-start.4) | collective-permute-done | bytes 294944 | tf_op jit(solution)/shard_map/w/ppermute | solution.py:688
  40.5 3.2 %collective-permute-start.7 = (bf16[192,512]{1,0:T(8,128)(2,1)S(1)}, bf16[192,512]{1,0:T(8,128)(2,1)S(1)}, u32[]{:S(2)}, u32[]{:S(2)}) collective-permute-start(bf16[192,512]{1,0:T(8,128)(2,1)S(1)} %get-tuple-element.114.a0), channel_id=1, source_target_pairs={{0,3},{1,2},{2,1},{3,0},{4,7},{5,6},{6,5},{7,4},{8,11},{9,10},{10,... | collective-permute-start | bytes 589832 | tf_op jit(solution)/shard_map/att/ppermute | solution.py:688
  43.7 0.2 collective-permute-start.6
  43.9 1.0 collective-permute-start.5
  44.9 3.3 %collective-permute-done.8.c1 = bf16[128,768]{1,0:T(8,128)(2,1)S(1)} collective-permute-done((bf16[128,768]{1,0:T(8,128)(2,1)S(1)}, bf16[128,768]{1,0:T(8,128)(2,1)S(1)}, u32[]{:S(2)}, u32[]{:S(2)}) %collective-permute-start.8) | collective-permute-done | bytes 196640 | tf_op jit(solution)/shard_map/dy/ppermute | solution.py:688
  48.3 1.0 out_weight_kernel.1
  49.2 4.5 %collective-permute-done.7.a3 = bf16[192,512]{1,0:T(8,128)(2,1)S(1)} collective-permute-done((bf16[192,512]{1,0:T(8,128)(2,1)S(1)}, bf16[192,512]{1,0:T(8,128)(2,1)S(1)}, u32[]{:S(2)}, u32[]{:S(2)}) %collective-permute-start.7) | collective-permute-done | bytes 196640 | tf_op jit(solution)/shard_map/att/ppermute | solution.py:688
  53.7 7.9 %collective-permute-done.6.a2 = bf16[192,512]{1,0:T(8,128)(2,1)S(1)} collective-permute-done((bf16[192,512]{1,0:T(8,128)(2,1)S(1)}, bf16[192,512]{1,0:T(8,128)(2,1)S(1)}, u32[]{:S(2)}, u32[]{:S(2)}) %collective-permute-start.6) | collective-permute-done | bytes 196640 | tf_op jit(solution)/shard_map/att/ppermute | solution.py:688
  61.6 4.1 %up_kernel.1 = (bf16[768,512]{1,0:T(8,128)(2,1)S(1)}, f32[768,512]{1,0:T(8,128)S(1)}, f32[768,512]{1,0:T(8,128)S(1)}, f32[8,512]{1,0:T(8,128)S(1)}, bf16[768,512...) custom-call(s32[2]{0:T(128)S(1)} %pad_add_fusion.place, ...), custom_call_target="tpu_custom_call" | custom-call | flops 11500000256 | bytes 8 | tf_op jit(solution)/shard_map/up_kernel/pallas_call | solution.py:21
  65.8 4.5 %down_kernel.1 = (bf16[192,512]{1,0:T(8,128)(2,1)S(1)}, bf16[192,512]{1,0:T(8,128)(2,1)S(1)}, bf16[192,512]{1,0:T(8,128)(2,1)S(1)}, bf16[192,512]{1,0:T(8,128)(2...) custom-call(s32[2]{0:T(128)S(1)} %pad_add_fusion.place, ...), custom_call_target="tpu_custom_call" | custom-call | flops 11500000256 | bytes 8 | tf_op jit(solution)/shard_map/down_kernel/pallas_call | solution.py:21
  70.3 2.0 %collective-permute-start.12 = (bf16[192,512]{1,0:T(8,128)(2,1)S(1)}, bf16[192,512]{1,0:T(8,128)(2,1)S(1)}, u32[]{:S(2)}, u32[]{:S(2)}) collective-permute-start(bf16[192,512]{1,0:T(8,128)(2,1)S(1)} %get-tuple-element.130), channel_id=1, source_target_pairs={{0,1},{1,0},{2,3},{3,2},{4,5},{5,4},{6,7},{7,6},{8,9},{9,8},{10,11... | collective-permute-start | bytes 589832 | tf_op jit(solution)/shard_map/d_att/ppermute | solution.py:688
  72.3 1.2 collective-permute-start.13
  73.6 1.4 %collective-permute-start.14 = (bf16[192,512]{1,0:T(8,128)(2,1)S(1)}, bf16[192,512]{1,0:T(8,128)(2,1)S(1)}, u32[]{:S(2)}, u32[]{:S(2)}) collective-permute-start(bf16[192,512]{1,0:T(8,128)(2,1)S(1)} %get-tuple-element.132), channel_id=1, source_target_pairs={{0,3},{1,2},{2,1},{3,0},{4,7},{5,6},{6,5},{7,4},{8,11},{9,10},{10,... | collective-permute-start | bytes 589832 | tf_op jit(solution)/shard_map/d_att/ppermute | solution.py:688
  75.0 2.6 %mlp_grad_kernel.1 = (f32[8,768]{1,0:T(8,128)S(1)}, bf16[384,1152]{1,0:T(8,128)(2,1)S(1)}, bf16[384,1152]{1,0:T(8,128)(2,1)S(1)}, bf16[384,1152]{1,0:T(8,128)(2,1)S(1)}, bf16[384,1152]{1,0:T(8,128)(2,1)S(1)}) custom-call(s32[2]{0:T(128)S(1)} %pad_add_fusion.place, f32[8,768]{1,0:T(8,128)S(1)} %get-tuple-element.140.vec, ...), custom_call_target="tpu_custom_call" | custom-call | flops 11500000 | bytes 8 | tf_op jit(solution)/shard_map/mlp_grad_kernel/pallas_call | solution.py:21
  77.6 1.4 %collective-permute-start.19 = (bf16[384,1152]{1,0:T(8,128)(2,1)S(1)}, bf16[384,1152]{1,0:T(8,128)(2,1)S(1)}, u32[]{:S(2)}, u32[]{:S(2)}) collective-permute-start(bf16[384,1152]{1,0:T(8,128)(2,1)S(1)} %get-tuple-element.165), channel_id=1, source_target_pairs={{0,8},{4,12},{8,0},{12,4},{16,24},{20,28},{24,16},{28,20},{1,9},{5... | collective-permute-start | bytes 2654216 | tf_op jit(solution)/shard_map/grads_a/ppermute | solution.py:688
  78.9 2.9 %collective-permute-done.10.recv = bf16[1536,128]{1,0:T(8,128)(2,1)S(1)} collective-permute-done((bf16[1536,128]{1,0:T(8,128)(2,1)S(1)}, bf16[1536,128]{1,0:T(8,128)(2,1)S(1)}, u32[]{:S(2)}, u32[]{:S(2)}) %collective-permute-start.10) | collective-permute-done | bytes 393248 | tf_op jit(solution)/shard_map/mlp/ppermute | solution.py:688
  81.8 1.4 %collective-permute-start.20 = (bf16[384,1152]{1,0:T(8,128)(2,1)S(1)}, bf16[384,1152]{1,0:T(8,128)(2,1)S(1)}, u32[]{:S(2)}, u32[]{:S(2)}) collective-permute-start(bf16[384,1152]{1,0:T(8,128)(2,1)S(1)} %get-tuple-element.167), channel_id=1, source_target_pairs={{0,16},{4,20},{8,24},{12,28},{16,0},{20,4},{24,8},{28,12},{1,17},{... | collective-permute-start | bytes 2654216 | tf_op jit(solution)/shard_map/grads_b/ppermute | solution.py:688
  83.3 1.9 %collective-permute-done.12.d1 = bf16[192,512]{1,0:T(8,128)(2,1)S(1)} collective-permute-done((bf16[192,512]{1,0:T(8,128)(2,1)S(1)}, bf16[192,512]{1,0:T(8,128)(2,1)S(1)}, u32[]{:S(2)}, u32[]{:S(2)}) %collective-permute-start.12) | collective-permute-done | bytes 196640 | tf_op jit(solution)/shard_map/d_att/ppermute | solution.py:688
  85.2 4.3 %collective-permute-done.14.d3 = bf16[192,512]{1,0:T(8,128)(2,1)S(1)} collective-permute-done((bf16[192,512]{1,0:T(8,128)(2,1)S(1)}, bf16[192,512]{1,0:T(8,128)(2,1)S(1)}, u32[]{:S(2)}, u32[]{:S(2)}) %collective-permute-start.14) | collective-permute-done | bytes 196640 | tf_op jit(solution)/shard_map/d_att/ppermute | solution.py:688
  89.5 4.3 %collective-permute-start.15 = (bf16[768,128]{1,0:T(8,128)(2,1)S(1)}, bf16[768,128]{1,0:T(8,128)(2,1)S(1)}, u32[]{:S(2)}, u32[]{:S(2)}) collective-permute-start(bf16[768,128]{1,0:T(8,128)(2,1)S(1)} %get-tuple-element.133), channel_id=1, source_target_pairs={{0,2},{1,3},{2,0},{3,1},{4,6},{5,7},{6,4},{7,5},{8,10},{9,11},{10,... | collective-permute-start | bytes 589832 | tf_op jit(solution)/shard_map/mlp/ppermute | solution.py:688
  93.8 6.3 %back_kernel.1 = (f32[768,128]{1,0:T(8,128)S(1)}, f32[768,128]{1,0:T(8,128)S(1)}, bf16[1536,128]{1,0:T(8,128)(2,1)S(1)}, bf16[576,512]{1,0:T(8,128)(2,1)S(1)}, f32[8,768]{1,0:T(8,128)S(1)}) custom-call(s32[2]{0:T(128)S(1)} %pad_add_fusion.place, s32[1,8]{1,0:T(1,128)S(1)} %copy-done.7, bf16[192,512]{1,0:T(8,128)(2,1)S(1)} %get-tuple-element.135.d0, ...), custom_call_target="tpu_custom_call" | custom-call | flops 11500000256 | bytes 8 | tf_op jit(solution)/shard_map/back_kernel/pallas_call | solution.py:21
  100.1 1.4 %qkv_grad_kernel.1 = (bf16[416,576]{1,0:T(8,128)(2,1)S(1)}, bf16[384,576]{1,0:T(8,128)(2,1)S(1)}) custom-call(s32[2]{0:T(128)S(1)} %pad_add_fusion.place, bf16[768,512]{1,0:T(8,128)(2,1)S(1)} %get-tuple-element.157.h1, bf16[576,512]{1,0:T(8,128)(2,1)S(1)} %get-tuple-element.158.dqkv, f32[8,768]{1,0:T(8,128)S(1)} %get-tuple-element.156.vec), custom_call_target="tpu_custom_call" | custom-call | flops 11500000 | bytes 8 | tf_op jit(solution)/shard_map/qkv_grad_kernel/pallas_call | solution.py:21
  101.7 1.8 %collective-permute-done.18.recv = bf16[416,576]{1,0:T(8,128)(2,1)S(1)} collective-permute-done((bf16[416,576]{1,0:T(8,128)(2,1)S(1)}, bf16[416,576]{1,0:T(8,128)(2,1)S(1)}, u32[]{:S(2)}, u32[]{:S(2)}) %collective-permute-start.18) | collective-permute-done | bytes 479264 | tf_op jit(solution)/shard_map/qkv_core/ppermute | solution.py:688
  103.5 0.7 qkv_second_kernel.1
  104.2 1.0 grads_second_kernel.1
  105.2 0.2 collective-permute-start.21
  105.4 0.4 collective-permute-start.22
  105.9 1.6 %collective-permute-start.24 = (bf16[224,576]{1,0:T(8,128)(2,1)S(1)}, bf16[224,576]{1,0:T(8,128)(2,1)S(1)}, u32[]{:S(2)}, u32[]{:S(2)}) collective-permute-start(bf16[224,576]{1,0:T(8,128)(2,1)S(1)} %get-tuple-element.175), channel_id=1, source_target_pairs={{0,8},{4,12},{8,0},{12,4},{16,24},{20,28},{24,16},{28,20},{1,9},{5... | collective-permute-start | bytes 774152 | tf_op jit(solution)/shard_map/qkv_x/ppermute | solution.py:688
  107.7 0.7 grads_third_kernel.1
  108.5 1.6 %collective-permute-start.25 = (bf16[96,1152]{1,0:T(8,128)(2,1)S(1)}, bf16[96,1152]{1,0:T(8,128)(2,1)S(1)}, u32[]{:S(2)}, u32[]{:S(2)}) collective-permute-start(bf16[96,1152]{1,0:T(8,128)(2,1)S(1)} %get-tuple-element.178), channel_id=1, source_target_pairs={{0,8},{4,12},{8,0},{12,4},{16,24},{20,28},{24,16},{28,20},{1,9},{5... | collective-permute-start | bytes 663560 | tf_op jit(solution)/shard_map/grads_b/ppermute | solution.py:688
  110.1 3.0 %collective-permute-done.16.recv = bf16[1536,128]{1,0:T(8,128)(2,1)S(1)} collective-permute-done((bf16[1536,128]{1,0:T(8,128)(2,1)S(1)}, bf16[1536,128]{1,0:T(8,128)(2,1)S(1)}, u32[]{:S(2)}, u32[]{:S(2)}) %collective-permute-start.16) | collective-permute-done | bytes 393248 | tf_op jit(solution)/shard_map/back/ppermute | solution.py:688
  113.3 2.3 %collective-permute-done.24.recv = bf16[224,576]{1,0:T(8,128)(2,1)S(1)} collective-permute-done((bf16[224,576]{1,0:T(8,128)(2,1)S(1)}, bf16[224,576]{1,0:T(8,128)(2,1)S(1)}, u32[]{:S(2)}, u32[]{:S(2)}) %collective-permute-start.24) | collective-permute-done | bytes 258080 | tf_op jit(solution)/shard_map/qkv_x/ppermute | solution.py:688
  115.6 0.6 qkv_third_kernel.1
  116.2 1.7 %collective-permute-start.26 = (bf16[128,576]{1,0:T(8,128)(2,1)S(1)}, bf16[128,576]{1,0:T(8,128)(2,1)S(1)}, u32[]{:S(2)}, u32[]{:S(2)}) collective-permute-start(bf16[128,576]{1,0:T(8,128)(2,1)S(1)} %get-tuple-element.179), channel_id=1, source_target_pairs={{0,16},{4,20},{8,24},{12,28},{16,0},{20,4},{24,8},{28,12},{1,17},{... | collective-permute-start | bytes 442376 | tf_op jit(solution)/shard_map/qkv_y/ppermute | solution.py:688
  117.9 0.9 output_kernel.1
  118.8 0.4 collective-permute-start.30
  119.2 3.8 %collective-permute-done.26.q_recv = bf16[128,576]{1,0:T(8,128)(2,1)S(1)} collective-permute-done((bf16[128,576]{1,0:T(8,128)(2,1)S(1)}, bf16[128,576]{1,0:T(8,128)(2,1)S(1)}, u32[]{:S(2)}, u32[]{:S(2)}) %collective-permute-start.26) | collective-permute-done | bytes 147488 | tf_op jit(solution)/shard_map/qkv_y/ppermute | solution.py:688
  123.0 0.7 message_kernel.1
  123.8 0.7 collective-permute-start.28
  124.5 2.0 %collective-permute-start.29 = (bf16[288,128]{1,0:T(8,128)(2,1)S(1)}, bf16[288,128]{1,0:T(8,128)(2,1)S(1)}, u32[]{:S(2)}, u32[]{:S(2)}) collective-permute-start(bf16[288,128]{1,0:T(8,128)(2,1)S(1)} %get-tuple-element.184), channel_id=1, source_target_pairs={{0,3},{1,2},{2,1},{3,0},{4,7},{5,6},{6,5},{7,4},{8,11},{9,10},{10,... | collective-permute-start | bytes 221192 | tf_op jit(solution)/shard_map/out/ppermute | solution.py:688
  126.5 0.9 collective-permute-start.27
  127.4 0.9 input_kernel.1
  128.2 1.0 last_kernel.1
  129.2 0.4 collective-permute-done.28.o2
  129.6 1.2 collective-permute-done.29.o3
  130.8 0.7 collective-permute-done.27.o1
  131.5 0.7 small_kernel.1
  (42 shorter events, 1.7 us)
Async XLA Ops:
  0.6 1.0 copy-start
  0.7 24.9 %copy-start.1 = (bf16[768,768]{1,0:T(8,128)(2,1)S(1)}, bf16[768,768]{1,0:T(8,128)(2,1)}, u32[]{:S(2)}) copy-start(bf16[768,768]{1,0:T(8,128)(2,1)} %w_up.1) | copy-start | bytes 3538948
  2.6 16.5 %collective-permute-start.1 = (bf16[176,768]{1,0:T(8,128)(2,1)S(1)}, bf16[176,768]{1,0:T(8,128)(2,1)S(1)}, u32[]{:S(2)}, u32[]{:S(2)}) collective-permute-start(bf16[176,768]{1,0:T(8,128)(2,1)S(1)} %pad_maximum_fusion.x0), channel_id=1, source_target_pairs={{0,2},{1,3},{2,0},{3,1},{4,6},{5,7},{6,4},{7,5},{8,10},{9,11},{10,... | collective-permute-start | bytes 811016 | tf_op jit(solution)/shard_map/x/ppermute | solution.py:688
  6.7 12.6 %collective-permute-start = (bf16[176,768]{1,0:T(8,128)(2,1)S(1)}, bf16[176,768]{1,0:T(8,128)(2,1)S(1)}, u32[]{:S(2)}, u32[]{:S(2)}) collective-permute-start(bf16[176,768]{1,0:T(8,128)(2,1)S(1)} %pad_maximum_fusion.x0), channel_id=1, source_target_pairs={{0,1},{1,0},{2,3},{3,2},{4,5},{5,4},{6,7},{7,6},{8,9},{9,8},{10,11... | collective-permute-start | bytes 811016 | tf_op jit(solution)/shard_map/x/ppermute | solution.py:688
  19.2 11.3 %collective-permute-start.3 = (bf16[128,768]{1,0:T(8,128)(2,1)}, bf16[128,768]{1,0:T(8,128)(2,1)S(1)}, u32[]{:S(2)}, u32[]{:S(2)}) collective-permute-start(bf16[128,768]{1,0:T(8,128)(2,1)} %dy.1), channel_id=1, source_target_pairs={{0,2},{1,3},{2,0},{3,1},{4,6},{5,7},{6,4},{7,5},{8,10},{9,11},{10,... | collective-permute-start | bytes 589832 | tf_op jit(solution)/shard_map/dy/ppermute | solution.py:688
  20.6 11.4 %collective-permute-start.2 = (bf16[176,768]{1,0:T(8,128)(2,1)S(1)}, bf16[176,768]{1,0:T(8,128)(2,1)S(1)}, u32[]{:S(2)}, u32[]{:S(2)}) collective-permute-start(bf16[176,768]{1,0:T(8,128)(2,1)S(1)} %collective-permute-done.1.x2), channel_id=1, source_target_pairs={{0,1},{1,0},{2,3},{3,2},{4,5},{5,4},{6,7},{7,6},{8,9},{9,8},{10,11... | collective-permute-start | bytes 811016 | tf_op jit(solution)/shard_map/x/ppermute | solution.py:688
  25.5 1.3 copy-start.2
  26.8 1.2 copy-start.4
  28.0 5.3 %copy-start.5 = (bf16[768,3,192]{0,2,1:T(8,128)(2,1)S(1)}, bf16[768,3,192]{0,2,1:T(8,128)(2,1)}, u32[]{:S(2)}) copy-start(bf16[768,3,192]{0,2,1:T(8,128)(2,1)} %param.16) | copy-start | bytes 2654212
  28.0 5.4 %copy-start.7 = (s32[1,8]{1,0:T(1,128)S(1)}, s32[1,8]{1,0:T(1,128)}, u32[]{:S(2)}) copy-start(s32[1,8]{1,0:T(1,128)} %lengths.3) | copy-start | bytes 100
  32.0 8.2 %collective-permute-start.4 = (bf16[4,48,768]{2,1,0:T(8,128)(2,1)S(1)}, bf16[4,48,768]{2,1,0:T(8,128)(2,1)S(1)}, u32[]{:S(2)}, u32[]{:S(2)}) collective-permute-start(bf16[4,48,768]{2,1,0:T(8,128)(2,1)S(1)} %pieces_kernel.1.a), channel_id=1, source_target_pairs={{0,8},{4,12},{8,0},{12,4},{16,24},{20,28},{24,16},{28,20},{1,9},{5... | collective-permute-start | bytes 884744 | tf_op jit(solution)/shard_map/w/ppermute | solution.py:688
  33.3 7.0 %copy-start.6 = (bf16[128,768]{1,0:T(8,128)(2,1)S(1)}, bf16[128,768]{1,0:T(8,128)(2,1)}, u32[]{:S(2)}) copy-start(bf16[128,768]{1,0:T(8,128)(2,1)} %dy.1) | copy-start | bytes 589828
  40.2 8.0 %collective-permute-start.9 = (bf16[8,48,768]{2,1,0:T(8,128)(2,1)S(1)}, bf16[8,48,768]{2,1,0:T(8,128)(2,1)S(1)}, u32[]{:S(2)}, u32[]{:S(2)}) collective-permute-start(bf16[8,48,768]{2,1,0:T(8,128)(2,1)S(1)} %pair_kernel.1.here), channel_id=1, source_target_pairs={{0,4},{4,0},{8,12},{12,8},{16,20},{20,16},{24,28},{28,24},{1,5},{5... | collective-permute-start | bytes 1769480 | tf_op jit(solution)/shard_map/w/ppermute | solution.py:688
  40.3 7.8 %collective-permute-start.8 = (bf16[128,768]{1,0:T(8,128)(2,1)S(1)}, bf16[128,768]{1,0:T(8,128)(2,1)S(1)}, u32[]{:S(2)}, u32[]{:S(2)}) collective-permute-start(bf16[128,768]{1,0:T(8,128)(2,1)S(1)} %copy-done.6), channel_id=1, source_target_pairs={{0,1},{1,0},{2,3},{3,2},{4,5},{5,4},{6,7},{7,6},{8,9},{9,8},{10,11... | collective-permute-start | bytes 589832 | tf_op jit(solution)/shard_map/dy/ppermute | solution.py:688
  40.5 13.2 %collective-permute-start.7 = (bf16[192,512]{1,0:T(8,128)(2,1)S(1)}, bf16[192,512]{1,0:T(8,128)(2,1)S(1)}, u32[]{:S(2)}, u32[]{:S(2)}) collective-permute-start(bf16[192,512]{1,0:T(8,128)(2,1)S(1)} %get-tuple-element.114.a0), channel_id=1, source_target_pairs={{0,3},{1,2},{2,1},{3,0},{4,7},{5,6},{6,5},{7,4},{8,11},{9,10},{10,... | collective-permute-start | bytes 589832 | tf_op jit(solution)/shard_map/att/ppermute | solution.py:688
  43.7 17.9 %collective-permute-start.6 = (bf16[192,512]{1,0:T(8,128)(2,1)S(1)}, bf16[192,512]{1,0:T(8,128)(2,1)S(1)}, u32[]{:S(2)}, u32[]{:S(2)}) collective-permute-start(bf16[192,512]{1,0:T(8,128)(2,1)S(1)} %get-tuple-element.114.a0), channel_id=1, source_target_pairs={{0,2},{1,3},{2,0},{3,1},{4,6},{5,7},{6,4},{7,5},{8,10},{9,11},{10,... | collective-permute-start | bytes 589832 | tf_op jit(solution)/shard_map/att/ppermute | solution.py:688
  43.9 17.7 %collective-permute-start.5 = (bf16[192,512]{1,0:T(8,128)(2,1)S(1)}, bf16[192,512]{1,0:T(8,128)(2,1)S(1)}, u32[]{:S(2)}, u32[]{:S(2)}) collective-permute-start(bf16[192,512]{1,0:T(8,128)(2,1)S(1)} %get-tuple-element.114.a0), channel_id=1, source_target_pairs={{0,1},{1,0},{2,3},{3,2},{4,5},{5,4},{6,7},{7,6},{8,9},{9,8},{10,11... | collective-permute-start | bytes 589832 | tf_op jit(solution)/shard_map/att/ppermute | solution.py:688
  48.2 17.6 %collective-permute-start.11 = (bf16[128,768]{1,0:T(8,128)(2,1)S(1)}, bf16[128,768]{1,0:T(8,128)(2,1)S(1)}, u32[]{:S(2)}, u32[]{:S(2)}) collective-permute-start(bf16[128,768]{1,0:T(8,128)(2,1)S(1)} %collective-permute-done.3.c2), channel_id=1, source_target_pairs={{0,1},{1,0},{2,3},{3,2},{4,5},{5,4},{6,7},{7,6},{8,9},{9,8},{10,11... | collective-permute-start | bytes 589832 | tf_op jit(solution)/shard_map/dy/ppermute | solution.py:688
  61.6 4.2 %copy-start.3 = (bf16[768,768]{1,0:T(8,128)(2,1)S(1)}, bf16[768,768]{1,0:T(8,128)(2,1)}, u32[]{:S(2)}) copy-start(bf16[768,768]{1,0:T(8,128)(2,1)} %w_down.1) | copy-start | bytes 3538948
  65.7 16.1 %collective-permute-start.10 = (bf16[1536,128]{1,0:T(8,128)(2,1)S(1)}, bf16[1536,128]{1,0:T(8,128)(2,1)S(1)}, u32[]{:S(2)}, u32[]{:S(2)}) collective-permute-start(bf16[1536,128]{1,0:T(8,128)(2,1)S(1)} %get-tuple-element.121), channel_id=1, source_target_pairs={{0,1},{1,0},{2,3},{3,2},{4,5},{5,4},{6,7},{7,6},{8,9},{9,8},{10,11... | collective-permute-start | bytes 1179656 | tf_op jit(solution)/shard_map/mlp/ppermute | solution.py:688
  70.3 14.9 %collective-permute-start.12 = (bf16[192,512]{1,0:T(8,128)(2,1)S(1)}, bf16[192,512]{1,0:T(8,128)(2,1)S(1)}, u32[]{:S(2)}, u32[]{:S(2)}) collective-permute-start(bf16[192,512]{1,0:T(8,128)(2,1)S(1)} %get-tuple-element.130), channel_id=1, source_target_pairs={{0,1},{1,0},{2,3},{3,2},{4,5},{5,4},{6,7},{7,6},{8,9},{9,8},{10,11... | collective-permute-start | bytes 589832 | tf_op jit(solution)/shard_map/d_att/ppermute | solution.py:688
  72.3 12.9 %collective-permute-start.13 = (bf16[192,512]{1,0:T(8,128)(2,1)S(1)}, bf16[192,512]{1,0:T(8,128)(2,1)S(1)}, u32[]{:S(2)}, u32[]{:S(2)}) collective-permute-start(bf16[192,512]{1,0:T(8,128)(2,1)S(1)} %get-tuple-element.131), channel_id=1, source_target_pairs={{0,2},{1,3},{2,0},{3,1},{4,6},{5,7},{6,4},{7,5},{8,10},{9,11},{10,... | collective-permute-start | bytes 589832 | tf_op jit(solution)/shard_map/d_att/ppermute | solution.py:688
  73.6 15.9 %collective-permute-start.14 = (bf16[192,512]{1,0:T(8,128)(2,1)S(1)}, bf16[192,512]{1,0:T(8,128)(2,1)S(1)}, u32[]{:S(2)}, u32[]{:S(2)}) collective-permute-start(bf16[192,512]{1,0:T(8,128)(2,1)S(1)} %get-tuple-element.132), channel_id=1, source_target_pairs={{0,3},{1,2},{2,1},{3,0},{4,7},{5,6},{6,5},{7,4},{8,11},{9,10},{10,... | collective-permute-start | bytes 589832 | tf_op jit(solution)/shard_map/d_att/ppermute | solution.py:688
  77.6 26.6 %collective-permute-start.19 = (bf16[384,1152]{1,0:T(8,128)(2,1)S(1)}, bf16[384,1152]{1,0:T(8,128)(2,1)S(1)}, u32[]{:S(2)}, u32[]{:S(2)}) collective-permute-start(bf16[384,1152]{1,0:T(8,128)(2,1)S(1)} %get-tuple-element.165), channel_id=1, source_target_pairs={{0,8},{4,12},{8,0},{12,4},{16,24},{20,28},{24,16},{28,20},{1,9},{5... | collective-permute-start | bytes 2654216 | tf_op jit(solution)/shard_map/grads_a/ppermute | solution.py:688
  81.8 22.4 %collective-permute-start.20 = (bf16[384,1152]{1,0:T(8,128)(2,1)S(1)}, bf16[384,1152]{1,0:T(8,128)(2,1)S(1)}, u32[]{:S(2)}, u32[]{:S(2)}) collective-permute-start(bf16[384,1152]{1,0:T(8,128)(2,1)S(1)} %get-tuple-element.167), channel_id=1, source_target_pairs={{0,16},{4,20},{8,24},{12,28},{16,0},{20,4},{24,8},{28,12},{1,17},{... | collective-permute-start | bytes 2654216 | tf_op jit(solution)/shard_map/grads_b/ppermute | solution.py:688
  89.5 12.0 %collective-permute-start.15 = (bf16[768,128]{1,0:T(8,128)(2,1)S(1)}, bf16[768,128]{1,0:T(8,128)(2,1)S(1)}, u32[]{:S(2)}, u32[]{:S(2)}) collective-permute-start(bf16[768,128]{1,0:T(8,128)(2,1)S(1)} %get-tuple-element.133), channel_id=1, source_target_pairs={{0,2},{1,3},{2,0},{3,1},{4,6},{5,7},{6,4},{7,5},{8,10},{9,11},{10,... | collective-permute-start | bytes 589832 | tf_op jit(solution)/shard_map/mlp/ppermute | solution.py:688
  101.5 2.0 %collective-permute-start.18 = (bf16[416,576]{1,0:T(8,128)(2,1)S(1)}, bf16[416,576]{1,0:T(8,128)(2,1)S(1)}, u32[]{:S(2)}, u32[]{:S(2)}) collective-permute-start(bf16[416,576]{1,0:T(8,128)(2,1)S(1)} %get-tuple-element.161), channel_id=1, source_target_pairs={{0,4},{4,0},{8,12},{12,8},{16,20},{20,16},{24,28},{28,24},{1,5},{5... | collective-permute-start | bytes 1437704 | tf_op jit(solution)/shard_map/qkv_core/ppermute | solution.py:688
  101.6 11.5 %collective-permute-start.16 = (bf16[1536,128]{1,0:T(8,128)(2,1)S(1)}, bf16[1536,128]{1,0:T(8,128)(2,1)S(1)}, u32[]{:S(2)}, u32[]{:S(2)}) collective-permute-start(bf16[1536,128]{1,0:T(8,128)(2,1)S(1)} %get-tuple-element.153), channel_id=1, source_target_pairs={{0,1},{1,0},{2,3},{3,2},{4,5},{5,4},{6,7},{7,6},{8,9},{9,8},{10,11... | collective-permute-start | bytes 1179656 | tf_op jit(solution)/shard_map/back/ppermute | solution.py:688
  105.2 2.3 %collective-permute-start.21 = (bf16[192,768]{1,0:T(8,128)(2,1)S(1)}, bf16[192,768]{1,0:T(8,128)(2,1)S(1)}, u32[]{:S(2)}, u32[]{:S(2)}) collective-permute-start(bf16[192,768]{1,0:T(8,128)(2,1)S(1)} %get-tuple-element.169), channel_id=1, source_target_pairs={{0,4},{4,0},{8,12},{12,8},{16,20},{20,16},{24,28},{28,24},{1,5},{5... | collective-permute-start | bytes 884744 | tf_op jit(solution)/shard_map/grads_core/ppermute | solution.py:688
  105.4 2.1 %collective-permute-start.22 = (bf16[192,768]{1,0:T(8,128)(2,1)S(1)}, bf16[192,768]{1,0:T(8,128)(2,1)S(1)}, u32[]{:S(2)}, u32[]{:S(2)}) collective-permute-start(bf16[192,768]{1,0:T(8,128)(2,1)S(1)} %get-tuple-element.170), channel_id=1, source_target_pairs={{0,4},{4,0},{8,12},{12,8},{16,20},{20,16},{24,28},{28,24},{1,5},{5... | collective-permute-start | bytes 884744 | tf_op jit(solution)/shard_map/grads_core/ppermute | solution.py:688
  105.8 1.9 %collective-permute-start.23 = (bf16[192,768]{1,0:T(8,128)(2,1)S(1)}, bf16[192,768]{1,0:T(8,128)(2,1)S(1)}, u32[]{:S(2)}, u32[]{:S(2)}) collective-permute-start(bf16[192,768]{1,0:T(8,128)(2,1)S(1)} %get-tuple-element.171), channel_id=1, source_target_pairs={{0,4},{4,0},{8,12},{12,8},{16,20},{20,16},{24,28},{28,24},{1,5},{5... | collective-permute-start | bytes 884744 | tf_op jit(solution)/shard_map/grads_core/ppermute | solution.py:688
  105.9 9.7 %collective-permute-start.24 = (bf16[224,576]{1,0:T(8,128)(2,1)S(1)}, bf16[224,576]{1,0:T(8,128)(2,1)S(1)}, u32[]{:S(2)}, u32[]{:S(2)}) collective-permute-start(bf16[224,576]{1,0:T(8,128)(2,1)S(1)} %get-tuple-element.175), channel_id=1, source_target_pairs={{0,8},{4,12},{8,0},{12,4},{16,24},{20,28},{24,16},{28,20},{1,9},{5... | collective-permute-start | bytes 774152 | tf_op jit(solution)/shard_map/qkv_x/ppermute | solution.py:688
  108.5 14.6 %collective-permute-start.25 = (bf16[96,1152]{1,0:T(8,128)(2,1)S(1)}, bf16[96,1152]{1,0:T(8,128)(2,1)S(1)}, u32[]{:S(2)}, u32[]{:S(2)}) collective-permute-start(bf16[96,1152]{1,0:T(8,128)(2,1)S(1)} %get-tuple-element.178), channel_id=1, source_target_pairs={{0,8},{4,12},{8,0},{12,4},{16,24},{20,28},{24,16},{28,20},{1,9},{5... | collective-permute-start | bytes 663560 | tf_op jit(solution)/shard_map/grads_b/ppermute | solution.py:688
  113.2 14.2 %collective-permute-start.17 = (bf16[768,128]{1,0:T(8,128)(2,1)S(1)}, bf16[768,128]{1,0:T(8,128)(2,1)S(1)}, u32[]{:S(2)}, u32[]{:S(2)}) collective-permute-start(bf16[768,128]{1,0:T(8,128)(2,1)S(1)} %get-tuple-element.155), channel_id=1, source_target_pairs={{0,2},{1,3},{2,0},{3,1},{4,6},{5,7},{6,4},{7,5},{8,10},{9,11},{10,... | collective-permute-start | bytes 589832 | tf_op jit(solution)/shard_map/back/ppermute | solution.py:688
  116.2 6.8 %collective-permute-start.26 = (bf16[128,576]{1,0:T(8,128)(2,1)S(1)}, bf16[128,576]{1,0:T(8,128)(2,1)S(1)}, u32[]{:S(2)}, u32[]{:S(2)}) collective-permute-start(bf16[128,576]{1,0:T(8,128)(2,1)S(1)} %get-tuple-element.179), channel_id=1, source_target_pairs={{0,16},{4,20},{8,24},{12,28},{16,0},{20,4},{24,8},{28,12},{1,17},{... | collective-permute-start | bytes 442376 | tf_op jit(solution)/shard_map/qkv_y/ppermute | solution.py:688
  118.8 9.4 %collective-permute-start.30 = (bf16[96,1152]{1,0:T(8,128)(2,1)S(1)}, bf16[96,1152]{1,0:T(8,128)(2,1)S(1)}, u32[]{:S(2)}, u32[]{:S(2)}) collective-permute-start(bf16[96,1152]{1,0:T(8,128)(2,1)S(1)} %get-tuple-element.188), channel_id=1, source_target_pairs={{0,16},{4,20},{8,24},{12,28},{16,0},{20,4},{24,8},{28,12},{1,17},{... | collective-permute-start | bytes 663560 | tf_op jit(solution)/shard_map/grads_a/ppermute | solution.py:688
  123.8 5.8 %collective-permute-start.28 = (bf16[288,128]{1,0:T(8,128)(2,1)S(1)}, bf16[288,128]{1,0:T(8,128)(2,1)S(1)}, u32[]{:S(2)}, u32[]{:S(2)}) collective-permute-start(bf16[288,128]{1,0:T(8,128)(2,1)S(1)} %get-tuple-element.183), channel_id=1, source_target_pairs={{0,2},{1,3},{2,0},{3,1},{4,6},{5,7},{6,4},{7,5},{8,10},{9,11},{10,... | collective-permute-start | bytes 221192 | tf_op jit(solution)/shard_map/out/ppermute | solution.py:688
  124.5 6.3 %collective-permute-start.29 = (bf16[288,128]{1,0:T(8,128)(2,1)S(1)}, bf16[288,128]{1,0:T(8,128)(2,1)S(1)}, u32[]{:S(2)}, u32[]{:S(2)}) collective-permute-start(bf16[288,128]{1,0:T(8,128)(2,1)S(1)} %get-tuple-element.184), channel_id=1, source_target_pairs={{0,3},{1,2},{2,1},{3,0},{4,7},{5,6},{6,5},{7,4},{8,11},{9,10},{10,... | collective-permute-start | bytes 221192 | tf_op jit(solution)/shard_map/out/ppermute | solution.py:688
  126.5 5.1 %collective-permute-start.27 = (bf16[288,128]{1,0:T(8,128)(2,1)S(1)}, bf16[288,128]{1,0:T(8,128)(2,1)S(1)}, u32[]{:S(2)}, u32[]{:S(2)}) collective-permute-start(bf16[288,128]{1,0:T(8,128)(2,1)S(1)} %get-tuple-element.182), channel_id=1, source_target_pairs={{0,1},{1,0},{2,3},{3,2},{4,5},{5,4},{6,7},{7,6},{8,9},{9,8},{10,11... | collective-permute-start | bytes 221192 | tf_op jit(solution)/shard_map/out/ppermute | solution.py:688

commit v6 on v5

--- a/solution.py
+++ b/solution.py
@@ -400,10 +400,10 @@
 
 
 def back_kernel(
-    place, lengths, d0, d1, d2, d3, qkv, pt, xt, stat, nb, cols, wq_t, vec,
-    p0, p2, p13, dqkv_o, vec_o,
-    score, ds, acc, buckets_of, wide, sums,
+    place, lengths, d0, d1, d2, d3, qkv, pt, xt, h1, stat, nb, cols, wq_t, vec,
+    p0, p2, p13, vec_o, *rest,
 ):
+    grads, (dqkv_o, score, ds, acc, buckets_of, wide, sums) = rest[:-7], rest[-7:]
     m = place[0]
     channels, tokens = d0.shape
     heads = channels // HEAD_DIM
@@ -473,6 +473,7 @@
 
     lax.fori_loop(0, heads, one_head, 0, unroll=True)
     wide[...] = nn(wq_t[...], dqkv_o[...])
+    weight_grad = nt(h1[...], dqkv_o[...]).astype(BF16)
     mean, rstd = stat[0:1, :], stat[1:2, :]
     zero = jnp.zeros((8, tokens), F32)
 
@@ -504,12 +505,9 @@
     lane = lax.broadcasted_iota(jnp.int32, shape, 1)
     row = lax.broadcasted_iota(jnp.int32, shape, 0)
     vec_o[6:7, :] = across(jnp.where(lane == row + m * n_rows, each, 0.0))
-
-
-def qkv_grad_kernel(place, h1, dqkv, vec, *grads):
-    put_blocks([nt(h1[...], dqkv[...]).astype(BF16)], place[1] & 1, grads)
+    put_blocks([weight_grad], place[1] & 1, grads)
     if len(grads) > 1:
-        put_vec(vec[...], grads[0])
+        put_vec(vec_o[...], grads[0])
 
 
 def put_vec(vec, ref):
@@ -701,7 +699,7 @@
     sent = jnp.concatenate([tokens, lax.dynamic_slice_in_dim(w_out, (d & 3) * piece, piece, 0)])
     x1, x2 = swap(sent, 1, name="x"), swap(sent, 2, name="x")
     x = [sent, x1, x2, swap(after(x2, x1), 1, name="x")]
-    dy2 = swap(after(cotangent, x1, x2), 2, name="dy")
+    dy2 = swap(after(cotangent, *x[1:]), 2, name="dy")
     wq_t, w_up_t, w_down_t = call(
         turn_kernel,
         [like((width, 3 * channels), BF16), like((hidden, width), BF16), like((width, hidden), BF16)],
@@ -710,7 +708,7 @@
     x[1:] = lax.optimization_barrier((x[1:], wq_t))[0]
     (part,) = call(pieces_kernel, [like((4, piece, width), BF16)], x)
     part_x = swap(part, 2, "dp", name="w")
-    wq_now = after(wq, wq_t, w_up_t, w_down_t, dy2)
+    wq_now = after(wq, wq_t, w_up_t, w_down_t)
     xt, h1, stat, qkv, pt, att = call(
         head_kernel,
         [
@@ -730,7 +728,7 @@
         ],
         us=10,
     )
-    (parts,) = call(pair_kernel, [like((8, piece, width), BF16)], [part, after(part_x, att)])
+    (parts,) = call(pair_kernel, [like((8, piece, width), BF16)], [part, after(part_x, att, dy2)])
     att_sent = after(att, parts)
     dy1 = swap(after(cotangent, parts), 1, name="dy")
     atts = [att] + [swap(att_sent, k, name="att") for k in (1, 2, 3)]
@@ -791,12 +789,19 @@
 
     mlp = halved(m0, m2, m_recv, "mlp", seen=d_att[1:])
 
-    p0, p2, p13, dqkv, vec = call(
+    n = 3 * channels
+    extra = 4 * vec.shape[0]
+    if fast:
+        grad_like = [like((width // 2 + extra, n), BF16), like((width // 2, n), BF16)]
+    else:
+        grad_like = [like((width, n), BF16)]
+    p0, p2, p13, vec, *qkv_grads = call(
         back_kernel,
-        blocks + [like((3 * channels, group), BF16), like((8, width), F32)],
-        [place, page_lengths] + d_att + [qkv, pt, xt, stat, nb, cols, wq_t, vec],
+        blocks + [like((8, width), F32)] + grad_like,
+        [place, page_lengths] + d_att + [qkv, pt, xt, h1, stat, nb, cols, wq_t, vec],
         n_smem=2,
         scratch=[
+            pltpu.VMEM((n, group), BF16),
             pltpu.VMEM((group, group), F32),
             pltpu.VMEM((group, group), BF16),
             pltpu.VMEM((5, 128, 128), F32),
@@ -808,13 +813,6 @@
     )
     p_recv = swap(after(p13, mlp[1]), 1, name="back")
     back = halved(p0, p2, p_recv, "back", us=10)
-    n = 3 * channels
-    extra = 4 * vec.shape[0]
-    if fast:
-        grad_like = [like((width // 2 + extra, n), BF16), like((width // 2, n), BF16)]
-    else:
-        grad_like = [like((width, n), BF16)]
-    qkv_grads = call(qkv_grad_kernel, grad_like, [place, h1, dqkv, vec], n_smem=1)
 
     def reduced(g):
         g = g.reshape(dp, width // dp, g.shape[1])

time: 133 us -> 131 us (0.985)
  waiting for transfers between devices: 54.4 us -> 50.8 us
  starting transfers between devices: 37.1 us -> 40.1 us
    ppermute x31, waiting for transfers between devices: 54.4 us -> 50.8 us  [swap(): return lax.ppermute(v, axis, [(i, i ^ k) for i in range(n)])]
    ppermute x31, starting transfers between devices: 37.1 us -> 40.1 us  [swap(): return lax.ppermute(v, axis, [(i, i ^ k) for i in range(n)])]
    pallas_call x21 -> x20, Pallas kernels: 32.9 us -> 31.7 us  [call(): pl.pallas_call(kernel, out_shape=tuple(outs), in_specs=[SMEM] * n_smem +...]
where the time goes in v6:
time: 131 us; the launch traced here: 130 us
  waiting for transfers between devices  50.8 us (39%)
  starting transfers between devices  40.1 us (31%)
  Pallas kernels  31.7 us (24%)
  local copies, waits for them, and re-layouts  5.87 us (4%)
    ppermute x31, waiting for transfers between devices, swap(): return lax.ppermute(v, axis, [(i, i ^ k) for i in range(n)])  50.8 us
    ppermute x31, starting transfers between devices, swap(): return lax.ppermute(v, axis, [(i, i ^ k) for i in range(n)])  40.1 us
    pallas_call x20, Pallas kernels, call(): pl.pallas_call(kernel, out_shape=tuple(outs), in_specs=[SMEM] * n_smem +...  31.7 us
    unnamed x17, local copies, waits for them, and re-layouts  4.17 us
  transfers between devices with their start and end apart: 31, of which 19 were waited for; matrix products, arithmetic and copies ran while one was open for 2% of the time, Pallas kernels for 24%

profile of v6, /device:TPU:0, one launch (start us, length us, event | category | flops | bytes accessed | tf_op | source)
XLA Modules:
  0.0 130.4 jit_solution(16725365548885519159)
XLA Ops:
  0.7 0.9 copy-done
  1.6 0.9 pad_maximum_fusion.x0
  2.6 4.1 %collective-permute-start.1 = (bf16[176,768]{1,0:T(8,128)(2,1)S(1)}, bf16[176,768]{1,0:T(8,128)(2,1)S(1)}, u32[]{:S(2)}, u32[]{:S(2)}) collective-permute-start(bf16[176,768]{1,0:T(8,128)(2,1)S(1)} %pad_maximum_fusion.x0), channel_id=1, source_target_pairs={{0,2},{1,3},{2,0},{3,1},{4,6},{5,7},{6,4},{7,5},{8,10},{9,11},{10,... | collective-permute-start | bytes 811016 | tf_op jit(solution)/shard_map/x/ppermute | solution.py:686
  6.7 1.6 %collective-permute-start = (bf16[176,768]{1,0:T(8,128)(2,1)S(1)}, bf16[176,768]{1,0:T(8,128)(2,1)S(1)}, u32[]{:S(2)}, u32[]{:S(2)}) collective-permute-start(bf16[176,768]{1,0:T(8,128)(2,1)S(1)} %pad_maximum_fusion.x0), channel_id=1, source_target_pairs={{0,1},{1,0},{2,3},{3,2},{4,5},{5,4},{6,7},{7,6},{8,9},{9,8},{10,11... | collective-permute-start | bytes 811016 | tf_op jit(solution)/shard_map/x/ppermute | solution.py:686
  8.2 0.8 copy.28.table
  9.0 10.0 %collective-permute-done.1.x2 = bf16[176,768]{1,0:T(8,128)(2,1)S(1)} collective-permute-done((bf16[176,768]{1,0:T(8,128)(2,1)S(1)}, bf16[176,768]{1,0:T(8,128)(2,1)S(1)}, u32[]{:S(2)}, u32[]{:S(2)}) %collective-permute-start.1) | collective-permute-done | bytes 270368 | tf_op jit(solution)/shard_map/x/ppermute | solution.py:686
  19.2 1.5 %collective-permute-start.2 = (bf16[176,768]{1,0:T(8,128)(2,1)S(1)}, bf16[176,768]{1,0:T(8,128)(2,1)S(1)}, u32[]{:S(2)}, u32[]{:S(2)}) collective-permute-start(bf16[176,768]{1,0:T(8,128)(2,1)S(1)} %collective-permute-done.1.x2), channel_id=1, source_target_pairs={{0,1},{1,0},{2,3},{3,2},{4,5},{5,4},{6,7},{7,6},{8,9},{9,8},{10,11... | collective-permute-start | bytes 811016 | tf_op jit(solution)/shard_map/x/ppermute | solution.py:686
  20.7 0.8 fusion
  21.5 0.7 concatenate.7
  22.4 1.3 copy-done.2
  23.7 1.2 copy-done.4
  24.9 0.9 turn_kernel.1
  25.9 0.8 collective-permute-done.2.x3
  26.7 3.0 %collective-permute-start.4 = (bf16[128,768]{1,0:T(8,128)(2,1)S(1)}, bf16[128,768]{1,0:T(8,128)(2,1)S(1)}, u32[]{:S(2)}, u32[]{:S(2)}) collective-permute-start(bf16[128,768]{1,0:T(8,128)(2,1)S(1)} %copy-done.6), channel_id=1, source_target_pairs={{0,2},{1,3},{2,0},{3,1},{4,6},{5,7},{6,4},{7,5},{8,10},{9,11},{10,... | collective-permute-start | bytes 589832 | tf_op jit(solution)/shard_map/dy/ppermute | solution.py:686
  29.7 1.6 %collective-permute-start.3 = (bf16[4,48,768]{2,1,0:T(8,128)(2,1)S(1)}, bf16[4,48,768]{2,1,0:T(8,128)(2,1)S(1)}, u32[]{:S(2)}, u32[]{:S(2)}) collective-permute-start(bf16[4,48,768]{2,1,0:T(8,128)(2,1)S(1)} %pieces_kernel.1.a), channel_id=1, source_target_pairs={{0,8},{4,12},{8,0},{12,4},{16,24},{20,28},{24,16},{28,20},{1,9},{5... | collective-permute-start | bytes 884744 | tf_op jit(solution)/shard_map/w/ppermute | solution.py:686
  31.3 4.7 %head_kernel.1 = (bf16[768,512]{1,0:T(8,128)(2,1)S(1)}, bf16[768,512]{1,0:T(8,128)(2,1)S(1)}, f32[8,512]{1,0:T(8,128)S(1)}, bf16[576,512]{1,0:T(8,128)(2,1)S(1)}...) custom-call(s32[2]{0:T(128)S(1)} %pad_add_fusion.place, s32[1,8]{1,0:T(1,128)S(1)} %copy-done.7, ...), custom_call_target="tpu_custom_call" | custom-call | flops 11500000256 | bytes 8 | tf_op jit(solution)/shard_map/head_kernel/pallas_call | solution.py:21
  36.0 2.5 %collective-permute-done.4.c2 = bf16[128,768]{1,0:T(8,128)(2,1)S(1)} collective-permute-done((bf16[128,768]{1,0:T(8,128)(2,1)S(1)}, bf16[128,768]{1,0:T(8,128)(2,1)S(1)}, u32[]{:S(2)}, u32[]{:S(2)}) %collective-permute-start.4) | collective-permute-done | bytes 196640 | tf_op jit(solution)/shard_map/dy/ppermute | solution.py:686
  38.6 0.9 collective-permute-start.8
  39.5 2.7 %collective-permute-start.7 = (bf16[192,512]{1,0:T(8,128)(2,1)S(1)}, bf16[192,512]{1,0:T(8,128)(2,1)S(1)}, u32[]{:S(2)}, u32[]{:S(2)}) collective-permute-start(bf16[192,512]{1,0:T(8,128)(2,1)S(1)} %get-tuple-element.113.a0), channel_id=1, source_target_pairs={{0,3},{1,2},{2,1},{3,0},{4,7},{5,6},{6,5},{7,4},{8,11},{9,10},{10,... | collective-permute-start | bytes 589832 | tf_op jit(solution)/shard_map/att/ppermute | solution.py:686
  42.3 0.5 collective-permute-start.6
  42.7 1.2 collective-permute-start.5
  43.9 2.4 %collective-permute-done.8.c1 = bf16[128,768]{1,0:T(8,128)(2,1)S(1)} collective-permute-done((bf16[128,768]{1,0:T(8,128)(2,1)S(1)}, bf16[128,768]{1,0:T(8,128)(2,1)S(1)}, u32[]{:S(2)}, u32[]{:S(2)}) %collective-permute-start.8) | collective-permute-done | bytes 196640 | tf_op jit(solution)/shard_map/dy/ppermute | solution.py:686
  46.4 0.9 collective-permute-start.11
  47.2 1.0 out_weight_kernel.1
  48.2 4.0 %collective-permute-done.7.a3 = bf16[192,512]{1,0:T(8,128)(2,1)S(1)} collective-permute-done((bf16[192,512]{1,0:T(8,128)(2,1)S(1)}, bf16[192,512]{1,0:T(8,128)(2,1)S(1)}, u32[]{:S(2)}, u32[]{:S(2)}) %collective-permute-start.7) | collective-permute-done | bytes 196640 | tf_op jit(solution)/shard_map/att/ppermute | solution.py:686
  52.2 8.5 %collective-permute-done.6.a2 = bf16[192,512]{1,0:T(8,128)(2,1)S(1)} collective-permute-done((bf16[192,512]{1,0:T(8,128)(2,1)S(1)}, bf16[192,512]{1,0:T(8,128)(2,1)S(1)}, u32[]{:S(2)}, u32[]{:S(2)}) %collective-permute-start.6) | collective-permute-done | bytes 196640 | tf_op jit(solution)/shard_map/att/ppermute | solution.py:686
  60.7 4.1 %up_kernel.1 = (bf16[768,512]{1,0:T(8,128)(2,1)S(1)}, f32[768,512]{1,0:T(8,128)S(1)}, f32[768,512]{1,0:T(8,128)S(1)}, f32[8,512]{1,0:T(8,128)S(1)}, bf16[768,512...) custom-call(s32[2]{0:T(128)S(1)} %pad_add_fusion.place, ...), custom_call_target="tpu_custom_call" | custom-call | flops 11500000256 | bytes 8 | tf_op jit(solution)/shard_map/up_kernel/pallas_call | solution.py:21
  65.0 4.5 %down_kernel.1 = (bf16[192,512]{1,0:T(8,128)(2,1)S(1)}, bf16[192,512]{1,0:T(8,128)(2,1)S(1)}, bf16[192,512]{1,0:T(8,128)(2,1)S(1)}, bf16[192,512]{1,0:T(8,128)(2...) custom-call(s32[2]{0:T(128)S(1)} %pad_add_fusion.place, ...), custom_call_target="tpu_custom_call" | custom-call | flops 11500000256 | bytes 8 | tf_op jit(solution)/shard_map/down_kernel/pallas_call | solution.py:21
  69.4 2.1 %collective-permute-start.12 = (bf16[192,512]{1,0:T(8,128)(2,1)S(1)}, bf16[192,512]{1,0:T(8,128)(2,1)S(1)}, u32[]{:S(2)}, u32[]{:S(2)}) collective-permute-start(bf16[192,512]{1,0:T(8,128)(2,1)S(1)} %get-tuple-element.129), channel_id=1, source_target_pairs={{0,1},{1,0},{2,3},{3,2},{4,5},{5,4},{6,7},{7,6},{8,9},{9,8},{10,11... | collective-permute-start | bytes 589832 | tf_op jit(solution)/shard_map/d_att/ppermute | solution.py:686
  71.5 1.4 %collective-permute-start.13 = (bf16[192,512]{1,0:T(8,128)(2,1)S(1)}, bf16[192,512]{1,0:T(8,128)(2,1)S(1)}, u32[]{:S(2)}, u32[]{:S(2)}) collective-permute-start(bf16[192,512]{1,0:T(8,128)(2,1)S(1)} %get-tuple-element.130), channel_id=1, source_target_pairs={{0,2},{1,3},{2,0},{3,1},{4,6},{5,7},{6,4},{7,5},{8,10},{9,11},{10,... | collective-permute-start | bytes 589832 | tf_op jit(solution)/shard_map/d_att/ppermute | solution.py:686
  72.9 1.2 collective-permute-start.14
  74.1 2.6 %mlp_grad_kernel.1 = (f32[8,768]{1,0:T(8,128)S(1)}, bf16[384,1152]{1,0:T(8,128)(2,1)S(1)}, bf16[384,1152]{1,0:T(8,128)(2,1)S(1)}, bf16[384,1152]{1,0:T(8,128)(2,1)S(1)}, bf16[384,1152]{1,0:T(8,128)(2,1)S(1)}) custom-call(s32[2]{0:T(128)S(1)} %pad_add_fusion.place, f32[8,768]{1,0:T(8,128)S(1)} %get-tuple-element.140.vec, ...), custom_call_target="tpu_custom_call" | custom-call | flops 11500000 | bytes 8 | tf_op jit(solution)/shard_map/mlp_grad_kernel/pallas_call | solution.py:21
  76.7 1.6 %collective-permute-start.19 = (bf16[384,1152]{1,0:T(8,128)(2,1)S(1)}, bf16[384,1152]{1,0:T(8,128)(2,1)S(1)}, u32[]{:S(2)}, u32[]{:S(2)}) collective-permute-start(bf16[384,1152]{1,0:T(8,128)(2,1)S(1)} %get-tuple-element.163), channel_id=1, source_target_pairs={{0,8},{4,12},{8,0},{12,4},{16,24},{20,28},{24,16},{28,20},{1,9},{5... | collective-permute-start | bytes 2654216 | tf_op jit(solution)/shard_map/grads_a/ppermute | solution.py:686
  78.3 2.8 %collective-permute-done.10.recv = bf16[1536,128]{1,0:T(8,128)(2,1)S(1)} collective-permute-done((bf16[1536,128]{1,0:T(8,128)(2,1)S(1)}, bf16[1536,128]{1,0:T(8,128)(2,1)S(1)}, u32[]{:S(2)}, u32[]{:S(2)}) %collective-permute-start.10) | collective-permute-done | bytes 393248 | tf_op jit(solution)/shard_map/mlp/ppermute | solution.py:686
  81.0 1.5 %collective-permute-start.20 = (bf16[384,1152]{1,0:T(8,128)(2,1)S(1)}, bf16[384,1152]{1,0:T(8,128)(2,1)S(1)}, u32[]{:S(2)}, u32[]{:S(2)}) collective-permute-start(bf16[384,1152]{1,0:T(8,128)(2,1)S(1)} %get-tuple-element.165), channel_id=1, source_target_pairs={{0,16},{4,20},{8,24},{12,28},{16,0},{20,4},{24,8},{28,12},{1,17},{... | collective-permute-start | bytes 2654216 | tf_op jit(solution)/shard_map/grads_b/ppermute | solution.py:686
  82.6 2.1 %collective-permute-done.12.d1 = bf16[192,512]{1,0:T(8,128)(2,1)S(1)} collective-permute-done((bf16[192,512]{1,0:T(8,128)(2,1)S(1)}, bf16[192,512]{1,0:T(8,128)(2,1)S(1)}, u32[]{:S(2)}, u32[]{:S(2)}) %collective-permute-start.12) | collective-permute-done | bytes 196640 | tf_op jit(solution)/shard_map/d_att/ppermute | solution.py:686
  84.8 4.1 %collective-permute-done.14.d3 = bf16[192,512]{1,0:T(8,128)(2,1)S(1)} collective-permute-done((bf16[192,512]{1,0:T(8,128)(2,1)S(1)}, bf16[192,512]{1,0:T(8,128)(2,1)S(1)}, u32[]{:S(2)}, u32[]{:S(2)}) %collective-permute-start.14) | collective-permute-done | bytes 196640 | tf_op jit(solution)/shard_map/d_att/ppermute | solution.py:686
  88.9 3.8 %collective-permute-start.15 = (bf16[768,128]{1,0:T(8,128)(2,1)S(1)}, bf16[768,128]{1,0:T(8,128)(2,1)S(1)}, u32[]{:S(2)}, u32[]{:S(2)}) collective-permute-start(bf16[768,128]{1,0:T(8,128)(2,1)S(1)} %get-tuple-element.132), channel_id=1, source_target_pairs={{0,2},{1,3},{2,0},{3,1},{4,6},{5,7},{6,4},{7,5},{8,10},{9,11},{10,... | collective-permute-start | bytes 589832 | tf_op jit(solution)/shard_map/mlp/ppermute | solution.py:686
  92.6 6.5 %back_kernel.1 = (f32[768,128]{1,0:T(8,128)S(1)}, f32[768,128]{1,0:T(8,128)S(1)}, bf16[1536,128]{1,0:T(8,128)(2,1)S(1)}, f32[8,768]{1,0:T(8,128)S(1)}, bf16[416,...) custom-call(s32[2]{0:T(128)S(1)} %pad_add_fusion.place, s32[1,8]{1,0:T(1,128)S(1)} %copy-done.7, ...), custom_call_target="tpu_custom_call" | custom-call | flops 11500000256 | bytes 8 | tf_op jit(solution)/shard_map/back_kernel/pallas_call | solution.py:21
  99.5 1.9 %collective-permute-done.18.recv = bf16[416,576]{1,0:T(8,128)(2,1)S(1)} collective-permute-done((bf16[416,576]{1,0:T(8,128)(2,1)S(1)}, bf16[416,576]{1,0:T(8,128)(2,1)S(1)}, u32[]{:S(2)}, u32[]{:S(2)}) %collective-permute-start.18) | collective-permute-done | bytes 479264 | tf_op jit(solution)/shard_map/qkv_core/ppermute | solution.py:686
  101.4 0.7 qkv_second_kernel.1
  102.1 1.0 grads_second_kernel.1
  103.3 0.4 collective-permute-start.22
  103.8 1.5 %collective-permute-start.24 = (bf16[224,576]{1,0:T(8,128)(2,1)S(1)}, bf16[224,576]{1,0:T(8,128)(2,1)S(1)}, u32[]{:S(2)}, u32[]{:S(2)}) collective-permute-start(bf16[224,576]{1,0:T(8,128)(2,1)S(1)} %get-tuple-element.173), channel_id=1, source_target_pairs={{0,8},{4,12},{8,0},{12,4},{16,24},{20,28},{24,16},{28,20},{1,9},{5... | collective-permute-start | bytes 774152 | tf_op jit(solution)/shard_map/qkv_x/ppermute | solution.py:686
  105.6 0.7 grads_third_kernel.1
  106.3 1.5 %collective-permute-start.25 = (bf16[96,1152]{1,0:T(8,128)(2,1)S(1)}, bf16[96,1152]{1,0:T(8,128)(2,1)S(1)}, u32[]{:S(2)}, u32[]{:S(2)}) collective-permute-start(bf16[96,1152]{1,0:T(8,128)(2,1)S(1)} %get-tuple-element.176), channel_id=1, source_target_pairs={{0,8},{4,12},{8,0},{12,4},{16,24},{20,28},{24,16},{28,20},{1,9},{5... | collective-permute-start | bytes 663560 | tf_op jit(solution)/shard_map/grads_b/ppermute | solution.py:686
  107.8 3.1 %collective-permute-done.16.recv = bf16[1536,128]{1,0:T(8,128)(2,1)S(1)} collective-permute-done((bf16[1536,128]{1,0:T(8,128)(2,1)S(1)}, bf16[1536,128]{1,0:T(8,128)(2,1)S(1)}, u32[]{:S(2)}, u32[]{:S(2)}) %collective-permute-start.16) | collective-permute-done | bytes 393248 | tf_op jit(solution)/shard_map/back/ppermute | solution.py:686
  111.1 1.1 collective-permute-start.17
  112.2 1.3 collective-permute-done.24.recv
  113.4 0.6 qkv_third_kernel.1
  114.0 1.6 %collective-permute-start.26 = (bf16[128,576]{1,0:T(8,128)(2,1)S(1)}, bf16[128,576]{1,0:T(8,128)(2,1)S(1)}, u32[]{:S(2)}, u32[]{:S(2)}) collective-permute-start(bf16[128,576]{1,0:T(8,128)(2,1)S(1)} %get-tuple-element.177), channel_id=1, source_target_pairs={{0,16},{4,20},{8,24},{12,28},{16,0},{20,4},{24,8},{28,12},{1,17},{... | collective-permute-start | bytes 442376 | tf_op jit(solution)/shard_map/qkv_y/ppermute | solution.py:686
  115.6 0.9 output_kernel.1
  116.6 0.5 collective-permute-start.30
  117.1 3.9 %collective-permute-done.26.q_recv = bf16[128,576]{1,0:T(8,128)(2,1)S(1)} collective-permute-done((bf16[128,576]{1,0:T(8,128)(2,1)S(1)}, bf16[128,576]{1,0:T(8,128)(2,1)S(1)}, u32[]{:S(2)}, u32[]{:S(2)}) %collective-permute-start.26) | collective-permute-done | bytes 147488 | tf_op jit(solution)/shard_map/qkv_y/ppermute | solution.py:686
  121.0 0.7 message_kernel.1
  121.7 0.9 collective-permute-start.28
  122.6 2.1 %collective-permute-start.29 = (bf16[288,128]{1,0:T(8,128)(2,1)S(1)}, bf16[288,128]{1,0:T(8,128)(2,1)S(1)}, u32[]{:S(2)}, u32[]{:S(2)}) collective-permute-start(bf16[288,128]{1,0:T(8,128)(2,1)S(1)} %get-tuple-element.182), channel_id=1, source_target_pairs={{0,3},{1,2},{2,1},{3,0},{4,7},{5,6},{6,5},{7,4},{8,11},{9,10},{10,... | collective-permute-start | bytes 221192 | tf_op jit(solution)/shard_map/out/ppermute | solution.py:686
  124.7 0.6 collective-permute-start.27
  125.3 0.9 input_kernel.1
  126.2 1.0 last_kernel.1
  127.1 0.7 collective-permute-done.28.o2
  127.8 1.1 collective-permute-done.29.o3
  129.0 0.7 collective-permute-done.27.o1
  129.7 0.7 small_kernel.1
  (41 shorter events, 1.8 us)
Async XLA Ops:
  0.6 1.0 copy-start
  0.7 21.8 %copy-start.1 = (bf16[768,768]{1,0:T(8,128)(2,1)S(1)}, bf16[768,768]{1,0:T(8,128)(2,1)}, u32[]{:S(2)}) copy-start(bf16[768,768]{1,0:T(8,128)(2,1)} %w_up.1) | copy-start | bytes 3538948
  2.6 16.5 %collective-permute-start.1 = (bf16[176,768]{1,0:T(8,128)(2,1)S(1)}, bf16[176,768]{1,0:T(8,128)(2,1)S(1)}, u32[]{:S(2)}, u32[]{:S(2)}) collective-permute-start(bf16[176,768]{1,0:T(8,128)(2,1)S(1)} %pad_maximum_fusion.x0), channel_id=1, source_target_pairs={{0,2},{1,3},{2,0},{3,1},{4,6},{5,7},{6,4},{7,5},{8,10},{9,11},{10,... | collective-permute-start | bytes 811016 | tf_op jit(solution)/shard_map/x/ppermute | solution.py:686
  6.7 12.6 %collective-permute-start = (bf16[176,768]{1,0:T(8,128)(2,1)S(1)}, bf16[176,768]{1,0:T(8,128)(2,1)S(1)}, u32[]{:S(2)}, u32[]{:S(2)}) collective-permute-start(bf16[176,768]{1,0:T(8,128)(2,1)S(1)} %pad_maximum_fusion.x0), channel_id=1, source_target_pairs={{0,1},{1,0},{2,3},{3,2},{4,5},{5,4},{6,7},{7,6},{8,9},{9,8},{10,11... | collective-permute-start | bytes 811016 | tf_op jit(solution)/shard_map/x/ppermute | solution.py:686
  19.2 7.4 %collective-permute-start.2 = (bf16[176,768]{1,0:T(8,128)(2,1)S(1)}, bf16[176,768]{1,0:T(8,128)(2,1)S(1)}, u32[]{:S(2)}, u32[]{:S(2)}) collective-permute-start(bf16[176,768]{1,0:T(8,128)(2,1)S(1)} %collective-permute-done.1.x2), channel_id=1, source_target_pairs={{0,1},{1,0},{2,3},{3,2},{4,5},{5,4},{6,7},{7,6},{8,9},{9,8},{10,11... | collective-permute-start | bytes 811016 | tf_op jit(solution)/shard_map/x/ppermute | solution.py:686
  22.4 1.3 copy-start.2
  23.7 1.2 copy-start.4
  24.9 1.8 %copy-start.6 = (bf16[128,768]{1,0:T(8,128)(2,1)S(1)}, bf16[128,768]{1,0:T(8,128)(2,1)}, u32[]{:S(2)}) copy-start(bf16[128,768]{1,0:T(8,128)(2,1)} %dy.1) | copy-start | bytes 589828
  24.9 6.4 %copy-start.5 = (bf16[768,3,192]{0,2,1:T(8,128)(2,1)S(1)}, bf16[768,3,192]{0,2,1:T(8,128)(2,1)}, u32[]{:S(2)}) copy-start(bf16[768,3,192]{0,2,1:T(8,128)(2,1)} %param.16) | copy-start | bytes 2654212
  24.9 6.4 %copy-start.7 = (s32[1,8]{1,0:T(1,128)S(1)}, s32[1,8]{1,0:T(1,128)}, u32[]{:S(2)}) copy-start(s32[1,8]{1,0:T(1,128)} %lengths.3) | copy-start | bytes 100
  26.7 11.8 %collective-permute-start.4 = (bf16[128,768]{1,0:T(8,128)(2,1)S(1)}, bf16[128,768]{1,0:T(8,128)(2,1)S(1)}, u32[]{:S(2)}, u32[]{:S(2)}) collective-permute-start(bf16[128,768]{1,0:T(8,128)(2,1)S(1)} %copy-done.6), channel_id=1, source_target_pairs={{0,2},{1,3},{2,0},{3,1},{4,6},{5,7},{6,4},{7,5},{8,10},{9,11},{10,... | collective-permute-start | bytes 589832 | tf_op jit(solution)/shard_map/dy/ppermute | solution.py:686
  29.7 8.7 %collective-permute-start.3 = (bf16[4,48,768]{2,1,0:T(8,128)(2,1)S(1)}, bf16[4,48,768]{2,1,0:T(8,128)(2,1)S(1)}, u32[]{:S(2)}, u32[]{:S(2)}) collective-permute-start(bf16[4,48,768]{2,1,0:T(8,128)(2,1)S(1)} %pieces_kernel.1.a), channel_id=1, source_target_pairs={{0,8},{4,12},{8,0},{12,4},{16,24},{20,28},{24,16},{28,20},{1,9},{5... | collective-permute-start | bytes 884744 | tf_op jit(solution)/shard_map/w/ppermute | solution.py:686
  38.5 8.7 %collective-permute-start.9 = (bf16[8,48,768]{2,1,0:T(8,128)(2,1)S(1)}, bf16[8,48,768]{2,1,0:T(8,128)(2,1)S(1)}, u32[]{:S(2)}, u32[]{:S(2)}) collective-permute-start(bf16[8,48,768]{2,1,0:T(8,128)(2,1)S(1)} %pair_kernel.1.here), channel_id=1, source_target_pairs={{0,4},{4,0},{8,12},{12,8},{16,20},{20,16},{24,28},{28,24},{1,5},{5... | collective-permute-start | bytes 1769480 | tf_op jit(solution)/shard_map/w/ppermute | solution.py:686
  38.6 7.8 %collective-permute-start.8 = (bf16[128,768]{1,0:T(8,128)(2,1)S(1)}, bf16[128,768]{1,0:T(8,128)(2,1)S(1)}, u32[]{:S(2)}, u32[]{:S(2)}) collective-permute-start(bf16[128,768]{1,0:T(8,128)(2,1)S(1)} %copy-done.6), channel_id=1, source_target_pairs={{0,1},{1,0},{2,3},{3,2},{4,5},{5,4},{6,7},{7,6},{8,9},{9,8},{10,11... | collective-permute-start | bytes 589832 | tf_op jit(solution)/shard_map/dy/ppermute | solution.py:686
  39.5 12.7 %collective-permute-start.7 = (bf16[192,512]{1,0:T(8,128)(2,1)S(1)}, bf16[192,512]{1,0:T(8,128)(2,1)S(1)}, u32[]{:S(2)}, u32[]{:S(2)}) collective-permute-start(bf16[192,512]{1,0:T(8,128)(2,1)S(1)} %get-tuple-element.113.a0), channel_id=1, source_target_pairs={{0,3},{1,2},{2,1},{3,0},{4,7},{5,6},{6,5},{7,4},{8,11},{9,10},{10,... | collective-permute-start | bytes 589832 | tf_op jit(solution)/shard_map/att/ppermute | solution.py:686
  42.3 18.5 %collective-permute-start.6 = (bf16[192,512]{1,0:T(8,128)(2,1)S(1)}, bf16[192,512]{1,0:T(8,128)(2,1)S(1)}, u32[]{:S(2)}, u32[]{:S(2)}) collective-permute-start(bf16[192,512]{1,0:T(8,128)(2,1)S(1)} %get-tuple-element.113.a0), channel_id=1, source_target_pairs={{0,2},{1,3},{2,0},{3,1},{4,6},{5,7},{6,4},{7,5},{8,10},{9,11},{10,... | collective-permute-start | bytes 589832 | tf_op jit(solution)/shard_map/att/ppermute | solution.py:686
  42.7 18.0 %collective-permute-start.5 = (bf16[192,512]{1,0:T(8,128)(2,1)S(1)}, bf16[192,512]{1,0:T(8,128)(2,1)S(1)}, u32[]{:S(2)}, u32[]{:S(2)}) collective-permute-start(bf16[192,512]{1,0:T(8,128)(2,1)S(1)} %get-tuple-element.113.a0), channel_id=1, source_target_pairs={{0,1},{1,0},{2,3},{3,2},{4,5},{5,4},{6,7},{7,6},{8,9},{9,8},{10,11... | collective-permute-start | bytes 589832 | tf_op jit(solution)/shard_map/att/ppermute | solution.py:686
  46.4 18.6 %collective-permute-start.11 = (bf16[128,768]{1,0:T(8,128)(2,1)S(1)}, bf16[128,768]{1,0:T(8,128)(2,1)S(1)}, u32[]{:S(2)}, u32[]{:S(2)}) collective-permute-start(bf16[128,768]{1,0:T(8,128)(2,1)S(1)} %collective-permute-done.4.c2), channel_id=1, source_target_pairs={{0,1},{1,0},{2,3},{3,2},{4,5},{5,4},{6,7},{7,6},{8,9},{9,8},{10,11... | collective-permute-start | bytes 589832 | tf_op jit(solution)/shard_map/dy/ppermute | solution.py:686
  60.7 4.2 %copy-start.3 = (bf16[768,768]{1,0:T(8,128)(2,1)S(1)}, bf16[768,768]{1,0:T(8,128)(2,1)}, u32[]{:S(2)}) copy-start(bf16[768,768]{1,0:T(8,128)(2,1)} %w_down.1) | copy-start | bytes 3538948
  64.9 16.2 %collective-permute-start.10 = (bf16[1536,128]{1,0:T(8,128)(2,1)S(1)}, bf16[1536,128]{1,0:T(8,128)(2,1)S(1)}, u32[]{:S(2)}, u32[]{:S(2)}) collective-permute-start(bf16[1536,128]{1,0:T(8,128)(2,1)S(1)} %get-tuple-element.120), channel_id=1, source_target_pairs={{0,1},{1,0},{2,3},{3,2},{4,5},{5,4},{6,7},{7,6},{8,9},{9,8},{10,11... | collective-permute-start | bytes 1179656 | tf_op jit(solution)/shard_map/mlp/ppermute | solution.py:686
  69.4 15.3 %collective-permute-start.12 = (bf16[192,512]{1,0:T(8,128)(2,1)S(1)}, bf16[192,512]{1,0:T(8,128)(2,1)S(1)}, u32[]{:S(2)}, u32[]{:S(2)}) collective-permute-start(bf16[192,512]{1,0:T(8,128)(2,1)S(1)} %get-tuple-element.129), channel_id=1, source_target_pairs={{0,1},{1,0},{2,3},{3,2},{4,5},{5,4},{6,7},{7,6},{8,9},{9,8},{10,11... | collective-permute-start | bytes 589832 | tf_op jit(solution)/shard_map/d_att/ppermute | solution.py:686
  71.5 13.3 %collective-permute-start.13 = (bf16[192,512]{1,0:T(8,128)(2,1)S(1)}, bf16[192,512]{1,0:T(8,128)(2,1)S(1)}, u32[]{:S(2)}, u32[]{:S(2)}) collective-permute-start(bf16[192,512]{1,0:T(8,128)(2,1)S(1)} %get-tuple-element.130), channel_id=1, source_target_pairs={{0,2},{1,3},{2,0},{3,1},{4,6},{5,7},{6,4},{7,5},{8,10},{9,11},{10,... | collective-permute-start | bytes 589832 | tf_op jit(solution)/shard_map/d_att/ppermute | solution.py:686
  72.9 15.9 %collective-permute-start.14 = (bf16[192,512]{1,0:T(8,128)(2,1)S(1)}, bf16[192,512]{1,0:T(8,128)(2,1)S(1)}, u32[]{:S(2)}, u32[]{:S(2)}) collective-permute-start(bf16[192,512]{1,0:T(8,128)(2,1)S(1)} %get-tuple-element.131), channel_id=1, source_target_pairs={{0,3},{1,2},{2,1},{3,0},{4,7},{5,6},{6,5},{7,4},{8,11},{9,10},{10,... | collective-permute-start | bytes 589832 | tf_op jit(solution)/shard_map/d_att/ppermute | solution.py:686
  76.7 25.4 %collective-permute-start.19 = (bf16[384,1152]{1,0:T(8,128)(2,1)S(1)}, bf16[384,1152]{1,0:T(8,128)(2,1)S(1)}, u32[]{:S(2)}, u32[]{:S(2)}) collective-permute-start(bf16[384,1152]{1,0:T(8,128)(2,1)S(1)} %get-tuple-element.163), channel_id=1, source_target_pairs={{0,8},{4,12},{8,0},{12,4},{16,24},{20,28},{24,16},{28,20},{1,9},{5... | collective-permute-start | bytes 2654216 | tf_op jit(solution)/shard_map/grads_a/ppermute | solution.py:686
  81.0 21.1 %collective-permute-start.20 = (bf16[384,1152]{1,0:T(8,128)(2,1)S(1)}, bf16[384,1152]{1,0:T(8,128)(2,1)S(1)}, u32[]{:S(2)}, u32[]{:S(2)}) collective-permute-start(bf16[384,1152]{1,0:T(8,128)(2,1)S(1)} %get-tuple-element.165), channel_id=1, source_target_pairs={{0,16},{4,20},{8,24},{12,28},{16,0},{20,4},{24,8},{28,12},{1,17},{... | collective-permute-start | bytes 2654216 | tf_op jit(solution)/shard_map/grads_b/ppermute | solution.py:686
  88.9 10.6 %collective-permute-start.15 = (bf16[768,128]{1,0:T(8,128)(2,1)S(1)}, bf16[768,128]{1,0:T(8,128)(2,1)S(1)}, u32[]{:S(2)}, u32[]{:S(2)}) collective-permute-start(bf16[768,128]{1,0:T(8,128)(2,1)S(1)} %get-tuple-element.132), channel_id=1, source_target_pairs={{0,2},{1,3},{2,0},{3,1},{4,6},{5,7},{6,4},{7,5},{8,10},{9,11},{10,... | collective-permute-start | bytes 589832 | tf_op jit(solution)/shard_map/mlp/ppermute | solution.py:686
  99.4 1.9 %collective-permute-start.18 = (bf16[416,576]{1,0:T(8,128)(2,1)S(1)}, bf16[416,576]{1,0:T(8,128)(2,1)S(1)}, u32[]{:S(2)}, u32[]{:S(2)}) collective-permute-start(bf16[416,576]{1,0:T(8,128)(2,1)S(1)} %get-tuple-element.159), channel_id=1, source_target_pairs={{0,4},{4,0},{8,12},{12,8},{16,20},{20,16},{24,28},{28,24},{1,5},{5... | collective-permute-start | bytes 1437704 | tf_op jit(solution)/shard_map/qkv_core/ppermute | solution.py:686
  99.5 11.5 %collective-permute-start.16 = (bf16[1536,128]{1,0:T(8,128)(2,1)S(1)}, bf16[1536,128]{1,0:T(8,128)(2,1)S(1)}, u32[]{:S(2)}, u32[]{:S(2)}) collective-permute-start(bf16[1536,128]{1,0:T(8,128)(2,1)S(1)} %get-tuple-element.153), channel_id=1, source_target_pairs={{0,1},{1,0},{2,3},{3,2},{4,5},{5,4},{6,7},{7,6},{8,9},{9,8},{10,11... | collective-permute-start | bytes 1179656 | tf_op jit(solution)/shard_map/back/ppermute | solution.py:686
  103.1 2.2 %collective-permute-start.21 = (bf16[192,768]{1,0:T(8,128)(2,1)S(1)}, bf16[192,768]{1,0:T(8,128)(2,1)S(1)}, u32[]{:S(2)}, u32[]{:S(2)}) collective-permute-start(bf16[192,768]{1,0:T(8,128)(2,1)S(1)} %get-tuple-element.167), channel_id=1, source_target_pairs={{0,4},{4,0},{8,12},{12,8},{16,20},{20,16},{24,28},{28,24},{1,5},{5... | collective-permute-start | bytes 884744 | tf_op jit(solution)/shard_map/grads_core/ppermute | solution.py:686
  103.3 2.0 %collective-permute-start.22 = (bf16[192,768]{1,0:T(8,128)(2,1)S(1)}, bf16[192,768]{1,0:T(8,128)(2,1)S(1)}, u32[]{:S(2)}, u32[]{:S(2)}) collective-permute-start(bf16[192,768]{1,0:T(8,128)(2,1)S(1)} %get-tuple-element.168), channel_id=1, source_target_pairs={{0,4},{4,0},{8,12},{12,8},{16,20},{20,16},{24,28},{28,24},{1,5},{5... | collective-permute-start | bytes 884744 | tf_op jit(solution)/shard_map/grads_core/ppermute | solution.py:686
  103.6 1.9 %collective-permute-start.23 = (bf16[192,768]{1,0:T(8,128)(2,1)S(1)}, bf16[192,768]{1,0:T(8,128)(2,1)S(1)}, u32[]{:S(2)}, u32[]{:S(2)}) collective-permute-start(bf16[192,768]{1,0:T(8,128)(2,1)S(1)} %get-tuple-element.169), channel_id=1, source_target_pairs={{0,4},{4,0},{8,12},{12,8},{16,20},{20,16},{24,28},{28,24},{1,5},{5... | collective-permute-start | bytes 884744 | tf_op jit(solution)/shard_map/grads_core/ppermute | solution.py:686
  103.8 9.7 %collective-permute-start.24 = (bf16[224,576]{1,0:T(8,128)(2,1)S(1)}, bf16[224,576]{1,0:T(8,128)(2,1)S(1)}, u32[]{:S(2)}, u32[]{:S(2)}) collective-permute-start(bf16[224,576]{1,0:T(8,128)(2,1)S(1)} %get-tuple-element.173), channel_id=1, source_target_pairs={{0,8},{4,12},{8,0},{12,4},{16,24},{20,28},{24,16},{28,20},{1,9},{5... | collective-permute-start | bytes 774152 | tf_op jit(solution)/shard_map/qkv_x/ppermute | solution.py:686
  106.3 14.7 %collective-permute-start.25 = (bf16[96,1152]{1,0:T(8,128)(2,1)S(1)}, bf16[96,1152]{1,0:T(8,128)(2,1)S(1)}, u32[]{:S(2)}, u32[]{:S(2)}) collective-permute-start(bf16[96,1152]{1,0:T(8,128)(2,1)S(1)} %get-tuple-element.176), channel_id=1, source_target_pairs={{0,8},{4,12},{8,0},{12,4},{16,24},{20,28},{24,16},{28,20},{1,9},{5... | collective-permute-start | bytes 663560 | tf_op jit(solution)/shard_map/grads_b/ppermute | solution.py:686
  111.1 14.2 %collective-permute-start.17 = (bf16[768,128]{1,0:T(8,128)(2,1)S(1)}, bf16[768,128]{1,0:T(8,128)(2,1)S(1)}, u32[]{:S(2)}, u32[]{:S(2)}) collective-permute-start(bf16[768,128]{1,0:T(8,128)(2,1)S(1)} %get-tuple-element.155), channel_id=1, source_target_pairs={{0,2},{1,3},{2,0},{3,1},{4,6},{5,7},{6,4},{7,5},{8,10},{9,11},{10,... | collective-permute-start | bytes 589832 | tf_op jit(solution)/shard_map/back/ppermute | solution.py:686
  114.0 6.9 %collective-permute-start.26 = (bf16[128,576]{1,0:T(8,128)(2,1)S(1)}, bf16[128,576]{1,0:T(8,128)(2,1)S(1)}, u32[]{:S(2)}, u32[]{:S(2)}) collective-permute-start(bf16[128,576]{1,0:T(8,128)(2,1)S(1)} %get-tuple-element.177), channel_id=1, source_target_pairs={{0,16},{4,20},{8,24},{12,28},{16,0},{20,4},{24,8},{28,12},{1,17},{... | collective-permute-start | bytes 442376 | tf_op jit(solution)/shard_map/qkv_y/ppermute | solution.py:686
  116.6 9.6 %collective-permute-start.30 = (bf16[96,1152]{1,0:T(8,128)(2,1)S(1)}, bf16[96,1152]{1,0:T(8,128)(2,1)S(1)}, u32[]{:S(2)}, u32[]{:S(2)}) collective-permute-start(bf16[96,1152]{1,0:T(8,128)(2,1)S(1)} %get-tuple-element.186), channel_id=1, source_target_pairs={{0,16},{4,20},{8,24},{12,28},{16,0},{20,4},{24,8},{28,12},{1,17},{... | collective-permute-start | bytes 663560 | tf_op jit(solution)/shard_map/grads_a/ppermute | solution.py:686
  121.7 6.1 %collective-permute-start.28 = (bf16[288,128]{1,0:T(8,128)(2,1)S(1)}, bf16[288,128]{1,0:T(8,128)(2,1)S(1)}, u32[]{:S(2)}, u32[]{:S(2)}) collective-permute-start(bf16[288,128]{1,0:T(8,128)(2,1)S(1)} %get-tuple-element.181), channel_id=1, source_target_pairs={{0,2},{1,3},{2,0},{3,1},{4,6},{5,7},{6,4},{7,5},{8,10},{9,11},{10,... | collective-permute-start | bytes 221192 | tf_op jit(solution)/shard_map/out/ppermute | solution.py:686
  122.6 6.3 %collective-permute-start.29 = (bf16[288,128]{1,0:T(8,128)(2,1)S(1)}, bf16[288,128]{1,0:T(8,128)(2,1)S(1)}, u32[]{:S(2)}, u32[]{:S(2)}) collective-permute-start(bf16[288,128]{1,0:T(8,128)(2,1)S(1)} %get-tuple-element.182), channel_id=1, source_target_pairs={{0,3},{1,2},{2,1},{3,0},{4,7},{5,6},{6,5},{7,4},{8,11},{9,10},{10,... | collective-permute-start | bytes 221192 | tf_op jit(solution)/shard_map/out/ppermute | solution.py:686
  124.7 5.0 %collective-permute-start.27 = (bf16[288,128]{1,0:T(8,128)(2,1)S(1)}, bf16[288,128]{1,0:T(8,128)(2,1)S(1)}, u32[]{:S(2)}, u32[]{:S(2)}) collective-permute-start(bf16[288,128]{1,0:T(8,128)(2,1)S(1)} %get-tuple-element.180), channel_id=1, source_target_pairs={{0,1},{1,0},{2,3},{3,2},{4,5},{5,4},{6,7},{7,6},{8,9},{9,8},{10,11... | collective-permute-start | bytes 221192 | tf_op jit(solution)/shard_map/out/ppermute | solution.py:686

commit v7 on v6

--- a/solution.py
+++ b/solution.py
@@ -100,7 +100,7 @@
 
 def head_kernel(
     place, lengths, table, x0, x1, x2, x3, cols, wq,
-    xt_o, h1_o, stat_o, qkv_o, pt_o, att_o,
+    xt_o, h1_o, stat_o, qkv_o, pt_o, att_o, top_o, low_o,
     score, ids, pattern,
 ):
     m = place[0]
@@ -197,10 +197,12 @@
         return carry
 
     lax.fori_loop(0, heads, one_head, 0, unroll=True)
+    half_rows = channels // 2
+    top_o[...], low_o[...] = att_o[0:half_rows, :], att_o[half_rows:, :]
 
 
 def up_kernel(
-    place, a0, a1, a2, a3, xt, cols, w_out_t, w_up_t, w_down_t,
+    place, a0, a1, a2t, a2b, a3t, a3b, xt, cols, w_out_t, w_up_t, w_down_t,
     at_o, attn_o, hat_o, rstd_o, h2_o, act_o, slope_o, mid_o, mlp_o, m0, m2, m13,
     wide,
 ):
@@ -209,8 +211,10 @@
     channels = a0.shape[0]
     width, tokens = xt.shape
     hidden = act_o.shape[0]
-    for k, a in enumerate((a0, a1, a2, a3)):
-        at_o[pl.ds(pl.multiple_of((m ^ k) * channels, channels), channels), :] = a[...]
+    top = channels // 2
+    for k, first, a in ((0, 0, a0), (1, 0, a1), (2, 0, a2t), (2, top, a2b), (3, 0, a3t), (3, top, a3b)):
+        at = pl.multiple_of((m ^ k) * channels + first, top)
+        at_o[pl.ds(at, a.shape[0]), :] = a[...]
     attn_o[...] = nn(w_out_t[...], at_o[...])
     zero = jnp.zeros((8, tokens), F32)
 
@@ -700,6 +704,7 @@
     x1, x2 = swap(sent, 1, name="x"), swap(sent, 2, name="x")
     x = [sent, x1, x2, swap(after(x2, x1), 1, name="x")]
     dy2 = swap(after(cotangent, *x[1:]), 2, name="dy")
+    dy1 = swap(after(cotangent, *x[1:]), 1, name="dy")
     wq_t, w_up_t, w_down_t = call(
         turn_kernel,
         [like((width, 3 * channels), BF16), like((hidden, width), BF16), like((width, hidden), BF16)],
@@ -709,7 +714,7 @@
     (part,) = call(pieces_kernel, [like((4, piece, width), BF16)], x)
     part_x = swap(part, 2, "dp", name="w")
     wq_now = after(wq, wq_t, w_up_t, w_down_t)
-    xt, h1, stat, qkv, pt, att = call(
+    xt, h1, stat, qkv, pt, att, att_top, att_low = call(
         head_kernel,
         [
             like((width, group), BF16),
@@ -718,6 +723,8 @@
             like((3 * channels, group), BF16),
             like((heads, group, group), BF16),
             like((channels, group), BF16),
+            like((channels // 2, group), BF16),
+            like((channels // 2, group), BF16),
         ],
         [place, page_lengths, rel_table] + x + [cols, wq_now],
         n_smem=3,
@@ -728,10 +735,13 @@
         ],
         us=10,
     )
-    (parts,) = call(pair_kernel, [like((8, piece, width), BF16)], [part, after(part_x, att, dy2)])
-    att_sent = after(att, parts)
-    dy1 = swap(after(cotangent, parts), 1, name="dy")
-    atts = [att] + [swap(att_sent, k, name="att") for k in (1, 2, 3)]
+    (parts,) = call(
+        pair_kernel, [like((8, piece, width), BF16)], [part, after(part_x, att, dy1, dy2)]
+    )
+    att_top, att_low, att_sent = after(att_top, parts), after(att_low, parts), after(att, parts)
+    a2t, a2b = swap(att_top, 2, name="att"), swap(att_low, 2, name="att")
+    a3b, a1 = swap(att_low, 3, name="att"), swap(att_sent, 1, name="att")
+    atts = [att, a1, a2t, a2b, swap(a2t, 1, name="att"), a3b]
     dy = [cotangent, dy1, dy2, swap(after(dy2, parts), 1, name="dy")]
     w_pieces = [parts, swap(parts, 1, "dp", name="w")]
     w_out_full, w_out_t = call(

time: 131 us -> 127 us (0.969)
  waiting for transfers between devices: 50.8 us -> 43 us
  starting transfers between devices: 40.1 us -> 43.8 us
    ppermute x31 -> x33, waiting for transfers between devices: 50.8 us -> 43 us  [swap(): return lax.ppermute(v, axis, [(i, i ^ k) for i in range(n)])]
    ppermute x31 -> x33, starting transfers between devices: 40.1 us -> 43.8 us  [swap(): return lax.ppermute(v, axis, [(i, i ^ k) for i in range(n)])]
  transfers between devices with their start and end apart: 31 -> 33, of which waited for: 19 -> 20; matrix products, arithmetic and copies ran while one was open for 2% -> 2% of each run, Pallas kernels for 24% -> 25%
where the time goes in v7:
time: 127 us; the launch traced here: 126 us
  starting transfers between devices  43.8 us (34%)
  waiting for transfers between devices  43 us (34%)
  Pallas kernels  31.9 us (25%)
  local copies, waits for them, and re-layouts  5.87 us (5%)
    ppermute x33, starting transfers between devices, swap(): return lax.ppermute(v, axis, [(i, i ^ k) for i in range(n)])  43.8 us
    ppermute x33, waiting for transfers between devices, swap(): return lax.ppermute(v, axis, [(i, i ^ k) for i in range(n)])  43 us
    pallas_call x20, Pallas kernels, call(): pl.pallas_call(kernel, out_shape=tuple(outs), in_specs=[SMEM] * n_smem +...  31.9 us
    unnamed x17, local copies, waits for them, and re-layouts  4.17 us
  transfers between devices with their start and end apart: 33, of which 20 were waited for; matrix products, arithmetic and copies ran while one was open for 2% of the time, Pallas kernels for 25%

profile of v7, /device:TPU:0, one launch (start us, length us, event | category | flops | bytes accessed | tf_op | source)
XLA Modules:
  0.0 126.5 jit_solution(14639524060181374469)
XLA Ops:
  0.7 0.9 copy-done
  1.6 0.9 pad_maximum_fusion.x0
  2.6 4.1 %collective-permute-start.1 = (bf16[176,768]{1,0:T(8,128)(2,1)S(1)}, bf16[176,768]{1,0:T(8,128)(2,1)S(1)}, u32[]{:S(2)}, u32[]{:S(2)}) collective-permute-start(bf16[176,768]{1,0:T(8,128)(2,1)S(1)} %pad_maximum_fusion.x0), channel_id=1, source_target_pairs={{0,2},{1,3},{2,0},{3,1},{4,6},{5,7},{6,4},{7,5},{8,10},{9,11},{10,... | collective-permute-start | bytes 811016 | tf_op jit(solution)/shard_map/x/ppermute | solution.py:690
  6.7 1.6 %collective-permute-start = (bf16[176,768]{1,0:T(8,128)(2,1)S(1)}, bf16[176,768]{1,0:T(8,128)(2,1)S(1)}, u32[]{:S(2)}, u32[]{:S(2)}) collective-permute-start(bf16[176,768]{1,0:T(8,128)(2,1)S(1)} %pad_maximum_fusion.x0), channel_id=1, source_target_pairs={{0,1},{1,0},{2,3},{3,2},{4,5},{5,4},{6,7},{7,6},{8,9},{9,8},{10,11... | collective-permute-start | bytes 811016 | tf_op jit(solution)/shard_map/x/ppermute | solution.py:690
  8.2 0.8 copy.28.table
  9.0 10.0 %collective-permute-done.1.x2 = bf16[176,768]{1,0:T(8,128)(2,1)S(1)} collective-permute-done((bf16[176,768]{1,0:T(8,128)(2,1)S(1)}, bf16[176,768]{1,0:T(8,128)(2,1)S(1)}, u32[]{:S(2)}, u32[]{:S(2)}) %collective-permute-start.1) | collective-permute-done | bytes 270368 | tf_op jit(solution)/shard_map/x/ppermute | solution.py:690
  19.2 1.5 %collective-permute-start.2 = (bf16[176,768]{1,0:T(8,128)(2,1)S(1)}, bf16[176,768]{1,0:T(8,128)(2,1)S(1)}, u32[]{:S(2)}, u32[]{:S(2)}) collective-permute-start(bf16[176,768]{1,0:T(8,128)(2,1)S(1)} %collective-permute-done.1.x2), channel_id=1, source_target_pairs={{0,1},{1,0},{2,3},{3,2},{4,5},{5,4},{6,7},{7,6},{8,9},{9,8},{10,11... | collective-permute-start | bytes 811016 | tf_op jit(solution)/shard_map/x/ppermute | solution.py:690
  20.7 0.8 fusion
  21.5 0.7 concatenate.7
  22.4 1.3 copy-done.2
  23.7 1.2 copy-done.4
  24.9 0.9 turn_kernel.1
  25.9 0.8 collective-permute-done.2.x3
  26.7 3.0 %collective-permute-start.5 = (bf16[128,768]{1,0:T(8,128)(2,1)S(1)}, bf16[128,768]{1,0:T(8,128)(2,1)S(1)}, u32[]{:S(2)}, u32[]{:S(2)}) collective-permute-start(bf16[128,768]{1,0:T(8,128)(2,1)S(1)} %copy-done.6), channel_id=1, source_target_pairs={{0,2},{1,3},{2,0},{3,1},{4,6},{5,7},{6,4},{7,5},{8,10},{9,11},{10,... | collective-permute-start | bytes 589832 | tf_op jit(solution)/shard_map/dy/ppermute | solution.py:690
  29.7 1.7 %collective-permute-start.4 = (bf16[128,768]{1,0:T(8,128)(2,1)S(1)}, bf16[128,768]{1,0:T(8,128)(2,1)S(1)}, u32[]{:S(2)}, u32[]{:S(2)}) collective-permute-start(bf16[128,768]{1,0:T(8,128)(2,1)S(1)} %copy-done.6), channel_id=1, source_target_pairs={{0,1},{1,0},{2,3},{3,2},{4,5},{5,4},{6,7},{7,6},{8,9},{9,8},{10,11... | collective-permute-start | bytes 589832 | tf_op jit(solution)/shard_map/dy/ppermute | solution.py:690
  31.5 1.6 %collective-permute-start.3 = (bf16[4,48,768]{2,1,0:T(8,128)(2,1)S(1)}, bf16[4,48,768]{2,1,0:T(8,128)(2,1)S(1)}, u32[]{:S(2)}, u32[]{:S(2)}) collective-permute-start(bf16[4,48,768]{2,1,0:T(8,128)(2,1)S(1)} %pieces_kernel.1.a), channel_id=1, source_target_pairs={{0,8},{4,12},{8,0},{12,4},{16,24},{20,28},{24,16},{28,20},{1,9},{5... | collective-permute-start | bytes 884744 | tf_op jit(solution)/shard_map/w/ppermute | solution.py:690
  33.0 4.7 %head_kernel.1 = (bf16[768,512]{1,0:T(8,128)(2,1)S(1)}, bf16[768,512]{1,0:T(8,128)(2,1)S(1)}, f32[8,512]{1,0:T(8,128)S(1)}, bf16[576,512]{1,0:T(8,128)(2,1)S(1)}...) custom-call(s32[2]{0:T(128)S(1)} %pad_add_fusion.place, ...), custom_call_target="tpu_custom_call" | custom-call | flops 11500000256 | bytes 8 | tf_op jit(solution)/shard_map/head_kernel/pallas_call | solution.py:21
  37.8 0.8 collective-permute-done.5.c2
  38.6 0.4 collective-permute-done.4.c1
  39.2 1.3 %collective-permute-start.6 = (bf16[192,512]{1,0:T(8,128)(2,1)S(1)}, bf16[192,512]{1,0:T(8,128)(2,1)S(1)}, u32[]{:S(2)}, u32[]{:S(2)}) collective-permute-start(bf16[192,512]{1,0:T(8,128)(2,1)S(1)} %get-tuple-element.116.a0), channel_id=1, source_target_pairs={{0,1},{1,0},{2,3},{3,2},{4,5},{5,4},{6,7},{7,6},{8,9},{9,8},{10,11... | collective-permute-start | bytes 589832 | tf_op jit(solution)/shard_map/att/ppermute | solution.py:690
  40.5 2.3 %collective-permute-start.7 = (bf16[96,512]{1,0:T(8,128)(2,1)S(1)}, bf16[96,512]{1,0:T(8,128)(2,1)S(1)}, u32[]{:S(2)}, u32[]{:S(2)}) collective-permute-start(bf16[96,512]{1,0:T(8,128)(2,1)S(1)} %get-tuple-element.118), channel_id=1, source_target_pairs={{0,2},{1,3},{2,0},{3,1},{4,6},{5,7},{6,4},{7,5},{8,10},{9,11},{10,... | collective-permute-start | bytes 294920 | tf_op jit(solution)/shard_map/att/ppermute | solution.py:690
  42.7 0.9 collective-permute-start.10
  43.6 0.6 collective-permute-start.8
  44.3 3.5 %collective-permute-done.7.a2t = bf16[96,512]{1,0:T(8,128)(2,1)S(1)} collective-permute-done((bf16[96,512]{1,0:T(8,128)(2,1)S(1)}, bf16[96,512]{1,0:T(8,128)(2,1)S(1)}, u32[]{:S(2)}, u32[]{:S(2)}) %collective-permute-start.7) | collective-permute-done | bytes 98336 | tf_op jit(solution)/shard_map/att/ppermute | solution.py:690
  47.8 2.9 %collective-permute-start.9 = (bf16[96,512]{1,0:T(8,128)(2,1)S(1)}, bf16[96,512]{1,0:T(8,128)(2,1)S(1)}, u32[]{:S(2)}, u32[]{:S(2)}) collective-permute-start(bf16[96,512]{1,0:T(8,128)(2,1)S(1)} %collective-permute-done.7.a2t), channel_id=1, source_target_pairs={{0,1},{1,0},{2,3},{3,2},{4,5},{5,4},{6,7},{7,6},{8,9},{9,8},{10,11... | collective-permute-start | bytes 294920 | tf_op jit(solution)/shard_map/att/ppermute | solution.py:690
  50.7 1.0 out_weight_kernel.1
  51.7 0.5 collective-permute-done.10.a3b
  52.2 4.7 %collective-permute-done.8.a2b = bf16[96,512]{1,0:T(8,128)(2,1)S(1)} collective-permute-done((bf16[96,512]{1,0:T(8,128)(2,1)S(1)}, bf16[96,512]{1,0:T(8,128)(2,1)S(1)}, u32[]{:S(2)}, u32[]{:S(2)}) %collective-permute-start.8) | collective-permute-done | bytes 98336 | tf_op jit(solution)/shard_map/att/ppermute | solution.py:690
  56.9 4.1 %up_kernel.1 = (bf16[768,512]{1,0:T(8,128)(2,1)S(1)}, f32[768,512]{1,0:T(8,128)S(1)}, f32[768,512]{1,0:T(8,128)S(1)}, f32[8,512]{1,0:T(8,128)S(1)}, bf16[768,512...) custom-call(s32[2]{0:T(128)S(1)} %pad_add_fusion.place, ...), custom_call_target="tpu_custom_call" | custom-call | flops 11500000256 | bytes 8 | tf_op jit(solution)/shard_map/up_kernel/pallas_call | solution.py:21
  61.2 4.6 %down_kernel.1 = (bf16[192,512]{1,0:T(8,128)(2,1)S(1)}, bf16[192,512]{1,0:T(8,128)(2,1)S(1)}, bf16[192,512]{1,0:T(8,128)(2,1)S(1)}, bf16[192,512]{1,0:T(8,128)(2...) custom-call(s32[2]{0:T(128)S(1)} %pad_add_fusion.place, ...), custom_call_target="tpu_custom_call" | custom-call | flops 11500000256 | bytes 8 | tf_op jit(solution)/shard_map/down_kernel/pallas_call | solution.py:21
  65.8 2.0 %collective-permute-start.14 = (bf16[192,512]{1,0:T(8,128)(2,1)S(1)}, bf16[192,512]{1,0:T(8,128)(2,1)S(1)}, u32[]{:S(2)}, u32[]{:S(2)}) collective-permute-start(bf16[192,512]{1,0:T(8,128)(2,1)S(1)} %get-tuple-element.135), channel_id=1, source_target_pairs={{0,1},{1,0},{2,3},{3,2},{4,5},{5,4},{6,7},{7,6},{8,9},{9,8},{10,11... | collective-permute-start | bytes 589832 | tf_op jit(solution)/shard_map/d_att/ppermute | solution.py:690
  67.9 0.6 collective-permute-start.15
  68.5 1.8 %collective-permute-start.16 = (bf16[192,512]{1,0:T(8,128)(2,1)S(1)}, bf16[192,512]{1,0:T(8,128)(2,1)S(1)}, u32[]{:S(2)}, u32[]{:S(2)}) collective-permute-start(bf16[192,512]{1,0:T(8,128)(2,1)S(1)} %get-tuple-element.137), channel_id=1, source_target_pairs={{0,3},{1,2},{2,1},{3,0},{4,7},{5,6},{6,5},{7,4},{8,11},{9,10},{10,... | collective-permute-start | bytes 589832 | tf_op jit(solution)/shard_map/d_att/ppermute | solution.py:690
  70.3 2.6 %mlp_grad_kernel.1 = (f32[8,768]{1,0:T(8,128)S(1)}, bf16[384,1152]{1,0:T(8,128)(2,1)S(1)}, bf16[384,1152]{1,0:T(8,128)(2,1)S(1)}, bf16[384,1152]{1,0:T(8,128)(2,1)S(1)}, bf16[384,1152]{1,0:T(8,128)(2,1)S(1)}) custom-call(s32[2]{0:T(128)S(1)} %pad_add_fusion.place, f32[8,768]{1,0:T(8,128)S(1)} %get-tuple-element.146.vec, ...), custom_call_target="tpu_custom_call" | custom-call | flops 11500000 | bytes 8 | tf_op jit(solution)/shard_map/mlp_grad_kernel/pallas_call | solution.py:21
  72.9 1.6 %collective-permute-start.21 = (bf16[384,1152]{1,0:T(8,128)(2,1)S(1)}, bf16[384,1152]{1,0:T(8,128)(2,1)S(1)}, u32[]{:S(2)}, u32[]{:S(2)}) collective-permute-start(bf16[384,1152]{1,0:T(8,128)(2,1)S(1)} %get-tuple-element.169), channel_id=1, source_target_pairs={{0,8},{4,12},{8,0},{12,4},{16,24},{20,28},{24,16},{28,20},{1,9},{5... | collective-permute-start | bytes 2654216 | tf_op jit(solution)/shard_map/grads_a/ppermute | solution.py:690
  74.5 2.6 %collective-permute-done.12.recv = bf16[1536,128]{1,0:T(8,128)(2,1)S(1)} collective-permute-done((bf16[1536,128]{1,0:T(8,128)(2,1)S(1)}, bf16[1536,128]{1,0:T(8,128)(2,1)S(1)}, u32[]{:S(2)}, u32[]{:S(2)}) %collective-permute-start.12) | collective-permute-done | bytes 393248 | tf_op jit(solution)/shard_map/mlp/ppermute | solution.py:690
  77.1 1.5 %collective-permute-start.22 = (bf16[384,1152]{1,0:T(8,128)(2,1)S(1)}, bf16[384,1152]{1,0:T(8,128)(2,1)S(1)}, u32[]{:S(2)}, u32[]{:S(2)}) collective-permute-start(bf16[384,1152]{1,0:T(8,128)(2,1)S(1)} %get-tuple-element.171), channel_id=1, source_target_pairs={{0,16},{4,20},{8,24},{12,28},{16,0},{20,4},{24,8},{28,12},{1,17},{... | collective-permute-start | bytes 2654216 | tf_op jit(solution)/shard_map/grads_b/ppermute | solution.py:690
  78.7 1.3 %collective-permute-done.14.d1 = bf16[192,512]{1,0:T(8,128)(2,1)S(1)} collective-permute-done((bf16[192,512]{1,0:T(8,128)(2,1)S(1)}, bf16[192,512]{1,0:T(8,128)(2,1)S(1)}, u32[]{:S(2)}, u32[]{:S(2)}) %collective-permute-start.14) | collective-permute-done | bytes 196640 | tf_op jit(solution)/shard_map/d_att/ppermute | solution.py:690
  80.0 4.8 %collective-permute-done.15.d2 = bf16[192,512]{1,0:T(8,128)(2,1)S(1)} collective-permute-done((bf16[192,512]{1,0:T(8,128)(2,1)S(1)}, bf16[192,512]{1,0:T(8,128)(2,1)S(1)}, u32[]{:S(2)}, u32[]{:S(2)}) %collective-permute-start.15) | collective-permute-done | bytes 196640 | tf_op jit(solution)/shard_map/d_att/ppermute | solution.py:690
  84.8 4.4 %collective-permute-start.17 = (bf16[768,128]{1,0:T(8,128)(2,1)S(1)}, bf16[768,128]{1,0:T(8,128)(2,1)S(1)}, u32[]{:S(2)}, u32[]{:S(2)}) collective-permute-start(bf16[768,128]{1,0:T(8,128)(2,1)S(1)} %get-tuple-element.138), channel_id=1, source_target_pairs={{0,2},{1,3},{2,0},{3,1},{4,6},{5,7},{6,4},{7,5},{8,10},{9,11},{10,... | collective-permute-start | bytes 589832 | tf_op jit(solution)/shard_map/mlp/ppermute | solution.py:690
  89.2 6.5 %back_kernel.1 = (f32[768,128]{1,0:T(8,128)S(1)}, f32[768,128]{1,0:T(8,128)S(1)}, bf16[1536,128]{1,0:T(8,128)(2,1)S(1)}, f32[8,768]{1,0:T(8,128)S(1)}, bf16[416,...) custom-call(s32[2]{0:T(128)S(1)} %pad_add_fusion.place, s32[1,8]{1,0:T(1,128)S(1)} %copy-done.7, ...), custom_call_target="tpu_custom_call" | custom-call | flops 11500000256 | bytes 8 | tf_op jit(solution)/shard_map/back_kernel/pallas_call | solution.py:21
  95.8 1.8 %collective-permute-done.20.recv = bf16[416,576]{1,0:T(8,128)(2,1)S(1)} collective-permute-done((bf16[416,576]{1,0:T(8,128)(2,1)S(1)}, bf16[416,576]{1,0:T(8,128)(2,1)S(1)}, u32[]{:S(2)}, u32[]{:S(2)}) %collective-permute-start.20) | collective-permute-done | bytes 479264 | tf_op jit(solution)/shard_map/qkv_core/ppermute | solution.py:690
  97.7 0.7 qkv_second_kernel.1
  98.4 1.0 grads_second_kernel.1
  100.1 1.5 %collective-permute-start.26 = (bf16[224,576]{1,0:T(8,128)(2,1)S(1)}, bf16[224,576]{1,0:T(8,128)(2,1)S(1)}, u32[]{:S(2)}, u32[]{:S(2)}) collective-permute-start(bf16[224,576]{1,0:T(8,128)(2,1)S(1)} %get-tuple-element.179), channel_id=1, source_target_pairs={{0,8},{4,12},{8,0},{12,4},{16,24},{20,28},{24,16},{28,20},{1,9},{5... | collective-permute-start | bytes 774152 | tf_op jit(solution)/shard_map/qkv_x/ppermute | solution.py:690
  101.9 0.7 grads_third_kernel.1
  102.6 1.5 %collective-permute-start.27 = (bf16[96,1152]{1,0:T(8,128)(2,1)S(1)}, bf16[96,1152]{1,0:T(8,128)(2,1)S(1)}, u32[]{:S(2)}, u32[]{:S(2)}) collective-permute-start(bf16[96,1152]{1,0:T(8,128)(2,1)S(1)} %get-tuple-element.182), channel_id=1, source_target_pairs={{0,8},{4,12},{8,0},{12,4},{16,24},{20,28},{24,16},{28,20},{1,9},{5... | collective-permute-start | bytes 663560 | tf_op jit(solution)/shard_map/grads_b/ppermute | solution.py:690
  104.1 3.2 %collective-permute-done.18.recv = bf16[1536,128]{1,0:T(8,128)(2,1)S(1)} collective-permute-done((bf16[1536,128]{1,0:T(8,128)(2,1)S(1)}, bf16[1536,128]{1,0:T(8,128)(2,1)S(1)}, u32[]{:S(2)}, u32[]{:S(2)}) %collective-permute-start.18) | collective-permute-done | bytes 393248 | tf_op jit(solution)/shard_map/back/ppermute | solution.py:690
  107.4 0.7 collective-permute-start.19
  108.1 1.6 %collective-permute-done.26.recv = bf16[224,576]{1,0:T(8,128)(2,1)S(1)} collective-permute-done((bf16[224,576]{1,0:T(8,128)(2,1)S(1)}, bf16[224,576]{1,0:T(8,128)(2,1)S(1)}, u32[]{:S(2)}, u32[]{:S(2)}) %collective-permute-start.26) | collective-permute-done | bytes 258080 | tf_op jit(solution)/shard_map/qkv_x/ppermute | solution.py:690
  109.7 0.6 qkv_third_kernel.1
  110.3 1.6 %collective-permute-start.28 = (bf16[128,576]{1,0:T(8,128)(2,1)S(1)}, bf16[128,576]{1,0:T(8,128)(2,1)S(1)}, u32[]{:S(2)}, u32[]{:S(2)}) collective-permute-start(bf16[128,576]{1,0:T(8,128)(2,1)S(1)} %get-tuple-element.183), channel_id=1, source_target_pairs={{0,16},{4,20},{8,24},{12,28},{16,0},{20,4},{24,8},{28,12},{1,17},{... | collective-permute-start | bytes 442376 | tf_op jit(solution)/shard_map/qkv_y/ppermute | solution.py:690
  111.9 0.9 output_kernel.1
  112.9 0.5 collective-permute-start.32
  113.4 3.9 %collective-permute-done.28.q_recv = bf16[128,576]{1,0:T(8,128)(2,1)S(1)} collective-permute-done((bf16[128,576]{1,0:T(8,128)(2,1)S(1)}, bf16[128,576]{1,0:T(8,128)(2,1)S(1)}, u32[]{:S(2)}, u32[]{:S(2)}) %collective-permute-start.28) | collective-permute-done | bytes 147488 | tf_op jit(solution)/shard_map/qkv_y/ppermute | solution.py:690
  117.3 0.7 message_kernel.1
  118.0 0.7 collective-permute-start.30
  118.7 1.9 %collective-permute-start.31 = (bf16[288,128]{1,0:T(8,128)(2,1)S(1)}, bf16[288,128]{1,0:T(8,128)(2,1)S(1)}, u32[]{:S(2)}, u32[]{:S(2)}) collective-permute-start(bf16[288,128]{1,0:T(8,128)(2,1)S(1)} %get-tuple-element.188), channel_id=1, source_target_pairs={{0,3},{1,2},{2,1},{3,0},{4,7},{5,6},{6,5},{7,4},{8,11},{9,10},{10,... | collective-permute-start | bytes 221192 | tf_op jit(solution)/shard_map/out/ppermute | solution.py:690
  120.7 0.9 collective-permute-start.29
  121.6 0.9 input_kernel.1
  122.5 1.0 last_kernel.1
  123.8 1.3 %collective-permute-done.31.o3 = bf16[288,128]{1,0:T(8,128)(2,1)S(1)} collective-permute-done((bf16[288,128]{1,0:T(8,128)(2,1)S(1)}, bf16[288,128]{1,0:T(8,128)(2,1)S(1)}, u32[]{:S(2)}, u32[]{:S(2)}) %collective-permute-start.31) | collective-permute-done | bytes 73760 | tf_op jit(solution)/shard_map/out/ppermute | solution.py:690
  125.1 0.7 collective-permute-done.29.o1
  125.8 0.7 small_kernel.1
  (45 shorter events, 2.5 us)
Async XLA Ops:
  0.6 1.0 copy-start
  0.7 21.8 %copy-start.1 = (bf16[768,768]{1,0:T(8,128)(2,1)S(1)}, bf16[768,768]{1,0:T(8,128)(2,1)}, u32[]{:S(2)}) copy-start(bf16[768,768]{1,0:T(8,128)(2,1)} %w_up.1) | copy-start | bytes 3538948
  2.6 16.5 %collective-permute-start.1 = (bf16[176,768]{1,0:T(8,128)(2,1)S(1)}, bf16[176,768]{1,0:T(8,128)(2,1)S(1)}, u32[]{:S(2)}, u32[]{:S(2)}) collective-permute-start(bf16[176,768]{1,0:T(8,128)(2,1)S(1)} %pad_maximum_fusion.x0), channel_id=1, source_target_pairs={{0,2},{1,3},{2,0},{3,1},{4,6},{5,7},{6,4},{7,5},{8,10},{9,11},{10,... | collective-permute-start | bytes 811016 | tf_op jit(solution)/shard_map/x/ppermute | solution.py:690
  6.7 12.6 %collective-permute-start = (bf16[176,768]{1,0:T(8,128)(2,1)S(1)}, bf16[176,768]{1,0:T(8,128)(2,1)S(1)}, u32[]{:S(2)}, u32[]{:S(2)}) collective-permute-start(bf16[176,768]{1,0:T(8,128)(2,1)S(1)} %pad_maximum_fusion.x0), channel_id=1, source_target_pairs={{0,1},{1,0},{2,3},{3,2},{4,5},{5,4},{6,7},{7,6},{8,9},{9,8},{10,11... | collective-permute-start | bytes 811016 | tf_op jit(solution)/shard_map/x/ppermute | solution.py:690
  19.2 7.4 %collective-permute-start.2 = (bf16[176,768]{1,0:T(8,128)(2,1)S(1)}, bf16[176,768]{1,0:T(8,128)(2,1)S(1)}, u32[]{:S(2)}, u32[]{:S(2)}) collective-permute-start(bf16[176,768]{1,0:T(8,128)(2,1)S(1)} %collective-permute-done.1.x2), channel_id=1, source_target_pairs={{0,1},{1,0},{2,3},{3,2},{4,5},{5,4},{6,7},{7,6},{8,9},{9,8},{10,11... | collective-permute-start | bytes 811016 | tf_op jit(solution)/shard_map/x/ppermute | solution.py:690
  22.4 1.3 %copy-start.2 = (bf16[768,768]{1,0:T(8,128)(2,1)S(1)}, bf16[768,768]{1,0:T(8,128)(2,1)}, u32[]{:S(2)}) copy-start(bf16[768,768]{1,0:T(8,128)(2,1)} %w_down.1) | copy-start | bytes 3538948
  23.7 1.2 copy-start.4
  24.9 1.8 %copy-start.6 = (bf16[128,768]{1,0:T(8,128)(2,1)S(1)}, bf16[128,768]{1,0:T(8,128)(2,1)}, u32[]{:S(2)}) copy-start(bf16[128,768]{1,0:T(8,128)(2,1)} %dy.1) | copy-start | bytes 589828
  24.9 8.2 %copy-start.5 = (bf16[768,3,192]{0,2,1:T(8,128)(2,1)S(1)}, bf16[768,3,192]{0,2,1:T(8,128)(2,1)}, u32[]{:S(2)}) copy-start(bf16[768,3,192]{0,2,1:T(8,128)(2,1)} %param.16) | copy-start | bytes 2654212
  24.9 8.2 %copy-start.7 = (s32[1,8]{1,0:T(1,128)S(1)}, s32[1,8]{1,0:T(1,128)}, u32[]{:S(2)}) copy-start(s32[1,8]{1,0:T(1,128)} %lengths.3) | copy-start | bytes 100
  26.7 11.9 %collective-permute-start.5 = (bf16[128,768]{1,0:T(8,128)(2,1)S(1)}, bf16[128,768]{1,0:T(8,128)(2,1)S(1)}, u32[]{:S(2)}, u32[]{:S(2)}) collective-permute-start(bf16[128,768]{1,0:T(8,128)(2,1)S(1)} %copy-done.6), channel_id=1, source_target_pairs={{0,2},{1,3},{2,0},{3,1},{4,6},{5,7},{6,4},{7,5},{8,10},{9,11},{10,... | collective-permute-start | bytes 589832 | tf_op jit(solution)/shard_map/dy/ppermute | solution.py:690
  29.7 9.3 %collective-permute-start.4 = (bf16[128,768]{1,0:T(8,128)(2,1)S(1)}, bf16[128,768]{1,0:T(8,128)(2,1)S(1)}, u32[]{:S(2)}, u32[]{:S(2)}) collective-permute-start(bf16[128,768]{1,0:T(8,128)(2,1)S(1)} %copy-done.6), channel_id=1, source_target_pairs={{0,1},{1,0},{2,3},{3,2},{4,5},{5,4},{6,7},{7,6},{8,9},{9,8},{10,11... | collective-permute-start | bytes 589832 | tf_op jit(solution)/shard_map/dy/ppermute | solution.py:690
  31.5 7.6 %collective-permute-start.3 = (bf16[4,48,768]{2,1,0:T(8,128)(2,1)S(1)}, bf16[4,48,768]{2,1,0:T(8,128)(2,1)S(1)}, u32[]{:S(2)}, u32[]{:S(2)}) collective-permute-start(bf16[4,48,768]{2,1,0:T(8,128)(2,1)S(1)} %pieces_kernel.1.a), channel_id=1, source_target_pairs={{0,8},{4,12},{8,0},{12,4},{16,24},{20,28},{24,16},{28,20},{1,9},{5... | collective-permute-start | bytes 884744 | tf_op jit(solution)/shard_map/w/ppermute | solution.py:690
  39.1 11.6 %collective-permute-start.11 = (bf16[8,48,768]{2,1,0:T(8,128)(2,1)S(1)}, bf16[8,48,768]{2,1,0:T(8,128)(2,1)S(1)}, u32[]{:S(2)}, u32[]{:S(2)}) collective-permute-start(bf16[8,48,768]{2,1,0:T(8,128)(2,1)S(1)} %pair_kernel.1.here), channel_id=1, source_target_pairs={{0,4},{4,0},{8,12},{12,8},{16,20},{20,16},{24,28},{28,24},{1,5},{5... | collective-permute-start | bytes 1769480 | tf_op jit(solution)/shard_map/w/ppermute | solution.py:690
  39.2 17.7 %collective-permute-start.6 = (bf16[192,512]{1,0:T(8,128)(2,1)S(1)}, bf16[192,512]{1,0:T(8,128)(2,1)S(1)}, u32[]{:S(2)}, u32[]{:S(2)}) collective-permute-start(bf16[192,512]{1,0:T(8,128)(2,1)S(1)} %get-tuple-element.116.a0), channel_id=1, source_target_pairs={{0,1},{1,0},{2,3},{3,2},{4,5},{5,4},{6,7},{7,6},{8,9},{9,8},{10,11... | collective-permute-start | bytes 589832 | tf_op jit(solution)/shard_map/att/ppermute | solution.py:690
  40.5 7.4 %collective-permute-start.7 = (bf16[96,512]{1,0:T(8,128)(2,1)S(1)}, bf16[96,512]{1,0:T(8,128)(2,1)S(1)}, u32[]{:S(2)}, u32[]{:S(2)}) collective-permute-start(bf16[96,512]{1,0:T(8,128)(2,1)S(1)} %get-tuple-element.118), channel_id=1, source_target_pairs={{0,2},{1,3},{2,0},{3,1},{4,6},{5,7},{6,4},{7,5},{8,10},{9,11},{10,... | collective-permute-start | bytes 294920 | tf_op jit(solution)/shard_map/att/ppermute | solution.py:690
  42.7 9.5 %collective-permute-start.10 = (bf16[96,512]{1,0:T(8,128)(2,1)S(1)}, bf16[96,512]{1,0:T(8,128)(2,1)S(1)}, u32[]{:S(2)}, u32[]{:S(2)}) collective-permute-start(bf16[96,512]{1,0:T(8,128)(2,1)S(1)} %get-tuple-element.120), channel_id=1, source_target_pairs={{0,3},{1,2},{2,1},{3,0},{4,7},{5,6},{6,5},{7,4},{8,11},{9,10},{10,... | collective-permute-start | bytes 294920 | tf_op jit(solution)/shard_map/att/ppermute | solution.py:690
  43.6 13.3 %collective-permute-start.8 = (bf16[96,512]{1,0:T(8,128)(2,1)S(1)}, bf16[96,512]{1,0:T(8,128)(2,1)S(1)}, u32[]{:S(2)}, u32[]{:S(2)}) collective-permute-start(bf16[96,512]{1,0:T(8,128)(2,1)S(1)} %get-tuple-element.120), channel_id=1, source_target_pairs={{0,2},{1,3},{2,0},{3,1},{4,6},{5,7},{6,4},{7,5},{8,10},{9,11},{10,... | collective-permute-start | bytes 294920 | tf_op jit(solution)/shard_map/att/ppermute | solution.py:690
  47.8 9.1 %collective-permute-start.9 = (bf16[96,512]{1,0:T(8,128)(2,1)S(1)}, bf16[96,512]{1,0:T(8,128)(2,1)S(1)}, u32[]{:S(2)}, u32[]{:S(2)}) collective-permute-start(bf16[96,512]{1,0:T(8,128)(2,1)S(1)} %collective-permute-done.7.a2t), channel_id=1, source_target_pairs={{0,1},{1,0},{2,3},{3,2},{4,5},{5,4},{6,7},{7,6},{8,9},{9,8},{10,11... | collective-permute-start | bytes 294920 | tf_op jit(solution)/shard_map/att/ppermute | solution.py:690
  50.7 10.4 %collective-permute-start.13 = (bf16[128,768]{1,0:T(8,128)(2,1)S(1)}, bf16[128,768]{1,0:T(8,128)(2,1)S(1)}, u32[]{:S(2)}, u32[]{:S(2)}) collective-permute-start(bf16[128,768]{1,0:T(8,128)(2,1)S(1)} %collective-permute-done.5.c2), channel_id=1, source_target_pairs={{0,1},{1,0},{2,3},{3,2},{4,5},{5,4},{6,7},{7,6},{8,9},{9,8},{10,11... | collective-permute-start | bytes 589832 | tf_op jit(solution)/shard_map/dy/ppermute | solution.py:690
  56.9 4.2 %copy-start.3 = (bf16[768,768]{1,0:T(8,128)(2,1)S(1)}, bf16[768,768]{1,0:T(8,128)(2,1)}, u32[]{:S(2)}) copy-start(bf16[768,768]{1,0:T(8,128)(2,1)} %w_down.1) | copy-start | bytes 3538948
  61.1 16.0 %collective-permute-start.12 = (bf16[1536,128]{1,0:T(8,128)(2,1)S(1)}, bf16[1536,128]{1,0:T(8,128)(2,1)S(1)}, u32[]{:S(2)}, u32[]{:S(2)}) collective-permute-start(bf16[1536,128]{1,0:T(8,128)(2,1)S(1)} %get-tuple-element.126), channel_id=1, source_target_pairs={{0,1},{1,0},{2,3},{3,2},{4,5},{5,4},{6,7},{7,6},{8,9},{9,8},{10,11... | collective-permute-start | bytes 1179656 | tf_op jit(solution)/shard_map/mlp/ppermute | solution.py:690
  65.8 14.2 %collective-permute-start.14 = (bf16[192,512]{1,0:T(8,128)(2,1)S(1)}, bf16[192,512]{1,0:T(8,128)(2,1)S(1)}, u32[]{:S(2)}, u32[]{:S(2)}) collective-permute-start(bf16[192,512]{1,0:T(8,128)(2,1)S(1)} %get-tuple-element.135), channel_id=1, source_target_pairs={{0,1},{1,0},{2,3},{3,2},{4,5},{5,4},{6,7},{7,6},{8,9},{9,8},{10,11... | collective-permute-start | bytes 589832 | tf_op jit(solution)/shard_map/d_att/ppermute | solution.py:690
  67.9 17.0 %collective-permute-start.15 = (bf16[192,512]{1,0:T(8,128)(2,1)S(1)}, bf16[192,512]{1,0:T(8,128)(2,1)S(1)}, u32[]{:S(2)}, u32[]{:S(2)}) collective-permute-start(bf16[192,512]{1,0:T(8,128)(2,1)S(1)} %get-tuple-element.136), channel_id=1, source_target_pairs={{0,2},{1,3},{2,0},{3,1},{4,6},{5,7},{6,4},{7,5},{8,10},{9,11},{10,... | collective-permute-start | bytes 589832 | tf_op jit(solution)/shard_map/d_att/ppermute | solution.py:690
  68.5 16.4 %collective-permute-start.16 = (bf16[192,512]{1,0:T(8,128)(2,1)S(1)}, bf16[192,512]{1,0:T(8,128)(2,1)S(1)}, u32[]{:S(2)}, u32[]{:S(2)}) collective-permute-start(bf16[192,512]{1,0:T(8,128)(2,1)S(1)} %get-tuple-element.137), channel_id=1, source_target_pairs={{0,3},{1,2},{2,1},{3,0},{4,7},{5,6},{6,5},{7,4},{8,11},{9,10},{10,... | collective-permute-start | bytes 589832 | tf_op jit(solution)/shard_map/d_att/ppermute | solution.py:690
  72.9 25.5 %collective-permute-start.21 = (bf16[384,1152]{1,0:T(8,128)(2,1)S(1)}, bf16[384,1152]{1,0:T(8,128)(2,1)S(1)}, u32[]{:S(2)}, u32[]{:S(2)}) collective-permute-start(bf16[384,1152]{1,0:T(8,128)(2,1)S(1)} %get-tuple-element.169), channel_id=1, source_target_pairs={{0,8},{4,12},{8,0},{12,4},{16,24},{20,28},{24,16},{28,20},{1,9},{5... | collective-permute-start | bytes 2654216 | tf_op jit(solution)/shard_map/grads_a/ppermute | solution.py:690
  77.1 21.3 %collective-permute-start.22 = (bf16[384,1152]{1,0:T(8,128)(2,1)S(1)}, bf16[384,1152]{1,0:T(8,128)(2,1)S(1)}, u32[]{:S(2)}, u32[]{:S(2)}) collective-permute-start(bf16[384,1152]{1,0:T(8,128)(2,1)S(1)} %get-tuple-element.171), channel_id=1, source_target_pairs={{0,16},{4,20},{8,24},{12,28},{16,0},{20,4},{24,8},{28,12},{1,17},{... | collective-permute-start | bytes 2654216 | tf_op jit(solution)/shard_map/grads_b/ppermute | solution.py:690
  84.8 10.8 %collective-permute-start.17 = (bf16[768,128]{1,0:T(8,128)(2,1)S(1)}, bf16[768,128]{1,0:T(8,128)(2,1)S(1)}, u32[]{:S(2)}, u32[]{:S(2)}) collective-permute-start(bf16[768,128]{1,0:T(8,128)(2,1)S(1)} %get-tuple-element.138), channel_id=1, source_target_pairs={{0,2},{1,3},{2,0},{3,1},{4,6},{5,7},{6,4},{7,5},{8,10},{9,11},{10,... | collective-permute-start | bytes 589832 | tf_op jit(solution)/shard_map/mlp/ppermute | solution.py:690
  95.7 2.0 %collective-permute-start.20 = (bf16[416,576]{1,0:T(8,128)(2,1)S(1)}, bf16[416,576]{1,0:T(8,128)(2,1)S(1)}, u32[]{:S(2)}, u32[]{:S(2)}) collective-permute-start(bf16[416,576]{1,0:T(8,128)(2,1)S(1)} %get-tuple-element.165), channel_id=1, source_target_pairs={{0,4},{4,0},{8,12},{12,8},{16,20},{20,16},{24,28},{28,24},{1,5},{5... | collective-permute-start | bytes 1437704 | tf_op jit(solution)/shard_map/qkv_core/ppermute | solution.py:690
  95.8 11.5 %collective-permute-start.18 = (bf16[1536,128]{1,0:T(8,128)(2,1)S(1)}, bf16[1536,128]{1,0:T(8,128)(2,1)S(1)}, u32[]{:S(2)}, u32[]{:S(2)}) collective-permute-start(bf16[1536,128]{1,0:T(8,128)(2,1)S(1)} %get-tuple-element.159), channel_id=1, source_target_pairs={{0,1},{1,0},{2,3},{3,2},{4,5},{5,4},{6,7},{7,6},{8,9},{9,8},{10,11... | collective-permute-start | bytes 1179656 | tf_op jit(solution)/shard_map/back/ppermute | solution.py:690
  99.4 2.2 %collective-permute-start.23 = (bf16[192,768]{1,0:T(8,128)(2,1)S(1)}, bf16[192,768]{1,0:T(8,128)(2,1)S(1)}, u32[]{:S(2)}, u32[]{:S(2)}) collective-permute-start(bf16[192,768]{1,0:T(8,128)(2,1)S(1)} %get-tuple-element.173), channel_id=1, source_target_pairs={{0,4},{4,0},{8,12},{12,8},{16,20},{20,16},{24,28},{28,24},{1,5},{5... | collective-permute-start | bytes 884744 | tf_op jit(solution)/shard_map/grads_core/ppermute | solution.py:690
  99.6 2.0 %collective-permute-start.24 = (bf16[192,768]{1,0:T(8,128)(2,1)S(1)}, bf16[192,768]{1,0:T(8,128)(2,1)S(1)}, u32[]{:S(2)}, u32[]{:S(2)}) collective-permute-start(bf16[192,768]{1,0:T(8,128)(2,1)S(1)} %get-tuple-element.174), channel_id=1, source_target_pairs={{0,4},{4,0},{8,12},{12,8},{16,20},{20,16},{24,28},{28,24},{1,5},{5... | collective-permute-start | bytes 884744 | tf_op jit(solution)/shard_map/grads_core/ppermute | solution.py:690
  99.9 1.9 %collective-permute-start.25 = (bf16[192,768]{1,0:T(8,128)(2,1)S(1)}, bf16[192,768]{1,0:T(8,128)(2,1)S(1)}, u32[]{:S(2)}, u32[]{:S(2)}) collective-permute-start(bf16[192,768]{1,0:T(8,128)(2,1)S(1)} %get-tuple-element.175), channel_id=1, source_target_pairs={{0,4},{4,0},{8,12},{12,8},{16,20},{20,16},{24,28},{28,24},{1,5},{5... | collective-permute-start | bytes 884744 | tf_op jit(solution)/shard_map/grads_core/ppermute | solution.py:690
  100.1 9.7 %collective-permute-start.26 = (bf16[224,576]{1,0:T(8,128)(2,1)S(1)}, bf16[224,576]{1,0:T(8,128)(2,1)S(1)}, u32[]{:S(2)}, u32[]{:S(2)}) collective-permute-start(bf16[224,576]{1,0:T(8,128)(2,1)S(1)} %get-tuple-element.179), channel_id=1, source_target_pairs={{0,8},{4,12},{8,0},{12,4},{16,24},{20,28},{24,16},{28,20},{1,9},{5... | collective-permute-start | bytes 774152 | tf_op jit(solution)/shard_map/qkv_x/ppermute | solution.py:690
  102.6 14.7 %collective-permute-start.27 = (bf16[96,1152]{1,0:T(8,128)(2,1)S(1)}, bf16[96,1152]{1,0:T(8,128)(2,1)S(1)}, u32[]{:S(2)}, u32[]{:S(2)}) collective-permute-start(bf16[96,1152]{1,0:T(8,128)(2,1)S(1)} %get-tuple-element.182), channel_id=1, source_target_pairs={{0,8},{4,12},{8,0},{12,4},{16,24},{20,28},{24,16},{28,20},{1,9},{5... | collective-permute-start | bytes 663560 | tf_op jit(solution)/shard_map/grads_b/ppermute | solution.py:690
  107.4 14.2 %collective-permute-start.19 = (bf16[768,128]{1,0:T(8,128)(2,1)S(1)}, bf16[768,128]{1,0:T(8,128)(2,1)S(1)}, u32[]{:S(2)}, u32[]{:S(2)}) collective-permute-start(bf16[768,128]{1,0:T(8,128)(2,1)S(1)} %get-tuple-element.161), channel_id=1, source_target_pairs={{0,2},{1,3},{2,0},{3,1},{4,6},{5,7},{6,4},{7,5},{8,10},{9,11},{10,... | collective-permute-start | bytes 589832 | tf_op jit(solution)/shard_map/back/ppermute | solution.py:690
  110.3 6.9 %collective-permute-start.28 = (bf16[128,576]{1,0:T(8,128)(2,1)S(1)}, bf16[128,576]{1,0:T(8,128)(2,1)S(1)}, u32[]{:S(2)}, u32[]{:S(2)}) collective-permute-start(bf16[128,576]{1,0:T(8,128)(2,1)S(1)} %get-tuple-element.183), channel_id=1, source_target_pairs={{0,16},{4,20},{8,24},{12,28},{16,0},{20,4},{24,8},{28,12},{1,17},{... | collective-permute-start | bytes 442376 | tf_op jit(solution)/shard_map/qkv_y/ppermute | solution.py:690
  112.9 9.6 %collective-permute-start.32 = (bf16[96,1152]{1,0:T(8,128)(2,1)S(1)}, bf16[96,1152]{1,0:T(8,128)(2,1)S(1)}, u32[]{:S(2)}, u32[]{:S(2)}) collective-permute-start(bf16[96,1152]{1,0:T(8,128)(2,1)S(1)} %get-tuple-element.192), channel_id=1, source_target_pairs={{0,16},{4,20},{8,24},{12,28},{16,0},{20,4},{24,8},{28,12},{1,17},{... | collective-permute-start | bytes 663560 | tf_op jit(solution)/shard_map/grads_a/ppermute | solution.py:690
  118.0 5.7 %collective-permute-start.30 = (bf16[288,128]{1,0:T(8,128)(2,1)S(1)}, bf16[288,128]{1,0:T(8,128)(2,1)S(1)}, u32[]{:S(2)}, u32[]{:S(2)}) collective-permute-start(bf16[288,128]{1,0:T(8,128)(2,1)S(1)} %get-tuple-element.187), channel_id=1, source_target_pairs={{0,2},{1,3},{2,0},{3,1},{4,6},{5,7},{6,4},{7,5},{8,10},{9,11},{10,... | collective-permute-start | bytes 221192 | tf_op jit(solution)/shard_map/out/ppermute | solution.py:690
  118.7 6.3 %collective-permute-start.31 = (bf16[288,128]{1,0:T(8,128)(2,1)S(1)}, bf16[288,128]{1,0:T(8,128)(2,1)S(1)}, u32[]{:S(2)}, u32[]{:S(2)}) collective-permute-start(bf16[288,128]{1,0:T(8,128)(2,1)S(1)} %get-tuple-element.188), channel_id=1, source_target_pairs={{0,3},{1,2},{2,1},{3,0},{4,7},{5,6},{6,5},{7,4},{8,11},{9,10},{10,... | collective-permute-start | bytes 221192 | tf_op jit(solution)/shard_map/out/ppermute | solution.py:690
  120.7 5.1 %collective-permute-start.29 = (bf16[288,128]{1,0:T(8,128)(2,1)S(1)}, bf16[288,128]{1,0:T(8,128)(2,1)S(1)}, u32[]{:S(2)}, u32[]{:S(2)}) collective-permute-start(bf16[288,128]{1,0:T(8,128)(2,1)S(1)} %get-tuple-element.186), channel_id=1, source_target_pairs={{0,1},{1,0},{2,3},{3,2},{4,5},{5,4},{6,7},{7,6},{8,9},{9,8},{10,11... | collective-permute-start | bytes 221192 | tf_op jit(solution)/shard_map/out/ppermute | solution.py:690

commit v8 on v7

--- a/solution.py
+++ b/solution.py
@@ -98,10 +98,33 @@
     wt_o[...] = w_o[...].T
 
 
+def bias_kernel(place, lengths, table, pattern, ids):
+    buckets = table.shape[0]
+    half = buckets // 2
+    heads, _, blk, _ = pattern.shape
+    ids[...] = page_ids(lengths, ids.shape, 0, -2)
+    off = lax.broadcasted_iota(jnp.int32, (blk, blk), 1) - lax.broadcasted_iota(
+        jnp.int32, (blk, blk), 0
+    )
+    for h in range(heads):
+        col = place[0] * heads + h
+        low, high = table[0, col], table[buckets - 1, col]
+        near = jnp.where(off >= half - 1, high, low)
+        for b in range(1, buckets - 1):
+            near = jnp.where(off == b - half, table[b, col], near)
+        before = jnp.full((blk, blk), low, F32)
+        for b in range(1, half):
+            before = jnp.where(off - blk == b - half, table[b, col], before)
+        after = jnp.full((blk, blk), high, F32)
+        for b in range(half + 1, buckets - 1):
+            after = jnp.where(off + blk == b - half, table[b, col], after)
+        pattern[h, 0], pattern[h, 1], pattern[h, 2] = before, near, after
+
+
 def head_kernel(
-    place, lengths, table, x0, x1, x2, x3, cols, wq,
+    place, lengths, table, x0, x1, x2, x3, pattern, ids, cols, wq,
     xt_o, h1_o, stat_o, qkv_o, pt_o, att_o, top_o, low_o,
-    score, ids, pattern,
+    score,
 ):
     m = place[0]
     width, tokens = xt_o.shape
@@ -109,7 +132,6 @@
     channels = att_o.shape[0]
     heads = channels // HEAD_DIM
     buckets = table.shape[0]
-    half = buckets // 2
     for k, ref in enumerate((x0, x1, x2, x3)):
         at = pl.multiple_of((m ^ k) * rows, rows)
         xt_o[:, pl.ds(at, rows)] = ref[0:rows, :].T
@@ -138,36 +160,20 @@
     qkv_o[...] = nn(wq[...], h1_o[...]).astype(BF16)
     qkv_o[0:channels, :] = qkv_o[0:channels, :] * BF16(HEAD_DIM**-0.5)
 
-    ids[...] = page_ids(lengths, ids.shape, 0, -2)
     own_ids = page_ids(lengths, (1, tokens), 1, -1)
     live = (own_ids >= 0).astype(F32)
     blk = 128
     n_blk = tokens // blk
-    off = lax.broadcasted_iota(jnp.int32, (blk, blk), 1) - lax.broadcasted_iota(
-        jnp.int32, (blk, blk), 0
-    )
-
-    def one_head(h, carry):
+
+    def one_head(h):
         col = m * heads + h
         low, high = table[0, col], table[buckets - 1, col]
-        near = jnp.where(off >= half - 1, high, low)
-        for b in range(1, buckets - 1):
-            near = jnp.where(off == b - half, table[b, col], near)
-        pattern[1] = near
-        before = jnp.full((blk, blk), low, F32)
-        for b in range(1, half):
-            before = jnp.where(off - blk == b - half, table[b, col], before)
-        pattern[0] = before
-        after = jnp.full((blk, blk), high, F32)
-        for b in range(half + 1, buckets - 1):
-            after = jnp.where(off + blk == b - half, table[b, col], after)
-        pattern[2] = after
 
         def rows_of(which):
-            return pl.ds(pl.multiple_of(which * channels + h * HEAD_DIM, HEAD_DIM), HEAD_DIM)
+            return pl.ds(which * channels + h * HEAD_DIM, HEAD_DIM)
 
         q, k, v = qkv_o[rows_of(0), :], qkv_o[rows_of(1), :], qkv_o[rows_of(2), :]
-        score[...] = nn(k.T, q)
+        score[h] = nn(k.T, q)
         for i in range(n_blk):
             lanes = slice(i * blk, (i + 1) * blk)
             query_id = own_ids[:, lanes]
@@ -175,28 +181,28 @@
             for j in range(n_blk):
                 at = slice(j * blk, (j + 1) * blk)
                 if abs(i - j) <= 1:
-                    bias = pattern[i - j + 1]
+                    bias = pattern[h, i - j + 1]
                 else:
                     bias = low if i < j else high
-                s = jnp.where(ids[at, :] == query_id, score[at, lanes] + bias, masked_score)
-                score[at, lanes] = s
+                s = jnp.where(ids[at, :] == query_id, score[h, at, lanes] + bias, masked_score)
+                score[h, at, lanes] = s
                 top = jnp.maximum(top, jnp.max(s.reshape(blk // 8, 8, blk), axis=0))
             top = jnp.max(top, axis=0, keepdims=True)
             total = jnp.zeros((8, blk), F32)
             for j in range(n_blk):
                 at = slice(j * blk, (j + 1) * blk)
-                e = jnp.exp(score[at, lanes] - top)
-                score[at, lanes] = e
+                e = jnp.exp(score[h, at, lanes] - top)
+                score[h, at, lanes] = e
                 total = total + fold(e)
             scale = 1.0 / across(total)
             for j in range(n_blk):
                 at = slice(j * blk, (j + 1) * blk)
-                pt_o[h, at, lanes] = (score[at, lanes] * scale).astype(BF16)
+                pt_o[h, at, lanes] = (score[h, at, lanes] * scale).astype(BF16)
         mixed = nn(v, pt_o[h]) * live
-        att_o[pl.ds(pl.multiple_of(h * HEAD_DIM, HEAD_DIM), HEAD_DIM), :] = mixed.astype(BF16)
-        return carry
-
-    lax.fori_loop(0, heads, one_head, 0, unroll=True)
+        att_o[h * HEAD_DIM : (h + 1) * HEAD_DIM, :] = mixed.astype(BF16)
+
+    for h in range(heads):
+        one_head(h)
     half_rows = channels // 2
     top_o[...], low_o[...] = att_o[0:half_rows, :], att_o[half_rows:, :]
 
@@ -423,9 +429,9 @@
         jnp.int32, (blk, blk), 0
     )
 
-    def one_head(h, carry):
+    def one_head(h):
         def rows_of(which):
-            return pl.ds(pl.multiple_of(which * channels + h * HEAD_DIM, HEAD_DIM), HEAD_DIM)
+            return pl.ds(which * channels + h * HEAD_DIM, HEAD_DIM)
 
         q, k, v = qkv[rows_of(0), :], qkv[rows_of(1), :], qkv[rows_of(2), :]
         mine = rows_of(0)
@@ -435,36 +441,36 @@
         )
         d_att = (d_att.astype(BF16).astype(F32) * live).astype(BF16)
         dqkv_o[rows_of(2), :] = nt(d_att, pt[h]).astype(BF16)
-        score[...] = nn(v.T, d_att)
-        acc[...] = jnp.zeros(acc.shape, F32)
+        score[h] = nn(v.T, d_att)
+        acc[h] = jnp.zeros(acc.shape[1:], F32)
         for i in range(n_blk):
             lanes = slice(i * blk, (i + 1) * blk)
             total = jnp.zeros((8, blk), F32)
             for j in range(n_blk):
                 at = slice(j * blk, (j + 1) * blk)
-                prod = score[at, lanes] * pt[h, at, lanes].astype(F32)
-                score[at, lanes] = prod
+                prod = score[h, at, lanes] * pt[h, at, lanes].astype(F32)
+                score[h, at, lanes] = prod
                 total = total + fold(prod)
             total = across(total)
             for j in range(n_blk):
                 at = slice(j * blk, (j + 1) * blk)
-                g = score[at, lanes] - pt[h, at, lanes].astype(F32) * total
+                g = score[h, at, lanes] - pt[h, at, lanes].astype(F32) * total
                 g = g.astype(BF16)
-                ds[at, lanes] = g
+                ds[h, at, lanes] = g
                 slot = max(min(i - j, 2), -2) + 2
-                acc[slot] = acc[slot] + g.astype(F32)
-        dqkv_o[rows_of(0), :] = (nn(k, ds[...]) * HEAD_DIM**-0.5).astype(BF16)
-        dqkv_o[rows_of(1), :] = nt(q, ds[...]).astype(BF16)
-        near, before, after = acc[2], acc[1], acc[3]
+                acc[h, slot] = acc[h, slot] + g.astype(F32)
+        dqkv_o[rows_of(0), :] = (nn(k, ds[h]) * HEAD_DIM**-0.5).astype(BF16)
+        dqkv_o[rows_of(1), :] = nt(q, ds[h]).astype(BF16)
+        near, before, after = acc[h, 2], acc[h, 1], acc[h, 3]
         corner_b, off_b = before[0:16, :], off[0:16, :] - blk
         corner_a, off_a = after[blk - 16 : blk, :], off[blk - 16 : blk, :] + blk
         first = h * buckets
         for b in range(buckets):
             if b == 0:
-                v = fold(acc[0]) + fold(jnp.where(off - blk <= -half, before, 0.0))
+                v = fold(acc[h, 0]) + fold(jnp.where(off - blk <= -half, before, 0.0))
                 v = v + fold(jnp.where(off <= -half, near, 0.0))
             elif b == buckets - 1:
-                v = fold(acc[4]) + fold(jnp.where(off + blk >= half - 1, after, 0.0))
+                v = fold(acc[h, 4]) + fold(jnp.where(off + blk >= half - 1, after, 0.0))
                 v = v + fold(jnp.where(off >= half - 1, near, 0.0))
             else:
                 v = fold(jnp.where(off == b - half, near, 0.0))
@@ -472,10 +478,10 @@
                     v = v + fold(jnp.where(off_b == b - half, corner_b, 0.0))
                 elif b > half:
                     v = v + fold(jnp.where(off_a == b - half, corner_a, 0.0))
-            buckets_of[pl.ds(first + b, 1), :] = across(v)
-        return carry
-
-    lax.fori_loop(0, heads, one_head, 0, unroll=True)
+            buckets_of[first + b : first + b + 1, :] = across(v)
+
+    for h in range(heads):
+        one_head(h)
     wide[...] = nn(wq_t[...], dqkv_o[...])
     weight_grad = nt(h1[...], dqkv_o[...]).astype(BF16)
     mean, rstd = stat[0:1, :], stat[1:2, :]
@@ -710,7 +716,13 @@
         [like((width, 3 * channels), BF16), like((hidden, width), BF16), like((width, hidden), BF16)],
         [wq, w_up, w_down],
     )
-    x[1:] = lax.optimization_barrier((x[1:], wq_t))[0]
+    pattern, ids = call(
+        bias_kernel,
+        [like((heads, 3, 128, 128), F32), like((group, 128), jnp.int32)],
+        [place, page_lengths, rel_table],
+        n_smem=3,
+    )
+    x[1:] = lax.optimization_barrier((x[1:], wq_t, pattern))[0]
     (part,) = call(pieces_kernel, [like((4, piece, width), BF16)], x)
     part_x = swap(part, 2, "dp", name="w")
     wq_now = after(wq, wq_t, w_up_t, w_down_t)
@@ -726,13 +738,12 @@
             like((channels // 2, group), BF16),
             like((channels // 2, group), BF16),
         ],
-        [place, page_lengths, rel_table] + x + [cols, wq_now],
+        [place, page_lengths, rel_table] + x + [pattern, ids, cols, wq_now],
         n_smem=3,
         scratch=[
-            pltpu.VMEM((group, group), F32),
-            pltpu.VMEM((group, 128), jnp.int32),
-            pltpu.VMEM((3, 128, 128), F32),
+            pltpu.VMEM((heads, group, group), F32),
         ],
+        limit=24,
         us=10,
     )
     (parts,) = call(
@@ -812,13 +823,14 @@
         n_smem=2,
         scratch=[
             pltpu.VMEM((n, group), BF16),
-            pltpu.VMEM((group, group), F32),
-            pltpu.VMEM((group, group), BF16),
-            pltpu.VMEM((5, 128, 128), F32),
+            pltpu.VMEM((heads, group, group), F32),
+            pltpu.VMEM((heads, group, group), BF16),
+            pltpu.VMEM((heads, 5, 128, 128), F32),
             pltpu.VMEM((heads * buckets, 128), F32),
             pltpu.VMEM((width, group), F32),
             pltpu.VMEM((width, 128), F32),
         ],
+        limit=24,
         us=10,
     )
     p_recv = swap(after(p13, mlp[1]), 1, name="back")
@@ -874,7 +886,7 @@
         vec, o0, o1, o2, o3 = call(
             message_kernel,
             vec_like + [like((channels, share), F32)] + [message] * 3,
-            [place, vec, b_kept, b_recv, recv],
+            [place, after(vec, a_recv), b_kept, b_recv, recv],
             n_smem=1,
             scratch=[pltpu.VMEM((width, share), F32)],
         )

time: 127 us -> 126 us (level)
  starting transfers between devices: 43.8 us -> 42.3 us
    ppermute x33, starting transfers between devices: 43.8 us -> 42.3 us  [swap(): return lax.ppermute(v, axis, [(i, i ^ k) for i in range(n)])]
    pallas_call x20 -> x21, Pallas kernels: 31.9 us -> 32.9 us  [call(): pl.pallas_call(kernel, out_shape=tuple(outs), in_specs=[SMEM] * n_smem +...]
  transfers between devices with their start and end apart: 33 -> 33, of which waited for: 20 -> 18; matrix products, arithmetic and copies ran while one was open for 2% -> 2% of each run, Pallas kernels for 25% -> 26%
where the time goes in v8:
time: 126 us; the launch traced here: 125 us
  starting transfers between devices  42.3 us (34%)
  waiting for transfers between devices  42.3 us (34%)
  Pallas kernels  32.9 us (26%)
  local copies, waits for them, and re-layouts  5.87 us (5%)
    ppermute x33, starting transfers between devices, swap(): return lax.ppermute(v, axis, [(i, i ^ k) for i in range(n)])  42.3 us
    ppermute x33, waiting for transfers between devices, swap(): return lax.ppermute(v, axis, [(i, i ^ k) for i in range(n)])  42.3 us
    pallas_call x21, Pallas kernels, call(): pl.pallas_call(kernel, out_shape=tuple(outs), in_specs=[SMEM] * n_smem +...  32.9 us
    unnamed x17, local copies, waits for them, and re-layouts  4.17 us
  transfers between devices with their start and end apart: 33, of which 18 were waited for; matrix products, arithmetic and copies ran while one was open for 2% of the time, Pallas kernels for 26%

profile of v8, /device:TPU:0, one launch (start us, length us, event | category | flops | bytes accessed | tf_op | source)
XLA Modules:
  0.0 125.3 jit_solution(10103823117766645825)
XLA Ops:
  0.7 0.9 copy-done
  1.6 0.9 pad_maximum_fusion.x0
  2.6 4.1 %collective-permute-start.1 = (bf16[176,768]{1,0:T(8,128)(2,1)S(1)}, bf16[176,768]{1,0:T(8,128)(2,1)S(1)}, u32[]{:S(2)}, u32[]{:S(2)}) collective-permute-start(bf16[176,768]{1,0:T(8,128)(2,1)S(1)} %pad_maximum_fusion.x0), channel_id=1, source_target_pairs={{0,2},{1,3},{2,0},{3,1},{4,6},{5,7},{6,4},{7,5},{8,10},{9,11},{10,... | collective-permute-start | bytes 811016 | tf_op jit(solution)/shard_map/x/ppermute | solution.py:696
  6.7 1.6 %collective-permute-start = (bf16[176,768]{1,0:T(8,128)(2,1)S(1)}, bf16[176,768]{1,0:T(8,128)(2,1)S(1)}, u32[]{:S(2)}, u32[]{:S(2)}) collective-permute-start(bf16[176,768]{1,0:T(8,128)(2,1)S(1)} %pad_maximum_fusion.x0), channel_id=1, source_target_pairs={{0,1},{1,0},{2,3},{3,2},{4,5},{5,4},{6,7},{7,6},{8,9},{9,8},{10,11... | collective-permute-start | bytes 811016 | tf_op jit(solution)/shard_map/x/ppermute | solution.py:696
  8.2 0.8 copy.30.table
  9.0 10.0 %collective-permute-done.1.x2 = bf16[176,768]{1,0:T(8,128)(2,1)S(1)} collective-permute-done((bf16[176,768]{1,0:T(8,128)(2,1)S(1)}, bf16[176,768]{1,0:T(8,128)(2,1)S(1)}, u32[]{:S(2)}, u32[]{:S(2)}) %collective-permute-start.1) | collective-permute-done | bytes 270368 | tf_op jit(solution)/shard_map/x/ppermute | solution.py:696
  19.2 1.5 %collective-permute-start.2 = (bf16[176,768]{1,0:T(8,128)(2,1)S(1)}, bf16[176,768]{1,0:T(8,128)(2,1)S(1)}, u32[]{:S(2)}, u32[]{:S(2)}) collective-permute-start(bf16[176,768]{1,0:T(8,128)(2,1)S(1)} %collective-permute-done.1.x2), channel_id=1, source_target_pairs={{0,1},{1,0},{2,3},{3,2},{4,5},{5,4},{6,7},{7,6},{8,9},{9,8},{10,11... | collective-permute-start | bytes 811016 | tf_op jit(solution)/shard_map/x/ppermute | solution.py:696
  20.7 0.8 fusion
  21.5 0.7 concatenate.7
  22.4 1.3 %copy-done.2 = bf16[768,768]{1,0:T(8,128)(2,1)S(1)} copy-done((bf16[768,768]{1,0:T(8,128)(2,1)S(1)}, bf16[768,768]{1,0:T(8,128)(2,1)}, u32[]{:S(2)}) %copy-start.2) | copy-done | bytes 1179672
  23.7 1.2 copy-done.4
  24.9 0.9 turn_kernel.1
  25.9 1.5 %bias_kernel.1 = (f32[3,3,128,128]{3,2,1,0:T(8,128)S(1)}, s32[512,128]{1,0:T(8,128)S(1)}) custom-call(s32[2]{0:T(128)S(1)} %pad_add_fusion.place, s32[1,8]{1,0:T(1,128)S(1)} %copy-done.7, f32[32,12]{1,0:T(8,128)S(1)} %copy.30.table), custom_call_target="tpu_custom_call" | custom-call | flops 11500000 | bytes 8 | tf_op jit(solution)/shard_map/bias_kernel/pallas_call | solution.py:21
  27.4 2.4 %collective-permute-start.5 = (bf16[128,768]{1,0:T(8,128)(2,1)S(1)}, bf16[128,768]{1,0:T(8,128)(2,1)S(1)}, u32[]{:S(2)}, u32[]{:S(2)}) collective-permute-start(bf16[128,768]{1,0:T(8,128)(2,1)S(1)} %copy-done.6), channel_id=1, source_target_pairs={{0,2},{1,3},{2,0},{3,1},{4,6},{5,7},{6,4},{7,5},{8,10},{9,11},{10,... | collective-permute-start | bytes 589832 | tf_op jit(solution)/shard_map/dy/ppermute | solution.py:696
  29.8 1.7 %collective-permute-start.4 = (bf16[128,768]{1,0:T(8,128)(2,1)S(1)}, bf16[128,768]{1,0:T(8,128)(2,1)S(1)}, u32[]{:S(2)}, u32[]{:S(2)}) collective-permute-start(bf16[128,768]{1,0:T(8,128)(2,1)S(1)} %copy-done.6), channel_id=1, source_target_pairs={{0,1},{1,0},{2,3},{3,2},{4,5},{5,4},{6,7},{7,6},{8,9},{9,8},{10,11... | collective-permute-start | bytes 589832 | tf_op jit(solution)/shard_map/dy/ppermute | solution.py:696
  31.5 1.6 %collective-permute-start.3 = (bf16[4,48,768]{2,1,0:T(8,128)(2,1)S(1)}, bf16[4,48,768]{2,1,0:T(8,128)(2,1)S(1)}, u32[]{:S(2)}, u32[]{:S(2)}) collective-permute-start(bf16[4,48,768]{2,1,0:T(8,128)(2,1)S(1)} %pieces_kernel.1.a), channel_id=1, source_target_pairs={{0,8},{4,12},{8,0},{12,4},{16,24},{20,28},{24,16},{28,20},{1,9},{5... | collective-permute-start | bytes 884744 | tf_op jit(solution)/shard_map/w/ppermute | solution.py:696
  33.0 4.2 %head_kernel.1 = (bf16[768,512]{1,0:T(8,128)(2,1)S(1)}, bf16[768,512]{1,0:T(8,128)(2,1)S(1)}, f32[8,512]{1,0:T(8,128)S(1)}, bf16[576,512]{1,0:T(8,128)(2,1)S(1)}...) custom-call(s32[2]{0:T(128)S(1)} %pad_add_fusion.place, ...), custom_call_target="tpu_custom_call" | custom-call | flops 11500000256 | bytes 8 | tf_op jit(solution)/shard_map/head_kernel/pallas_call | solution.py:21
  37.2 1.7 %collective-permute-done.5.c2 = bf16[128,768]{1,0:T(8,128)(2,1)S(1)} collective-permute-done((bf16[128,768]{1,0:T(8,128)(2,1)S(1)}, bf16[128,768]{1,0:T(8,128)(2,1)S(1)}, u32[]{:S(2)}, u32[]{:S(2)}) %collective-permute-start.5) | collective-permute-done | bytes 196640 | tf_op jit(solution)/shard_map/dy/ppermute | solution.py:696
  38.9 0.7 collective-permute-done.4.c1
  39.7 1.0 collective-permute-start.6
  40.8 2.0 %collective-permute-start.7 = (bf16[96,512]{1,0:T(8,128)(2,1)S(1)}, bf16[96,512]{1,0:T(8,128)(2,1)S(1)}, u32[]{:S(2)}, u32[]{:S(2)}) collective-permute-start(bf16[96,512]{1,0:T(8,128)(2,1)S(1)} %get-tuple-element.123), channel_id=1, source_target_pairs={{0,2},{1,3},{2,0},{3,1},{4,6},{5,7},{6,4},{7,5},{8,10},{9,11},{10,... | collective-permute-start | bytes 294920 | tf_op jit(solution)/shard_map/att/ppermute | solution.py:696
  42.7 1.4 %collective-permute-start.10 = (bf16[96,512]{1,0:T(8,128)(2,1)S(1)}, bf16[96,512]{1,0:T(8,128)(2,1)S(1)}, u32[]{:S(2)}, u32[]{:S(2)}) collective-permute-start(bf16[96,512]{1,0:T(8,128)(2,1)S(1)} %get-tuple-element.125), channel_id=1, source_target_pairs={{0,3},{1,2},{2,1},{3,0},{4,7},{5,6},{6,5},{7,4},{8,11},{9,10},{10,... | collective-permute-start | bytes 294920 | tf_op jit(solution)/shard_map/att/ppermute | solution.py:696
  44.3 3.9 %collective-permute-done.7.a2t = bf16[96,512]{1,0:T(8,128)(2,1)S(1)} collective-permute-done((bf16[96,512]{1,0:T(8,128)(2,1)S(1)}, bf16[96,512]{1,0:T(8,128)(2,1)S(1)}, u32[]{:S(2)}, u32[]{:S(2)}) %collective-permute-start.7) | collective-permute-done | bytes 98336 | tf_op jit(solution)/shard_map/att/ppermute | solution.py:696
  48.1 2.6 %collective-permute-start.9 = (bf16[96,512]{1,0:T(8,128)(2,1)S(1)}, bf16[96,512]{1,0:T(8,128)(2,1)S(1)}, u32[]{:S(2)}, u32[]{:S(2)}) collective-permute-start(bf16[96,512]{1,0:T(8,128)(2,1)S(1)} %collective-permute-done.7.a2t), channel_id=1, source_target_pairs={{0,1},{1,0},{2,3},{3,2},{4,5},{5,4},{6,7},{7,6},{8,9},{9,8},{10,11... | collective-permute-start | bytes 294920 | tf_op jit(solution)/shard_map/att/ppermute | solution.py:696
  50.7 1.0 out_weight_kernel.1
  51.7 0.5 collective-permute-done.10.a3b
  52.2 5.0 %collective-permute-done.8.a2b = bf16[96,512]{1,0:T(8,128)(2,1)S(1)} collective-permute-done((bf16[96,512]{1,0:T(8,128)(2,1)S(1)}, bf16[96,512]{1,0:T(8,128)(2,1)S(1)}, u32[]{:S(2)}, u32[]{:S(2)}) %collective-permute-start.8) | collective-permute-done | bytes 98336 | tf_op jit(solution)/shard_map/att/ppermute | solution.py:696
  57.2 4.2 %up_kernel.1 = (bf16[768,512]{1,0:T(8,128)(2,1)S(1)}, f32[768,512]{1,0:T(8,128)S(1)}, f32[768,512]{1,0:T(8,128)S(1)}, f32[8,512]{1,0:T(8,128)S(1)}, bf16[768,512...) custom-call(s32[2]{0:T(128)S(1)} %pad_add_fusion.place, ...), custom_call_target="tpu_custom_call" | custom-call | flops 11500000256 | bytes 8 | tf_op jit(solution)/shard_map/up_kernel/pallas_call | solution.py:21
  61.5 4.6 %down_kernel.1 = (bf16[192,512]{1,0:T(8,128)(2,1)S(1)}, bf16[192,512]{1,0:T(8,128)(2,1)S(1)}, bf16[192,512]{1,0:T(8,128)(2,1)S(1)}, bf16[192,512]{1,0:T(8,128)(2...) custom-call(s32[2]{0:T(128)S(1)} %pad_add_fusion.place, ...), custom_call_target="tpu_custom_call" | custom-call | flops 11500000256 | bytes 8 | tf_op jit(solution)/shard_map/down_kernel/pallas_call | solution.py:21
  66.1 2.1 %collective-permute-start.14 = (bf16[192,512]{1,0:T(8,128)(2,1)S(1)}, bf16[192,512]{1,0:T(8,128)(2,1)S(1)}, u32[]{:S(2)}, u32[]{:S(2)}) collective-permute-start(bf16[192,512]{1,0:T(8,128)(2,1)S(1)} %get-tuple-element.140), channel_id=1, source_target_pairs={{0,1},{1,0},{2,3},{3,2},{4,5},{5,4},{6,7},{7,6},{8,9},{9,8},{10,11... | collective-permute-start | bytes 589832 | tf_op jit(solution)/shard_map/d_att/ppermute | solution.py:696
  68.5 2.2 %collective-permute-start.16 = (bf16[192,512]{1,0:T(8,128)(2,1)S(1)}, bf16[192,512]{1,0:T(8,128)(2,1)S(1)}, u32[]{:S(2)}, u32[]{:S(2)}) collective-permute-start(bf16[192,512]{1,0:T(8,128)(2,1)S(1)} %get-tuple-element.142), channel_id=1, source_target_pairs={{0,3},{1,2},{2,1},{3,0},{4,7},{5,6},{6,5},{7,4},{8,11},{9,10},{10,... | collective-permute-start | bytes 589832 | tf_op jit(solution)/shard_map/d_att/ppermute | solution.py:696
  70.6 2.6 %mlp_grad_kernel.1 = (f32[8,768]{1,0:T(8,128)S(1)}, bf16[384,1152]{1,0:T(8,128)(2,1)S(1)}, bf16[384,1152]{1,0:T(8,128)(2,1)S(1)}, bf16[384,1152]{1,0:T(8,128)(2,1)S(1)}, bf16[384,1152]{1,0:T(8,128)(2,1)S(1)}) custom-call(s32[2]{0:T(128)S(1)} %pad_add_fusion.place, f32[8,768]{1,0:T(8,128)S(1)} %get-tuple-element.151.vec, ...), custom_call_target="tpu_custom_call" | custom-call | flops 11500000 | bytes 8 | tf_op jit(solution)/shard_map/mlp_grad_kernel/pallas_call | solution.py:21
  73.2 1.6 %collective-permute-start.21 = (bf16[384,1152]{1,0:T(8,128)(2,1)S(1)}, bf16[384,1152]{1,0:T(8,128)(2,1)S(1)}, u32[]{:S(2)}, u32[]{:S(2)}) collective-permute-start(bf16[384,1152]{1,0:T(8,128)(2,1)S(1)} %get-tuple-element.174), channel_id=1, source_target_pairs={{0,8},{4,12},{8,0},{12,4},{16,24},{20,28},{24,16},{28,20},{1,9},{5... | collective-permute-start | bytes 2654216 | tf_op jit(solution)/shard_map/grads_a/ppermute | solution.py:696
  74.8 2.5 %collective-permute-done.12.recv = bf16[1536,128]{1,0:T(8,128)(2,1)S(1)} collective-permute-done((bf16[1536,128]{1,0:T(8,128)(2,1)S(1)}, bf16[1536,128]{1,0:T(8,128)(2,1)S(1)}, u32[]{:S(2)}, u32[]{:S(2)}) %collective-permute-start.12) | collective-permute-done | bytes 393248 | tf_op jit(solution)/shard_map/mlp/ppermute | solution.py:696
  77.3 1.5 %collective-permute-start.22 = (bf16[384,1152]{1,0:T(8,128)(2,1)S(1)}, bf16[384,1152]{1,0:T(8,128)(2,1)S(1)}, u32[]{:S(2)}, u32[]{:S(2)}) collective-permute-start(bf16[384,1152]{1,0:T(8,128)(2,1)S(1)} %get-tuple-element.176), channel_id=1, source_target_pairs={{0,16},{4,20},{8,24},{12,28},{16,0},{20,4},{24,8},{28,12},{1,17},{... | collective-permute-start | bytes 2654216 | tf_op jit(solution)/shard_map/grads_b/ppermute | solution.py:696
  78.9 1.4 %collective-permute-done.14.d1 = bf16[192,512]{1,0:T(8,128)(2,1)S(1)} collective-permute-done((bf16[192,512]{1,0:T(8,128)(2,1)S(1)}, bf16[192,512]{1,0:T(8,128)(2,1)S(1)}, u32[]{:S(2)}, u32[]{:S(2)}) %collective-permute-start.14) | collective-permute-done | bytes 196640 | tf_op jit(solution)/shard_map/d_att/ppermute | solution.py:696
  80.3 4.8 %collective-permute-done.15.d2 = bf16[192,512]{1,0:T(8,128)(2,1)S(1)} collective-permute-done((bf16[192,512]{1,0:T(8,128)(2,1)S(1)}, bf16[192,512]{1,0:T(8,128)(2,1)S(1)}, u32[]{:S(2)}, u32[]{:S(2)}) %collective-permute-start.15) | collective-permute-done | bytes 196640 | tf_op jit(solution)/shard_map/d_att/ppermute | solution.py:696
  85.1 3.4 %collective-permute-start.17 = (bf16[768,128]{1,0:T(8,128)(2,1)S(1)}, bf16[768,128]{1,0:T(8,128)(2,1)S(1)}, u32[]{:S(2)}, u32[]{:S(2)}) collective-permute-start(bf16[768,128]{1,0:T(8,128)(2,1)S(1)} %get-tuple-element.143), channel_id=1, source_target_pairs={{0,2},{1,3},{2,0},{3,1},{4,6},{5,7},{6,4},{7,5},{8,10},{9,11},{10,... | collective-permute-start | bytes 589832 | tf_op jit(solution)/shard_map/mlp/ppermute | solution.py:696
  88.6 6.5 %back_kernel.1 = (f32[768,128]{1,0:T(8,128)S(1)}, f32[768,128]{1,0:T(8,128)S(1)}, bf16[1536,128]{1,0:T(8,128)(2,1)S(1)}, f32[8,768]{1,0:T(8,128)S(1)}, bf16[416,...) custom-call(s32[2]{0:T(128)S(1)} %pad_add_fusion.place, s32[1,8]{1,0:T(1,128)S(1)} %copy-done.7, ...), custom_call_target="tpu_custom_call" | custom-call | flops 11500000256 | bytes 8 | tf_op jit(solution)/shard_map/back_kernel/pallas_call | solution.py:21
  95.1 0.6 collective-permute-done.17.recv
  95.7 1.9 %collective-permute-done.20.recv = bf16[416,576]{1,0:T(8,128)(2,1)S(1)} collective-permute-done((bf16[416,576]{1,0:T(8,128)(2,1)S(1)}, bf16[416,576]{1,0:T(8,128)(2,1)S(1)}, u32[]{:S(2)}, u32[]{:S(2)}) %collective-permute-start.20) | collective-permute-done | bytes 479264 | tf_op jit(solution)/shard_map/qkv_core/ppermute | solution.py:696
  97.6 0.7 qkv_second_kernel.1
  98.3 1.0 grads_second_kernel.1
  99.5 0.4 collective-permute-start.24
  100.0 1.5 %collective-permute-start.26 = (bf16[224,576]{1,0:T(8,128)(2,1)S(1)}, bf16[224,576]{1,0:T(8,128)(2,1)S(1)}, u32[]{:S(2)}, u32[]{:S(2)}) collective-permute-start(bf16[224,576]{1,0:T(8,128)(2,1)S(1)} %get-tuple-element.184), channel_id=1, source_target_pairs={{0,8},{4,12},{8,0},{12,4},{16,24},{20,28},{24,16},{28,20},{1,9},{5... | collective-permute-start | bytes 774152 | tf_op jit(solution)/shard_map/qkv_x/ppermute | solution.py:696
  101.8 0.7 grads_third_kernel.1
  102.5 1.6 %collective-permute-start.27 = (bf16[96,1152]{1,0:T(8,128)(2,1)S(1)}, bf16[96,1152]{1,0:T(8,128)(2,1)S(1)}, u32[]{:S(2)}, u32[]{:S(2)}) collective-permute-start(bf16[96,1152]{1,0:T(8,128)(2,1)S(1)} %get-tuple-element.186), channel_id=1, source_target_pairs={{0,16},{4,20},{8,24},{12,28},{16,0},{20,4},{24,8},{28,12},{1,17},{... | collective-permute-start | bytes 663560 | tf_op jit(solution)/shard_map/grads_a/ppermute | solution.py:696
  104.1 1.5 %collective-permute-start.28 = (bf16[96,1152]{1,0:T(8,128)(2,1)S(1)}, bf16[96,1152]{1,0:T(8,128)(2,1)S(1)}, u32[]{:S(2)}, u32[]{:S(2)}) collective-permute-start(bf16[96,1152]{1,0:T(8,128)(2,1)S(1)} %get-tuple-element.189), channel_id=1, source_target_pairs={{0,8},{4,12},{8,0},{12,4},{16,24},{20,28},{24,16},{28,20},{1,9},{5... | collective-permute-start | bytes 663560 | tf_op jit(solution)/shard_map/grads_b/ppermute | solution.py:696
  105.6 1.6 %collective-permute-done.18.recv = bf16[1536,128]{1,0:T(8,128)(2,1)S(1)} collective-permute-done((bf16[1536,128]{1,0:T(8,128)(2,1)S(1)}, bf16[1536,128]{1,0:T(8,128)(2,1)S(1)}, u32[]{:S(2)}, u32[]{:S(2)}) %collective-permute-start.18) | collective-permute-done | bytes 393248 | tf_op jit(solution)/shard_map/back/ppermute | solution.py:696
  107.3 0.8 collective-permute-start.19
  108.1 1.6 %collective-permute-done.26.recv = bf16[224,576]{1,0:T(8,128)(2,1)S(1)} collective-permute-done((bf16[224,576]{1,0:T(8,128)(2,1)S(1)}, bf16[224,576]{1,0:T(8,128)(2,1)S(1)}, u32[]{:S(2)}, u32[]{:S(2)}) %collective-permute-start.26) | collective-permute-done | bytes 258080 | tf_op jit(solution)/shard_map/qkv_x/ppermute | solution.py:696
  109.7 0.6 qkv_third_kernel.1
  110.3 1.6 %collective-permute-start.29 = (bf16[128,576]{1,0:T(8,128)(2,1)S(1)}, bf16[128,576]{1,0:T(8,128)(2,1)S(1)}, u32[]{:S(2)}, u32[]{:S(2)}) collective-permute-start(bf16[128,576]{1,0:T(8,128)(2,1)S(1)} %get-tuple-element.190), channel_id=1, source_target_pairs={{0,16},{4,20},{8,24},{12,28},{16,0},{20,4},{24,8},{28,12},{1,17},{... | collective-permute-start | bytes 442376 | tf_op jit(solution)/shard_map/qkv_y/ppermute | solution.py:696
  111.9 0.9 output_kernel.1
  112.8 2.9 %collective-permute-done.29.q_recv = bf16[128,576]{1,0:T(8,128)(2,1)S(1)} collective-permute-done((bf16[128,576]{1,0:T(8,128)(2,1)S(1)}, bf16[128,576]{1,0:T(8,128)(2,1)S(1)}, u32[]{:S(2)}, u32[]{:S(2)}) %collective-permute-start.29) | collective-permute-done | bytes 147488 | tf_op jit(solution)/shard_map/qkv_y/ppermute | solution.py:696
  115.7 0.7 message_kernel.1
  116.4 0.9 collective-permute-start.31
  117.3 1.9 %collective-permute-start.32 = (bf16[288,128]{1,0:T(8,128)(2,1)S(1)}, bf16[288,128]{1,0:T(8,128)(2,1)S(1)}, u32[]{:S(2)}, u32[]{:S(2)}) collective-permute-start(bf16[288,128]{1,0:T(8,128)(2,1)S(1)} %get-tuple-element.195), channel_id=1, source_target_pairs={{0,3},{1,2},{2,1},{3,0},{4,7},{5,6},{6,5},{7,4},{8,11},{9,10},{10,... | collective-permute-start | bytes 221192 | tf_op jit(solution)/shard_map/out/ppermute | solution.py:696
  119.3 0.7 collective-permute-start.30
  120.0 0.9 input_kernel.1
  120.8 1.0 last_kernel.1
  121.8 2.3 %collective-permute-done.31.o2 = bf16[288,128]{1,0:T(8,128)(2,1)S(1)} collective-permute-done((bf16[288,128]{1,0:T(8,128)(2,1)S(1)}, bf16[288,128]{1,0:T(8,128)(2,1)S(1)}, u32[]{:S(2)}, u32[]{:S(2)}) %collective-permute-start.31) | collective-permute-done | bytes 73760 | tf_op jit(solution)/shard_map/out/ppermute | solution.py:696
  124.1 0.5 collective-permute-done.30.o1
  124.6 0.7 small_kernel.1
  (46 shorter events, 1.9 us)
Async XLA Ops:
  0.6 1.0 copy-start
  0.7 21.8 %copy-start.1 = (bf16[768,768]{1,0:T(8,128)(2,1)S(1)}, bf16[768,768]{1,0:T(8,128)(2,1)}, u32[]{:S(2)}) copy-start(bf16[768,768]{1,0:T(8,128)(2,1)} %w_up.1) | copy-start | bytes 3538948
  2.6 16.5 %collective-permute-start.1 = (bf16[176,768]{1,0:T(8,128)(2,1)S(1)}, bf16[176,768]{1,0:T(8,128)(2,1)S(1)}, u32[]{:S(2)}, u32[]{:S(2)}) collective-permute-start(bf16[176,768]{1,0:T(8,128)(2,1)S(1)} %pad_maximum_fusion.x0), channel_id=1, source_target_pairs={{0,2},{1,3},{2,0},{3,1},{4,6},{5,7},{6,4},{7,5},{8,10},{9,11},{10,... | collective-permute-start | bytes 811016 | tf_op jit(solution)/shard_map/x/ppermute | solution.py:696
  6.7 12.6 %collective-permute-start = (bf16[176,768]{1,0:T(8,128)(2,1)S(1)}, bf16[176,768]{1,0:T(8,128)(2,1)S(1)}, u32[]{:S(2)}, u32[]{:S(2)}) collective-permute-start(bf16[176,768]{1,0:T(8,128)(2,1)S(1)} %pad_maximum_fusion.x0), channel_id=1, source_target_pairs={{0,1},{1,0},{2,3},{3,2},{4,5},{5,4},{6,7},{7,6},{8,9},{9,8},{10,11... | collective-permute-start | bytes 811016 | tf_op jit(solution)/shard_map/x/ppermute | solution.py:696
  19.2 8.1 %collective-permute-start.2 = (bf16[176,768]{1,0:T(8,128)(2,1)S(1)}, bf16[176,768]{1,0:T(8,128)(2,1)S(1)}, u32[]{:S(2)}, u32[]{:S(2)}) collective-permute-start(bf16[176,768]{1,0:T(8,128)(2,1)S(1)} %collective-permute-done.1.x2), channel_id=1, source_target_pairs={{0,1},{1,0},{2,3},{3,2},{4,5},{5,4},{6,7},{7,6},{8,9},{9,8},{10,11... | collective-permute-start | bytes 811016 | tf_op jit(solution)/shard_map/x/ppermute | solution.py:696
  22.4 1.3 %copy-start.2 = (bf16[768,768]{1,0:T(8,128)(2,1)S(1)}, bf16[768,768]{1,0:T(8,128)(2,1)}, u32[]{:S(2)}) copy-start(bf16[768,768]{1,0:T(8,128)(2,1)} %w_down.1) | copy-start | bytes 3538948
  23.7 1.2 copy-start.4
  24.9 1.0 copy-start.7
  24.9 2.5 %copy-start.6 = (bf16[128,768]{1,0:T(8,128)(2,1)S(1)}, bf16[128,768]{1,0:T(8,128)(2,1)}, u32[]{:S(2)}) copy-start(bf16[128,768]{1,0:T(8,128)(2,1)} %dy.1) | copy-start | bytes 589828
  24.9 8.2 %copy-start.5 = (bf16[768,3,192]{0,2,1:T(8,128)(2,1)S(1)}, bf16[768,3,192]{0,2,1:T(8,128)(2,1)}, u32[]{:S(2)}) copy-start(bf16[768,3,192]{0,2,1:T(8,128)(2,1)} %param.16) | copy-start | bytes 2654212
  27.4 11.5 %collective-permute-start.5 = (bf16[128,768]{1,0:T(8,128)(2,1)S(1)}, bf16[128,768]{1,0:T(8,128)(2,1)S(1)}, u32[]{:S(2)}, u32[]{:S(2)}) collective-permute-start(bf16[128,768]{1,0:T(8,128)(2,1)S(1)} %copy-done.6), channel_id=1, source_target_pairs={{0,2},{1,3},{2,0},{3,1},{4,6},{5,7},{6,4},{7,5},{8,10},{9,11},{10,... | collective-permute-start | bytes 589832 | tf_op jit(solution)/shard_map/dy/ppermute | solution.py:696
  29.8 9.8 %collective-permute-start.4 = (bf16[128,768]{1,0:T(8,128)(2,1)S(1)}, bf16[128,768]{1,0:T(8,128)(2,1)S(1)}, u32[]{:S(2)}, u32[]{:S(2)}) collective-permute-start(bf16[128,768]{1,0:T(8,128)(2,1)S(1)} %copy-done.6), channel_id=1, source_target_pairs={{0,1},{1,0},{2,3},{3,2},{4,5},{5,4},{6,7},{7,6},{8,9},{9,8},{10,11... | collective-permute-start | bytes 589832 | tf_op jit(solution)/shard_map/dy/ppermute | solution.py:696
  31.5 8.1 %collective-permute-start.3 = (bf16[4,48,768]{2,1,0:T(8,128)(2,1)S(1)}, bf16[4,48,768]{2,1,0:T(8,128)(2,1)S(1)}, u32[]{:S(2)}, u32[]{:S(2)}) collective-permute-start(bf16[4,48,768]{2,1,0:T(8,128)(2,1)S(1)} %pieces_kernel.1.a), channel_id=1, source_target_pairs={{0,8},{4,12},{8,0},{12,4},{16,24},{20,28},{24,16},{28,20},{1,9},{5... | collective-permute-start | bytes 884744 | tf_op jit(solution)/shard_map/w/ppermute | solution.py:696
  39.6 11.1 %collective-permute-start.11 = (bf16[8,48,768]{2,1,0:T(8,128)(2,1)S(1)}, bf16[8,48,768]{2,1,0:T(8,128)(2,1)S(1)}, u32[]{:S(2)}, u32[]{:S(2)}) collective-permute-start(bf16[8,48,768]{2,1,0:T(8,128)(2,1)S(1)} %pair_kernel.1.here), channel_id=1, source_target_pairs={{0,4},{4,0},{8,12},{12,8},{16,20},{20,16},{24,28},{28,24},{1,5},{5... | collective-permute-start | bytes 1769480 | tf_op jit(solution)/shard_map/w/ppermute | solution.py:696
  39.7 17.5 %collective-permute-start.6 = (bf16[192,512]{1,0:T(8,128)(2,1)S(1)}, bf16[192,512]{1,0:T(8,128)(2,1)S(1)}, u32[]{:S(2)}, u32[]{:S(2)}) collective-permute-start(bf16[192,512]{1,0:T(8,128)(2,1)S(1)} %get-tuple-element.121.a0), channel_id=1, source_target_pairs={{0,1},{1,0},{2,3},{3,2},{4,5},{5,4},{6,7},{7,6},{8,9},{9,8},{10,11... | collective-permute-start | bytes 589832 | tf_op jit(solution)/shard_map/att/ppermute | solution.py:696
  40.8 7.4 %collective-permute-start.7 = (bf16[96,512]{1,0:T(8,128)(2,1)S(1)}, bf16[96,512]{1,0:T(8,128)(2,1)S(1)}, u32[]{:S(2)}, u32[]{:S(2)}) collective-permute-start(bf16[96,512]{1,0:T(8,128)(2,1)S(1)} %get-tuple-element.123), channel_id=1, source_target_pairs={{0,2},{1,3},{2,0},{3,1},{4,6},{5,7},{6,4},{7,5},{8,10},{9,11},{10,... | collective-permute-start | bytes 294920 | tf_op jit(solution)/shard_map/att/ppermute | solution.py:696
  42.7 9.5 %collective-permute-start.10 = (bf16[96,512]{1,0:T(8,128)(2,1)S(1)}, bf16[96,512]{1,0:T(8,128)(2,1)S(1)}, u32[]{:S(2)}, u32[]{:S(2)}) collective-permute-start(bf16[96,512]{1,0:T(8,128)(2,1)S(1)} %get-tuple-element.125), channel_id=1, source_target_pairs={{0,3},{1,2},{2,1},{3,0},{4,7},{5,6},{6,5},{7,4},{8,11},{9,10},{10,... | collective-permute-start | bytes 294920 | tf_op jit(solution)/shard_map/att/ppermute | solution.py:696
  44.2 13.0 %collective-permute-start.8 = (bf16[96,512]{1,0:T(8,128)(2,1)S(1)}, bf16[96,512]{1,0:T(8,128)(2,1)S(1)}, u32[]{:S(2)}, u32[]{:S(2)}) collective-permute-start(bf16[96,512]{1,0:T(8,128)(2,1)S(1)} %get-tuple-element.125), channel_id=1, source_target_pairs={{0,2},{1,3},{2,0},{3,1},{4,6},{5,7},{6,4},{7,5},{8,10},{9,11},{10,... | collective-permute-start | bytes 294920 | tf_op jit(solution)/shard_map/att/ppermute | solution.py:696
  48.1 9.1 %collective-permute-start.9 = (bf16[96,512]{1,0:T(8,128)(2,1)S(1)}, bf16[96,512]{1,0:T(8,128)(2,1)S(1)}, u32[]{:S(2)}, u32[]{:S(2)}) collective-permute-start(bf16[96,512]{1,0:T(8,128)(2,1)S(1)} %collective-permute-done.7.a2t), channel_id=1, source_target_pairs={{0,1},{1,0},{2,3},{3,2},{4,5},{5,4},{6,7},{7,6},{8,9},{9,8},{10,11... | collective-permute-start | bytes 294920 | tf_op jit(solution)/shard_map/att/ppermute | solution.py:696
  50.7 10.8 %collective-permute-start.13 = (bf16[128,768]{1,0:T(8,128)(2,1)S(1)}, bf16[128,768]{1,0:T(8,128)(2,1)S(1)}, u32[]{:S(2)}, u32[]{:S(2)}) collective-permute-start(bf16[128,768]{1,0:T(8,128)(2,1)S(1)} %collective-permute-done.5.c2), channel_id=1, source_target_pairs={{0,1},{1,0},{2,3},{3,2},{4,5},{5,4},{6,7},{7,6},{8,9},{9,8},{10,11... | collective-permute-start | bytes 589832 | tf_op jit(solution)/shard_map/dy/ppermute | solution.py:696
  57.2 4.3 %copy-start.3 = (bf16[768,768]{1,0:T(8,128)(2,1)S(1)}, bf16[768,768]{1,0:T(8,128)(2,1)}, u32[]{:S(2)}) copy-start(bf16[768,768]{1,0:T(8,128)(2,1)} %w_down.1) | copy-start | bytes 3538948
  61.4 15.9 %collective-permute-start.12 = (bf16[1536,128]{1,0:T(8,128)(2,1)S(1)}, bf16[1536,128]{1,0:T(8,128)(2,1)S(1)}, u32[]{:S(2)}, u32[]{:S(2)}) collective-permute-start(bf16[1536,128]{1,0:T(8,128)(2,1)S(1)} %get-tuple-element.131), channel_id=1, source_target_pairs={{0,1},{1,0},{2,3},{3,2},{4,5},{5,4},{6,7},{7,6},{8,9},{9,8},{10,11... | collective-permute-start | bytes 1179656 | tf_op jit(solution)/shard_map/mlp/ppermute | solution.py:696
  66.1 14.2 %collective-permute-start.14 = (bf16[192,512]{1,0:T(8,128)(2,1)S(1)}, bf16[192,512]{1,0:T(8,128)(2,1)S(1)}, u32[]{:S(2)}, u32[]{:S(2)}) collective-permute-start(bf16[192,512]{1,0:T(8,128)(2,1)S(1)} %get-tuple-element.140), channel_id=1, source_target_pairs={{0,1},{1,0},{2,3},{3,2},{4,5},{5,4},{6,7},{7,6},{8,9},{9,8},{10,11... | collective-permute-start | bytes 589832 | tf_op jit(solution)/shard_map/d_att/ppermute | solution.py:696
  68.2 17.0 %collective-permute-start.15 = (bf16[192,512]{1,0:T(8,128)(2,1)S(1)}, bf16[192,512]{1,0:T(8,128)(2,1)S(1)}, u32[]{:S(2)}, u32[]{:S(2)}) collective-permute-start(bf16[192,512]{1,0:T(8,128)(2,1)S(1)} %get-tuple-element.141), channel_id=1, source_target_pairs={{0,2},{1,3},{2,0},{3,1},{4,6},{5,7},{6,4},{7,5},{8,10},{9,11},{10,... | collective-permute-start | bytes 589832 | tf_op jit(solution)/shard_map/d_att/ppermute | solution.py:696
  68.5 16.7 %collective-permute-start.16 = (bf16[192,512]{1,0:T(8,128)(2,1)S(1)}, bf16[192,512]{1,0:T(8,128)(2,1)S(1)}, u32[]{:S(2)}, u32[]{:S(2)}) collective-permute-start(bf16[192,512]{1,0:T(8,128)(2,1)S(1)} %get-tuple-element.142), channel_id=1, source_target_pairs={{0,3},{1,2},{2,1},{3,0},{4,7},{5,6},{6,5},{7,4},{8,11},{9,10},{10,... | collective-permute-start | bytes 589832 | tf_op jit(solution)/shard_map/d_att/ppermute | solution.py:696
  73.2 25.1 %collective-permute-start.21 = (bf16[384,1152]{1,0:T(8,128)(2,1)S(1)}, bf16[384,1152]{1,0:T(8,128)(2,1)S(1)}, u32[]{:S(2)}, u32[]{:S(2)}) collective-permute-start(bf16[384,1152]{1,0:T(8,128)(2,1)S(1)} %get-tuple-element.174), channel_id=1, source_target_pairs={{0,8},{4,12},{8,0},{12,4},{16,24},{20,28},{24,16},{28,20},{1,9},{5... | collective-permute-start | bytes 2654216 | tf_op jit(solution)/shard_map/grads_a/ppermute | solution.py:696
  77.3 21.0 %collective-permute-start.22 = (bf16[384,1152]{1,0:T(8,128)(2,1)S(1)}, bf16[384,1152]{1,0:T(8,128)(2,1)S(1)}, u32[]{:S(2)}, u32[]{:S(2)}) collective-permute-start(bf16[384,1152]{1,0:T(8,128)(2,1)S(1)} %get-tuple-element.176), channel_id=1, source_target_pairs={{0,16},{4,20},{8,24},{12,28},{16,0},{20,4},{24,8},{28,12},{1,17},{... | collective-permute-start | bytes 2654216 | tf_op jit(solution)/shard_map/grads_b/ppermute | solution.py:696
  85.1 10.5 %collective-permute-start.17 = (bf16[768,128]{1,0:T(8,128)(2,1)S(1)}, bf16[768,128]{1,0:T(8,128)(2,1)S(1)}, u32[]{:S(2)}, u32[]{:S(2)}) collective-permute-start(bf16[768,128]{1,0:T(8,128)(2,1)S(1)} %get-tuple-element.143), channel_id=1, source_target_pairs={{0,2},{1,3},{2,0},{3,1},{4,6},{5,7},{6,4},{7,5},{8,10},{9,11},{10,... | collective-permute-start | bytes 589832 | tf_op jit(solution)/shard_map/mlp/ppermute | solution.py:696
  95.7 1.9 %collective-permute-start.20 = (bf16[416,576]{1,0:T(8,128)(2,1)S(1)}, bf16[416,576]{1,0:T(8,128)(2,1)S(1)}, u32[]{:S(2)}, u32[]{:S(2)}) collective-permute-start(bf16[416,576]{1,0:T(8,128)(2,1)S(1)} %get-tuple-element.170), channel_id=1, source_target_pairs={{0,4},{4,0},{8,12},{12,8},{16,20},{20,16},{24,28},{28,24},{1,5},{5... | collective-permute-start | bytes 1437704 | tf_op jit(solution)/shard_map/qkv_core/ppermute | solution.py:696
  95.7 11.5 %collective-permute-start.18 = (bf16[1536,128]{1,0:T(8,128)(2,1)S(1)}, bf16[1536,128]{1,0:T(8,128)(2,1)S(1)}, u32[]{:S(2)}, u32[]{:S(2)}) collective-permute-start(bf16[1536,128]{1,0:T(8,128)(2,1)S(1)} %get-tuple-element.164), channel_id=1, source_target_pairs={{0,1},{1,0},{2,3},{3,2},{4,5},{5,4},{6,7},{7,6},{8,9},{9,8},{10,11... | collective-permute-start | bytes 1179656 | tf_op jit(solution)/shard_map/back/ppermute | solution.py:696
  99.3 2.2 %collective-permute-start.23 = (bf16[192,768]{1,0:T(8,128)(2,1)S(1)}, bf16[192,768]{1,0:T(8,128)(2,1)S(1)}, u32[]{:S(2)}, u32[]{:S(2)}) collective-permute-start(bf16[192,768]{1,0:T(8,128)(2,1)S(1)} %get-tuple-element.178), channel_id=1, source_target_pairs={{0,4},{4,0},{8,12},{12,8},{16,20},{20,16},{24,28},{28,24},{1,5},{5... | collective-permute-start | bytes 884744 | tf_op jit(solution)/shard_map/grads_core/ppermute | solution.py:696
  99.5 2.0 %collective-permute-start.24 = (bf16[192,768]{1,0:T(8,128)(2,1)S(1)}, bf16[192,768]{1,0:T(8,128)(2,1)S(1)}, u32[]{:S(2)}, u32[]{:S(2)}) collective-permute-start(bf16[192,768]{1,0:T(8,128)(2,1)S(1)} %get-tuple-element.179), channel_id=1, source_target_pairs={{0,4},{4,0},{8,12},{12,8},{16,20},{20,16},{24,28},{28,24},{1,5},{5... | collective-permute-start | bytes 884744 | tf_op jit(solution)/shard_map/grads_core/ppermute | solution.py:696
  99.9 1.9 %collective-permute-start.25 = (bf16[192,768]{1,0:T(8,128)(2,1)S(1)}, bf16[192,768]{1,0:T(8,128)(2,1)S(1)}, u32[]{:S(2)}, u32[]{:S(2)}) collective-permute-start(bf16[192,768]{1,0:T(8,128)(2,1)S(1)} %get-tuple-element.180), channel_id=1, source_target_pairs={{0,4},{4,0},{8,12},{12,8},{16,20},{20,16},{24,28},{28,24},{1,5},{5... | collective-permute-start | bytes 884744 | tf_op jit(solution)/shard_map/grads_core/ppermute | solution.py:696
  100.0 9.7 %collective-permute-start.26 = (bf16[224,576]{1,0:T(8,128)(2,1)S(1)}, bf16[224,576]{1,0:T(8,128)(2,1)S(1)}, u32[]{:S(2)}, u32[]{:S(2)}) collective-permute-start(bf16[224,576]{1,0:T(8,128)(2,1)S(1)} %get-tuple-element.184), channel_id=1, source_target_pairs={{0,8},{4,12},{8,0},{12,4},{16,24},{20,28},{24,16},{28,20},{1,9},{5... | collective-permute-start | bytes 774152 | tf_op jit(solution)/shard_map/qkv_x/ppermute | solution.py:696
  102.5 10.3 %collective-permute-start.27 = (bf16[96,1152]{1,0:T(8,128)(2,1)S(1)}, bf16[96,1152]{1,0:T(8,128)(2,1)S(1)}, u32[]{:S(2)}, u32[]{:S(2)}) collective-permute-start(bf16[96,1152]{1,0:T(8,128)(2,1)S(1)} %get-tuple-element.186), channel_id=1, source_target_pairs={{0,16},{4,20},{8,24},{12,28},{16,0},{20,4},{24,8},{28,12},{1,17},{... | collective-permute-start | bytes 663560 | tf_op jit(solution)/shard_map/grads_a/ppermute | solution.py:696
  104.1 11.6 %collective-permute-start.28 = (bf16[96,1152]{1,0:T(8,128)(2,1)S(1)}, bf16[96,1152]{1,0:T(8,128)(2,1)S(1)}, u32[]{:S(2)}, u32[]{:S(2)}) collective-permute-start(bf16[96,1152]{1,0:T(8,128)(2,1)S(1)} %get-tuple-element.189), channel_id=1, source_target_pairs={{0,8},{4,12},{8,0},{12,4},{16,24},{20,28},{24,16},{28,20},{1,9},{5... | collective-permute-start | bytes 663560 | tf_op jit(solution)/shard_map/grads_b/ppermute | solution.py:696
  107.3 12.7 %collective-permute-start.19 = (bf16[768,128]{1,0:T(8,128)(2,1)S(1)}, bf16[768,128]{1,0:T(8,128)(2,1)S(1)}, u32[]{:S(2)}, u32[]{:S(2)}) collective-permute-start(bf16[768,128]{1,0:T(8,128)(2,1)S(1)} %get-tuple-element.166), channel_id=1, source_target_pairs={{0,2},{1,3},{2,0},{3,1},{4,6},{5,7},{6,4},{7,5},{8,10},{9,11},{10,... | collective-permute-start | bytes 589832 | tf_op jit(solution)/shard_map/back/ppermute | solution.py:696
  110.3 5.4 %collective-permute-start.29 = (bf16[128,576]{1,0:T(8,128)(2,1)S(1)}, bf16[128,576]{1,0:T(8,128)(2,1)S(1)}, u32[]{:S(2)}, u32[]{:S(2)}) collective-permute-start(bf16[128,576]{1,0:T(8,128)(2,1)S(1)} %get-tuple-element.190), channel_id=1, source_target_pairs={{0,16},{4,20},{8,24},{12,28},{16,0},{20,4},{24,8},{28,12},{1,17},{... | collective-permute-start | bytes 442376 | tf_op jit(solution)/shard_map/qkv_y/ppermute | solution.py:696
  116.4 7.7 %collective-permute-start.31 = (bf16[288,128]{1,0:T(8,128)(2,1)S(1)}, bf16[288,128]{1,0:T(8,128)(2,1)S(1)}, u32[]{:S(2)}, u32[]{:S(2)}) collective-permute-start(bf16[288,128]{1,0:T(8,128)(2,1)S(1)} %get-tuple-element.194), channel_id=1, source_target_pairs={{0,2},{1,3},{2,0},{3,1},{4,6},{5,7},{6,4},{7,5},{8,10},{9,11},{10,... | collective-permute-start | bytes 221192 | tf_op jit(solution)/shard_map/out/ppermute | solution.py:696
  117.3 6.8 %collective-permute-start.32 = (bf16[288,128]{1,0:T(8,128)(2,1)S(1)}, bf16[288,128]{1,0:T(8,128)(2,1)S(1)}, u32[]{:S(2)}, u32[]{:S(2)}) collective-permute-start(bf16[288,128]{1,0:T(8,128)(2,1)S(1)} %get-tuple-element.195), channel_id=1, source_target_pairs={{0,3},{1,2},{2,1},{3,0},{4,7},{5,6},{6,5},{7,4},{8,11},{9,10},{10,... | collective-permute-start | bytes 221192 | tf_op jit(solution)/shard_map/out/ppermute | solution.py:696
  119.3 5.3 %collective-permute-start.30 = (bf16[288,128]{1,0:T(8,128)(2,1)S(1)}, bf16[288,128]{1,0:T(8,128)(2,1)S(1)}, u32[]{:S(2)}, u32[]{:S(2)}) collective-permute-start(bf16[288,128]{1,0:T(8,128)(2,1)S(1)} %get-tuple-element.193), channel_id=1, source_target_pairs={{0,1},{1,0},{2,3},{3,2},{4,5},{5,4},{6,7},{7,6},{8,9},{9,8},{10,11... | collective-permute-start | bytes 221192 | tf_op jit(solution)/shard_map/out/ppermute | solution.py:696

commit v9 on v8

--- a/solution.py
+++ b/solution.py
@@ -708,9 +708,6 @@
     piece = channels // 4
     sent = jnp.concatenate([tokens, lax.dynamic_slice_in_dim(w_out, (d & 3) * piece, piece, 0)])
     x1, x2 = swap(sent, 1, name="x"), swap(sent, 2, name="x")
-    x = [sent, x1, x2, swap(after(x2, x1), 1, name="x")]
-    dy2 = swap(after(cotangent, *x[1:]), 2, name="dy")
-    dy1 = swap(after(cotangent, *x[1:]), 1, name="dy")
     wq_t, w_up_t, w_down_t = call(
         turn_kernel,
         [like((width, 3 * channels), BF16), like((hidden, width), BF16), like((width, hidden), BF16)],
@@ -722,6 +719,9 @@
         [place, page_lengths, rel_table],
         n_smem=3,
     )
+    x = [sent, x1, x2, swap(after(x2, x1, wq_t, pattern, cols), 1, name="x")]
+    dy2 = swap(after(cotangent, *x[1:]), 2, name="dy")
+    dy1 = swap(after(cotangent, *x[1:]), 1, name="dy")
     x[1:] = lax.optimization_barrier((x[1:], wq_t, pattern))[0]
     (part,) = call(pieces_kernel, [like((4, piece, width), BF16)], x)
     part_x = swap(part, 2, "dp", name="w")
@@ -833,7 +833,7 @@
         limit=24,
         us=10,
     )
-    p_recv = swap(after(p13, mlp[1]), 1, name="back")
+    p_recv = swap(p13, 1, name="back")
     back = halved(p0, p2, p_recv, "back", us=10)
 
     def reduced(g):

time: 126 us -> 126 us (level)
  waiting for transfers between devices: 42.3 us -> 39.2 us
  starting transfers between devices: 42.3 us -> 44.8 us
    ppermute x33, waiting for transfers between devices: 42.3 us -> 39.2 us  [swap(): return lax.ppermute(v, axis, [(i, i ^ k) for i in range(n)])]
    ppermute x33, starting transfers between devices: 42.3 us -> 44.8 us  [swap(): return lax.ppermute(v, axis, [(i, i ^ k) for i in range(n)])]
    unnamed x17 -> x19, local copies, waits for them, and re-layouts: 4.17 us -> 4.83 us
  transfers between devices with their start and end apart: 33 -> 33, of which waited for: 18 -> 19; matrix products, arithmetic and copies ran while one was open for 2% -> 2% of each run, Pallas kernels for 26% -> 26%
where the time goes in v9:
time: 126 us; the launch traced here: 125 us
  starting transfers between devices  44.8 us (36%)
  waiting for transfers between devices  39.2 us (31%)
  Pallas kernels  32.9 us (26%)
  local copies, waits for them, and re-layouts  6.52 us (5%)
    ppermute x33, starting transfers between devices, swap(): return lax.ppermute(v, axis, [(i, i ^ k) for i in range(n)])  44.8 us
    ppermute x33, waiting for transfers between devices, swap(): return lax.ppermute(v, axis, [(i, i ^ k) for i in range(n)])  39.2 us
    pallas_call x21, Pallas kernels, call(): pl.pallas_call(kernel, out_shape=tuple(outs), in_specs=[SMEM] * n_smem +...  32.9 us
    unnamed x19, local copies, waits for them, and re-layouts  4.83 us
  transfers between devices with their start and end apart: 33, of which 19 were waited for; matrix products, arithmetic and copies ran while one was open for 2% of the time, Pallas kernels for 26%

profile of v9, /device:TPU:0, one launch (start us, length us, event | category | flops | bytes accessed | tf_op | source)
XLA Modules:
  0.0 125.3 jit_solution(13514678635226470288)
XLA Ops:
  0.7 0.9 copy-done
  1.6 0.9 pad_maximum_fusion.x0
  2.6 4.1 %collective-permute-start.1 = (bf16[176,768]{1,0:T(8,128)(2,1)S(1)}, bf16[176,768]{1,0:T(8,128)(2,1)S(1)}, u32[]{:S(2)}, u32[]{:S(2)}) collective-permute-start(bf16[176,768]{1,0:T(8,128)(2,1)S(1)} %pad_maximum_fusion.x0), channel_id=1, source_target_pairs={{0,2},{1,3},{2,0},{3,1},{4,6},{5,7},{6,4},{7,5},{8,10},{9,11},{10,... | collective-permute-start | bytes 811016 | tf_op jit(solution)/shard_map/x/ppermute | solution.py:696
  6.7 1.6 %collective-permute-start = (bf16[176,768]{1,0:T(8,128)(2,1)S(1)}, bf16[176,768]{1,0:T(8,128)(2,1)S(1)}, u32[]{:S(2)}, u32[]{:S(2)}) collective-permute-start(bf16[176,768]{1,0:T(8,128)(2,1)S(1)} %pad_maximum_fusion.x0), channel_id=1, source_target_pairs={{0,1},{1,0},{2,3},{3,2},{4,5},{5,4},{6,7},{7,6},{8,9},{9,8},{10,11... | collective-permute-start | bytes 811016 | tf_op jit(solution)/shard_map/x/ppermute | solution.py:696
  8.2 0.8 copy.30.table
  9.0 0.8 fusion
  9.8 0.7 concatenate.7
  10.8 0.7 copy-done.7
  11.5 1.5 %bias_kernel.1 = (f32[3,3,128,128]{3,2,1,0:T(8,128)S(1)}, s32[512,128]{1,0:T(8,128)S(1)}) custom-call(s32[2]{0:T(128)S(1)} %pad_add_fusion.place, s32[1,8]{1,0:T(1,128)S(1)} %copy-done.7, f32[32,12]{1,0:T(8,128)S(1)} %copy.30.table), custom_call_target="tpu_custom_call" | custom-call | flops 11500000 | bytes 8 | tf_op jit(solution)/shard_map/bias_kernel/pallas_call | solution.py:21
  13.0 1.3 %copy-done.2 = bf16[768,768]{1,0:T(8,128)(2,1)S(1)} copy-done((bf16[768,768]{1,0:T(8,128)(2,1)S(1)}, bf16[768,768]{1,0:T(8,128)(2,1)}, u32[]{:S(2)}) %copy-start.2) | copy-done | bytes 1179672
  14.2 1.2 copy-done.4
  15.4 0.9 turn_kernel.1
  16.3 2.7 %collective-permute-done.1.x2 = bf16[176,768]{1,0:T(8,128)(2,1)S(1)} collective-permute-done((bf16[176,768]{1,0:T(8,128)(2,1)S(1)}, bf16[176,768]{1,0:T(8,128)(2,1)S(1)}, u32[]{:S(2)}, u32[]{:S(2)}) %collective-permute-start.1) | collective-permute-done | bytes 270368 | tf_op jit(solution)/shard_map/x/ppermute | solution.py:696
  19.2 1.5 %collective-permute-start.2 = (bf16[176,768]{1,0:T(8,128)(2,1)S(1)}, bf16[176,768]{1,0:T(8,128)(2,1)S(1)}, u32[]{:S(2)}, u32[]{:S(2)}) collective-permute-start(bf16[176,768]{1,0:T(8,128)(2,1)S(1)} %collective-permute-done.1.x2), channel_id=1, source_target_pairs={{0,1},{1,0},{2,3},{3,2},{4,5},{5,4},{6,7},{7,6},{8,9},{9,8},{10,11... | collective-permute-start | bytes 811016 | tf_op jit(solution)/shard_map/x/ppermute | solution.py:696
  20.7 5.9 %collective-permute-done.2.x3 = bf16[176,768]{1,0:T(8,128)(2,1)S(1)} collective-permute-done((bf16[176,768]{1,0:T(8,128)(2,1)S(1)}, bf16[176,768]{1,0:T(8,128)(2,1)S(1)}, u32[]{:S(2)}, u32[]{:S(2)}) %collective-permute-start.2) | collective-permute-done | bytes 270368 | tf_op jit(solution)/shard_map/x/ppermute | solution.py:696
  26.7 3.0 %collective-permute-start.5 = (bf16[128,768]{1,0:T(8,128)(2,1)S(1)}, bf16[128,768]{1,0:T(8,128)(2,1)S(1)}, u32[]{:S(2)}, u32[]{:S(2)}) collective-permute-start(bf16[128,768]{1,0:T(8,128)(2,1)S(1)} %copy-done.6), channel_id=1, source_target_pairs={{0,2},{1,3},{2,0},{3,1},{4,6},{5,7},{6,4},{7,5},{8,10},{9,11},{10,... | collective-permute-start | bytes 589832 | tf_op jit(solution)/shard_map/dy/ppermute | solution.py:696
  29.7 1.7 %collective-permute-start.4 = (bf16[128,768]{1,0:T(8,128)(2,1)S(1)}, bf16[128,768]{1,0:T(8,128)(2,1)S(1)}, u32[]{:S(2)}, u32[]{:S(2)}) collective-permute-start(bf16[128,768]{1,0:T(8,128)(2,1)S(1)} %copy-done.6), channel_id=1, source_target_pairs={{0,1},{1,0},{2,3},{3,2},{4,5},{5,4},{6,7},{7,6},{8,9},{9,8},{10,11... | collective-permute-start | bytes 589832 | tf_op jit(solution)/shard_map/dy/ppermute | solution.py:696
  31.5 1.6 %collective-permute-start.3 = (bf16[4,48,768]{2,1,0:T(8,128)(2,1)S(1)}, bf16[4,48,768]{2,1,0:T(8,128)(2,1)S(1)}, u32[]{:S(2)}, u32[]{:S(2)}) collective-permute-start(bf16[4,48,768]{2,1,0:T(8,128)(2,1)S(1)} %pieces_kernel.1.a), channel_id=1, source_target_pairs={{0,8},{4,12},{8,0},{12,4},{16,24},{20,28},{24,16},{28,20},{1,9},{5... | collective-permute-start | bytes 884744 | tf_op jit(solution)/shard_map/w/ppermute | solution.py:696
  33.0 4.2 %head_kernel.1 = (bf16[768,512]{1,0:T(8,128)(2,1)S(1)}, bf16[768,512]{1,0:T(8,128)(2,1)S(1)}, f32[8,512]{1,0:T(8,128)S(1)}, bf16[576,512]{1,0:T(8,128)(2,1)S(1)}...) custom-call(s32[2]{0:T(128)S(1)} %pad_add_fusion.place, ...), custom_call_target="tpu_custom_call" | custom-call | flops 11500000256 | bytes 8 | tf_op jit(solution)/shard_map/head_kernel/pallas_call | solution.py:21
  37.2 1.4 %collective-permute-done.5.c2 = bf16[128,768]{1,0:T(8,128)(2,1)S(1)} collective-permute-done((bf16[128,768]{1,0:T(8,128)(2,1)S(1)}, bf16[128,768]{1,0:T(8,128)(2,1)S(1)}, u32[]{:S(2)}, u32[]{:S(2)}) %collective-permute-start.5) | collective-permute-done | bytes 196640 | tf_op jit(solution)/shard_map/dy/ppermute | solution.py:696
  39.2 1.3 %collective-permute-start.6 = (bf16[192,512]{1,0:T(8,128)(2,1)S(1)}, bf16[192,512]{1,0:T(8,128)(2,1)S(1)}, u32[]{:S(2)}, u32[]{:S(2)}) collective-permute-start(bf16[192,512]{1,0:T(8,128)(2,1)S(1)} %get-tuple-element.120.a0), channel_id=1, source_target_pairs={{0,1},{1,0},{2,3},{3,2},{4,5},{5,4},{6,7},{7,6},{8,9},{9,8},{10,11... | collective-permute-start | bytes 589832 | tf_op jit(solution)/shard_map/att/ppermute | solution.py:696
  40.5 2.3 %collective-permute-start.7 = (bf16[96,512]{1,0:T(8,128)(2,1)S(1)}, bf16[96,512]{1,0:T(8,128)(2,1)S(1)}, u32[]{:S(2)}, u32[]{:S(2)}) collective-permute-start(bf16[96,512]{1,0:T(8,128)(2,1)S(1)} %get-tuple-element.122), channel_id=1, source_target_pairs={{0,2},{1,3},{2,0},{3,1},{4,6},{5,7},{6,4},{7,5},{8,10},{9,11},{10,... | collective-permute-start | bytes 294920 | tf_op jit(solution)/shard_map/att/ppermute | solution.py:696
  42.7 0.9 collective-permute-start.10
  43.6 0.6 collective-permute-start.8
  44.3 3.5 %collective-permute-done.7.a2t = bf16[96,512]{1,0:T(8,128)(2,1)S(1)} collective-permute-done((bf16[96,512]{1,0:T(8,128)(2,1)S(1)}, bf16[96,512]{1,0:T(8,128)(2,1)S(1)}, u32[]{:S(2)}, u32[]{:S(2)}) %collective-permute-start.7) | collective-permute-done | bytes 98336 | tf_op jit(solution)/shard_map/att/ppermute | solution.py:696
  47.8 2.9 %collective-permute-start.9 = (bf16[96,512]{1,0:T(8,128)(2,1)S(1)}, bf16[96,512]{1,0:T(8,128)(2,1)S(1)}, u32[]{:S(2)}, u32[]{:S(2)}) collective-permute-start(bf16[96,512]{1,0:T(8,128)(2,1)S(1)} %collective-permute-done.7.a2t), channel_id=1, source_target_pairs={{0,1},{1,0},{2,3},{3,2},{4,5},{5,4},{6,7},{7,6},{8,9},{9,8},{10,11... | collective-permute-start | bytes 294920 | tf_op jit(solution)/shard_map/att/ppermute | solution.py:696
  50.7 1.0 out_weight_kernel.1
  51.7 0.5 collective-permute-done.10.a3b
  52.2 4.7 %collective-permute-done.8.a2b = bf16[96,512]{1,0:T(8,128)(2,1)S(1)} collective-permute-done((bf16[96,512]{1,0:T(8,128)(2,1)S(1)}, bf16[96,512]{1,0:T(8,128)(2,1)S(1)}, u32[]{:S(2)}, u32[]{:S(2)}) %collective-permute-start.8) | collective-permute-done | bytes 98336 | tf_op jit(solution)/shard_map/att/ppermute | solution.py:696
  56.9 4.1 %up_kernel.1 = (bf16[768,512]{1,0:T(8,128)(2,1)S(1)}, f32[768,512]{1,0:T(8,128)S(1)}, f32[768,512]{1,0:T(8,128)S(1)}, f32[8,512]{1,0:T(8,128)S(1)}, bf16[768,512...) custom-call(s32[2]{0:T(128)S(1)} %pad_add_fusion.place, ...), custom_call_target="tpu_custom_call" | custom-call | flops 11500000256 | bytes 8 | tf_op jit(solution)/shard_map/up_kernel/pallas_call | solution.py:21
  61.2 4.6 %down_kernel.1 = (bf16[192,512]{1,0:T(8,128)(2,1)S(1)}, bf16[192,512]{1,0:T(8,128)(2,1)S(1)}, bf16[192,512]{1,0:T(8,128)(2,1)S(1)}, bf16[192,512]{1,0:T(8,128)(2...) custom-call(s32[2]{0:T(128)S(1)} %pad_add_fusion.place, ...), custom_call_target="tpu_custom_call" | custom-call | flops 11500000256 | bytes 8 | tf_op jit(solution)/shard_map/down_kernel/pallas_call | solution.py:21
  65.8 2.1 %collective-permute-start.14 = (bf16[192,512]{1,0:T(8,128)(2,1)S(1)}, bf16[192,512]{1,0:T(8,128)(2,1)S(1)}, u32[]{:S(2)}, u32[]{:S(2)}) collective-permute-start(bf16[192,512]{1,0:T(8,128)(2,1)S(1)} %get-tuple-element.139), channel_id=1, source_target_pairs={{0,1},{1,0},{2,3},{3,2},{4,5},{5,4},{6,7},{7,6},{8,9},{9,8},{10,11... | collective-permute-start | bytes 589832 | tf_op jit(solution)/shard_map/d_att/ppermute | solution.py:696
  67.9 0.6 collective-permute-start.15
  68.5 1.8 %collective-permute-start.16 = (bf16[192,512]{1,0:T(8,128)(2,1)S(1)}, bf16[192,512]{1,0:T(8,128)(2,1)S(1)}, u32[]{:S(2)}, u32[]{:S(2)}) collective-permute-start(bf16[192,512]{1,0:T(8,128)(2,1)S(1)} %get-tuple-element.141), channel_id=1, source_target_pairs={{0,3},{1,2},{2,1},{3,0},{4,7},{5,6},{6,5},{7,4},{8,11},{9,10},{10,... | collective-permute-start | bytes 589832 | tf_op jit(solution)/shard_map/d_att/ppermute | solution.py:696
  70.3 2.6 %mlp_grad_kernel.1 = (f32[8,768]{1,0:T(8,128)S(1)}, bf16[384,1152]{1,0:T(8,128)(2,1)S(1)}, bf16[384,1152]{1,0:T(8,128)(2,1)S(1)}, bf16[384,1152]{1,0:T(8,128)(2,1)S(1)}, bf16[384,1152]{1,0:T(8,128)(2,1)S(1)}) custom-call(s32[2]{0:T(128)S(1)} %pad_add_fusion.place, f32[8,768]{1,0:T(8,128)S(1)} %get-tuple-element.150.vec, ...), custom_call_target="tpu_custom_call" | custom-call | flops 11500000 | bytes 8 | tf_op jit(solution)/shard_map/mlp_grad_kernel/pallas_call | solution.py:21
  72.9 1.6 %collective-permute-start.21 = (bf16[384,1152]{1,0:T(8,128)(2,1)S(1)}, bf16[384,1152]{1,0:T(8,128)(2,1)S(1)}, u32[]{:S(2)}, u32[]{:S(2)}) collective-permute-start(bf16[384,1152]{1,0:T(8,128)(2,1)S(1)} %get-tuple-element.172), channel_id=1, source_target_pairs={{0,8},{4,12},{8,0},{12,4},{16,24},{20,28},{24,16},{28,20},{1,9},{5... | collective-permute-start | bytes 2654216 | tf_op jit(solution)/shard_map/grads_a/ppermute | solution.py:696
  74.5 2.6 %collective-permute-done.12.recv = bf16[1536,128]{1,0:T(8,128)(2,1)S(1)} collective-permute-done((bf16[1536,128]{1,0:T(8,128)(2,1)S(1)}, bf16[1536,128]{1,0:T(8,128)(2,1)S(1)}, u32[]{:S(2)}, u32[]{:S(2)}) %collective-permute-start.12) | collective-permute-done | bytes 393248 | tf_op jit(solution)/shard_map/mlp/ppermute | solution.py:696
  77.1 1.5 %collective-permute-start.22 = (bf16[384,1152]{1,0:T(8,128)(2,1)S(1)}, bf16[384,1152]{1,0:T(8,128)(2,1)S(1)}, u32[]{:S(2)}, u32[]{:S(2)}) collective-permute-start(bf16[384,1152]{1,0:T(8,128)(2,1)S(1)} %get-tuple-element.174), channel_id=1, source_target_pairs={{0,16},{4,20},{8,24},{12,28},{16,0},{20,4},{24,8},{28,12},{1,17},{... | collective-permute-start | bytes 2654216 | tf_op jit(solution)/shard_map/grads_b/ppermute | solution.py:696
  78.7 1.3 %collective-permute-done.14.d1 = bf16[192,512]{1,0:T(8,128)(2,1)S(1)} collective-permute-done((bf16[192,512]{1,0:T(8,128)(2,1)S(1)}, bf16[192,512]{1,0:T(8,128)(2,1)S(1)}, u32[]{:S(2)}, u32[]{:S(2)}) %collective-permute-start.14) | collective-permute-done | bytes 196640 | tf_op jit(solution)/shard_map/d_att/ppermute | solution.py:696
  80.0 4.8 %collective-permute-done.15.d2 = bf16[192,512]{1,0:T(8,128)(2,1)S(1)} collective-permute-done((bf16[192,512]{1,0:T(8,128)(2,1)S(1)}, bf16[192,512]{1,0:T(8,128)(2,1)S(1)}, u32[]{:S(2)}, u32[]{:S(2)}) %collective-permute-start.15) | collective-permute-done | bytes 196640 | tf_op jit(solution)/shard_map/d_att/ppermute | solution.py:696
  84.8 4.3 %collective-permute-start.17 = (bf16[768,128]{1,0:T(8,128)(2,1)S(1)}, bf16[768,128]{1,0:T(8,128)(2,1)S(1)}, u32[]{:S(2)}, u32[]{:S(2)}) collective-permute-start(bf16[768,128]{1,0:T(8,128)(2,1)S(1)} %get-tuple-element.142), channel_id=1, source_target_pairs={{0,2},{1,3},{2,0},{3,1},{4,6},{5,7},{6,4},{7,5},{8,10},{9,11},{10,... | collective-permute-start | bytes 589832 | tf_op jit(solution)/shard_map/mlp/ppermute | solution.py:696
  89.1 6.5 %back_kernel.1 = (f32[768,128]{1,0:T(8,128)S(1)}, f32[768,128]{1,0:T(8,128)S(1)}, bf16[1536,128]{1,0:T(8,128)(2,1)S(1)}, f32[8,768]{1,0:T(8,128)S(1)}, bf16[416,...) custom-call(s32[2]{0:T(128)S(1)} %pad_add_fusion.place, s32[1,8]{1,0:T(1,128)S(1)} %copy-done.8, ...), custom_call_target="tpu_custom_call" | custom-call | flops 11500000256 | bytes 8 | tf_op jit(solution)/shard_map/back_kernel/pallas_call | solution.py:21
  95.9 1.8 %collective-permute-done.20.recv = bf16[416,576]{1,0:T(8,128)(2,1)S(1)} collective-permute-done((bf16[416,576]{1,0:T(8,128)(2,1)S(1)}, bf16[416,576]{1,0:T(8,128)(2,1)S(1)}, u32[]{:S(2)}, u32[]{:S(2)}) %collective-permute-start.20) | collective-permute-done | bytes 479264 | tf_op jit(solution)/shard_map/qkv_core/ppermute | solution.py:696
  97.7 0.7 qkv_second_kernel.1
  98.4 1.0 grads_second_kernel.1
  100.1 1.5 %collective-permute-start.26 = (bf16[224,576]{1,0:T(8,128)(2,1)S(1)}, bf16[224,576]{1,0:T(8,128)(2,1)S(1)}, u32[]{:S(2)}, u32[]{:S(2)}) collective-permute-start(bf16[224,576]{1,0:T(8,128)(2,1)S(1)} %get-tuple-element.182), channel_id=1, source_target_pairs={{0,8},{4,12},{8,0},{12,4},{16,24},{20,28},{24,16},{28,20},{1,9},{5... | collective-permute-start | bytes 774152 | tf_op jit(solution)/shard_map/qkv_x/ppermute | solution.py:696
  101.9 0.7 grads_third_kernel.1
  102.6 1.6 %collective-permute-start.27 = (bf16[96,1152]{1,0:T(8,128)(2,1)S(1)}, bf16[96,1152]{1,0:T(8,128)(2,1)S(1)}, u32[]{:S(2)}, u32[]{:S(2)}) collective-permute-start(bf16[96,1152]{1,0:T(8,128)(2,1)S(1)} %get-tuple-element.184), channel_id=1, source_target_pairs={{0,16},{4,20},{8,24},{12,28},{16,0},{20,4},{24,8},{28,12},{1,17},{... | collective-permute-start | bytes 663560 | tf_op jit(solution)/shard_map/grads_a/ppermute | solution.py:696
  104.2 1.5 %collective-permute-start.28 = (bf16[96,1152]{1,0:T(8,128)(2,1)S(1)}, bf16[96,1152]{1,0:T(8,128)(2,1)S(1)}, u32[]{:S(2)}, u32[]{:S(2)}) collective-permute-start(bf16[96,1152]{1,0:T(8,128)(2,1)S(1)} %get-tuple-element.187), channel_id=1, source_target_pairs={{0,8},{4,12},{8,0},{12,4},{16,24},{20,28},{24,16},{28,20},{1,9},{5... | collective-permute-start | bytes 663560 | tf_op jit(solution)/shard_map/grads_b/ppermute | solution.py:696
  105.7 1.6 %collective-permute-done.18.recv = bf16[1536,128]{1,0:T(8,128)(2,1)S(1)} collective-permute-done((bf16[1536,128]{1,0:T(8,128)(2,1)S(1)}, bf16[1536,128]{1,0:T(8,128)(2,1)S(1)}, u32[]{:S(2)}, u32[]{:S(2)}) %collective-permute-start.18) | collective-permute-done | bytes 393248 | tf_op jit(solution)/shard_map/back/ppermute | solution.py:696
  107.4 0.7 collective-permute-start.19
  108.1 1.7 %collective-permute-done.26.recv = bf16[224,576]{1,0:T(8,128)(2,1)S(1)} collective-permute-done((bf16[224,576]{1,0:T(8,128)(2,1)S(1)}, bf16[224,576]{1,0:T(8,128)(2,1)S(1)}, u32[]{:S(2)}, u32[]{:S(2)}) %collective-permute-start.26) | collective-permute-done | bytes 258080 | tf_op jit(solution)/shard_map/qkv_x/ppermute | solution.py:696
  109.8 0.6 qkv_third_kernel.1
  110.4 1.6 %collective-permute-start.29 = (bf16[128,576]{1,0:T(8,128)(2,1)S(1)}, bf16[128,576]{1,0:T(8,128)(2,1)S(1)}, u32[]{:S(2)}, u32[]{:S(2)}) collective-permute-start(bf16[128,576]{1,0:T(8,128)(2,1)S(1)} %get-tuple-element.188), channel_id=1, source_target_pairs={{0,16},{4,20},{8,24},{12,28},{16,0},{20,4},{24,8},{28,12},{1,17},{... | collective-permute-start | bytes 442376 | tf_op jit(solution)/shard_map/qkv_y/ppermute | solution.py:696
  112.0 0.9 output_kernel.1
  112.9 2.9 %collective-permute-done.29.q_recv = bf16[128,576]{1,0:T(8,128)(2,1)S(1)} collective-permute-done((bf16[128,576]{1,0:T(8,128)(2,1)S(1)}, bf16[128,576]{1,0:T(8,128)(2,1)S(1)}, u32[]{:S(2)}, u32[]{:S(2)}) %collective-permute-start.29) | collective-permute-done | bytes 147488 | tf_op jit(solution)/shard_map/qkv_y/ppermute | solution.py:696
  115.8 0.7 message_kernel.1
  116.5 0.9 collective-permute-start.31
  117.4 1.9 %collective-permute-start.32 = (bf16[288,128]{1,0:T(8,128)(2,1)S(1)}, bf16[288,128]{1,0:T(8,128)(2,1)S(1)}, u32[]{:S(2)}, u32[]{:S(2)}) collective-permute-start(bf16[288,128]{1,0:T(8,128)(2,1)S(1)} %get-tuple-element.193), channel_id=1, source_target_pairs={{0,3},{1,2},{2,1},{3,0},{4,7},{5,6},{6,5},{7,4},{8,11},{9,10},{10,... | collective-permute-start | bytes 221192 | tf_op jit(solution)/shard_map/out/ppermute | solution.py:696
  119.3 0.8 collective-permute-start.30
  120.1 0.9 input_kernel.1
  120.9 1.0 last_kernel.1
  121.9 2.3 %collective-permute-done.31.o2 = bf16[288,128]{1,0:T(8,128)(2,1)S(1)} collective-permute-done((bf16[288,128]{1,0:T(8,128)(2,1)S(1)}, bf16[288,128]{1,0:T(8,128)(2,1)S(1)}, u32[]{:S(2)}, u32[]{:S(2)}) %collective-permute-start.31) | collective-permute-done | bytes 73760 | tf_op jit(solution)/shard_map/out/ppermute | solution.py:696
  124.6 0.7 small_kernel.1
  (48 shorter events, 3.0 us)
Async XLA Ops:
  0.6 1.0 copy-start
  0.7 12.3 %copy-start.1 = (bf16[768,768]{1,0:T(8,128)(2,1)S(1)}, bf16[768,768]{1,0:T(8,128)(2,1)}, u32[]{:S(2)}) copy-start(bf16[768,768]{1,0:T(8,128)(2,1)} %w_up.1) | copy-start | bytes 3538948
  2.6 16.5 %collective-permute-start.1 = (bf16[176,768]{1,0:T(8,128)(2,1)S(1)}, bf16[176,768]{1,0:T(8,128)(2,1)S(1)}, u32[]{:S(2)}, u32[]{:S(2)}) collective-permute-start(bf16[176,768]{1,0:T(8,128)(2,1)S(1)} %pad_maximum_fusion.x0), channel_id=1, source_target_pairs={{0,2},{1,3},{2,0},{3,1},{4,6},{5,7},{6,4},{7,5},{8,10},{9,11},{10,... | collective-permute-start | bytes 811016 | tf_op jit(solution)/shard_map/x/ppermute | solution.py:696
  6.7 12.6 %collective-permute-start = (bf16[176,768]{1,0:T(8,128)(2,1)S(1)}, bf16[176,768]{1,0:T(8,128)(2,1)S(1)}, u32[]{:S(2)}, u32[]{:S(2)}) collective-permute-start(bf16[176,768]{1,0:T(8,128)(2,1)S(1)} %pad_maximum_fusion.x0), channel_id=1, source_target_pairs={{0,1},{1,0},{2,3},{3,2},{4,5},{5,4},{6,7},{7,6},{8,9},{9,8},{10,11... | collective-permute-start | bytes 811016 | tf_op jit(solution)/shard_map/x/ppermute | solution.py:696
  10.8 0.7 copy-start.7
  12.9 1.3 %copy-start.2 = (bf16[768,768]{1,0:T(8,128)(2,1)S(1)}, bf16[768,768]{1,0:T(8,128)(2,1)}, u32[]{:S(2)}) copy-start(bf16[768,768]{1,0:T(8,128)(2,1)} %w_down.1) | copy-start | bytes 3538948
  14.2 1.2 copy-start.4
  15.4 11.3 %copy-start.6 = (bf16[128,768]{1,0:T(8,128)(2,1)S(1)}, bf16[128,768]{1,0:T(8,128)(2,1)}, u32[]{:S(2)}) copy-start(bf16[128,768]{1,0:T(8,128)(2,1)} %dy.1) | copy-start | bytes 589828
  15.4 17.6 %copy-start.5 = (bf16[768,3,192]{0,2,1:T(8,128)(2,1)S(1)}, bf16[768,3,192]{0,2,1:T(8,128)(2,1)}, u32[]{:S(2)}) copy-start(bf16[768,3,192]{0,2,1:T(8,128)(2,1)} %param.16) | copy-start | bytes 2654212
  15.4 17.6 %copy-start.8 = (s32[1,8]{1,0:T(1,128)S(1)}, s32[1,8]{1,0:T(1,128)}, u32[]{:S(2)}) copy-start(s32[1,8]{1,0:T(1,128)} %lengths.5) | copy-start | bytes 100
  19.2 7.4 %collective-permute-start.2 = (bf16[176,768]{1,0:T(8,128)(2,1)S(1)}, bf16[176,768]{1,0:T(8,128)(2,1)S(1)}, u32[]{:S(2)}, u32[]{:S(2)}) collective-permute-start(bf16[176,768]{1,0:T(8,128)(2,1)S(1)} %collective-permute-done.1.x2), channel_id=1, source_target_pairs={{0,1},{1,0},{2,3},{3,2},{4,5},{5,4},{6,7},{7,6},{8,9},{9,8},{10,11... | collective-permute-start | bytes 811016 | tf_op jit(solution)/shard_map/x/ppermute | solution.py:696
  26.7 11.9 %collective-permute-start.5 = (bf16[128,768]{1,0:T(8,128)(2,1)S(1)}, bf16[128,768]{1,0:T(8,128)(2,1)S(1)}, u32[]{:S(2)}, u32[]{:S(2)}) collective-permute-start(bf16[128,768]{1,0:T(8,128)(2,1)S(1)} %copy-done.6), channel_id=1, source_target_pairs={{0,2},{1,3},{2,0},{3,1},{4,6},{5,7},{6,4},{7,5},{8,10},{9,11},{10,... | collective-permute-start | bytes 589832 | tf_op jit(solution)/shard_map/dy/ppermute | solution.py:696
  29.7 9.3 %collective-permute-start.4 = (bf16[128,768]{1,0:T(8,128)(2,1)S(1)}, bf16[128,768]{1,0:T(8,128)(2,1)S(1)}, u32[]{:S(2)}, u32[]{:S(2)}) collective-permute-start(bf16[128,768]{1,0:T(8,128)(2,1)S(1)} %copy-done.6), channel_id=1, source_target_pairs={{0,1},{1,0},{2,3},{3,2},{4,5},{5,4},{6,7},{7,6},{8,9},{9,8},{10,11... | collective-permute-start | bytes 589832 | tf_op jit(solution)/shard_map/dy/ppermute | solution.py:696
  31.5 7.6 %collective-permute-start.3 = (bf16[4,48,768]{2,1,0:T(8,128)(2,1)S(1)}, bf16[4,48,768]{2,1,0:T(8,128)(2,1)S(1)}, u32[]{:S(2)}, u32[]{:S(2)}) collective-permute-start(bf16[4,48,768]{2,1,0:T(8,128)(2,1)S(1)} %pieces_kernel.1.a), channel_id=1, source_target_pairs={{0,8},{4,12},{8,0},{12,4},{16,24},{20,28},{24,16},{28,20},{1,9},{5... | collective-permute-start | bytes 884744 | tf_op jit(solution)/shard_map/w/ppermute | solution.py:696
  39.1 11.6 %collective-permute-start.11 = (bf16[8,48,768]{2,1,0:T(8,128)(2,1)S(1)}, bf16[8,48,768]{2,1,0:T(8,128)(2,1)S(1)}, u32[]{:S(2)}, u32[]{:S(2)}) collective-permute-start(bf16[8,48,768]{2,1,0:T(8,128)(2,1)S(1)} %pair_kernel.1.here), channel_id=1, source_target_pairs={{0,4},{4,0},{8,12},{12,8},{16,20},{20,16},{24,28},{28,24},{1,5},{5... | collective-permute-start | bytes 1769480 | tf_op jit(solution)/shard_map/w/ppermute | solution.py:696
  39.2 17.7 %collective-permute-start.6 = (bf16[192,512]{1,0:T(8,128)(2,1)S(1)}, bf16[192,512]{1,0:T(8,128)(2,1)S(1)}, u32[]{:S(2)}, u32[]{:S(2)}) collective-permute-start(bf16[192,512]{1,0:T(8,128)(2,1)S(1)} %get-tuple-element.120.a0), channel_id=1, source_target_pairs={{0,1},{1,0},{2,3},{3,2},{4,5},{5,4},{6,7},{7,6},{8,9},{9,8},{10,11... | collective-permute-start | bytes 589832 | tf_op jit(solution)/shard_map/att/ppermute | solution.py:696
  40.5 7.4 %collective-permute-start.7 = (bf16[96,512]{1,0:T(8,128)(2,1)S(1)}, bf16[96,512]{1,0:T(8,128)(2,1)S(1)}, u32[]{:S(2)}, u32[]{:S(2)}) collective-permute-start(bf16[96,512]{1,0:T(8,128)(2,1)S(1)} %get-tuple-element.122), channel_id=1, source_target_pairs={{0,2},{1,3},{2,0},{3,1},{4,6},{5,7},{6,4},{7,5},{8,10},{9,11},{10,... | collective-permute-start | bytes 294920 | tf_op jit(solution)/shard_map/att/ppermute | solution.py:696
  42.7 9.5 %collective-permute-start.10 = (bf16[96,512]{1,0:T(8,128)(2,1)S(1)}, bf16[96,512]{1,0:T(8,128)(2,1)S(1)}, u32[]{:S(2)}, u32[]{:S(2)}) collective-permute-start(bf16[96,512]{1,0:T(8,128)(2,1)S(1)} %get-tuple-element.124), channel_id=1, source_target_pairs={{0,3},{1,2},{2,1},{3,0},{4,7},{5,6},{6,5},{7,4},{8,11},{9,10},{10,... | collective-permute-start | bytes 294920 | tf_op jit(solution)/shard_map/att/ppermute | solution.py:696
  43.6 13.3 %collective-permute-start.8 = (bf16[96,512]{1,0:T(8,128)(2,1)S(1)}, bf16[96,512]{1,0:T(8,128)(2,1)S(1)}, u32[]{:S(2)}, u32[]{:S(2)}) collective-permute-start(bf16[96,512]{1,0:T(8,128)(2,1)S(1)} %get-tuple-element.124), channel_id=1, source_target_pairs={{0,2},{1,3},{2,0},{3,1},{4,6},{5,7},{6,4},{7,5},{8,10},{9,11},{10,... | collective-permute-start | bytes 294920 | tf_op jit(solution)/shard_map/att/ppermute | solution.py:696
  47.8 9.1 %collective-permute-start.9 = (bf16[96,512]{1,0:T(8,128)(2,1)S(1)}, bf16[96,512]{1,0:T(8,128)(2,1)S(1)}, u32[]{:S(2)}, u32[]{:S(2)}) collective-permute-start(bf16[96,512]{1,0:T(8,128)(2,1)S(1)} %collective-permute-done.7.a2t), channel_id=1, source_target_pairs={{0,1},{1,0},{2,3},{3,2},{4,5},{5,4},{6,7},{7,6},{8,9},{9,8},{10,11... | collective-permute-start | bytes 294920 | tf_op jit(solution)/shard_map/att/ppermute | solution.py:696
  50.7 10.4 %collective-permute-start.13 = (bf16[128,768]{1,0:T(8,128)(2,1)S(1)}, bf16[128,768]{1,0:T(8,128)(2,1)S(1)}, u32[]{:S(2)}, u32[]{:S(2)}) collective-permute-start(bf16[128,768]{1,0:T(8,128)(2,1)S(1)} %collective-permute-done.5.c2), channel_id=1, source_target_pairs={{0,1},{1,0},{2,3},{3,2},{4,5},{5,4},{6,7},{7,6},{8,9},{9,8},{10,11... | collective-permute-start | bytes 589832 | tf_op jit(solution)/shard_map/dy/ppermute | solution.py:696
  56.9 4.3 %copy-start.3 = (bf16[768,768]{1,0:T(8,128)(2,1)S(1)}, bf16[768,768]{1,0:T(8,128)(2,1)}, u32[]{:S(2)}) copy-start(bf16[768,768]{1,0:T(8,128)(2,1)} %w_down.1) | copy-start | bytes 3538948
  61.1 16.0 %collective-permute-start.12 = (bf16[1536,128]{1,0:T(8,128)(2,1)S(1)}, bf16[1536,128]{1,0:T(8,128)(2,1)S(1)}, u32[]{:S(2)}, u32[]{:S(2)}) collective-permute-start(bf16[1536,128]{1,0:T(8,128)(2,1)S(1)} %get-tuple-element.130), channel_id=1, source_target_pairs={{0,1},{1,0},{2,3},{3,2},{4,5},{5,4},{6,7},{7,6},{8,9},{9,8},{10,11... | collective-permute-start | bytes 1179656 | tf_op jit(solution)/shard_map/mlp/ppermute | solution.py:696
  65.8 14.2 %collective-permute-start.14 = (bf16[192,512]{1,0:T(8,128)(2,1)S(1)}, bf16[192,512]{1,0:T(8,128)(2,1)S(1)}, u32[]{:S(2)}, u32[]{:S(2)}) collective-permute-start(bf16[192,512]{1,0:T(8,128)(2,1)S(1)} %get-tuple-element.139), channel_id=1, source_target_pairs={{0,1},{1,0},{2,3},{3,2},{4,5},{5,4},{6,7},{7,6},{8,9},{9,8},{10,11... | collective-permute-start | bytes 589832 | tf_op jit(solution)/shard_map/d_att/ppermute | solution.py:696
  67.9 17.0 %collective-permute-start.15 = (bf16[192,512]{1,0:T(8,128)(2,1)S(1)}, bf16[192,512]{1,0:T(8,128)(2,1)S(1)}, u32[]{:S(2)}, u32[]{:S(2)}) collective-permute-start(bf16[192,512]{1,0:T(8,128)(2,1)S(1)} %get-tuple-element.140), channel_id=1, source_target_pairs={{0,2},{1,3},{2,0},{3,1},{4,6},{5,7},{6,4},{7,5},{8,10},{9,11},{10,... | collective-permute-start | bytes 589832 | tf_op jit(solution)/shard_map/d_att/ppermute | solution.py:696
  68.5 16.4 %collective-permute-start.16 = (bf16[192,512]{1,0:T(8,128)(2,1)S(1)}, bf16[192,512]{1,0:T(8,128)(2,1)S(1)}, u32[]{:S(2)}, u32[]{:S(2)}) collective-permute-start(bf16[192,512]{1,0:T(8,128)(2,1)S(1)} %get-tuple-element.141), channel_id=1, source_target_pairs={{0,3},{1,2},{2,1},{3,0},{4,7},{5,6},{6,5},{7,4},{8,11},{9,10},{10,... | collective-permute-start | bytes 589832 | tf_op jit(solution)/shard_map/d_att/ppermute | solution.py:696
  72.9 25.5 %collective-permute-start.21 = (bf16[384,1152]{1,0:T(8,128)(2,1)S(1)}, bf16[384,1152]{1,0:T(8,128)(2,1)S(1)}, u32[]{:S(2)}, u32[]{:S(2)}) collective-permute-start(bf16[384,1152]{1,0:T(8,128)(2,1)S(1)} %get-tuple-element.172), channel_id=1, source_target_pairs={{0,8},{4,12},{8,0},{12,4},{16,24},{20,28},{24,16},{28,20},{1,9},{5... | collective-permute-start | bytes 2654216 | tf_op jit(solution)/shard_map/grads_a/ppermute | solution.py:696
  77.1 21.3 %collective-permute-start.22 = (bf16[384,1152]{1,0:T(8,128)(2,1)S(1)}, bf16[384,1152]{1,0:T(8,128)(2,1)S(1)}, u32[]{:S(2)}, u32[]{:S(2)}) collective-permute-start(bf16[384,1152]{1,0:T(8,128)(2,1)S(1)} %get-tuple-element.174), channel_id=1, source_target_pairs={{0,16},{4,20},{8,24},{12,28},{16,0},{20,4},{24,8},{28,12},{1,17},{... | collective-permute-start | bytes 2654216 | tf_op jit(solution)/shard_map/grads_b/ppermute | solution.py:696
  84.8 10.9 %collective-permute-start.17 = (bf16[768,128]{1,0:T(8,128)(2,1)S(1)}, bf16[768,128]{1,0:T(8,128)(2,1)S(1)}, u32[]{:S(2)}, u32[]{:S(2)}) collective-permute-start(bf16[768,128]{1,0:T(8,128)(2,1)S(1)} %get-tuple-element.142), channel_id=1, source_target_pairs={{0,2},{1,3},{2,0},{3,1},{4,6},{5,7},{6,4},{7,5},{8,10},{9,11},{10,... | collective-permute-start | bytes 589832 | tf_op jit(solution)/shard_map/mlp/ppermute | solution.py:696
  95.7 2.0 %collective-permute-start.20 = (bf16[416,576]{1,0:T(8,128)(2,1)S(1)}, bf16[416,576]{1,0:T(8,128)(2,1)S(1)}, u32[]{:S(2)}, u32[]{:S(2)}) collective-permute-start(bf16[416,576]{1,0:T(8,128)(2,1)S(1)} %get-tuple-element.168), channel_id=1, source_target_pairs={{0,4},{4,0},{8,12},{12,8},{16,20},{20,16},{24,28},{28,24},{1,5},{5... | collective-permute-start | bytes 1437704 | tf_op jit(solution)/shard_map/qkv_core/ppermute | solution.py:696
  95.8 11.5 %collective-permute-start.18 = (bf16[1536,128]{1,0:T(8,128)(2,1)S(1)}, bf16[1536,128]{1,0:T(8,128)(2,1)S(1)}, u32[]{:S(2)}, u32[]{:S(2)}) collective-permute-start(bf16[1536,128]{1,0:T(8,128)(2,1)S(1)} %get-tuple-element.162), channel_id=1, source_target_pairs={{0,1},{1,0},{2,3},{3,2},{4,5},{5,4},{6,7},{7,6},{8,9},{9,8},{10,11... | collective-permute-start | bytes 1179656 | tf_op jit(solution)/shard_map/back/ppermute | solution.py:696
  99.4 2.2 %collective-permute-start.23 = (bf16[192,768]{1,0:T(8,128)(2,1)S(1)}, bf16[192,768]{1,0:T(8,128)(2,1)S(1)}, u32[]{:S(2)}, u32[]{:S(2)}) collective-permute-start(bf16[192,768]{1,0:T(8,128)(2,1)S(1)} %get-tuple-element.176), channel_id=1, source_target_pairs={{0,4},{4,0},{8,12},{12,8},{16,20},{20,16},{24,28},{28,24},{1,5},{5... | collective-permute-start | bytes 884744 | tf_op jit(solution)/shard_map/grads_core/ppermute | solution.py:696
  99.6 2.0 %collective-permute-start.24 = (bf16[192,768]{1,0:T(8,128)(2,1)S(1)}, bf16[192,768]{1,0:T(8,128)(2,1)S(1)}, u32[]{:S(2)}, u32[]{:S(2)}) collective-permute-start(bf16[192,768]{1,0:T(8,128)(2,1)S(1)} %get-tuple-element.177), channel_id=1, source_target_pairs={{0,4},{4,0},{8,12},{12,8},{16,20},{20,16},{24,28},{28,24},{1,5},{5... | collective-permute-start | bytes 884744 | tf_op jit(solution)/shard_map/grads_core/ppermute | solution.py:696
  100.0 1.9 %collective-permute-start.25 = (bf16[192,768]{1,0:T(8,128)(2,1)S(1)}, bf16[192,768]{1,0:T(8,128)(2,1)S(1)}, u32[]{:S(2)}, u32[]{:S(2)}) collective-permute-start(bf16[192,768]{1,0:T(8,128)(2,1)S(1)} %get-tuple-element.178), channel_id=1, source_target_pairs={{0,4},{4,0},{8,12},{12,8},{16,20},{20,16},{24,28},{28,24},{1,5},{5... | collective-permute-start | bytes 884744 | tf_op jit(solution)/shard_map/grads_core/ppermute | solution.py:696
  100.1 9.7 %collective-permute-start.26 = (bf16[224,576]{1,0:T(8,128)(2,1)S(1)}, bf16[224,576]{1,0:T(8,128)(2,1)S(1)}, u32[]{:S(2)}, u32[]{:S(2)}) collective-permute-start(bf16[224,576]{1,0:T(8,128)(2,1)S(1)} %get-tuple-element.182), channel_id=1, source_target_pairs={{0,8},{4,12},{8,0},{12,4},{16,24},{20,28},{24,16},{28,20},{1,9},{5... | collective-permute-start | bytes 774152 | tf_op jit(solution)/shard_map/qkv_x/ppermute | solution.py:696
  102.6 10.3 %collective-permute-start.27 = (bf16[96,1152]{1,0:T(8,128)(2,1)S(1)}, bf16[96,1152]{1,0:T(8,128)(2,1)S(1)}, u32[]{:S(2)}, u32[]{:S(2)}) collective-permute-start(bf16[96,1152]{1,0:T(8,128)(2,1)S(1)} %get-tuple-element.184), channel_id=1, source_target_pairs={{0,16},{4,20},{8,24},{12,28},{16,0},{20,4},{24,8},{28,12},{1,17},{... | collective-permute-start | bytes 663560 | tf_op jit(solution)/shard_map/grads_a/ppermute | solution.py:696
  104.2 11.6 %collective-permute-start.28 = (bf16[96,1152]{1,0:T(8,128)(2,1)S(1)}, bf16[96,1152]{1,0:T(8,128)(2,1)S(1)}, u32[]{:S(2)}, u32[]{:S(2)}) collective-permute-start(bf16[96,1152]{1,0:T(8,128)(2,1)S(1)} %get-tuple-element.187), channel_id=1, source_target_pairs={{0,8},{4,12},{8,0},{12,4},{16,24},{20,28},{24,16},{28,20},{1,9},{5... | collective-permute-start | bytes 663560 | tf_op jit(solution)/shard_map/grads_b/ppermute | solution.py:696
  107.4 12.7 %collective-permute-start.19 = (bf16[768,128]{1,0:T(8,128)(2,1)S(1)}, bf16[768,128]{1,0:T(8,128)(2,1)S(1)}, u32[]{:S(2)}, u32[]{:S(2)}) collective-permute-start(bf16[768,128]{1,0:T(8,128)(2,1)S(1)} %get-tuple-element.164), channel_id=1, source_target_pairs={{0,2},{1,3},{2,0},{3,1},{4,6},{5,7},{6,4},{7,5},{8,10},{9,11},{10,... | collective-permute-start | bytes 589832 | tf_op jit(solution)/shard_map/back/ppermute | solution.py:696
  110.4 5.4 %collective-permute-start.29 = (bf16[128,576]{1,0:T(8,128)(2,1)S(1)}, bf16[128,576]{1,0:T(8,128)(2,1)S(1)}, u32[]{:S(2)}, u32[]{:S(2)}) collective-permute-start(bf16[128,576]{1,0:T(8,128)(2,1)S(1)} %get-tuple-element.188), channel_id=1, source_target_pairs={{0,16},{4,20},{8,24},{12,28},{16,0},{20,4},{24,8},{28,12},{1,17},{... | collective-permute-start | bytes 442376 | tf_op jit(solution)/shard_map/qkv_y/ppermute | solution.py:696
  116.5 7.6 %collective-permute-start.31 = (bf16[288,128]{1,0:T(8,128)(2,1)S(1)}, bf16[288,128]{1,0:T(8,128)(2,1)S(1)}, u32[]{:S(2)}, u32[]{:S(2)}) collective-permute-start(bf16[288,128]{1,0:T(8,128)(2,1)S(1)} %get-tuple-element.192), channel_id=1, source_target_pairs={{0,2},{1,3},{2,0},{3,1},{4,6},{5,7},{6,4},{7,5},{8,10},{9,11},{10,... | collective-permute-start | bytes 221192 | tf_op jit(solution)/shard_map/out/ppermute | solution.py:696
  117.4 6.8 %collective-permute-start.32 = (bf16[288,128]{1,0:T(8,128)(2,1)S(1)}, bf16[288,128]{1,0:T(8,128)(2,1)S(1)}, u32[]{:S(2)}, u32[]{:S(2)}) collective-permute-start(bf16[288,128]{1,0:T(8,128)(2,1)S(1)} %get-tuple-element.193), channel_id=1, source_target_pairs={{0,3},{1,2},{2,1},{3,0},{4,7},{5,6},{6,5},{7,4},{8,11},{9,10},{10,... | collective-permute-start | bytes 221192 | tf_op jit(solution)/shard_map/out/ppermute | solution.py:696
  119.3 5.4 %collective-permute-start.30 = (bf16[288,128]{1,0:T(8,128)(2,1)S(1)}, bf16[288,128]{1,0:T(8,128)(2,1)S(1)}, u32[]{:S(2)}, u32[]{:S(2)}) collective-permute-start(bf16[288,128]{1,0:T(8,128)(2,1)S(1)} %get-tuple-element.191), channel_id=1, source_target_pairs={{0,1},{1,0},{2,3},{3,2},{4,5},{5,4},{6,7},{7,6},{8,9},{9,8},{10,11... | collective-permute-start | bytes 221192 | tf_op jit(solution)/shard_map/out/ppermute | solution.py:696

commit v10 on v8

--- a/solution.py
+++ b/solution.py
@@ -878,7 +878,7 @@
         sent, kept, vec = call(
             qkv_third_kernel,
             [like((share + extra, n), BF16), like((share, n), F32)] + vec_like,
-            [place, after(vec, a_kept, back[0]), kept, recv],
+            [place, after(vec, a_recv, back[0]), kept, recv],
             n_smem=1,
         )
         recv = swap(sent, 4, "dp", name="qkv_y")

time: 126 us -> 126 us (level)
  transfers between devices with their start and end apart: 33 -> 33, of which waited for: 18 -> 19; matrix products, arithmetic and copies ran while one was open for 2% -> 2% of each run, Pallas kernels for 26% -> 26%
where the time goes in v10:
time: 126 us
  waiting for transfers between devices  42.7 us (34%)
  starting transfers between devices  42.3 us (34%)
  Pallas kernels  32.9 us (26%)
  local copies, waits for them, and re-layouts  5.87 us (5%)
    ppermute x33, waiting for transfers between devices, swap(): return lax.ppermute(v, axis, [(i, i ^ k) for i in range(n)])  42.7 us
    ppermute x33, starting transfers between devices, swap(): return lax.ppermute(v, axis, [(i, i ^ k) for i in range(n)])  42.3 us
    pallas_call x21, Pallas kernels, call(): pl.pallas_call(kernel, out_shape=tuple(outs), in_specs=[SMEM] * n_smem +...  32.9 us
    unnamed x17, local copies, waits for them, and re-layouts  4.17 us
  transfers between devices with their start and end apart: 33, of which 19 were waited for; matrix products, arithmetic and copies ran while one was open for 2% of the time, Pallas kernels for 26%

profile of v10, /device:TPU:0, one launch (start us, length us, event | category | flops | bytes accessed | tf_op | source)
XLA Modules:
  0.0 125.7 jit_solution(17578556396716344049)
XLA Ops:
  0.7 0.9 copy-done
  1.6 0.9 pad_maximum_fusion.x0
  2.6 4.1 %collective-permute-start.1 = (bf16[176,768]{1,0:T(8,128)(2,1)S(1)}, bf16[176,768]{1,0:T(8,128)(2,1)S(1)}, u32[]{:S(2)}, u32[]{:S(2)}) collective-permute-start(bf16[176,768]{1,0:T(8,128)(2,1)S(1)} %pad_maximum_fusion.x0), channel_id=1, source_target_pairs={{0,2},{1,3},{2,0},{3,1},{4,6},{5,7},{6,4},{7,5},{8,10},{9,11},{10,... | collective-permute-start | bytes 811016 | tf_op jit(solution)/shard_map/x/ppermute | solution.py:696
  6.7 1.6 %collective-permute-start = (bf16[176,768]{1,0:T(8,128)(2,1)S(1)}, bf16[176,768]{1,0:T(8,128)(2,1)S(1)}, u32[]{:S(2)}, u32[]{:S(2)}) collective-permute-start(bf16[176,768]{1,0:T(8,128)(2,1)S(1)} %pad_maximum_fusion.x0), channel_id=1, source_target_pairs={{0,1},{1,0},{2,3},{3,2},{4,5},{5,4},{6,7},{7,6},{8,9},{9,8},{10,11... | collective-permute-start | bytes 811016 | tf_op jit(solution)/shard_map/x/ppermute | solution.py:696
  8.2 0.8 copy.30.table
  9.0 10.0 %collective-permute-done.1.x2 = bf16[176,768]{1,0:T(8,128)(2,1)S(1)} collective-permute-done((bf16[176,768]{1,0:T(8,128)(2,1)S(1)}, bf16[176,768]{1,0:T(8,128)(2,1)S(1)}, u32[]{:S(2)}, u32[]{:S(2)}) %collective-permute-start.1) | collective-permute-done | bytes 270368 | tf_op jit(solution)/shard_map/x/ppermute | solution.py:696
  19.2 1.5 %collective-permute-start.2 = (bf16[176,768]{1,0:T(8,128)(2,1)S(1)}, bf16[176,768]{1,0:T(8,128)(2,1)S(1)}, u32[]{:S(2)}, u32[]{:S(2)}) collective-permute-start(bf16[176,768]{1,0:T(8,128)(2,1)S(1)} %collective-permute-done.1.x2), channel_id=1, source_target_pairs={{0,1},{1,0},{2,3},{3,2},{4,5},{5,4},{6,7},{7,6},{8,9},{9,8},{10,11... | collective-permute-start | bytes 811016 | tf_op jit(solution)/shard_map/x/ppermute | solution.py:696
  20.7 0.8 fusion
  21.5 0.7 concatenate.7
  22.4 1.3 %copy-done.2 = bf16[768,768]{1,0:T(8,128)(2,1)S(1)} copy-done((bf16[768,768]{1,0:T(8,128)(2,1)S(1)}, bf16[768,768]{1,0:T(8,128)(2,1)}, u32[]{:S(2)}) %copy-start.2) | copy-done | bytes 1179672
  23.7 1.2 copy-done.4
  24.9 0.9 turn_kernel.1
  25.9 1.5 %bias_kernel.1 = (f32[3,3,128,128]{3,2,1,0:T(8,128)S(1)}, s32[512,128]{1,0:T(8,128)S(1)}) custom-call(s32[2]{0:T(128)S(1)} %pad_add_fusion.place, s32[1,8]{1,0:T(1,128)S(1)} %copy-done.7, f32[32,12]{1,0:T(8,128)S(1)} %copy.30.table), custom_call_target="tpu_custom_call" | custom-call | flops 11500000 | bytes 8 | tf_op jit(solution)/shard_map/bias_kernel/pallas_call | solution.py:21
  27.4 2.4 %collective-permute-start.5 = (bf16[128,768]{1,0:T(8,128)(2,1)S(1)}, bf16[128,768]{1,0:T(8,128)(2,1)S(1)}, u32[]{:S(2)}, u32[]{:S(2)}) collective-permute-start(bf16[128,768]{1,0:T(8,128)(2,1)S(1)} %copy-done.6), channel_id=1, source_target_pairs={{0,2},{1,3},{2,0},{3,1},{4,6},{5,7},{6,4},{7,5},{8,10},{9,11},{10,... | collective-permute-start | bytes 589832 | tf_op jit(solution)/shard_map/dy/ppermute | solution.py:696
  29.8 1.7 %collective-permute-start.4 = (bf16[128,768]{1,0:T(8,128)(2,1)S(1)}, bf16[128,768]{1,0:T(8,128)(2,1)S(1)}, u32[]{:S(2)}, u32[]{:S(2)}) collective-permute-start(bf16[128,768]{1,0:T(8,128)(2,1)S(1)} %copy-done.6), channel_id=1, source_target_pairs={{0,1},{1,0},{2,3},{3,2},{4,5},{5,4},{6,7},{7,6},{8,9},{9,8},{10,11... | collective-permute-start | bytes 589832 | tf_op jit(solution)/shard_map/dy/ppermute | solution.py:696
  31.5 1.6 %collective-permute-start.3 = (bf16[4,48,768]{2,1,0:T(8,128)(2,1)S(1)}, bf16[4,48,768]{2,1,0:T(8,128)(2,1)S(1)}, u32[]{:S(2)}, u32[]{:S(2)}) collective-permute-start(bf16[4,48,768]{2,1,0:T(8,128)(2,1)S(1)} %pieces_kernel.1.a), channel_id=1, source_target_pairs={{0,8},{4,12},{8,0},{12,4},{16,24},{20,28},{24,16},{28,20},{1,9},{5... | collective-permute-start | bytes 884744 | tf_op jit(solution)/shard_map/w/ppermute | solution.py:696
  33.0 4.2 %head_kernel.1 = (bf16[768,512]{1,0:T(8,128)(2,1)S(1)}, bf16[768,512]{1,0:T(8,128)(2,1)S(1)}, f32[8,512]{1,0:T(8,128)S(1)}, bf16[576,512]{1,0:T(8,128)(2,1)S(1)}...) custom-call(s32[2]{0:T(128)S(1)} %pad_add_fusion.place, ...), custom_call_target="tpu_custom_call" | custom-call | flops 11500000256 | bytes 8 | tf_op jit(solution)/shard_map/head_kernel/pallas_call | solution.py:21
  37.2 1.7 %collective-permute-done.5.c2 = bf16[128,768]{1,0:T(8,128)(2,1)S(1)} collective-permute-done((bf16[128,768]{1,0:T(8,128)(2,1)S(1)}, bf16[128,768]{1,0:T(8,128)(2,1)S(1)}, u32[]{:S(2)}, u32[]{:S(2)}) %collective-permute-start.5) | collective-permute-done | bytes 196640 | tf_op jit(solution)/shard_map/dy/ppermute | solution.py:696
  38.9 0.7 collective-permute-done.4.c1
  39.7 1.0 collective-permute-start.6
  40.8 2.0 %collective-permute-start.7 = (bf16[96,512]{1,0:T(8,128)(2,1)S(1)}, bf16[96,512]{1,0:T(8,128)(2,1)S(1)}, u32[]{:S(2)}, u32[]{:S(2)}) collective-permute-start(bf16[96,512]{1,0:T(8,128)(2,1)S(1)} %get-tuple-element.123), channel_id=1, source_target_pairs={{0,2},{1,3},{2,0},{3,1},{4,6},{5,7},{6,4},{7,5},{8,10},{9,11},{10,... | collective-permute-start | bytes 294920 | tf_op jit(solution)/shard_map/att/ppermute | solution.py:696
  42.7 1.4 %collective-permute-start.10 = (bf16[96,512]{1,0:T(8,128)(2,1)S(1)}, bf16[96,512]{1,0:T(8,128)(2,1)S(1)}, u32[]{:S(2)}, u32[]{:S(2)}) collective-permute-start(bf16[96,512]{1,0:T(8,128)(2,1)S(1)} %get-tuple-element.125), channel_id=1, source_target_pairs={{0,3},{1,2},{2,1},{3,0},{4,7},{5,6},{6,5},{7,4},{8,11},{9,10},{10,... | collective-permute-start | bytes 294920 | tf_op jit(solution)/shard_map/att/ppermute | solution.py:696
  44.3 3.9 %collective-permute-done.7.a2t = bf16[96,512]{1,0:T(8,128)(2,1)S(1)} collective-permute-done((bf16[96,512]{1,0:T(8,128)(2,1)S(1)}, bf16[96,512]{1,0:T(8,128)(2,1)S(1)}, u32[]{:S(2)}, u32[]{:S(2)}) %collective-permute-start.7) | collective-permute-done | bytes 98336 | tf_op jit(solution)/shard_map/att/ppermute | solution.py:696
  48.1 2.6 %collective-permute-start.9 = (bf16[96,512]{1,0:T(8,128)(2,1)S(1)}, bf16[96,512]{1,0:T(8,128)(2,1)S(1)}, u32[]{:S(2)}, u32[]{:S(2)}) collective-permute-start(bf16[96,512]{1,0:T(8,128)(2,1)S(1)} %collective-permute-done.7.a2t), channel_id=1, source_target_pairs={{0,1},{1,0},{2,3},{3,2},{4,5},{5,4},{6,7},{7,6},{8,9},{9,8},{10,11... | collective-permute-start | bytes 294920 | tf_op jit(solution)/shard_map/att/ppermute | solution.py:696
  50.7 1.0 out_weight_kernel.1
  51.7 0.5 collective-permute-done.10.a3b
  52.2 5.0 %collective-permute-done.8.a2b = bf16[96,512]{1,0:T(8,128)(2,1)S(1)} collective-permute-done((bf16[96,512]{1,0:T(8,128)(2,1)S(1)}, bf16[96,512]{1,0:T(8,128)(2,1)S(1)}, u32[]{:S(2)}, u32[]{:S(2)}) %collective-permute-start.8) | collective-permute-done | bytes 98336 | tf_op jit(solution)/shard_map/att/ppermute | solution.py:696
  57.2 4.2 %up_kernel.1 = (bf16[768,512]{1,0:T(8,128)(2,1)S(1)}, f32[768,512]{1,0:T(8,128)S(1)}, f32[768,512]{1,0:T(8,128)S(1)}, f32[8,512]{1,0:T(8,128)S(1)}, bf16[768,512...) custom-call(s32[2]{0:T(128)S(1)} %pad_add_fusion.place, ...), custom_call_target="tpu_custom_call" | custom-call | flops 11500000256 | bytes 8 | tf_op jit(solution)/shard_map/up_kernel/pallas_call | solution.py:21
  61.5 4.6 %down_kernel.1 = (bf16[192,512]{1,0:T(8,128)(2,1)S(1)}, bf16[192,512]{1,0:T(8,128)(2,1)S(1)}, bf16[192,512]{1,0:T(8,128)(2,1)S(1)}, bf16[192,512]{1,0:T(8,128)(2...) custom-call(s32[2]{0:T(128)S(1)} %pad_add_fusion.place, ...), custom_call_target="tpu_custom_call" | custom-call | flops 11500000256 | bytes 8 | tf_op jit(solution)/shard_map/down_kernel/pallas_call | solution.py:21
  66.1 2.1 %collective-permute-start.14 = (bf16[192,512]{1,0:T(8,128)(2,1)S(1)}, bf16[192,512]{1,0:T(8,128)(2,1)S(1)}, u32[]{:S(2)}, u32[]{:S(2)}) collective-permute-start(bf16[192,512]{1,0:T(8,128)(2,1)S(1)} %get-tuple-element.140), channel_id=1, source_target_pairs={{0,1},{1,0},{2,3},{3,2},{4,5},{5,4},{6,7},{7,6},{8,9},{9,8},{10,11... | collective-permute-start | bytes 589832 | tf_op jit(solution)/shard_map/d_att/ppermute | solution.py:696
  68.5 2.2 %collective-permute-start.16 = (bf16[192,512]{1,0:T(8,128)(2,1)S(1)}, bf16[192,512]{1,0:T(8,128)(2,1)S(1)}, u32[]{:S(2)}, u32[]{:S(2)}) collective-permute-start(bf16[192,512]{1,0:T(8,128)(2,1)S(1)} %get-tuple-element.142), channel_id=1, source_target_pairs={{0,3},{1,2},{2,1},{3,0},{4,7},{5,6},{6,5},{7,4},{8,11},{9,10},{10,... | collective-permute-start | bytes 589832 | tf_op jit(solution)/shard_map/d_att/ppermute | solution.py:696
  70.6 2.6 %mlp_grad_kernel.1 = (f32[8,768]{1,0:T(8,128)S(1)}, bf16[384,1152]{1,0:T(8,128)(2,1)S(1)}, bf16[384,1152]{1,0:T(8,128)(2,1)S(1)}, bf16[384,1152]{1,0:T(8,128)(2,1)S(1)}, bf16[384,1152]{1,0:T(8,128)(2,1)S(1)}) custom-call(s32[2]{0:T(128)S(1)} %pad_add_fusion.place, f32[8,768]{1,0:T(8,128)S(1)} %get-tuple-element.151.vec, ...), custom_call_target="tpu_custom_call" | custom-call | flops 11500000 | bytes 8 | tf_op jit(solution)/shard_map/mlp_grad_kernel/pallas_call | solution.py:21
  73.2 1.6 %collective-permute-start.21 = (bf16[384,1152]{1,0:T(8,128)(2,1)S(1)}, bf16[384,1152]{1,0:T(8,128)(2,1)S(1)}, u32[]{:S(2)}, u32[]{:S(2)}) collective-permute-start(bf16[384,1152]{1,0:T(8,128)(2,1)S(1)} %get-tuple-element.174), channel_id=1, source_target_pairs={{0,8},{4,12},{8,0},{12,4},{16,24},{20,28},{24,16},{28,20},{1,9},{5... | collective-permute-start | bytes 2654216 | tf_op jit(solution)/shard_map/grads_a/ppermute | solution.py:696
  74.8 2.5 %collective-permute-done.12.recv = bf16[1536,128]{1,0:T(8,128)(2,1)S(1)} collective-permute-done((bf16[1536,128]{1,0:T(8,128)(2,1)S(1)}, bf16[1536,128]{1,0:T(8,128)(2,1)S(1)}, u32[]{:S(2)}, u32[]{:S(2)}) %collective-permute-start.12) | collective-permute-done | bytes 393248 | tf_op jit(solution)/shard_map/mlp/ppermute | solution.py:696
  77.3 1.5 %collective-permute-start.22 = (bf16[384,1152]{1,0:T(8,128)(2,1)S(1)}, bf16[384,1152]{1,0:T(8,128)(2,1)S(1)}, u32[]{:S(2)}, u32[]{:S(2)}) collective-permute-start(bf16[384,1152]{1,0:T(8,128)(2,1)S(1)} %get-tuple-element.176), channel_id=1, source_target_pairs={{0,16},{4,20},{8,24},{12,28},{16,0},{20,4},{24,8},{28,12},{1,17},{... | collective-permute-start | bytes 2654216 | tf_op jit(solution)/shard_map/grads_b/ppermute | solution.py:696
  78.9 1.4 %collective-permute-done.14.d1 = bf16[192,512]{1,0:T(8,128)(2,1)S(1)} collective-permute-done((bf16[192,512]{1,0:T(8,128)(2,1)S(1)}, bf16[192,512]{1,0:T(8,128)(2,1)S(1)}, u32[]{:S(2)}, u32[]{:S(2)}) %collective-permute-start.14) | collective-permute-done | bytes 196640 | tf_op jit(solution)/shard_map/d_att/ppermute | solution.py:696
  80.3 4.8 %collective-permute-done.15.d2 = bf16[192,512]{1,0:T(8,128)(2,1)S(1)} collective-permute-done((bf16[192,512]{1,0:T(8,128)(2,1)S(1)}, bf16[192,512]{1,0:T(8,128)(2,1)S(1)}, u32[]{:S(2)}, u32[]{:S(2)}) %collective-permute-start.15) | collective-permute-done | bytes 196640 | tf_op jit(solution)/shard_map/d_att/ppermute | solution.py:696
  85.1 3.4 %collective-permute-start.17 = (bf16[768,128]{1,0:T(8,128)(2,1)S(1)}, bf16[768,128]{1,0:T(8,128)(2,1)S(1)}, u32[]{:S(2)}, u32[]{:S(2)}) collective-permute-start(bf16[768,128]{1,0:T(8,128)(2,1)S(1)} %get-tuple-element.143), channel_id=1, source_target_pairs={{0,2},{1,3},{2,0},{3,1},{4,6},{5,7},{6,4},{7,5},{8,10},{9,11},{10,... | collective-permute-start | bytes 589832 | tf_op jit(solution)/shard_map/mlp/ppermute | solution.py:696
  88.6 6.5 %back_kernel.1 = (f32[768,128]{1,0:T(8,128)S(1)}, f32[768,128]{1,0:T(8,128)S(1)}, bf16[1536,128]{1,0:T(8,128)(2,1)S(1)}, f32[8,768]{1,0:T(8,128)S(1)}, bf16[416,...) custom-call(s32[2]{0:T(128)S(1)} %pad_add_fusion.place, s32[1,8]{1,0:T(1,128)S(1)} %copy-done.7, ...), custom_call_target="tpu_custom_call" | custom-call | flops 11500000256 | bytes 8 | tf_op jit(solution)/shard_map/back_kernel/pallas_call | solution.py:21
  95.1 0.6 collective-permute-done.17.recv
  95.7 1.9 %collective-permute-done.20.recv = bf16[416,576]{1,0:T(8,128)(2,1)S(1)} collective-permute-done((bf16[416,576]{1,0:T(8,128)(2,1)S(1)}, bf16[416,576]{1,0:T(8,128)(2,1)S(1)}, u32[]{:S(2)}, u32[]{:S(2)}) %collective-permute-start.20) | collective-permute-done | bytes 479264 | tf_op jit(solution)/shard_map/qkv_core/ppermute | solution.py:696
  97.6 0.7 qkv_second_kernel.1
  98.3 1.0 grads_second_kernel.1
  100.0 1.5 %collective-permute-start.27 = (bf16[224,576]{1,0:T(8,128)(2,1)S(1)}, bf16[224,576]{1,0:T(8,128)(2,1)S(1)}, u32[]{:S(2)}, u32[]{:S(2)}) collective-permute-start(bf16[224,576]{1,0:T(8,128)(2,1)S(1)} %get-tuple-element.184), channel_id=1, source_target_pairs={{0,8},{4,12},{8,0},{12,4},{16,24},{20,28},{24,16},{28,20},{1,9},{5... | collective-permute-start | bytes 774152 | tf_op jit(solution)/shard_map/qkv_x/ppermute | solution.py:696
  101.8 0.7 grads_third_kernel.1
  102.5 1.6 %collective-permute-start.26 = (bf16[96,1152]{1,0:T(8,128)(2,1)S(1)}, bf16[96,1152]{1,0:T(8,128)(2,1)S(1)}, u32[]{:S(2)}, u32[]{:S(2)}) collective-permute-start(bf16[96,1152]{1,0:T(8,128)(2,1)S(1)} %get-tuple-element.181), channel_id=1, source_target_pairs={{0,16},{4,20},{8,24},{12,28},{16,0},{20,4},{24,8},{28,12},{1,17},{... | collective-permute-start | bytes 663560 | tf_op jit(solution)/shard_map/grads_a/ppermute | solution.py:696
  104.1 1.5 %collective-permute-start.28 = (bf16[96,1152]{1,0:T(8,128)(2,1)S(1)}, bf16[96,1152]{1,0:T(8,128)(2,1)S(1)}, u32[]{:S(2)}, u32[]{:S(2)}) collective-permute-start(bf16[96,1152]{1,0:T(8,128)(2,1)S(1)} %get-tuple-element.188), channel_id=1, source_target_pairs={{0,8},{4,12},{8,0},{12,4},{16,24},{20,28},{24,16},{28,20},{1,9},{5... | collective-permute-start | bytes 663560 | tf_op jit(solution)/shard_map/grads_b/ppermute | solution.py:696
  105.6 1.6 %collective-permute-done.18.recv = bf16[1536,128]{1,0:T(8,128)(2,1)S(1)} collective-permute-done((bf16[1536,128]{1,0:T(8,128)(2,1)S(1)}, bf16[1536,128]{1,0:T(8,128)(2,1)S(1)}, u32[]{:S(2)}, u32[]{:S(2)}) %collective-permute-start.18) | collective-permute-done | bytes 393248 | tf_op jit(solution)/shard_map/back/ppermute | solution.py:696
  107.3 0.8 collective-permute-start.19
  108.1 2.0 %collective-permute-done.26.a_recv = bf16[96,1152]{1,0:T(8,128)(2,1)S(1)} collective-permute-done((bf16[96,1152]{1,0:T(8,128)(2,1)S(1)}, bf16[96,1152]{1,0:T(8,128)(2,1)S(1)}, u32[]{:S(2)}, u32[]{:S(2)}) %collective-permute-start.26) | collective-permute-done | bytes 221216 | tf_op jit(solution)/shard_map/grads_a/ppermute | solution.py:696
  110.1 0.6 qkv_third_kernel.1
  110.7 1.6 %collective-permute-start.29 = (bf16[128,576]{1,0:T(8,128)(2,1)S(1)}, bf16[128,576]{1,0:T(8,128)(2,1)S(1)}, u32[]{:S(2)}, u32[]{:S(2)}) collective-permute-start(bf16[128,576]{1,0:T(8,128)(2,1)S(1)} %get-tuple-element.189), channel_id=1, source_target_pairs={{0,16},{4,20},{8,24},{12,28},{16,0},{20,4},{24,8},{28,12},{1,17},{... | collective-permute-start | bytes 442376 | tf_op jit(solution)/shard_map/qkv_y/ppermute | solution.py:696
  112.3 0.9 output_kernel.1
  113.2 0.6 collective-permute-done.28.b_recv
  113.9 2.3 %collective-permute-done.29.q_recv = bf16[128,576]{1,0:T(8,128)(2,1)S(1)} collective-permute-done((bf16[128,576]{1,0:T(8,128)(2,1)S(1)}, bf16[128,576]{1,0:T(8,128)(2,1)S(1)}, u32[]{:S(2)}, u32[]{:S(2)}) %collective-permute-start.29) | collective-permute-done | bytes 147488 | tf_op jit(solution)/shard_map/qkv_y/ppermute | solution.py:696
  116.2 0.7 message_kernel.1
  116.9 0.8 collective-permute-start.31
  117.7 1.9 %collective-permute-start.32 = (bf16[288,128]{1,0:T(8,128)(2,1)S(1)}, bf16[288,128]{1,0:T(8,128)(2,1)S(1)}, u32[]{:S(2)}, u32[]{:S(2)}) collective-permute-start(bf16[288,128]{1,0:T(8,128)(2,1)S(1)} %get-tuple-element.194), channel_id=1, source_target_pairs={{0,3},{1,2},{2,1},{3,0},{4,7},{5,6},{6,5},{7,4},{8,11},{9,10},{10,... | collective-permute-start | bytes 221192 | tf_op jit(solution)/shard_map/out/ppermute | solution.py:696
  119.6 0.8 collective-permute-start.30
  120.5 0.9 input_kernel.1
  121.3 1.0 last_kernel.1
  122.3 2.2 %collective-permute-done.31.o2 = bf16[288,128]{1,0:T(8,128)(2,1)S(1)} collective-permute-done((bf16[288,128]{1,0:T(8,128)(2,1)S(1)}, bf16[288,128]{1,0:T(8,128)(2,1)S(1)}, u32[]{:S(2)}, u32[]{:S(2)}) %collective-permute-start.31) | collective-permute-done | bytes 73760 | tf_op jit(solution)/shard_map/out/ppermute | solution.py:696
  124.5 0.5 collective-permute-done.30.o1
  125.0 0.7 small_kernel.1
  (46 shorter events, 2.3 us)
Async XLA Ops:
  0.6 1.0 copy-start
  0.7 21.8 %copy-start.1 = (bf16[768,768]{1,0:T(8,128)(2,1)S(1)}, bf16[768,768]{1,0:T(8,128)(2,1)}, u32[]{:S(2)}) copy-start(bf16[768,768]{1,0:T(8,128)(2,1)} %w_up.1) | copy-start | bytes 3538948
  2.6 16.5 %collective-permute-start.1 = (bf16[176,768]{1,0:T(8,128)(2,1)S(1)}, bf16[176,768]{1,0:T(8,128)(2,1)S(1)}, u32[]{:S(2)}, u32[]{:S(2)}) collective-permute-start(bf16[176,768]{1,0:T(8,128)(2,1)S(1)} %pad_maximum_fusion.x0), channel_id=1, source_target_pairs={{0,2},{1,3},{2,0},{3,1},{4,6},{5,7},{6,4},{7,5},{8,10},{9,11},{10,... | collective-permute-start | bytes 811016 | tf_op jit(solution)/shard_map/x/ppermute | solution.py:696
  6.7 12.6 %collective-permute-start = (bf16[176,768]{1,0:T(8,128)(2,1)S(1)}, bf16[176,768]{1,0:T(8,128)(2,1)S(1)}, u32[]{:S(2)}, u32[]{:S(2)}) collective-permute-start(bf16[176,768]{1,0:T(8,128)(2,1)S(1)} %pad_maximum_fusion.x0), channel_id=1, source_target_pairs={{0,1},{1,0},{2,3},{3,2},{4,5},{5,4},{6,7},{7,6},{8,9},{9,8},{10,11... | collective-permute-start | bytes 811016 | tf_op jit(solution)/shard_map/x/ppermute | solution.py:696
  19.2 8.1 %collective-permute-start.2 = (bf16[176,768]{1,0:T(8,128)(2,1)S(1)}, bf16[176,768]{1,0:T(8,128)(2,1)S(1)}, u32[]{:S(2)}, u32[]{:S(2)}) collective-permute-start(bf16[176,768]{1,0:T(8,128)(2,1)S(1)} %collective-permute-done.1.x2), channel_id=1, source_target_pairs={{0,1},{1,0},{2,3},{3,2},{4,5},{5,4},{6,7},{7,6},{8,9},{9,8},{10,11... | collective-permute-start | bytes 811016 | tf_op jit(solution)/shard_map/x/ppermute | solution.py:696
  22.4 1.3 %copy-start.2 = (bf16[768,768]{1,0:T(8,128)(2,1)S(1)}, bf16[768,768]{1,0:T(8,128)(2,1)}, u32[]{:S(2)}) copy-start(bf16[768,768]{1,0:T(8,128)(2,1)} %w_down.1) | copy-start | bytes 3538948
  23.7 1.2 copy-start.4
  24.9 1.0 copy-start.7
  24.9 2.5 %copy-start.6 = (bf16[128,768]{1,0:T(8,128)(2,1)S(1)}, bf16[128,768]{1,0:T(8,128)(2,1)}, u32[]{:S(2)}) copy-start(bf16[128,768]{1,0:T(8,128)(2,1)} %dy.1) | copy-start | bytes 589828
  24.9 8.2 %copy-start.5 = (bf16[768,3,192]{0,2,1:T(8,128)(2,1)S(1)}, bf16[768,3,192]{0,2,1:T(8,128)(2,1)}, u32[]{:S(2)}) copy-start(bf16[768,3,192]{0,2,1:T(8,128)(2,1)} %param.16) | copy-start | bytes 2654212
  27.4 11.5 %collective-permute-start.5 = (bf16[128,768]{1,0:T(8,128)(2,1)S(1)}, bf16[128,768]{1,0:T(8,128)(2,1)S(1)}, u32[]{:S(2)}, u32[]{:S(2)}) collective-permute-start(bf16[128,768]{1,0:T(8,128)(2,1)S(1)} %copy-done.6), channel_id=1, source_target_pairs={{0,2},{1,3},{2,0},{3,1},{4,6},{5,7},{6,4},{7,5},{8,10},{9,11},{10,... | collective-permute-start | bytes 589832 | tf_op jit(solution)/shard_map/dy/ppermute | solution.py:696
  29.8 9.8 %collective-permute-start.4 = (bf16[128,768]{1,0:T(8,128)(2,1)S(1)}, bf16[128,768]{1,0:T(8,128)(2,1)S(1)}, u32[]{:S(2)}, u32[]{:S(2)}) collective-permute-start(bf16[128,768]{1,0:T(8,128)(2,1)S(1)} %copy-done.6), channel_id=1, source_target_pairs={{0,1},{1,0},{2,3},{3,2},{4,5},{5,4},{6,7},{7,6},{8,9},{9,8},{10,11... | collective-permute-start | bytes 589832 | tf_op jit(solution)/shard_map/dy/ppermute | solution.py:696
  31.5 8.1 %collective-permute-start.3 = (bf16[4,48,768]{2,1,0:T(8,128)(2,1)S(1)}, bf16[4,48,768]{2,1,0:T(8,128)(2,1)S(1)}, u32[]{:S(2)}, u32[]{:S(2)}) collective-permute-start(bf16[4,48,768]{2,1,0:T(8,128)(2,1)S(1)} %pieces_kernel.1.a), channel_id=1, source_target_pairs={{0,8},{4,12},{8,0},{12,4},{16,24},{20,28},{24,16},{28,20},{1,9},{5... | collective-permute-start | bytes 884744 | tf_op jit(solution)/shard_map/w/ppermute | solution.py:696
  39.6 11.1 %collective-permute-start.11 = (bf16[8,48,768]{2,1,0:T(8,128)(2,1)S(1)}, bf16[8,48,768]{2,1,0:T(8,128)(2,1)S(1)}, u32[]{:S(2)}, u32[]{:S(2)}) collective-permute-start(bf16[8,48,768]{2,1,0:T(8,128)(2,1)S(1)} %pair_kernel.1.here), channel_id=1, source_target_pairs={{0,4},{4,0},{8,12},{12,8},{16,20},{20,16},{24,28},{28,24},{1,5},{5... | collective-permute-start | bytes 1769480 | tf_op jit(solution)/shard_map/w/ppermute | solution.py:696
  39.7 17.5 %collective-permute-start.6 = (bf16[192,512]{1,0:T(8,128)(2,1)S(1)}, bf16[192,512]{1,0:T(8,128)(2,1)S(1)}, u32[]{:S(2)}, u32[]{:S(2)}) collective-permute-start(bf16[192,512]{1,0:T(8,128)(2,1)S(1)} %get-tuple-element.121.a0), channel_id=1, source_target_pairs={{0,1},{1,0},{2,3},{3,2},{4,5},{5,4},{6,7},{7,6},{8,9},{9,8},{10,11... | collective-permute-start | bytes 589832 | tf_op jit(solution)/shard_map/att/ppermute | solution.py:696
  40.8 7.4 %collective-permute-start.7 = (bf16[96,512]{1,0:T(8,128)(2,1)S(1)}, bf16[96,512]{1,0:T(8,128)(2,1)S(1)}, u32[]{:S(2)}, u32[]{:S(2)}) collective-permute-start(bf16[96,512]{1,0:T(8,128)(2,1)S(1)} %get-tuple-element.123), channel_id=1, source_target_pairs={{0,2},{1,3},{2,0},{3,1},{4,6},{5,7},{6,4},{7,5},{8,10},{9,11},{10,... | collective-permute-start | bytes 294920 | tf_op jit(solution)/shard_map/att/ppermute | solution.py:696
  42.7 9.5 %collective-permute-start.10 = (bf16[96,512]{1,0:T(8,128)(2,1)S(1)}, bf16[96,512]{1,0:T(8,128)(2,1)S(1)}, u32[]{:S(2)}, u32[]{:S(2)}) collective-permute-start(bf16[96,512]{1,0:T(8,128)(2,1)S(1)} %get-tuple-element.125), channel_id=1, source_target_pairs={{0,3},{1,2},{2,1},{3,0},{4,7},{5,6},{6,5},{7,4},{8,11},{9,10},{10,... | collective-permute-start | bytes 294920 | tf_op jit(solution)/shard_map/att/ppermute | solution.py:696
  44.2 13.0 %collective-permute-start.8 = (bf16[96,512]{1,0:T(8,128)(2,1)S(1)}, bf16[96,512]{1,0:T(8,128)(2,1)S(1)}, u32[]{:S(2)}, u32[]{:S(2)}) collective-permute-start(bf16[96,512]{1,0:T(8,128)(2,1)S(1)} %get-tuple-element.125), channel_id=1, source_target_pairs={{0,2},{1,3},{2,0},{3,1},{4,6},{5,7},{6,4},{7,5},{8,10},{9,11},{10,... | collective-permute-start | bytes 294920 | tf_op jit(solution)/shard_map/att/ppermute | solution.py:696
  48.1 9.1 %collective-permute-start.9 = (bf16[96,512]{1,0:T(8,128)(2,1)S(1)}, bf16[96,512]{1,0:T(8,128)(2,1)S(1)}, u32[]{:S(2)}, u32[]{:S(2)}) collective-permute-start(bf16[96,512]{1,0:T(8,128)(2,1)S(1)} %collective-permute-done.7.a2t), channel_id=1, source_target_pairs={{0,1},{1,0},{2,3},{3,2},{4,5},{5,4},{6,7},{7,6},{8,9},{9,8},{10,11... | collective-permute-start | bytes 294920 | tf_op jit(solution)/shard_map/att/ppermute | solution.py:696
  50.7 10.8 %collective-permute-start.13 = (bf16[128,768]{1,0:T(8,128)(2,1)S(1)}, bf16[128,768]{1,0:T(8,128)(2,1)S(1)}, u32[]{:S(2)}, u32[]{:S(2)}) collective-permute-start(bf16[128,768]{1,0:T(8,128)(2,1)S(1)} %collective-permute-done.5.c2), channel_id=1, source_target_pairs={{0,1},{1,0},{2,3},{3,2},{4,5},{5,4},{6,7},{7,6},{8,9},{9,8},{10,11... | collective-permute-start | bytes 589832 | tf_op jit(solution)/shard_map/dy/ppermute | solution.py:696
  57.2 4.3 %copy-start.3 = (bf16[768,768]{1,0:T(8,128)(2,1)S(1)}, bf16[768,768]{1,0:T(8,128)(2,1)}, u32[]{:S(2)}) copy-start(bf16[768,768]{1,0:T(8,128)(2,1)} %w_down.1) | copy-start | bytes 3538948
  61.4 15.9 %collective-permute-start.12 = (bf16[1536,128]{1,0:T(8,128)(2,1)S(1)}, bf16[1536,128]{1,0:T(8,128)(2,1)S(1)}, u32[]{:S(2)}, u32[]{:S(2)}) collective-permute-start(bf16[1536,128]{1,0:T(8,128)(2,1)S(1)} %get-tuple-element.131), channel_id=1, source_target_pairs={{0,1},{1,0},{2,3},{3,2},{4,5},{5,4},{6,7},{7,6},{8,9},{9,8},{10,11... | collective-permute-start | bytes 1179656 | tf_op jit(solution)/shard_map/mlp/ppermute | solution.py:696
  66.1 14.2 %collective-permute-start.14 = (bf16[192,512]{1,0:T(8,128)(2,1)S(1)}, bf16[192,512]{1,0:T(8,128)(2,1)S(1)}, u32[]{:S(2)}, u32[]{:S(2)}) collective-permute-start(bf16[192,512]{1,0:T(8,128)(2,1)S(1)} %get-tuple-element.140), channel_id=1, source_target_pairs={{0,1},{1,0},{2,3},{3,2},{4,5},{5,4},{6,7},{7,6},{8,9},{9,8},{10,11... | collective-permute-start | bytes 589832 | tf_op jit(solution)/shard_map/d_att/ppermute | solution.py:696
  68.2 17.0 %collective-permute-start.15 = (bf16[192,512]{1,0:T(8,128)(2,1)S(1)}, bf16[192,512]{1,0:T(8,128)(2,1)S(1)}, u32[]{:S(2)}, u32[]{:S(2)}) collective-permute-start(bf16[192,512]{1,0:T(8,128)(2,1)S(1)} %get-tuple-element.141), channel_id=1, source_target_pairs={{0,2},{1,3},{2,0},{3,1},{4,6},{5,7},{6,4},{7,5},{8,10},{9,11},{10,... | collective-permute-start | bytes 589832 | tf_op jit(solution)/shard_map/d_att/ppermute | solution.py:696
  68.5 16.7 %collective-permute-start.16 = (bf16[192,512]{1,0:T(8,128)(2,1)S(1)}, bf16[192,512]{1,0:T(8,128)(2,1)S(1)}, u32[]{:S(2)}, u32[]{:S(2)}) collective-permute-start(bf16[192,512]{1,0:T(8,128)(2,1)S(1)} %get-tuple-element.142), channel_id=1, source_target_pairs={{0,3},{1,2},{2,1},{3,0},{4,7},{5,6},{6,5},{7,4},{8,11},{9,10},{10,... | collective-permute-start | bytes 589832 | tf_op jit(solution)/shard_map/d_att/ppermute | solution.py:696
  73.2 25.1 %collective-permute-start.21 = (bf16[384,1152]{1,0:T(8,128)(2,1)S(1)}, bf16[384,1152]{1,0:T(8,128)(2,1)S(1)}, u32[]{:S(2)}, u32[]{:S(2)}) collective-permute-start(bf16[384,1152]{1,0:T(8,128)(2,1)S(1)} %get-tuple-element.174), channel_id=1, source_target_pairs={{0,8},{4,12},{8,0},{12,4},{16,24},{20,28},{24,16},{28,20},{1,9},{5... | collective-permute-start | bytes 2654216 | tf_op jit(solution)/shard_map/grads_a/ppermute | solution.py:696
  77.3 21.0 %collective-permute-start.22 = (bf16[384,1152]{1,0:T(8,128)(2,1)S(1)}, bf16[384,1152]{1,0:T(8,128)(2,1)S(1)}, u32[]{:S(2)}, u32[]{:S(2)}) collective-permute-start(bf16[384,1152]{1,0:T(8,128)(2,1)S(1)} %get-tuple-element.176), channel_id=1, source_target_pairs={{0,16},{4,20},{8,24},{12,28},{16,0},{20,4},{24,8},{28,12},{1,17},{... | collective-permute-start | bytes 2654216 | tf_op jit(solution)/shard_map/grads_b/ppermute | solution.py:696
  85.1 10.5 %collective-permute-start.17 = (bf16[768,128]{1,0:T(8,128)(2,1)S(1)}, bf16[768,128]{1,0:T(8,128)(2,1)S(1)}, u32[]{:S(2)}, u32[]{:S(2)}) collective-permute-start(bf16[768,128]{1,0:T(8,128)(2,1)S(1)} %get-tuple-element.143), channel_id=1, source_target_pairs={{0,2},{1,3},{2,0},{3,1},{4,6},{5,7},{6,4},{7,5},{8,10},{9,11},{10,... | collective-permute-start | bytes 589832 | tf_op jit(solution)/shard_map/mlp/ppermute | solution.py:696
  95.7 1.9 %collective-permute-start.20 = (bf16[416,576]{1,0:T(8,128)(2,1)S(1)}, bf16[416,576]{1,0:T(8,128)(2,1)S(1)}, u32[]{:S(2)}, u32[]{:S(2)}) collective-permute-start(bf16[416,576]{1,0:T(8,128)(2,1)S(1)} %get-tuple-element.170), channel_id=1, source_target_pairs={{0,4},{4,0},{8,12},{12,8},{16,20},{20,16},{24,28},{28,24},{1,5},{5... | collective-permute-start | bytes 1437704 | tf_op jit(solution)/shard_map/qkv_core/ppermute | solution.py:696
  95.7 11.5 %collective-permute-start.18 = (bf16[1536,128]{1,0:T(8,128)(2,1)S(1)}, bf16[1536,128]{1,0:T(8,128)(2,1)S(1)}, u32[]{:S(2)}, u32[]{:S(2)}) collective-permute-start(bf16[1536,128]{1,0:T(8,128)(2,1)S(1)} %get-tuple-element.164), channel_id=1, source_target_pairs={{0,1},{1,0},{2,3},{3,2},{4,5},{5,4},{6,7},{7,6},{8,9},{9,8},{10,11... | collective-permute-start | bytes 1179656 | tf_op jit(solution)/shard_map/back/ppermute | solution.py:696
  99.3 2.2 %collective-permute-start.23 = (bf16[192,768]{1,0:T(8,128)(2,1)S(1)}, bf16[192,768]{1,0:T(8,128)(2,1)S(1)}, u32[]{:S(2)}, u32[]{:S(2)}) collective-permute-start(bf16[192,768]{1,0:T(8,128)(2,1)S(1)} %get-tuple-element.178), channel_id=1, source_target_pairs={{0,4},{4,0},{8,12},{12,8},{16,20},{20,16},{24,28},{28,24},{1,5},{5... | collective-permute-start | bytes 884744 | tf_op jit(solution)/shard_map/grads_core/ppermute | solution.py:696
  99.5 2.0 %collective-permute-start.24 = (bf16[192,768]{1,0:T(8,128)(2,1)S(1)}, bf16[192,768]{1,0:T(8,128)(2,1)S(1)}, u32[]{:S(2)}, u32[]{:S(2)}) collective-permute-start(bf16[192,768]{1,0:T(8,128)(2,1)S(1)} %get-tuple-element.179), channel_id=1, source_target_pairs={{0,4},{4,0},{8,12},{12,8},{16,20},{20,16},{24,28},{28,24},{1,5},{5... | collective-permute-start | bytes 884744 | tf_op jit(solution)/shard_map/grads_core/ppermute | solution.py:696
  99.9 1.9 %collective-permute-start.25 = (bf16[192,768]{1,0:T(8,128)(2,1)S(1)}, bf16[192,768]{1,0:T(8,128)(2,1)S(1)}, u32[]{:S(2)}, u32[]{:S(2)}) collective-permute-start(bf16[192,768]{1,0:T(8,128)(2,1)S(1)} %get-tuple-element.180), channel_id=1, source_target_pairs={{0,4},{4,0},{8,12},{12,8},{16,20},{20,16},{24,28},{28,24},{1,5},{5... | collective-permute-start | bytes 884744 | tf_op jit(solution)/shard_map/grads_core/ppermute | solution.py:696
  100.0 10.1 %collective-permute-start.27 = (bf16[224,576]{1,0:T(8,128)(2,1)S(1)}, bf16[224,576]{1,0:T(8,128)(2,1)S(1)}, u32[]{:S(2)}, u32[]{:S(2)}) collective-permute-start(bf16[224,576]{1,0:T(8,128)(2,1)S(1)} %get-tuple-element.184), channel_id=1, source_target_pairs={{0,8},{4,12},{8,0},{12,4},{16,24},{20,28},{24,16},{28,20},{1,9},{5... | collective-permute-start | bytes 774152 | tf_op jit(solution)/shard_map/qkv_x/ppermute | solution.py:696
  102.5 7.5 %collective-permute-start.26 = (bf16[96,1152]{1,0:T(8,128)(2,1)S(1)}, bf16[96,1152]{1,0:T(8,128)(2,1)S(1)}, u32[]{:S(2)}, u32[]{:S(2)}) collective-permute-start(bf16[96,1152]{1,0:T(8,128)(2,1)S(1)} %get-tuple-element.181), channel_id=1, source_target_pairs={{0,16},{4,20},{8,24},{12,28},{16,0},{20,4},{24,8},{28,12},{1,17},{... | collective-permute-start | bytes 663560 | tf_op jit(solution)/shard_map/grads_a/ppermute | solution.py:696
  104.1 9.7 %collective-permute-start.28 = (bf16[96,1152]{1,0:T(8,128)(2,1)S(1)}, bf16[96,1152]{1,0:T(8,128)(2,1)S(1)}, u32[]{:S(2)}, u32[]{:S(2)}) collective-permute-start(bf16[96,1152]{1,0:T(8,128)(2,1)S(1)} %get-tuple-element.188), channel_id=1, source_target_pairs={{0,8},{4,12},{8,0},{12,4},{16,24},{20,28},{24,16},{28,20},{1,9},{5... | collective-permute-start | bytes 663560 | tf_op jit(solution)/shard_map/grads_b/ppermute | solution.py:696
  107.3 13.2 %collective-permute-start.19 = (bf16[768,128]{1,0:T(8,128)(2,1)S(1)}, bf16[768,128]{1,0:T(8,128)(2,1)S(1)}, u32[]{:S(2)}, u32[]{:S(2)}) collective-permute-start(bf16[768,128]{1,0:T(8,128)(2,1)S(1)} %get-tuple-element.166), channel_id=1, source_target_pairs={{0,2},{1,3},{2,0},{3,1},{4,6},{5,7},{6,4},{7,5},{8,10},{9,11},{10,... | collective-permute-start | bytes 589832 | tf_op jit(solution)/shard_map/back/ppermute | solution.py:696
  110.7 5.5 %collective-permute-start.29 = (bf16[128,576]{1,0:T(8,128)(2,1)S(1)}, bf16[128,576]{1,0:T(8,128)(2,1)S(1)}, u32[]{:S(2)}, u32[]{:S(2)}) collective-permute-start(bf16[128,576]{1,0:T(8,128)(2,1)S(1)} %get-tuple-element.189), channel_id=1, source_target_pairs={{0,16},{4,20},{8,24},{12,28},{16,0},{20,4},{24,8},{28,12},{1,17},{... | collective-permute-start | bytes 442376 | tf_op jit(solution)/shard_map/qkv_y/ppermute | solution.py:696
  116.9 7.5 %collective-permute-start.31 = (bf16[288,128]{1,0:T(8,128)(2,1)S(1)}, bf16[288,128]{1,0:T(8,128)(2,1)S(1)}, u32[]{:S(2)}, u32[]{:S(2)}) collective-permute-start(bf16[288,128]{1,0:T(8,128)(2,1)S(1)} %get-tuple-element.193), channel_id=1, source_target_pairs={{0,2},{1,3},{2,0},{3,1},{4,6},{5,7},{6,4},{7,5},{8,10},{9,11},{10,... | collective-permute-start | bytes 221192 | tf_op jit(solution)/shard_map/out/ppermute | solution.py:696
  117.7 6.7 %collective-permute-start.32 = (bf16[288,128]{1,0:T(8,128)(2,1)S(1)}, bf16[288,128]{1,0:T(8,128)(2,1)S(1)}, u32[]{:S(2)}, u32[]{:S(2)}) collective-permute-start(bf16[288,128]{1,0:T(8,128)(2,1)S(1)} %get-tuple-element.194), channel_id=1, source_target_pairs={{0,3},{1,2},{2,1},{3,0},{4,7},{5,6},{6,5},{7,4},{8,11},{9,10},{10,... | collective-permute-start | bytes 221192 | tf_op jit(solution)/shard_map/out/ppermute | solution.py:696
  119.6 5.4 %collective-permute-start.30 = (bf16[288,128]{1,0:T(8,128)(2,1)S(1)}, bf16[288,128]{1,0:T(8,128)(2,1)S(1)}, u32[]{:S(2)}, u32[]{:S(2)}) collective-permute-start(bf16[288,128]{1,0:T(8,128)(2,1)S(1)} %get-tuple-element.192), channel_id=1, source_target_pairs={{0,1},{1,0},{2,3},{3,2},{4,5},{5,4},{6,7},{7,6},{8,9},{9,8},{10,11... | collective-permute-start | bytes 221192 | tf_op jit(solution)/shard_map/out/ppermute | solution.py:696
